TPU v7x, 32 devices: a whole 2x2x4 slice. The times are simulated.
32 devices in a mesh: items: 4 (over y, x), heads: 8 (over z, core).
Axes of the slice: x: 2, y: 2, z: 4, core: 2. Of those that a mesh axis runs over, the one named last changes fastest.
Arguments:
- frames: bfloat16 [2, 8192, 1024], P(None, ('items', 'heads')), may hold values from -6 to 6
- cotangent: bfloat16 [2, 8192, 1024], P(None, ('items', 'heads')), may hold values from -6 to 6
- bucket_counts: int32 [2, 4, 2], P(None, 'items'), may hold values from 0 to 4, as said below
- gains: float32 [6, 1024], replicated, may hold values from 0.1 to 1.9
- w_ffn1_in: bfloat16 [1024, 4096], replicated, may hold values from -0.1875 to 0.1875
- w_ffn1_out: bfloat16 [4096, 1024], replicated, may hold values from -0.1875 to 0.1875
- w_qkv: bfloat16 [1024, 3072], replicated, may hold values from -0.1875 to 0.1875
- w_out: bfloat16 [1024, 1024], replicated, may hold values from -1 to 1
- w_point_in: bfloat16 [1024, 2048], replicated, may hold values from -0.1875 to 0.1875
- w_depth: bfloat16 [5, 1024], replicated, may hold values from -2.5 to 2.5
- w_point_out: bfloat16 [1024, 1024], replicated, may hold values from -0.1875 to 0.1875
- w_ffn2_in: bfloat16 [1024, 4096], replicated, may hold values from -0.1875 to 0.1875
- w_ffn2_out: bfloat16 [4096, 1024], replicated, may hold values from -0.1875 to 0.1875
Outputs:
- layer_out: bfloat16 [2, 8192, 1024], P(None, ('items', 'heads'))
- frames_grad: bfloat16 [2, 8192, 1024], P(None, ('items', 'heads'))
- gains_grad: float32 [6, 1024], replicated
- ffn1_in_grad: float32 [1024, 4096], P('heads', 'items')
- ffn1_out_grad: float32 [4096, 1024], P('heads', 'items')
- qkv_grad: float32 [1024, 3072], P('heads', 'items')
- out_grad: float32 [1024, 1024], P('heads', 'items')
- point_in_grad: float32 [1024, 2048], P('heads', 'items')
- depth_grad: float32 [5, 1024], replicated
- point_out_grad: float32 [1024, 1024], P('heads', 'items')
- ffn2_in_grad: float32 [1024, 4096], P('heads', 'items')
- ffn2_out_grad: float32 [4096, 1024], P('heads', 'items')
Inputs may be any that keep to these rules, and one draw needn't show every extreme that they name: bucket_counts[m, g] = (n_long, n_short): group g of micro-batch m holds n_long utterances of 1500 frames first, then n_short = (2048 - n_long 1500) // 500 utterances of 500 frames, then any remaining frames as one more utterance.
All inputs are finite; a program needn't handle non-finite values.
Results may differ from a plain program's by a relative error of at most 0.02.
Values may be sent and summed in bfloat16 or wider, within the bound.
No kernel may reach another device: no remote copies, remote signals or barrier semaphores. Data moves between devices by JAX's collectives and lax.ppermute only.
A program may use at most 320 MiB of HBM per device.

v0:
```python
import copy
import functools

import jax
import jax.numpy as jnp
from jax import lax
from jax.experimental import pallas as pl
from jax.experimental.pallas import tpu as pltpu
from jax.sharding import PartitionSpec as P

HEADS = 16
KERNEL = 5
LONG = 1500
SHORT = 500
EPS = 1e-05
ROPE_BASE = 10000.0
BLOCK = 512
INNER_FWD = 1024
INNER_BWD = 512
LANES = 128
BIG = 1e30
VMEM_LIMIT = 56 << 20
F32 = jnp.float32
BF16 = jnp.bfloat16
NN = (((1,), (0,)), ((), ()))
NT = (((1,), (1,)), ((), ()))
EVERY = ("items", "heads")
FIRST = [("items", 1), ("items", 2)]


def dot(left, right, dims=NN):
    return lax.dot_general(left, right, dims, preferred_element_type=F32)


def silu_slope(field):
    gate_sig = jax.nn.sigmoid(field)
    return gate_sig * (1.0 + field * (1.0 - gate_sig))


def layer_norm(field, gain_row):
    centred = field - jnp.mean(field, -1, keepdims=True)
    inverse = lax.rsqrt(jnp.mean(centred * centred, -1, keepdims=True) + EPS)
    normed = centred * inverse
    return (normed * gain_row, normed, inverse)


def norm_back(upstream, normed, inverse, gain_row):
    scaled = upstream * gain_row
    through = inverse * (
        scaled
        - jnp.mean(scaled, -1, keepdims=True)
        - normed * jnp.mean(scaled * normed, -1, keepdims=True)
    )
    return (through, jnp.sum(upstream * normed, 0, keepdims=True))


def segment_ids(position, long_count, short_count, group_len):
    long_end = long_count * LONG
    short_end = long_end + short_count * SHORT
    segments = jnp.where(
        position < long_end, position // LONG, long_count + (position - long_end) // SHORT
    )
    segments = jnp.where(position < short_end, segments, long_count + short_count)
    return jnp.where((position < 0) | (position >= group_len), -1, segments)


def compiler_params():
    return pltpu.CompilerParams(vmem_limit_bytes=VMEM_LIMIT)


def whole(shape):
    return pl.BlockSpec(shape, lambda *_: (0,) * len(shape))


def cost(flops, bytes_accessed, transcendentals=0):
    return pl.CostEstimate(
        flops=flops, bytes_accessed=bytes_accessed, transcendentals=transcendentals
    )


def segment_bounds(counts, place, group):
    longs, shorts = counts
    long_end = longs * LONG
    short_end = long_end + shorts * SHORT
    start = jnp.where(place < longs, place * LONG, long_end + (place - longs) * SHORT)
    size = jnp.where(place < longs, LONG, SHORT)
    last = place == longs + shorts
    return (jnp.where(last, short_end, start), jnp.where(last, group, start + size), place <= longs + shorts)


def member_lanes(counts, first, rows, group, shift=0):
    shape = (rows, LANES)
    place = lax.broadcasted_iota(jnp.int32, (8, LANES), 1) - shift
    start, end, there = segment_bounds(counts, place, group)
    start = jnp.where(there & (place >= 0), start, group)
    start, end = start[:1], end[:1]
    frame = first + lax.broadcasted_iota(jnp.int32, shape, 0)
    return (frame >= start) & (frame < end)


def block_range(counts, step, group, inner):
    longs, shorts = counts
    long_end = longs * LONG
    short_end = long_end + shorts * SHORT

    def number(frame):
        place = jnp.where(frame < long_end, frame // LONG, longs + (frame - long_end) // SHORT)
        return jnp.where(frame < short_end, place, longs + shorts)

    first = segment_bounds(counts, number(step * BLOCK), group)[0]
    last = segment_bounds(counts, number(step * BLOCK + BLOCK - 1), group)[1]
    return (first // inner, (last + inner - 1) // inner)


def head_lanes(shape, head, size):
    lane = lax.broadcasted_iota(jnp.int32, shape, 1)
    return (lane >= head * size) & (lane < (head + 1) * size)


def split_three(v):
    hi = v.astype(BF16).astype(F32)
    rest = v - hi
    mid = rest.astype(BF16).astype(F32)
    return (hi, mid, rest - mid)


def spread_columns(columns, shape):
    lane = lax.broadcasted_iota(jnp.int32, shape, 1)
    out = jnp.zeros(shape, F32)
    for place, column in enumerate(columns):
        out = jnp.where(lane == place, column, out)
    return out


def chunk_rows(ref, lead, step):
    places, chunks, frames = ref.shape[0], ref.shape[-3], ref.shape[-2]
    per = BLOCK // frames
    steps = places // per
    at = (pl.ds(step % steps * per, per),) + lead + (step // steps,)
    return ref[at].reshape(BLOCK, LANES)


def attn_fwd_kernel(
    heads, size, group, counts_ref, qkv_ref, out_ref, full_ref, lse_ref, kcat, v_all, s_scr
):
    step = pl.program_id(0)
    counts = (counts_ref[0], counts_ref[1])

    @pl.when(step == 0)
    def _():
        chunks = qkv_ref.shape[2]
        span = group // chunks
        for chunk in range(chunks):
            rows = slice(chunk * span, (chunk + 1) * span)
            kcat[rows, :LANES] = qkv_ref[:, 1, chunk].reshape(span, LANES)
            v_all[rows, :] = qkv_ref[:, 2, chunk].reshape(span, LANES)
        kcat[:, LANES:] = jnp.where(member_lanes(counts, 0, group, group), 0.0, -BIG).astype(BF16)

    q = chunk_rows(qkv_ref, (0,), step).astype(F32) * (size ** -0.5)
    member = jnp.where(member_lanes(counts, step * BLOCK, BLOCK, group), 1.0, 0.0).astype(BF16)
    queries = []
    for head in range(heads):
        mine = jnp.where(head_lanes(q.shape, head, size), q, 0.0).astype(BF16)
        queries.append(jnp.concatenate([mine, member], 1))
    low, high = block_range(counts, step, group, INNER_FWD)

    def scores(j, tops):
        keys = kcat[pl.ds(pl.multiple_of(j * INNER_FWD, INNER_FWD), INNER_FWD), :]
        new = []
        for head in range(heads):
            s = dot(queries[head], keys, NT)
            s_scr[head, j] = s
            top = tops[head]
            for part in range(INNER_FWD // LANES):
                top = jnp.maximum(top, s[:, part * LANES : (part + 1) * LANES])
            new.append(top)
        return tuple(new)

    start = tuple(jnp.full((BLOCK, LANES), -BIG, F32) for _ in range(heads))
    tops = lax.fori_loop(low, high, scores, start)
    tops = [jnp.max(t, 1, keepdims=True) for t in tops]
    tops = [jnp.broadcast_to(t, (BLOCK, LANES)) for t in tops]

    def weigh(j, carried):
        sums, accs = carried
        values = v_all[pl.ds(pl.multiple_of(j * INNER_FWD, INNER_FWD), INNER_FWD), :]
        new_sums, new_accs = [], []
        for head in range(heads):
            total = sums[head]
            parts = []
            for part in range(INNER_FWD // LANES):
                p = jnp.exp(s_scr[head, j, :, part * LANES : (part + 1) * LANES] - tops[head])
                total = total + p
                parts.append(p.astype(BF16))
            new_sums.append(total)
            new_accs.append(accs[head] + dot(jnp.concatenate(parts, 1), values))
        return (tuple(new_sums), tuple(new_accs))

    zeros = tuple(jnp.zeros((BLOCK, LANES), F32) for _ in range(heads))
    sums, accs = lax.fori_loop(low, high, weigh, (zeros, zeros))
    result = None
    for head in range(heads):
        total = jnp.sum(sums[head], 1, keepdims=True)
        mine = accs[head] / total
        if result is None:
            result = mine
        else:
            result = jnp.where(head_lanes(mine.shape, head, size), mine, result)
        lse_ref[head] = tops[head] + jnp.log(jnp.broadcast_to(total, (BLOCK, LANES)))
    full_ref[...] = result
    out_ref[...] = result.astype(BF16).reshape(out_ref.shape)


def attend_forward(qkv, counts, size):
    places, _, chunks, frames, _ = qkv.shape
    group = places * chunks * frames
    heads = LANES // size
    per = BLOCK // frames
    each = places // per
    return pl.pallas_call(
        functools.partial(attn_fwd_kernel, heads, size, group),
        grid=(group // BLOCK,),
        in_specs=[pl.BlockSpec(memory_space=pltpu.SMEM), whole(qkv.shape)],
        out_specs=[
            pl.BlockSpec((per, 1, frames, LANES), lambda i: (i % each, i // each, 0, 0)),
            pl.BlockSpec((BLOCK, LANES), lambda i: (i, 0)),
            pl.BlockSpec((heads, BLOCK, LANES), lambda i: (0, i, 0)),
        ],
        out_shape=[
            jax.ShapeDtypeStruct((places, chunks, frames, LANES), BF16),
            jax.ShapeDtypeStruct((group, LANES), F32),
            jax.ShapeDtypeStruct((heads, group, LANES), F32),
        ],
        scratch_shapes=[
            pltpu.VMEM((group, 2 * LANES), BF16),
            pltpu.VMEM((group, LANES), BF16),
            pltpu.VMEM((heads, group // INNER_FWD, BLOCK, INNER_FWD), F32),
        ],
        compiler_params=compiler_params(),
        cost_estimate=cost(16 * group * group * LANES, 6 << 20, heads * group * group),
        name="attend_forward",
    )(counts, qkv)


def attn_bwd_kernel(
    heads, size, group, counts_ref, qkv_ref, full_ref, lse_ref, grad_ref, out_ref,
    qcat, gcat, k_turned, dq_turned,
):
    step = pl.program_id(0)
    counts = (counts_ref[0], counts_ref[1])
    blocks = group // BLOCK
    places, _, _, frames, _ = qkv_ref.shape
    per = BLOCK // frames
    each = places // per

    def put(part, j, value):
        out_ref[pl.ds(j % each * per, per), part, j // each] = value.astype(BF16).reshape(
            per, frames, LANES
        )

    @pl.when(step == 0)
    def _():
        dq_turned[...] = jnp.zeros_like(dq_turned)

        def prepare(j, _):
            rows = pl.ds(pl.multiple_of(j * BLOCK, BLOCK), BLOCK)
            lane = lax.broadcasted_iota(jnp.int32, (BLOCK, LANES), 1)
            q = chunk_rows(qkv_ref, (0,), j).astype(F32) * (size ** -0.5)
            g = chunk_rows(grad_ref, (), j).astype(F32)
            product = g * full_ref[rows, :]
            member = jnp.where(member_lanes(counts, j * BLOCK, BLOCK, group, 3), 1.0, 0.0)
            for head in range(heads):
                own = head_lanes((BLOCK, LANES), head, size)
                lse = lse_ref[head, rows, :]
                spread = spread_columns(split_three(lse), (BLOCK, LANES))
                delta = jnp.sum(jnp.where(own, product, 0.0), 1, keepdims=True)
                delta = jnp.broadcast_to(delta, (BLOCK, LANES))
                qcat[head, rows, :LANES] = jnp.where(own, q, 0.0).astype(BF16)
                qcat[head, rows, LANES:] = jnp.where(lane < 3, -spread, member).astype(BF16)
                gcat[head, rows, :LANES] = jnp.where(own, g, 0.0).astype(BF16)
                spread = spread_columns(split_three(delta), (BLOCK, LANES))
                gcat[head, rows, LANES:] = (-spread).astype(BF16)
            k = chunk_rows(qkv_ref, (1,), j).astype(F32)
            k_turned[j] = jnp.transpose(k).astype(BF16)
            return 0

        lax.fori_loop(0, blocks, prepare, 0)

    lane = lax.broadcasted_iota(jnp.int32, (BLOCK, LANES), 1)
    member = member_lanes(counts, step * BLOCK, BLOCK, group, 3)
    tail = jnp.where(lane < 3, 1.0, jnp.where(member, 0.0, -BIG)).astype(BF16)
    keys = jnp.concatenate([chunk_rows(qkv_ref, (1,), step), tail], 1)
    ones = jnp.where(lane < 3, 1.0, 0.0).astype(BF16)
    values = jnp.concatenate([chunk_rows(qkv_ref, (2,), step), ones], 1)

    def one(j, carried):
        dk, dv = carried
        cols = pl.ds(pl.multiple_of(j * INNER_BWD, INNER_BWD), INNER_BWD)
        for head in range(heads):
            qc = qcat[head, cols, :]
            gc = gcat[head, cols, :]
            p = jnp.exp(dot(keys, qc, NT))
            ds = (p * dot(values, gc, NT)).astype(BF16)
            dv = dv + dot(p.astype(BF16), gc[:, :LANES])
            dk = dk + dot(ds, qc[:, :LANES])
            mine = slice(head * size, (head + 1) * size)
            dq_turned[j, mine, :] += dot(k_turned[step, mine, :], ds)
        return (dk, dv)

    zero = jnp.zeros((BLOCK, LANES), F32)
    low, high = block_range(counts, step, group, INNER_BWD)
    dk, dv = lax.fori_loop(low, high, one, (zero, zero))
    put(1, step, dk)
    put(2, step, dv)

    @pl.when(step == blocks - 1)
    def _():
        def finish(j, _):
            put(0, j, jnp.transpose(dq_turned[j]) * (size ** -0.5))
            return 0

        lax.fori_loop(0, blocks, finish, 0)


def attend_backward(qkv, counts, size, full, lse, grad):
    places, _, chunks, frames, _ = qkv.shape
    group = places * chunks * frames
    heads = LANES // size
    steps = group // BLOCK
    return pl.pallas_call(
        functools.partial(attn_bwd_kernel, heads, size, group),
        grid=(steps,),
        in_specs=[
            pl.BlockSpec(memory_space=pltpu.SMEM),
            whole(qkv.shape),
            whole(full.shape),
            whole(lse.shape),
            whole(grad.shape),
        ],
        out_specs=whole(qkv.shape),
        out_shape=jax.ShapeDtypeStruct(qkv.shape, BF16),
        scratch_shapes=[
            pltpu.VMEM((heads, group, 2 * LANES), BF16),
            pltpu.VMEM((heads, group, 2 * LANES), BF16),
            pltpu.VMEM((steps, LANES, BLOCK), BF16),
            pltpu.VMEM((group // INNER_BWD, LANES, INNER_BWD), F32),
        ],
        compiler_params=compiler_params(),
        cost_estimate=cost(32 * group * group * LANES, 9 << 20, heads * group * group),
        name="attend_backward",
    )(counts, qkv, full, lse, grad)


def half_gate(field):
    return 0.5 * jnp.tanh(0.5 * field) + 0.5


def hidden_units(pre):
    gate = half_gate(pre)
    hidden = pre * gate
    return (hidden.astype(BF16), (gate + hidden * (1.0 - gate)).astype(BF16))


def ffn_fwd_kernel(
    x_ref, gain_ref, last_gain_ref, up_ref, win_ref, wout_ref,
    out_ref, down_ref, gain_grad_ref, slope_ref, hid_ref, entered_ref, total,
):
    step = pl.program_id(0)

    @pl.when(step == 0)
    def _():
        entered_ref[...] = layer_norm(x_ref[...], gain_ref[...])[0].astype(BF16)
        total[...] = jnp.zeros_like(total)

    hidden, slope = hidden_units(dot(entered_ref[...], win_ref[...]))
    slope_ref[...] = slope
    hid_ref[...] = hidden
    total[...] += dot(hidden, wout_ref[...])

    @pl.when(step == pl.num_programs(0) - 1)
    def _():
        gain = last_gain_ref[...]
        shaped, normed, inverse = layer_norm(x_ref[...] + 0.5 * total[...], gain)
        out_ref[...] = shaped.astype(BF16)
        through, grad_gain = norm_back(up_ref[...].astype(F32), normed, inverse, gain)
        down_ref[...] = through
        gain_grad_ref[...] = grad_gain


def ffn_forward(stream, gain_row, weight_in, weight_out, last_gain, upstream):
    rows, model = stream.shape
    units = weight_in.shape[1]
    wide = 512
    return pl.pallas_call(
        ffn_fwd_kernel,
        grid=(units // wide,),
        in_specs=[
            whole((rows, model)),
            whole((1, model)),
            whole((1, model)),
            whole((rows, model)),
            pl.BlockSpec((model, wide), lambda s: (0, s)),
            pl.BlockSpec((wide, model), lambda s: (s, 0)),
        ],
        out_specs=[whole((rows, model)), whole((rows, model)), whole((1, model))]
        + [pl.BlockSpec((rows, wide), lambda s: (0, s))] * 2
        + [whole((rows, model))],
        out_shape=[
            jax.ShapeDtypeStruct((rows, model), BF16),
            jax.ShapeDtypeStruct((rows, model), F32),
            jax.ShapeDtypeStruct((1, model), F32),
            jax.ShapeDtypeStruct((rows, units), BF16),
            jax.ShapeDtypeStruct((rows, units), BF16),
            jax.ShapeDtypeStruct((rows, model), BF16),
        ],
        scratch_shapes=[pltpu.VMEM((rows, model), F32)],
        compiler_params=compiler_params(),
        cost_estimate=cost(4 * rows * model * units, 4 * model * units + 4 * rows * units),
        name="ffn_forward",
    )(stream, gain_row, last_gain, upstream, weight_in, weight_out)


def ffn_bwd_kernel(
    x_ref, gain_ref, up_ref, slope_ref, win_ref, wout_ref,
    down_ref, gain_grad_ref, half_ref, grad_ref, total,
):
    step = pl.program_id(0)

    @pl.when(step == 0)
    def _():
        half_ref[...] = (0.5 * up_ref[...]).astype(BF16)
        total[...] = jnp.zeros_like(total)

    grad = (dot(half_ref[...], wout_ref[...], NT) * slope_ref[...].astype(F32)).astype(BF16)
    grad_ref[...] = grad
    total[...] += dot(grad, win_ref[...], NT)

    @pl.when(step == pl.num_programs(0) - 1)
    def _():
        gain = gain_ref[...]
        normed, inverse = layer_norm(x_ref[...].astype(F32), gain)[1:]
        through, grad_gain = norm_back(total[...], normed, inverse, gain)
        down_ref[...] = up_ref[...] + through
        gain_grad_ref[...] = grad_gain


def ffn_backward(upstream, stream, slope, gain_row, weight_in, weight_out):
    rows, model = stream.shape
    units = weight_in.shape[1]
    wide = 512
    return pl.pallas_call(
        ffn_bwd_kernel,
        grid=(units // wide,),
        in_specs=[
            whole((rows, model)),
            whole((1, model)),
            whole((rows, model)),
            pl.BlockSpec((rows, wide), lambda s: (0, s)),
            pl.BlockSpec((model, wide), lambda s: (0, s)),
            pl.BlockSpec((wide, model), lambda s: (s, 0)),
        ],
        out_specs=[
            whole((rows, model)),
            whole((1, model)),
            whole((rows, model)),
            pl.BlockSpec((rows, wide), lambda s: (0, s)),
        ],
        out_shape=[
            jax.ShapeDtypeStruct((rows, model), F32),
            jax.ShapeDtypeStruct((1, model), F32),
            jax.ShapeDtypeStruct((rows, model), BF16),
            jax.ShapeDtypeStruct((rows, units), BF16),
        ],
        scratch_shapes=[pltpu.VMEM((rows, model), F32)],
        compiler_params=compiler_params(),
        cost_estimate=cost(4 * rows * model * units, 4 * model * units + 6 * rows * units),
        name="ffn_backward",
    )(stream, gain_row, upstream, slope, weight_in, weight_out)


def hidden_kernel(up_ref, slope_ref, wout_ref, half_ref, grad_ref):
    @pl.when(pl.program_id(0) == 0)
    def _():
        half_ref[...] = (0.5 * up_ref[...]).astype(BF16)

    grad = dot(half_ref[...], wout_ref[...], NT) * slope_ref[...].astype(F32)
    grad_ref[...] = grad.astype(BF16)


def hidden_gradient(upstream, slope, weight_out):
    rows, model = upstream.shape
    units = weight_out.shape[0]
    wide = 512
    return pl.pallas_call(
        hidden_kernel,
        grid=(units // wide,),
        in_specs=[
            whole((rows, model)),
            pl.BlockSpec((rows, wide), lambda s: (0, s)),
            pl.BlockSpec((wide, model), lambda s: (s, 0)),
        ],
        out_specs=[whole((rows, model)), pl.BlockSpec((rows, wide), lambda s: (0, s))],
        out_shape=[
            jax.ShapeDtypeStruct((rows, model), BF16),
            jax.ShapeDtypeStruct((rows, units), BF16),
        ],
        compiler_params=compiler_params(),
        cost_estimate=cost(2 * rows * model * units, 2 * model * units + 6 * rows * units),
        name="hidden_gradient",
    )(upstream, slope, weight_out)


def down_kernel(
    x_ref, gain_ref, up_ref, grad_ref, weight_ref, down_ref, half_ref, gain_grad_ref, total
):
    step = pl.program_id(0)

    @pl.when(step == 0)
    def _():
        total[...] = jnp.zeros_like(total)

    total[...] += dot(grad_ref[...], weight_ref[...], NT)

    @pl.when(step == pl.num_programs(0) - 1)
    def _():
        gain = gain_ref[...]
        normed, inverse = layer_norm(x_ref[...].astype(F32), gain)[1:]
        through, grad_gain = norm_back(total[...], normed, inverse, gain)
        down = up_ref[...] + through
        down_ref[...] = down.astype(down_ref.dtype)
        half_ref[...] = (0.5 * down).astype(BF16)
        gain_grad_ref[...] = grad_gain


def stream_gradient(upstream, stream, grad, gain_row, weight, down_type):
    rows, model = stream.shape
    units = weight.shape[1]
    wide = 512
    return pl.pallas_call(
        down_kernel,
        grid=(units // wide,),
        in_specs=[
            whole((rows, model)),
            whole((1, model)),
            whole((rows, model)),
            pl.BlockSpec((rows, wide), lambda s: (0, s)),
            pl.BlockSpec((model, wide), lambda s: (0, s)),
        ],
        out_specs=[whole((rows, model)), whole((rows, model)), whole((1, model))],
        out_shape=[
            jax.ShapeDtypeStruct((rows, model), down_type),
            jax.ShapeDtypeStruct((rows, model), BF16),
            jax.ShapeDtypeStruct((1, model), F32),
        ],
        scratch_shapes=[pltpu.VMEM((rows, model), F32)],
        compiler_params=compiler_params(),
        cost_estimate=cost(2 * rows * model * units, 2 * model * units + 2 * rows * units),
        name="stream_gradient",
    )(stream, gain_row, upstream, grad, weight)


def turn(field, cosines, sines, size):
    lane = lax.broadcasted_iota(jnp.int32, field.shape, 1)
    half = size // 2
    width = field.shape[1]
    swapped = jnp.where(
        lane % size < half,
        pltpu.roll(field, width - half, 1),
        pltpu.roll(field, half, 1),
    )
    return field * cosines + swapped * sines


def rope_tables(position, size, width):
    half = size // 2
    freqs = jnp.exp(
        -jnp.log(jnp.float32(ROPE_BASE)) * jnp.arange(half, dtype=jnp.float32) / half
    )
    angles = position.astype(jnp.float32)[:, None] * freqs[None, :]
    cosines, sines = jnp.cos(angles), jnp.sin(angles)
    repeats = width // size
    return (
        jnp.tile(jnp.concatenate([cosines, cosines], 1), (1, repeats)),
        jnp.tile(jnp.concatenate([-sines, sines], 1), (1, repeats)),
    )


def front_kernel(
    size, ffn_steps, pieces, row_ref, x_ref, gain_ref, next_gain_ref, win_ref, wout_ref,
    wq_ref, wk_ref, wv_ref, cos_ref, sin_ref, *refs,
):
    refs = refs[-(6 + pieces) :]
    out_ref, slope_ref, hid_ref, entered_ref, next_ref = refs[:5]
    outs, total = refs[5:-1], refs[-1]
    step = pl.program_id(0)

    @pl.when(step == 0)
    def _():
        entered_ref[...] = layer_norm(x_ref[...].astype(F32), gain_ref[...])[0].astype(BF16)
        total[...] = jnp.zeros_like(total)

    @pl.when(step < ffn_steps)
    def _():
        hidden, slope = hidden_units(dot(entered_ref[...], win_ref[...]))
        slope_ref[...] = slope
        hid_ref[...] = hidden
        total[...] += dot(hidden, wout_ref[...])

    @pl.when(step == ffn_steps)
    def _():
        out = x_ref[...].astype(F32) + 0.5 * total[...]
        out_ref[...] = out
        next_ref[...] = layer_norm(out, next_gain_ref[...])[0].astype(BF16)

    each = (pl.num_programs(0) - ffn_steps) // pieces
    for piece, out in enumerate(outs):

        @pl.when((step >= ffn_steps) & ((step - ffn_steps) // each == piece))
        def _():
            for place, weight in enumerate((wq_ref, wk_ref, wv_ref)):
                made = dot(next_ref[...], weight[...])
                if place < 2:
                    made = turn(made, cos_ref[...], sin_ref[...], size)
                made = made.astype(BF16)
                for target in range(out.shape[0]):
                    out[target, place, 0] = made[:, target * LANES : (target + 1) * LANES]


def front(
    frames, row, gain_row, weight_in, weight_out, next_gain, weight, cosines, sines,
    places, chunks, size, before=(),
):
    rows, model = frames.shape
    units = weight_in.shape[1]
    wide = 512
    ffn_steps = units // wide
    turned_wide = cosines.shape[1]
    turns = model // turned_wide
    pieces = model // (places * LANES)
    each = turns // pieces
    piece = jax.ShapeDtypeStruct((places, 3, chunks, rows, LANES), BF16)

    def ffn_at(s, row):
        return jnp.minimum(s, ffn_steps - 1)

    def turn_at(s):
        return jnp.maximum(s - ffn_steps, 0)

    def piece_at(number):
        return lambda s, row: (
            jnp.clip(s - ffn_steps - number * each, 0, each - 1), 0, row[0], 0, 0
        )

    row_block = pl.BlockSpec((rows, model), lambda s, row: (row[0], 0))
    unit_block = pl.BlockSpec((rows, wide), lambda s, row: (row[0], ffn_at(s, row)))
    angle_block = pl.BlockSpec((rows, turned_wide), lambda s, row: (row[0], 0))
    out_shape = [
        jax.ShapeDtypeStruct((chunks * rows, model), F32),
        jax.ShapeDtypeStruct((chunks * rows, units), BF16),
        jax.ShapeDtypeStruct((chunks * rows, units), BF16),
        jax.ShapeDtypeStruct((chunks * rows, model), BF16),
        jax.ShapeDtypeStruct((chunks * rows, model), BF16),
    ] + [piece] * pieces
    in_specs = [
        whole((rows, model)),
        whole((1, model)),
        whole((1, model)),
        pl.BlockSpec((model, wide), lambda s, row: (0, ffn_at(s, row))),
        pl.BlockSpec((wide, model), lambda s, row: (ffn_at(s, row), 0)),
        pl.BlockSpec((model, turned_wide), lambda s, row: (0, turn_at(s))),
        pl.BlockSpec((model, turned_wide), lambda s, row: (0, turns + turn_at(s))),
        pl.BlockSpec((model, turned_wide), lambda s, row: (0, 2 * turns + turn_at(s))),
        angle_block,
        angle_block,
    ]
    grid_spec = pltpu.PrefetchScalarGridSpec(
        num_scalar_prefetch=1,
        grid=(ffn_steps + turns,),
        in_specs=in_specs + [pl.BlockSpec(memory_space=pl.ANY)] * len(before),
        out_specs=[row_block, unit_block, unit_block, row_block, row_block]
        + [
            pl.BlockSpec((turned_wide // LANES, 3, 1, rows, LANES), piece_at(number))
            for number in range(pieces)
        ],
        scratch_shapes=[pltpu.VMEM((rows, model), F32)],
    )
    return pl.pallas_call(
        functools.partial(front_kernel, size, ffn_steps, pieces),
        grid_spec=grid_spec,
        out_shape=out_shape,
        input_output_aliases={1 + len(in_specs) + i: i for i in range(len(before))},
        compiler_params=compiler_params(),
        cost_estimate=cost(
            4 * rows * model * units + 6 * rows * model * model,
            4 * model * units + 6 * model * model + 4 * rows * units + 16 * rows * model,
        ),
        name="front",
    )(
        row, frames, gain_row, next_gain, weight_in, weight_out, weight, weight, weight,
        cosines, sines, *before,
    )


def unturn_kernel(size, pieces, cos_ref, sin_ref, *refs):
    backs, out = refs[:pieces], refs[pieces]
    rotated = pl.program_id(0) < 2
    cosines = jnp.where(rotated, cos_ref[...], 1.0)
    sines = jnp.where(rotated, -sin_ref[...], 0.0)
    places, _, chunks, frames, _ = backs[0].shape
    wide = cosines.shape[1]
    per = wide // LANES
    for piece, back in enumerate(backs):
        for first in range(0, places, per):
            for chunk in range(chunks):
                rows = slice(chunk * frames, (chunk + 1) * frames)
                field = jnp.concatenate([back[first + i, 0, chunk] for i in range(per)], 1)
                made = turn(field.astype(F32), cosines[rows], sines[rows], size).astype(BF16)
                start = (piece * places + first) * LANES
                out[rows, start : start + wide] = made


def unturned(backs, cosines, sines, size):
    places, kinds, chunks, frames, _ = backs[0].shape
    pieces = len(backs)
    block = pl.BlockSpec((places, 1, chunks, frames, LANES), lambda s: (0, s, 0, 0, 0))
    model = pieces * places * LANES
    return pl.pallas_call(
        functools.partial(unturn_kernel, size, pieces),
        grid=(kinds,),
        in_specs=[whole(cosines.shape), whole(sines.shape)] + [block] * pieces,
        out_specs=pl.BlockSpec((chunks * frames, model), lambda s: (0, s)),
        out_shape=jax.ShapeDtypeStruct((chunks * frames, kinds * model), BF16),
        compiler_params=compiler_params(),
        cost_estimate=cost(0, 4 * chunks * frames * kinds * model),
        name="unturned",
    )(cosines, sines, *backs)


def flipped(axis_bit, count):
    axis, bit = axis_bit
    items, heads = count
    if axis == "items":
        return [(i * heads + h, (i ^ bit) * heads + h) for i in range(items) for h in range(heads)]
    return [(i * heads + h, i * heads + (h ^ bit)) for i in range(items) for h in range(heads)]


def swap(value, axis_bit):
    count = (lax.axis_size("items"), lax.axis_size("heads"))
    return lax.ppermute(value, EVERY, flipped(axis_bit, count))


def fenced(always, scatters, work):
    def run():
        return (work(), [scatter.move() for scatter in scatters])

    def empty():
        return jax.tree.map(lambda leaf: jnp.zeros(leaf.shape, leaf.dtype), jax.eval_shape(run))

    result, moved = lax.optimization_barrier(lax.cond(always, run, empty))
    for scatter, parts in zip(scatters, moved):
        scatter.take(parts)
    return result


def moved(scatter):
    scatter.take(scatter.move())


def other_core(value):
    return swap(value, ("heads", 1))


def exchange(value):
    half = lax.axis_size("heads") // 2
    groups = [[side * half + i for i in range(half)] for side in range(2)]
    return lax.all_to_all(
        value, "heads", split_axis=0, concat_axis=0, tiled=True, axis_index_groups=groups
    )


def across(value):
    return swap(value, ("heads", lax.axis_size("heads") // 2))


def gathered(own, other, side):
    return jnp.concatenate([jnp.where(side == 0, own, other), jnp.where(side == 0, other, own)], 0)


def parted(value, side):
    low, high = jnp.split(value, 2, 0)
    return (jnp.where(side == 0, low, high), jnp.where(side == 0, high, low))


def own_rows(left_ref, heads, core, target, first):
    rows, model = left_ref.shape
    each = model // heads
    for place in range(heads // 2):
        if each % LANES == 0:
            start = pl.multiple_of((2 * place + core) * each, each)
            mine = jnp.transpose(left_ref[:, pl.ds(start, each)].astype(F32)).astype(BF16)
        else:
            pair = left_ref[:, 2 * place * each : 2 * (place + 1) * each]
            pair = jnp.transpose(pair.astype(F32))
            mine = jnp.where(core == 0, pair[:each], pair[each:]).astype(BF16)
        for half in range(2):
            start = (half * (heads // 2) + place) * (each // 2)
            target[start : start + each // 2, first : first + rows] = mine[
                half * (each // 2) : (half + 1) * (each // 2)
            ]


def turned_items(left, items, own, target, first):
    rows, model = left.shape
    each = model // items
    for item in range(items):
        part = jnp.transpose(left[:, item * each : (item + 1) * each].astype(F32)).astype(BF16)
        place = pl.multiple_of((own ^ item) * each, each)
        target[pl.ds(place, each), first : first + rows] = part


def share_shapes(items, heads, model, columns):
    lead = 2 if items > 1 else 1
    shape = (lead, heads // 2, model // heads // 2, columns // items)
    return [jax.ShapeDtypeStruct(shape, BF16)] * (4 if items > 1 else 2)


def out_grad_kernel(place_ref, up_own, up_other, hid_own, hid_other, *refs):
    targets, turned = refs[:-1], refs[-1]
    rows, model = up_own.shape
    items = 4 if len(targets) == 4 else 1

    @pl.when(pl.program_id(0) == 0)
    def _():
        turned_items(up_own[...], items, place_ref[1], turned, 0)
        turned_items(up_other[...], items, place_ref[1], turned, rows)

    hidden = jnp.concatenate([hid_own[...], hid_other[...]], 0)
    grad = dot(turned[...], hidden).astype(BF16)
    wide = grad.shape[1]
    each = targets[0].shape[2]
    parts = model // items // (2 * each)
    for r in range(items):
        for part in range(parts):
            for half in range(2):
                first = ((r * parts + part) * 2 + half) * each
                piece = grad[first : first + each]
                if half == 0:
                    target, at = targets[2 * (r % 2)], r // 2
                else:
                    target, at = targets[1 + 2 * (r // 2)], r % 2
                target[at, 0, :, part * wide : (part + 1) * wide] = piece


def out_grad(upstream, hidden, heads, place, items):
    rows, model = upstream[0].shape
    units = hidden[0].shape[1]
    wide = units // heads
    shapes = share_shapes(items, heads, model, units)
    block = (shapes[0].shape[0], 1) + shapes[0].shape[2:]
    hid_block = pl.BlockSpec((rows, wide), lambda s, place: (0, 2 * s + place[0]))
    grid_spec = pltpu.PrefetchScalarGridSpec(
        num_scalar_prefetch=1,
        grid=(heads // 2,),
        in_specs=[whole((rows, model))] * 2 + [hid_block] * 2,
        out_specs=[pl.BlockSpec(block, lambda s, place: (0, s, 0, 0))] * len(shapes),
        scratch_shapes=[pltpu.VMEM((model, 2 * rows), BF16)],
    )
    return pl.pallas_call(
        out_grad_kernel,
        grid_spec=grid_spec,
        out_shape=shapes,
        compiler_params=compiler_params(),
        cost_estimate=cost(2 * rows * model * units, 2 * model * units + 4 * rows * units),
        name="out_grad",
    )(place, *upstream, *hidden)


def column_grad_kernel(heads, count, place_ref, *refs):
    lefts, refs = refs[: 2 * count], refs[2 * count :]
    rights, refs = refs[: 2 * count], refs[2 * count :]
    targets, turned = refs[:-count], refs[-count:]
    r = pl.program_id(0)
    rows = lefts[0].shape[0]

    @pl.when(r == 0)
    def _():
        for number in range(count):
            for other in range(2):
                own_rows(
                    lefts[2 * number + other], heads, place_ref[0], turned[number], other * rows
                )

    made = []
    for number in range(count):
        right = jnp.concatenate([rights[2 * number][...], rights[2 * number + 1][...]], 0)
        made.append(dot(turned[number][...], right).astype(BF16))
    made = made[0] if count == 1 else jnp.concatenate(made, 1)
    half = made.shape[0] // 2
    top, low = made[:half].reshape(targets[0].shape), made[half:].reshape(targets[0].shape)
    if len(targets) == 2:
        targets[0][...] = top
        targets[1][...] = low
        return

    @pl.when(r % 2 == 0)
    def _():
        targets[0][...] = top

    @pl.when(r % 2 == 1)
    def _():
        targets[2][...] = top

    @pl.when(r < 2)
    def _():
        targets[1][...] = low

    @pl.when(r >= 2)
    def _():
        targets[3][...] = low


def column_grads(lefts, rights, heads, place, items):
    rows, model = lefts[0][0].shape
    columns = sum(right[0].shape[1] for right in rights)
    shapes = share_shapes(items, heads, model, columns)
    block = (1,) + shapes[0].shape[1:]
    maps = [
        lambda r, place: (r // 2, 0, 0, 0),
        lambda r, place: (jnp.minimum(r, 1), 0, 0, 0),
        lambda r, place: (r // 3, 0, 0, 0),
        lambda r, place: (r // 3, 0, 0, 0),
    ]
    grid_spec = pltpu.PrefetchScalarGridSpec(
        num_scalar_prefetch=1,
        grid=(items,),
        in_specs=[whole((rows, model))] * (2 * len(lefts))
        + [
            pl.BlockSpec((rows, right[0].shape[1] // items), lambda r, place: (0, r ^ place[1]))
            for right in rights
            for _ in range(2)
        ],
        out_specs=[pl.BlockSpec(block, index) for index in maps[: len(shapes)]],
        scratch_shapes=[pltpu.VMEM((model // 2, 2 * rows), BF16)] * len(lefts),
    )
    return pl.pallas_call(
        functools.partial(column_grad_kernel, heads, len(lefts)),
        grid_spec=grid_spec,
        out_shape=shapes,
        compiler_params=compiler_params(),
        cost_estimate=cost(2 * rows * model * columns, 4 * model * columns),
        name="column_grads",
    )(place, *[part for left in lefts for part in left], *[part for right in rights for part in right])


class Scatter:
    def __init__(self, keep_top, keep_low, *sends):
        self.keep = [keep_top, keep_low]
        self.got, self.early = [], []
        self.route(list(sends), FIRST[: len(sends)])

    def route(self, sends, routes):
        self.sends, self.routes = sends, routes

    def move(self):
        return [swap(send, route) for send, route in zip(self.sends, self.routes)]

    def take(self, moved):
        self.early, self.got = self.got, moved
        self.route([], [])

    def second(self, sends):
        self.route(sends, FIRST[::-1][: len(sends)])


def second_kernel(*refs):
    count = len(refs) // 3
    for number in range(count):
        keep, got, out = refs[2 * number], refs[2 * number + 1], refs[2 * count + number]
        out[...] = (keep[0].astype(F32) + got[0].astype(F32)).astype(BF16)


def second_sums(*scatters):
    terms = [
        part
        for scatter in scatters
        if scatter.got
        for keep, got in zip(scatter.keep, scatter.got)
        for part in (keep, got)
    ]
    if not terms:
        return [[] for _ in scatters]
    shape = terms[0].shape
    outs = []
    in_specs, out_specs = [], []
    for term in terms:
        in_specs.append(
            pl.BlockSpec((1, 2) + term.shape[2:], lambda g: (1, g, 0, 0))
        )
    for term in terms[::2]:
        out_specs.append(pl.BlockSpec((2,) + term.shape[2:], lambda g: (g, 0, 0)))
        outs.append(jax.ShapeDtypeStruct(term.shape[1:], BF16))
    made = pl.pallas_call(
        second_kernel,
        grid=(shape[1] // 2,),
        in_specs=in_specs,
        out_specs=out_specs,
        out_shape=outs,
        compiler_params=compiler_params(),
        cost_estimate=cost(0, 6 * sum(out.size for out in outs)),
        name="second_sums",
    )(*terms)
    return [list(made[2 * i : 2 * i + 2]) for i in range(len(scatters))]


def last_kernel(*refs):
    out = refs[-1]
    for number in range(out.shape[1]):
        for half in range(2):
            terms = refs[6 * number + 3 * half : 6 * number + 3 * half + 3]
            out[:, number, half] = (
                terms[0][0].astype(F32) + terms[1][0].astype(F32) + terms[2][...].astype(F32)
            ).astype(BF16)


def last_sum(*scatters, columns=None):
    if not scatters[0].got:
        items = lax.axis_size("items")
        values = []
        for scatter in scatters:
            value = jnp.stack([keep[0] for keep in scatter.keep], 1)
            if columns is not None:
                starts = [sum(columns[:i]) for i in range(len(columns))]
                parts = [
                    value[..., start : start + size].reshape(value.shape[:3] + (items, -1))
                    for start, size in zip(starts, columns)
                ]
                value = jnp.concatenate(parts, 4).reshape(value.shape)
            values.append(lax.psum_scatter(value, "items", scatter_dimension=3, tiled=True))
        return jnp.stack(values, 1)
    terms = [
        part
        for scatter in scatters
        for parts in zip(scatter.keep, scatter.early, scatter.got)
        for part in parts
    ]
    _, places, rows, wide = terms[0].shape
    held = pl.BlockSpec((1, 2, rows, wide), lambda g: (0, g, 0, 0))
    late = pl.BlockSpec((2, rows, wide), lambda g: (g, 0, 0))
    shape = (places, len(scatters), 2, rows, wide)
    return pl.pallas_call(
        last_kernel,
        grid=(places // 2,),
        in_specs=[held, held, late] * (2 * len(scatters)),
        out_specs=pl.BlockSpec((2,) + shape[1:], lambda g: (g, 0, 0, 0, 0)),
        out_shape=jax.ShapeDtypeStruct(shape, BF16),
        compiler_params=compiler_params(),
        cost_estimate=cost(0, 8 * places * len(scatters) * 2 * rows * wide),
        name="last_sum",
    )(*terms)


def along_z(value):
    heads = lax.axis_size("heads")
    groups = [[core + 2 * z for z in range(heads // 2)] for core in range(2)]
    made = lax.psum_scatter(
        value, "heads", scatter_dimension=0, tiled=False, axis_index_groups=groups
    )
    return [made[i].reshape(-1, made.shape[-1]) for i in range(made.shape[0])]


def sum_everywhere(value):
    for axis in EVERY:
        bit = 1
        while bit < lax.axis_size(axis):
            value = value + swap(value, (axis, bit))
            bit *= 2
    return value


def edges(block, width):
    ways = lax.axis_size("heads")
    half = ways // 2
    place = lax.axis_index("heads") % half
    ring = [(side * half + i, side * half + (i + 1) % half) for side in range(2) for i in range(half)]
    low = lax.ppermute(block[:, block.shape[1] - width :], "heads", ring)
    high = lax.ppermute(block[:, :width], "heads", [(to, at) for at, to in ring])
    low = jnp.where(place == 0, jnp.roll(low, 1, 0), low)
    high = jnp.where(place == half - 1, jnp.roll(high, -1, 0), high)
    return jnp.concatenate([low, block, high], axis=1)


def body(
    frames, cotangent, bucket_counts, gains, w_ffn1_in, w_ffn1_out, w_qkv, w_out,
    w_point_in, w_depth, w_point_out, w_ffn2_in, w_ffn2_out,
):
    chunks, here, model = frames.shape
    ways = lax.axis_size("heads")
    half = ways // 2
    items = 4 if lax.axis_size("items") == 4 else 1
    span = here * half
    group_len = here * ways
    size = model // HEADS
    reach = (KERNEL - 1) // 2
    rows = chunks * here
    pieces = model // (half * LANES)
    place = lax.axis_index("heads")
    side = place // half
    where = jnp.stack(
        [place % 2, lax.axis_index("items") if items > 1 else 0 * place]
    ).astype(jnp.int32)
    always = jnp.min(bucket_counts) >= 0
    first = jnp.arange(chunks, dtype=jnp.int32)[:, None] * span + place % half * here
    position = first + jnp.arange(here, dtype=jnp.int32)[None]
    cosines, sines = rope_tables(position.reshape(-1), size, 2 * LANES)
    depth_rows = w_depth.astype(F32)
    gain = [gains[i : i + 1] for i in range(6)]
    counts = lax.dynamic_index_in_dim(bucket_counts[:, 0], side, 0, keepdims=False)
    wide_position = first - reach + jnp.arange(here + 2 * reach, dtype=jnp.int32)[None]
    seg_wide = segment_ids(wide_position, counts[0], counts[1], group_len)
    seg_own = seg_wide[:, reach : reach + here]

    def mine(value):
        return lax.dynamic_index_in_dim(value, side, 0, keepdims=False)

    def theirs(value):
        return lax.dynamic_index_in_dim(value, 1 - side, 0, keepdims=False)

    def begin(chunk, row, before=()):
        return front(
            chunk, row.reshape(1).astype(jnp.int32), gain[0], w_ffn1_in, w_ffn1_out, gain[1],
            w_qkv, cosines, sines, half, chunks, size, before,
        )

    own_frames = mine(frames)
    before, other_frames = fenced(
        always, (), lambda: (begin(own_frames, side), across(theirs(frames)))
    )
    stream = gathered(own_frames, other_frames, side)
    stream_one, slope_one, hid_one, ent_one, ent_att, *sent = begin(
        other_frames, 1 - side, before
    )
    qkv = [exchange(sent[0])]
    kept, contexts = [], []
    for number in range(pieces):

        def attend_now():
            return attend_forward(qkv[number], counts, size)

        def beside():
            extra = []
            if number + 1 < pieces:
                extra.append(exchange(sent[number + 1]))
            if number > 0:
                extra.append(exchange(kept[number - 1][0]))
            return extra

        def early():
            if number == 0:
                return [other_core(part) for part in (hid_one, ent_one, ent_att)]
            return [across(theirs(cotangent))] if number == 1 else []

        made, extra, others = fenced(always, (), lambda: (attend_now(), beside(), early()))
        kept.append(made)
        if number == 0:
            hid_one, ent_one, ent_att = zip((hid_one, ent_one, ent_att), others)
        elif number == 1:
            cot_other = others[0]
        if number + 1 < pieces:
            qkv.append(extra.pop(0))
        if number > 0:
            contexts.append(extra.pop(0))
    contexts.append(exchange(kept[-1][0]))
    if pieces == 1:
        cot_other = across(theirs(cotangent))
    fulls = [made[1] for made in kept]
    lses = [made[2] for made in kept]
    context = jnp.concatenate(
        [part.transpose(1, 2, 0, 3).reshape(rows, -1) for part in contexts], 1
    )
    stream_two = stream_one + dot(context, w_out)
    shaped, conv_normed, conv_inverse = layer_norm(stream_two, gain[2])
    conv_entered = shaped.astype(BF16)
    pointwise = dot(conv_entered, w_point_in)
    linear = pointwise[:, :model]
    sigmoid_gate = jax.nn.sigmoid(pointwise[:, model:])
    gated_low = (linear * sigmoid_gate).astype(BF16).reshape(chunks, here, model)
    widened = edges(gated_low, reach)
    depth_out = jnp.zeros((chunks, here, model), F32)
    for offset in range(KERNEL):
        same = (seg_wide[:, offset : offset + here] == seg_own)[:, :, None]
        depth_out = depth_out + depth_rows[offset] * jnp.where(
            same, widened[:, offset : offset + here], 0.0
        )
    depth_out = depth_out.reshape(rows, model)
    depth_shaped, depth_normed, depth_inverse = layer_norm(depth_out, gain[3])
    mixed_low = (depth_shaped * jax.nn.sigmoid(depth_shaped)).astype(BF16)
    stream_three = stream_two + dot(mixed_low, w_point_out)
    layer_out, grad_four, gain_five, slope_two, hid_two, ent_two = ffn_forward(
        stream_three, gain[4], w_ffn2_in, w_ffn2_out, gain[5],
        gathered(mine(cotangent), cot_other, side),
    )
    (grad_three, gain_four, half_two, grad_pre_two), hid_other, ent_other = fenced(
        always,
        (),
        lambda: (
            ffn_backward(grad_four, stream_three, slope_two, gain[4], w_ffn2_in, w_ffn2_out),
            other_core(hid_two),
            other_core(ent_two),
        ),
    )
    half_other, grad_pre_other = other_core(half_two), other_core(grad_pre_two)
    grad_mix = grad_three.astype(BF16)
    grad_norm_in = dot(grad_mix, w_point_out, NT) * silu_slope(depth_shaped)
    grad_depth, gain_three = norm_back(grad_norm_in, depth_normed, depth_inverse, gain[3])
    grad_depth_low = grad_depth.astype(BF16).reshape(chunks, here, model)
    grad_widened = edges(grad_depth_low, reach)
    grad_depth_full = grad_depth_low.astype(F32)
    taps = []
    grad_gated = jnp.zeros((chunks, here, model), F32)
    for offset in range(KERNEL):
        same = (seg_wide[:, offset : offset + here] == seg_own)[:, :, None]
        taps.append(
            jnp.sum(
                jnp.where(same, grad_depth_full * widened[:, offset : offset + here], 0.0), (0, 1)
            )
        )
        mirror = 2 * reach - offset
        same_back = (seg_wide[:, mirror : mirror + here] == seg_own)[:, :, None]
        grad_gated = grad_gated + depth_rows[offset] * jnp.where(
            same_back, grad_widened[:, mirror : mirror + here], 0.0
        )
    grad_gated = grad_gated.reshape(rows, model)
    grad_point = jnp.concatenate(
        [grad_gated * sigmoid_gate, grad_gated * linear * sigmoid_gate * (1.0 - sigmoid_gate)], 1
    ).astype(BF16)
    through, gain_two = norm_back(
        dot(grad_point, w_point_in, NT), conv_normed, conv_inverse, gain[2]
    )
    grad_two = grad_three + through
    grad_attn_out = grad_two.astype(BF16)
    grad_context = dot(grad_attn_out, w_out, NT).astype(BF16)
    grad_heads = []
    for number in range(pieces):
        columns = half * LANES
        part = grad_context[:, number * columns : (number + 1) * columns]
        grad_heads.append(part.reshape(chunks, here, half, LANES).transpose(2, 0, 1, 3))

    lefts = (mixed_low, conv_entered, context)
    rights = (grad_mix, grad_point, grad_attn_out)

    def ffn_grads():
        return (
            [other_core(part) for part in lefts + rights[:2]],
            exchange(grad_heads[0]),
            out_grad((half_two, half_other), (hid_two, hid_other), ways, where, items),
            column_grads(
                [(ent_two, ent_other)], [(grad_pre_two, grad_pre_other)], ways, where, items
            ),
        )

    others, grad_heads[0], shares_out, shares_in = fenced(always, (), ffn_grads)
    two_out, two_in = Scatter(*shares_out), Scatter(*shares_in)
    out_own, out_theirs = parted(layer_out, side)
    grads, backs = [], []
    for number in range(pieces):
        last = number == pieces - 1

        def beside():
            extra = []
            if not last:
                extra.append(exchange(grad_heads[number + 1]))
            if number > 0:
                extra.append(exchange(grads[number - 1]))
            if number == 0:
                extra.append(across(out_theirs))
                extra.append(other_core(rights[2]))
            return extra

        def attend_now():
            return attend_backward(
                qkv[number], counts, size, fulls[number], lses[number], grad_heads[number]
            )

        moving = (two_out,) if number == 0 else (two_out, two_in) if number == 1 else ()
        made, extra = fenced(always, moving, lambda: (attend_now(), beside()))
        grads.append(made)
        if not last:
            grad_heads[number + 1] = extra.pop(0)
        if number > 0:
            backs.append(extra.pop(0))
        if number == 0:
            out_other = extra.pop(0)
            others.append(extra.pop(0))
            two_out.second(second_sums(two_out)[0])
    two_in.second(second_sums(two_in)[0])

    def middle_part():
        back = exchange(grads[-1])
        scatter = copy.copy(two_in)
        moved(scatter)
        shares = column_grads(
            list(zip(lefts, others[:3])), list(zip(rights, others[3:])), ways, where, items
        )
        return (back, shares, last_sum(two_out, scatter))

    back, shares, two_sum = fenced(always, (), middle_part)
    backs.append(back)
    middle = Scatter(*shares)

    def attention_part():
        two_grads = along_z(two_sum)
        scatter = copy.copy(middle)

        def qkv_part():
            grad_proj = unturned(backs, cosines, sines, size)
            proj_other = other_core(grad_proj)
            down = stream_gradient(grad_two, stream_one, grad_proj, gain[1], w_qkv, F32)
            shares = column_grads(
                [ent_att], [(grad_proj, proj_other)], ways, where, items
            )
            return (down, shares)

        (grad_one, half_one, gain_one), shares = fenced(always, (scatter,), qkv_part)
        first = scatter.got
        scatter.second(second_sums(scatter)[0])
        attn = Scatter(*shares)
        (half_own, grad_pre), half_other = fenced(
            always,
            (attn,),
            lambda: (hidden_gradient(grad_one, slope_one, w_ffn1_out), other_core(half_one)),
        )
        pre_other, shares_out = fenced(
            always,
            (scatter,),
            lambda: (
                other_core(grad_pre),
                out_grad((half_own, half_other), hid_one, ways, where, items),
            ),
        )
        return (
            two_grads, first, scatter.got, (grad_one, gain_one), shares[:2], attn.got,
            (grad_pre, pre_other), shares_out,
        )

    two_grads, first, got, (grad_one, gain_one), shares, attn_got, grad_pre, shares_out = fenced(
        always, (), attention_part
    )
    middle.take(first)
    middle.take(got)
    attn = Scatter(*shares)
    attn.take(attn_got)
    attn.second(second_sums(attn)[0])
    one_out = Scatter(*shares_out)
    middle_columns = [w.shape[1] for w in (w_point_out, w_point_in, w_out)]
    middle_sum = last_sum(middle, columns=middle_columns)

    middle_grad, shares, (grad_zero, _, gain_zero) = fenced(
        always,
        (one_out, attn),
        lambda: (
            along_z(middle_sum),
            column_grads([ent_one], [grad_pre], ways, where, items),
            stream_gradient(grad_one, stream, grad_pre[0], gain[0], w_ffn1_in, BF16),
        ),
    )
    one_in = Scatter(*shares)
    one_out.second(second_sums(one_out)[0])
    attn_sum = last_sum(attn)
    grad_own, grad_theirs = parted(grad_zero, side)
    attn_grad, grad_other = fenced(
        always, (one_in, one_out), lambda: (along_z(attn_sum), across(grad_theirs))
    )
    one_in.second(second_sums(one_in)[0])

    def last_part():
        out_grads = along_z(last_sum(one_out))
        scatter = copy.copy(one_in)
        moved(scatter)
        small = sum_everywhere(
            jnp.concatenate(
                [gain_zero, gain_one, gain_two, gain_three, gain_four, gain_five]
                + [tap[None] for tap in taps],
                0,
            )
        )
        return (out_grads, along_z(last_sum(scatter)), small)

    one_out_grad, one_in_grad, small = fenced(always, (), last_part)
    hidden = w_ffn1_in.shape[1]

    def unfolded(share):
        each, wide = share.shape
        span = hidden // ways
        halves = share.reshape(2, each // 2, wide)
        parts = [
            halves[half, :, i * span : (i + 1) * span]
            for i in range(wide // span)
            for half in range(2)
        ]
        return jnp.concatenate(parts, 0).T.astype(F32)

    middle_parts = []
    start = 0
    for weight in (w_point_out, w_point_in, w_out):
        each = weight.shape[1] // lax.axis_size("items")
        middle_parts.append(middle_grad[0][:, start : start + each].astype(F32))
        start += each
    return (
        gathered(out_own[None], out_other[None], side),
        gathered(grad_own[None], grad_other[None], side),
        small[:6],
        one_in_grad[0].astype(F32),
        unfolded(one_out_grad[0]),
        attn_grad[0].astype(F32),
        middle_parts[2],
        middle_parts[1],
        small[6:],
        middle_parts[0],
        two_grads[1].astype(F32),
        unfolded(two_grads[0]),
    )


def solution(mesh):
    split = P(None, EVERY, None)
    shares = P("heads", "items")
    in_specs = (split, split, P(None, "items", None)) + (P(),) * 10
    out_specs = (split, split, P(), shares, shares, shares, shares, shares, P()) + (shares,) * 3
    return jax.shard_map(body, mesh=mesh, in_specs=in_specs, out_specs=out_specs, check_vma=False)
```

profile of v0, /device:TPU:0, one launch (start us, length us, event | category | flops | bytes accessed | tf_op | source)
XLA Modules:
  0.0 633.0 jit_solution(7673397656196242648)
XLA Ops:
  15.4 29.4 %conditional.15 = (f32[512,1024]{1,0:T(8,128)}, bf16[512,4096]{1,0:T(8,128)(2,1)}, bf16[512,4096]{1,0:T(8,128)(2,1)}, bf16[512,1024]{1,0:T(8,128)(2,1)}, bf16[51...) conditional(s32[]{:T(128)} %convert_element_type.145, ...), branch_computations={%region_1.2_spmd, %region_2.3_spmd} | conditional | flops 5905580032 | bytes 36700312 | solution.py:759
  23.3 19.8 %front.2 = (f32[512,1024]{1,0:T(8,128)}, bf16[512,4096]{1,0:T(8,128)(2,1)}, bf16[512,4096]{1,0:T(8,128)(2,1)}, bf16[512,1024]{1,0:T(8,128)(2,1)}, bf16[512,1024]...) custom-call(s32[1]{0:T(128)} %bitcast.row_ref, ...), custom_call_target="tpu_custom_call" | custom-call | flops 5905580032 | bytes 31457280 | tf_op jit(solution)/shard_map/cond/branch_1_fun/front/pallas_call | solution.py:687
  44.8 19.8 %front.3 = (f32[512,1024]{1,0:T(8,128)}, bf16[512,4096]{1,0:T(8,128)(2,1)}, bf16[512,4096]{1,0:T(8,128)(2,1)}, bf16[512,1024]{1,0:T(8,128)(2,1)}, bf16[512,1024]...) custom-call(s32[1]{0:T(128)} %bitcast.14.row_ref, ...), custom_call_target="tpu_custom_call", output_to_operand_aliasing={{0}: (11, {}), {1}: (12, {}), {2}: (13, {}), {3}: (14, {}),... | custom-call | flops 5905580032 | bytes 31457280 | tf_op jit(solution)/shard_map/front/pallas_call | solution.py:687
  64.6 4.5 all-to-all-start.6
  75.4 13.9 %all-to-all-done.6 = bf16[4,3,2,256,128]{4,3,2,1,0:T(8,128)(2,1)} async-done(((bf16[4,3,2,256,128]{4,3,2,1,0:T(8,128)(2,1)}), bf16[4,3,2,256,128]{4,3,2,1,0:T(8,128)(2,1)}, u32[]{:S(2)}, u32[]{:S(2)}) %all-to-all-start.6) | async-done | bytes 1572896 | tf_op jit(solution)/shard_map/all_to_all | solution.py:776
  89.3 25.4 %conditional.16 = (bf16[4,2,256,128]{3,2,1,0:T(8,128)(2,1)}, f32[2048,128]{1,0:T(8,128)}, f32[2,2048,128]{2,1,0:T(8,128)}, bf16[4,3,2,256,128]{4,3,2,1,0:T(8,128...) conditional(s32[]{:T(128)} %convert_element_type.145, () %tuple.133, ...), branch_computations={%region_3.4_spmd, %region_4.5_spmd} | conditional | flops 8589934592 | bytes 36176080 | solution.py:759
  89.3 4.8 all-to-all-start
  94.7 16.4 %attend_forward.2 = (bf16[4,2,256,128]{3,2,1,0:T(8,128)(2,1)}, f32[2048,128]{1,0:T(8,128)}, f32[2,2048,128]{2,1,0:T(8,128)}) custom-call(s32[2]{0:T(128)S(1)} %get-tuple-element.390.counts_ref, bf16[4,3,2,256,128]{4,3,2,1,0:T(8,128)(2,1)} %get-tuple-element.391.qkv_ref), custom_call_target="tpu_custom_call" | custom-call | flops 8589934592 | bytes 6291456 | tf_op jit(solution)/shard_map/cond/branch_1_fun/attend_forward/pallas_call | solution.py:220
  114.8 30.9 %conditional.17 = (bf16[4,2,256,128]{3,2,1,0:T(8,128)(2,1)}, f32[2048,128]{1,0:T(8,128)}, f32[2,2048,128]{2,1,0:T(8,128)}, bf16[4,2,256,128]{3,2,1,0:T(8,128)(2,1)}, bf16[256,1024]{1,0:T(8,128)(2,1)}) conditional(s32[]{:T(128)} %convert_element_type.145, () %tuple.132, (s32[2]{0:T(128)S(1)}, bf16[4,3,2,256,128]{4,3,2,1,0:T(8,128)(2,1)}, ...), branch_computations={%region_5.6_spmd, %region_6.7_spmd} | conditional | flops 8589934592 | bytes 11010210 | solution.py:759
  121.0 16.4 %attend_forward.3 = (bf16[4,2,256,128]{3,2,1,0:T(8,128)(2,1)}, f32[2048,128]{1,0:T(8,128)}, f32[2,2048,128]{2,1,0:T(8,128)}) custom-call(s32[2]{0:T(128)S(1)} %get-tuple-element.399.counts_ref, bf16[4,3,2,256,128]{4,3,2,1,0:T(8,128)(2,1)} %get-tuple-element.400.qkv_ref), custom_call_target="tpu_custom_call" | custom-call | flops 8589934592 | bytes 6291456 | tf_op jit(solution)/shard_map/cond/branch_1_fun/attend_forward/pallas_call | solution.py:220
  137.4 8.2 %collective-permute-done.46 = bf16[256,1024]{1,0:T(8,128)(2,1)} collective-permute-done((bf16[256,1024]{1,0:T(8,128)(2,1)S(1)}, bf16[256,1024]{1,0:T(8,128)(2,1)}, u32[]{:S(2)}, u32[]{:S(2)}) %collective-permute-start.46) | collective-permute-done | bytes 524320 | tf_op jit(solution)/shard_map/cond/branch_1_fun/ppermute | solution.py:749
  153.7 4.2 all-to-all-done.7
  184.1 19.9 %ffn_forward.1 = (bf16[512,1024]{1,0:T(8,128)(2,1)}, f32[512,1024]{1,0:T(8,128)}, f32[1,1024]{1,0:T(1,128)}, bf16[512,4096]{1,0:T(8,128)(2,1)}, bf16[512,4096]{1...) custom-call(f32[512,1024]{1,0:T(8,128)S(1)} %convolution_add_fusion.x_ref, f32[1,1024]{1,0:T(1,128)S(1)} %get-tuple-element.994.gain_ref, ...), custom_call_target="tpu_custom_call" | custom-call | flops 8589934592 | bytes 25165824 | tf_op jit(solution)/shard_map/ffn_forward/pallas_call | solution.py:394
  205.1 20.4 %conditional.18 = (f32[512,1024]{1,0:T(8,128)S(1)}, f32[1,1024]{1,0:T(1,128)}, bf16[512,1024]{1,0:T(8,128)(2,1)}, bf16[512,4096]{1,0:T(8,128)(2,1)}, bf16[512,40...) conditional(s32[]{:T(128)} %convert_element_type.145, () %tuple.138, (f32[512,1024]{1,0:T(8,128)S(1)}, ...), branch_computations={%region_11.12_spmd, %region_12.13_spmd} | conditional | flops 8589934592 | bytes 58720412 | solution.py:759
  206.4 18.8 %ffn_backward.1 = (f32[512,1024]{1,0:T(8,128)S(1)}, f32[1,1024]{1,0:T(1,128)}, bf16[512,1024]{1,0:T(8,128)(2,1)}, bf16[512,4096]{1,0:T(8,128)(2,1)}) custom-call(f32[512,1024]{1,0:T(8,128)} %copy-done.52, f32[1,1024]{1,0:T(1,128)S(1)} %get-tuple-element.408.gain_ref, f32[512,1024]{1,0:T(8,128)} %get-tuple-element.409.up_ref, ...), custom_call_target="tpu_custom_call" | custom-call | flops 8589934592 | bytes 29360128 | tf_op jit(solution)/shard_map/cond/branch_1_fun/ffn_backward/pallas_call | solution.py:451
  227.4 4.3 multiply_reduce_fusion
  258.4 24.7 %conditional.19 = (bf16[512,1024]{1,0:T(8,128)(2,1)}, bf16[512,1024]{1,0:T(8,128)(2,1)}, bf16[512,1024]{1,0:T(8,128)(2,1)}, bf16[512,1024]{1,0:T(8,128)(2,1)}, b...) conditional(s32[]{:T(128)} %convert_element_type.145, ...), branch_computations={%region_17.18_spmd, %region_18.19_spmd} | conditional | flops 8589934592 | bytes 64487796 | solution.py:759
  264.2 9.3 %out_grad.2 = (bf16[2,4,64,1024]{3,2,1,0:T(8,128)(2,1)}, bf16[2,4,64,1024]{3,2,1,0:T(8,128)(2,1)S(1)}, bf16[2,4,64,1024]{3,2,1,0:T(8,128)(2,1)}, bf16[2,4,64,1024]{3,2,1,0:T(8,128)(2,1)}) custom-call(s32[2]{0:T(128)S(1)} %get-tuple-element.425.place_ref, bf16[512,1024]{1,0:T(8,128)(2,1)} %get-tuple-element.426.up_own, ...), custom_call_target="tpu_custom_call" | custom-call | flops 4294967296 | bytes 16777216 | tf_op jit(solution)/shard_map/cond/branch_1_fun/out_grad/pallas_call | solution.py:868
  273.5 9.6 %column_grads.4 = (bf16[2,4,64,1024]{3,2,1,0:T(8,128)(2,1)S(1)}, bf16[2,4,64,1024]{3,2,1,0:T(8,128)(2,1)S(1)}, bf16[2,4,64,1024]{3,2,1,0:T(8,128)(2,1)}, bf16[2,4,64,1024]{3,2,1,0:T(8,128)(2,1)}) custom-call(s32[2]{0:T(128)S(1)} %get-tuple-element.425.place_ref, bf16[512,1024]{1,0:T(8,128)(2,1)S(1)} %copy-done.51, ...), custom_call_target="tpu_custom_call" | custom-call | flops 4294967296 | bytes 16777216 | tf_op jit(solution)/shard_map/cond/branch_1_fun/column_grads/pallas_call | solution.py:945
  283.1 32.8 %conditional.20 = (bf16[4,3,2,256,128]{4,3,2,1,0:T(8,128)(2,1)}, bf16[4,2,256,128]{3,2,1,0:T(8,128)(2,1)}, bf16[256,1024]{1,0:T(8,128)(2,1)}, bf16[512,1024]{1,0...) conditional(s32[]{:T(128)} %convert_element_type.145, () %tuple.136, ...), branch_computations={%region_19.20_spmd, %region_20.21_spmd} | conditional | flops 17179869184 | bytes 25690352 | solution.py:759
  292.0 23.3 %attend_backward.2 = bf16[4,3,2,256,128]{4,3,2,1,0:T(8,128)(2,1)} custom-call(s32[2]{0:T(128)S(1)} %get-tuple-element.442.counts_ref, bf16[4,3,2,256,128]{4,3,2,1,0:T(8,128)(2,1)} %get-tuple-element.443.qkv_ref, f32[2048,128]{1,0:T(8,128)} %get-tuple-element.444.full_ref, f32[2,2048,128]{2,1,0:T(8,128)} %get-tuple-element.445.lse_ref, ...), custom_call_target="tpu_custom_call" | custom-call | flops 17179869184 | bytes 9437184 | tf_op jit(solution)/shard_map/cond/branch_1_fun/attend_backward/pallas_call | solution.py:330
  318.1 44.1 %conditional.21 = (bf16[4,3,2,256,128]{4,3,2,1,0:T(8,128)(2,1)}, bf16[4,3,2,256,128]{4,3,2,1,0:T(8,128)(2,1)}, bf16[4,64,1024]{2,1,0:T(8,128)(2,1)}, bf16[4,64,1...) conditional(s32[]{:T(128)} %convert_element_type.145, () %tuple.144, ...), branch_computations={%region_21.22_spmd, %region_22.23_spmd} | conditional | flops 17179869184 | bytes 26738928 | solution.py:759
  318.1 4.3 all-to-all-start.3
  327.6 23.3 %attend_backward.3 = bf16[4,3,2,256,128]{4,3,2,1,0:T(8,128)(2,1)} custom-call(s32[2]{0:T(128)S(1)} %get-tuple-element.452.counts_ref, bf16[4,3,2,256,128]{4,3,2,1,0:T(8,128)(2,1)} %get-tuple-element.453.qkv_ref, f32[2048,128]{1,0:T(8,128)} %get-tuple-element.454.full_ref, f32[2,2048,128]{2,1,0:T(8,128)} %get-tuple-element.455.lse_ref, ...), custom_call_target="tpu_custom_call" | custom-call | flops 17179869184 | bytes 9437184 | tf_op jit(solution)/shard_map/cond/branch_1_fun/attend_backward/pallas_call | solution.py:330
  350.9 11.3 %collective-permute-done.16 = bf16[2,4,64,1024]{3,2,1,0:T(8,128)(2,1)} collective-permute-done((bf16[2,4,64,1024]{3,2,1,0:T(8,128)(2,1)}, bf16[2,4,64,1024]{3,2,1,0:T(8,128)(2,1)}, u32[]{:S(2)}, u32[]{:S(2)}) %collective-permute-start.16) | collective-permute-done | bytes 1048608 | tf_op jit(solution)/shard_map/cond/branch_1_fun/ppermute | solution.py:749
  364.3 24.7 %conditional.22 = (bf16[4,3,2,256,128]{4,3,2,1,0:T(8,128)(2,1)}, bf16[2,4,64,1024]{3,2,1,0:T(8,128)(2,1)}, bf16[2,4,64,1024]{3,2,1,0:T(8,128)(2,1)}, bf16[2,4,64...) conditional(s32[]{:T(128)} %convert_element_type.145, ...), branch_computations={%region_23.24_spmd, %region_24.25_spmd} | conditional | flops 4294967296 | bytes 38273240 | solution.py:759
  364.5 4.4 all-to-all-start.4
  369.5 12.5 %column_grads.5 = (bf16[2,4,64,1024]{3,2,1,0:T(8,128)(2,1)}, bf16[2,4,64,1024]{3,2,1,0:T(8,128)(2,1)}, bf16[2,4,64,1024]{3,2,1,0:T(8,128)(2,1)}, bf16[2,4,64,1024]{3,2,1,0:T(8,128)(2,1)}) custom-call(s32[2]{0:T(128)S(1)} %get-tuple-element.463.place_ref, bf16[512,1024]{1,0:T(8,128)(2,1)} %get-tuple-element.464.refs_0_, ...), custom_call_target="tpu_custom_call" | custom-call | flops 4294967296 | bytes 16777216 | tf_op jit(solution)/shard_map/cond/branch_1_fun/column_grads/pallas_call | solution.py:945
  389.0 73.5 %conditional.23 = (bf16[128,1024]{1,0:T(8,128)(2,1)S(1)}, bf16[128,1024]{1,0:T(8,128)(2,1)S(1)}, bf16[2,4,64,1024]{3,2,1,0:T(8,128)(2,1)}, bf16[2,4,64,1024]{3,2...) conditional(s32[]{:T(128)} %convert_element_type.145, ...), branch_computations={%region_25.26_spmd, %region_26.34_spmd} | conditional | flops 15032385536 | bytes 164119664 | solution.py:759
  391.2 31.8 %conditional = (f32[512,1024]{1,0:T(8,128)}, bf16[512,1024]{1,0:T(8,128)(2,1)S(1)}, f32[1,1024]{1,0:T(1,128)}, bf16[2,4,64,768]{3,2,1,0:T(8,128)(2,1)}, bf16[2,4...) conditional(s32[]{:T(128)} %convert_element_type.107, () %tuple.90, ...), branch_computations={%region_28.28_spmd, %region_29.29_spmd} | conditional | flops 6442450944 | bytes 61866204 | solution.py:759
  391.3 5.9 unturned.1.grad_ref.refs_2_
  398.4 11.1 %stream_gradient.2 = (f32[512,1024]{1,0:T(8,128)}, bf16[512,1024]{1,0:T(8,128)(2,1)S(1)}, f32[1,1024]{1,0:T(1,128)}) custom-call(f32[512,1024]{1,0:T(8,128)} %get-tuple-element.492.x_ref, f32[1,1024]{1,0:T(1,128)S(1)} %get-tuple-element.493.gain_ref, f32[512,1024]{1,0:T(8,128)S(1)} %get-tuple-element.494.up_ref, bf16[512,3072]{1,0:T(8,128)(2,1)} %unturned.1.grad_ref.refs_2_, ...), custom_call_target="tpu_custom_call" | custom-call | flops 3221225472 | bytes 9437184 | tf_op jit(solution)/shard_map/cond/branch_1_fun/cond/branch_1_fun/stream_gradient/pallas_call | solution.py:539
  411.2 8.8 %column_grads.6 = (bf16[2,4,64,768]{3,2,1,0:T(8,128)(2,1)}, bf16[2,4,64,768]{3,2,1,0:T(8,128)(2,1)}, bf16[2,4,64,768]{3,2,1,0:T(8,128)(2,1)S(1)}, bf16[2,4,64,768]{3,2,1,0:T(8,128)(2,1)S(1)}) custom-call(s32[2]{0:T(128)S(1)} %get-tuple-element.503.place_ref, bf16[512,1024]{1,0:T(8,128)(2,1)} %get-tuple-element.504.refs_0_, ...), custom_call_target="tpu_custom_call" | custom-call | flops 3221225472 | bytes 12582912 | tf_op jit(solution)/shard_map/cond/branch_1_fun/cond/branch_1_fun/column_grads/pallas_call | solution.py:945
  423.1 21.5 %conditional.1 = (bf16[512,1024]{1,0:T(8,128)(2,1)S(1)}, bf16[512,4096]{1,0:T(8,128)(2,1)}, bf16[512,1024]{1,0:T(8,128)(2,1)}, bf16[2,4,64,768]{3,2,1,0:T(8,128)(2,1)}, bf16[2,4,64,768]{3,2,1,0:T(8,128)(2,1)}) conditional(s32[]{:T(128)} %convert_element_type.107, () %tuple.93, (f32[512,1024]{1,0:T(8,128)}, bf16[512,4096]{1,0:T(8,128)(2,1)}, ...), branch_computations={%region_30.30_spmd, %region_31.31_spmd} | conditional | flops 4294967296 | bytes 31457440 | solution.py:759
  425.4 12.0 %hidden_gradient.1 = (bf16[512,1024]{1,0:T(8,128)(2,1)S(1)}, bf16[512,4096]{1,0:T(8,128)(2,1)}) custom-call(f32[512,1024]{1,0:T(8,128)} %get-tuple-element.512.up_ref, bf16[512,4096]{1,0:T(8,128)(2,1)} %get-tuple-element.513.slope_ref, bf16[4096,1024]{1,0:T(8,128)(2,1)} %get-tuple-element.514.wout_ref), custom_call_target="tpu_custom_call" | custom-call | flops 4294967296 | bytes 20971520 | tf_op jit(solution)/shard_map/cond/branch_1_fun/cond/branch_1_fun/hidden_gradient/pallas_call | solution.py:494
  437.5 5.7 collective-permute-done.24
  446.3 14.9 %conditional.2 = (bf16[512,4096]{1,0:T(8,128)(2,1)}, bf16[2,4,64,1024]{3,2,1,0:T(8,128)(2,1)}, bf16[2,4,64,1024]{3,2,1,0:T(8,128)(2,1)}, bf16[2,4,64,1024]{3,2,1...) conditional(s32[]{:T(128)} %convert_element_type.107, () %tuple.92, ...), branch_computations={%region_32.32_spmd, %region_33.33_spmd} | conditional | flops 4294967296 | bytes 37748912 | solution.py:759
  447.7 9.2 %out_grad.3 = (bf16[2,4,64,1024]{3,2,1,0:T(8,128)(2,1)}, bf16[2,4,64,1024]{3,2,1,0:T(8,128)(2,1)}, bf16[2,4,64,1024]{3,2,1,0:T(8,128)(2,1)}, bf16[2,4,64,1024]{3,2,1,0:T(8,128)(2,1)}) custom-call(s32[2]{0:T(128)S(1)} %get-tuple-element.521.place_ref, bf16[512,1024]{1,0:T(8,128)(2,1)S(1)} %get-tuple-element.522.up_own, ...), custom_call_target="tpu_custom_call" | custom-call | flops 4294967296 | bytes 16777216 | tf_op jit(solution)/shard_map/cond/branch_1_fun/cond/branch_1_fun/out_grad/pallas_call | solution.py:868
  468.1 34.3 %conditional.24 = (bf16[128,1024]{1,0:T(8,128)(2,1)}, bf16[2,4,64,1024]{3,2,1,0:T(8,128)(2,1)S(1)}, bf16[2,4,64,1024]{3,2,1,0:T(8,128)(2,1)S(1)}, bf16[2,4,64,10...) conditional(s32[]{:T(128)} %convert_element_type.145, ...), branch_computations={%region_34.35_spmd, %region_35.37_spmd} | conditional | flops 8589934592 | bytes 44826920 | solution.py:759
  472.9 13.4 %stream_gradient.3 = (bf16[512,1024]{1,0:T(8,128)(2,1)S(1)}, bf16[512,1024]{1,0:T(8,128)(2,1)}, f32[1,1024]{1,0:T(1,128)S(1)}) custom-call(bf16[512,1024]{1,0:T(8,128)(2,1)} %get-tuple-element.586.x_ref, f32[1,1024]{1,0:T(1,128)S(1)} %get-tuple-element.587.gain_ref, f32[512,1024]{1,0:T(8,128)} %get-tuple-element.588.up_ref, ...), custom_call_target="tpu_custom_call" | custom-call | flops 4294967296 | bytes 12582912 | tf_op jit(solution)/shard_map/cond/branch_1_fun/stream_gradient/pallas_call | solution.py:539
  486.3 9.9 %column_grads.7 = (bf16[2,4,64,1024]{3,2,1,0:T(8,128)(2,1)S(1)}, bf16[2,4,64,1024]{3,2,1,0:T(8,128)(2,1)S(1)}, bf16[2,4,64,1024]{3,2,1,0:T(8,128)(2,1)}, bf16[2,4,64,1024]{3,2,1,0:T(8,128)(2,1)}) custom-call(s32[2]{0:T(128)S(1)} %get-tuple-element.577.place_ref, bf16[512,1024]{1,0:T(8,128)(2,1)} %get-tuple-element.578.refs_0_, ...), custom_call_target="tpu_custom_call" | custom-call | flops 4294967296 | bytes 16777216 | tf_op jit(solution)/shard_map/cond/branch_1_fun/column_grads/pallas_call | solution.py:945
  496.2 6.1 collective-permute-done.31
  511.3 40.1 %conditional.25 = (bf16[128,768]{1,0:T(8,128)(2,1)}, bf16[256,1024]{1,0:T(8,128)(2,1)}, bf16[2,4,64,1024]{3,2,1,0:T(8,128)(2,1)}, bf16[2,4,64,1024]{3,2,1,0:T(8,...) conditional(s32[]{:T(128)} %convert_element_type.145, () %tuple.151, ...), branch_computations={%region_37.38_spmd, %region_38.40_spmd} | conditional | bytes 17629472 | solution.py:759
  518.4 33.1 %collective-permute-done.33 = bf16[256,1024]{1,0:T(8,128)(2,1)} collective-permute-done((bf16[256,1024]{1,0:T(8,128)(2,1)}, bf16[256,1024]{1,0:T(8,128)(2,1)}, u32[]{:S(2)}, u32[]{:S(2)}) %collective-permute-start.33) | collective-permute-done | bytes 524320 | tf_op jit(solution)/shard_map/cond/branch_1_fun/ppermute | solution.py:749
  553.6 58.2 %conditional.26 = (bf16[128,1024]{1,0:T(8,128)(2,1)}, bf16[128,1024]{1,0:T(8,128)(2,1)}, f32[11,1024]{1,0:T(8,128)S(1)}) conditional(s32[]{:T(128)} %convert_element_type.145, () %tuple.153, (bf16[2,4,64,1024]{3,2,1,0:T(8,128)(2,1)}, bf16[2,4,64,1024]{3,2,1,0:T(8,128)(2,1)}, bf16[4,64,1024]{2,1,0:T(8,128)(2,1)}, ...), branch_computations={%region_47.48_spmd, %region_48.51_spmd} | conditional | flops 56320 | bytes 26309048 | solution.py:759
  557.9 12.3 %collective-permute-done.38.refs_2_ = bf16[4,64,1024]{2,1,0:T(8,128)(2,1)S(1)} collective-permute-done((bf16[4,64,1024]{2,1,0:T(8,128)(2,1)}, bf16[4,64,1024]{2,1,0:T(8,128)(2,1)S(1)}, u32[]{:S(2)}, u32[]{:S(2)}) %collective-permute-start.38) | collective-permute-done | bytes 524320 | tf_op jit(solution)/shard_map/cond/branch_1_fun/ppermute | solution.py:749
  590.0 5.5 collective-permute-done.44
  595.5 16.3 %reduce-scatter.14.cloned.1.call-done = bf16[1,1,2,64,1024]{4,3,2,1,0:T(8,128)(2,1)} async-done(((bf16[4,1,2,64,1024]{4,3,2,1,0:T(8,128)(2,1)}), bf16[1,1,2,64,1024]{4,3,2,1,0:T(8,128)(2,1)}) %reduce-scatter.14.cloned.1.call-update) | async-done | bytes 262160 | tf_op jit(solution)/shard_map/cond/branch_1_fun/reduce_scatter | solution.py:1065
  (344 shorter events, 214.7 us)
Async XLA Ops:
  17.3 27.5 %collective-permute-start.45 = (bf16[256,1024]{1,0:T(8,128)(2,1)}, bf16[256,1024]{1,0:T(8,128)(2,1)}, u32[]{:S(2)}, u32[]{:S(2)}) collective-permute-start(bf16[256,1024]{1,0:T(8,128)(2,1)} %dynamic-slice_bitcast_fusion), channel_id=1, source_target_pairs={{0,4},{1,5},{2,6},{3,7},{4,0},{5,1},{6,2},{7,3},{8,12},{9,13},{10,... | collective-permute-start | bytes 1572872 | tf_op jit(solution)/shard_map/cond/branch_1_fun/ppermute | solution.py:749
  64.6 24.6 %all-to-all-start.6 = ((bf16[4,3,2,256,128]{4,3,2,1,0:T(8,128)(2,1)}), bf16[4,3,2,256,128]{4,3,2,1,0:T(8,128)(2,1)}, u32[]{:S(2)}, u32[]{:S(2)}) async-start(bf16[4,3,2,256,128]{4,3,2,1,0:T(8,128)(2,1)} %get-tuple-element.777), calls=%async_computation.11 | async-start | bytes 3145728 | tf_op jit(solution)/shard_map/all_to_all | solution.py:776
  89.3 24.9 %collective-permute-start = (bf16[512,4096]{1,0:T(8,128)(2,1)}, bf16[512,4096]{1,0:T(8,128)(2,1)}, u32[]{:S(2)}, u32[]{:S(2)}) collective-permute-start(bf16[512,4096]{1,0:T(8,128)(2,1)} %get-tuple-element.396), channel_id=1, source_target_pairs={{0,1},{1,0},{2,3},{3,2},{4,5},{5,4},{6,7},{7,6},{8,9},{9,8},{10,11... | collective-permute-start | bytes 12582920 | tf_op jit(solution)/shard_map/cond/branch_1_fun/ppermute | solution.py:749
  89.3 24.9 %all-to-all-start = ((bf16[4,3,2,256,128]{4,3,2,1,0:T(8,128)(2,1)}), bf16[4,3,2,256,128]{4,3,2,1,0:T(8,128)(2,1)}, u32[]{:S(2)}, u32[]{:S(2)}) async-start(bf16[4,3,2,256,128]{4,3,2,1,0:T(8,128)(2,1)} %get-tuple-element.395), calls=%async_computation | async-start | bytes 3145728 | tf_op jit(solution)/shard_map/cond/branch_1_fun/all_to_all | solution.py:776
  94.1 17.1 %collective-permute-start.1 = (bf16[512,1024]{1,0:T(8,128)(2,1)}, bf16[512,1024]{1,0:T(8,128)(2,1)}, u32[]{:S(2)}, u32[]{:S(2)}) collective-permute-start(bf16[512,1024]{1,0:T(8,128)(2,1)} %get-tuple-element.397), channel_id=1, source_target_pairs={{0,1},{1,0},{2,3},{3,2},{4,5},{5,4},{6,7},{7,6},{8,9},{9,8},{10,11... | collective-permute-start | bytes 3145736 | tf_op jit(solution)/shard_map/cond/branch_1_fun/ppermute | solution.py:749
  94.6 16.5 %collective-permute-start.2 = (bf16[512,1024]{1,0:T(8,128)(2,1)}, bf16[512,1024]{1,0:T(8,128)(2,1)}, u32[]{:S(2)}, u32[]{:S(2)}) collective-permute-start(bf16[512,1024]{1,0:T(8,128)(2,1)} %get-tuple-element.398), channel_id=1, source_target_pairs={{0,1},{1,0},{2,3},{3,2},{4,5},{5,4},{6,7},{7,6},{8,9},{9,8},{10,11... | collective-permute-start | bytes 3145736 | tf_op jit(solution)/shard_map/cond/branch_1_fun/ppermute | solution.py:749
  114.8 30.8 %all-to-all-start.5 = ((bf16[4,2,256,128]{3,2,1,0:T(8,128)(2,1)}), bf16[4,2,256,128]{3,2,1,0:T(8,128)(2,1)}, u32[]{:S(2)}, u32[]{:S(2)}) async-start(bf16[4,2,256,128]{3,2,1,0:T(8,128)(2,1)} %get-tuple-element.404), calls=%async_computation.9 | async-start | bytes 1048576 | tf_op jit(solution)/shard_map/cond/branch_1_fun/all_to_all | solution.py:776
  119.0 26.6 %collective-permute-start.46 = (bf16[256,1024]{1,0:T(8,128)(2,1)S(1)}, bf16[256,1024]{1,0:T(8,128)(2,1)}, u32[]{:S(2)}, u32[]{:S(2)}) collective-permute-start(bf16[256,1024]{1,0:T(8,128)(2,1)S(1)} %dynamic-slice_bitcast_fusion.1), channel_id=1, source_target_pairs={{0,4},{1,5},{2,6},{3,7},{4,0},{5,1},{6,2},{7,3},{8,12},{9,13},{10,... | collective-permute-start | bytes 1572872 | tf_op jit(solution)/shard_map/cond/branch_1_fun/ppermute | solution.py:749
  205.1 20.2 %collective-permute-start.3 = (bf16[512,4096]{1,0:T(8,128)(2,1)}, bf16[512,4096]{1,0:T(8,128)(2,1)}, u32[]{:S(2)}, u32[]{:S(2)}) collective-permute-start(bf16[512,4096]{1,0:T(8,128)(2,1)} %get-tuple-element.417), channel_id=1, source_target_pairs={{0,1},{1,0},{2,3},{3,2},{4,5},{5,4},{6,7},{7,6},{8,9},{9,8},{10,11... | collective-permute-start | bytes 12582920 | tf_op jit(solution)/shard_map/cond/branch_1_fun/ppermute | solution.py:749
  205.5 19.7 %collective-permute-start.4 = (bf16[512,1024]{1,0:T(8,128)(2,1)S(1)}, bf16[512,1024]{1,0:T(8,128)(2,1)}, u32[]{:S(2)}, u32[]{:S(2)}) collective-permute-start(bf16[512,1024]{1,0:T(8,128)(2,1)S(1)} %get-tuple-element.418), channel_id=1, source_target_pairs={{0,1},{1,0},{2,3},{3,2},{4,5},{5,4},{6,7},{7,6},{8,9},{9,8},{10,11... | collective-permute-start | bytes 3145736 | tf_op jit(solution)/shard_map/cond/branch_1_fun/ppermute | solution.py:749
  238.3 20.1 %collective-permute-start.51 = (bf16[512,1024]{1,0:T(8,128)(2,1)}, bf16[512,1024]{1,0:T(8,128)(2,1)}, u32[]{:S(2)}, u32[]{:S(2)}) collective-permute-start(bf16[512,1024]{1,0:T(8,128)(2,1)} %get-tuple-element.795), channel_id=1, source_target_pairs={{0,1},{1,0},{2,3},{3,2},{4,5},{5,4},{6,7},{7,6},{8,9},{9,8},{10,11... | collective-permute-start | bytes 3145736 | tf_op jit(solution)/shard_map/ppermute | solution.py:749
  238.8 19.7 %collective-permute-start.52 = (bf16[512,4096]{1,0:T(8,128)(2,1)}, bf16[512,4096]{1,0:T(8,128)(2,1)}, u32[]{:S(2)}, u32[]{:S(2)}) collective-permute-start(bf16[512,4096]{1,0:T(8,128)(2,1)} %get-tuple-element.798), channel_id=1, source_target_pairs={{0,1},{1,0},{2,3},{3,2},{4,5},{5,4},{6,7},{7,6},{8,9},{9,8},{10,11... | collective-permute-start | bytes 12582920 | tf_op jit(solution)/shard_map/ppermute | solution.py:749
  258.9 24.2 %collective-permute-start.9 = (bf16[512,2048]{1,0:T(8,128)(2,1)}, bf16[512,2048]{1,0:T(8,128)(2,1)}, u32[]{:S(2)}, u32[]{:S(2)}) collective-permute-start(bf16[512,2048]{1,0:T(8,128)(2,1)} %get-tuple-element.423), channel_id=1, source_target_pairs={{0,1},{1,0},{2,3},{3,2},{4,5},{5,4},{6,7},{7,6},{8,9},{9,8},{10,11... | collective-permute-start | bytes 6291464 | tf_op jit(solution)/shard_map/cond/branch_1_fun/ppermute | solution.py:749
  259.0 24.1 %collective-permute-start.5 = (bf16[512,1024]{1,0:T(8,128)(2,1)}, bf16[512,1024]{1,0:T(8,128)(2,1)}, u32[]{:S(2)}, u32[]{:S(2)}) collective-permute-start(bf16[512,1024]{1,0:T(8,128)(2,1)} %get-tuple-element.419), channel_id=1, source_target_pairs={{0,1},{1,0},{2,3},{3,2},{4,5},{5,4},{6,7},{7,6},{8,9},{9,8},{10,11... | collective-permute-start | bytes 3145736 | tf_op jit(solution)/shard_map/cond/branch_1_fun/ppermute | solution.py:749
  259.5 23.6 %collective-permute-start.6 = (bf16[512,1024]{1,0:T(8,128)(2,1)}, bf16[512,1024]{1,0:T(8,128)(2,1)}, u32[]{:S(2)}, u32[]{:S(2)}) collective-permute-start(bf16[512,1024]{1,0:T(8,128)(2,1)} %get-tuple-element.420), channel_id=1, source_target_pairs={{0,1},{1,0},{2,3},{3,2},{4,5},{5,4},{6,7},{7,6},{8,9},{9,8},{10,11... | collective-permute-start | bytes 3145736 | tf_op jit(solution)/shard_map/cond/branch_1_fun/ppermute | solution.py:749
  259.5 23.6 %collective-permute-start.7 = (bf16[512,1024]{1,0:T(8,128)(2,1)}, bf16[512,1024]{1,0:T(8,128)(2,1)}, u32[]{:S(2)}, u32[]{:S(2)}) collective-permute-start(bf16[512,1024]{1,0:T(8,128)(2,1)} %get-tuple-element.421), channel_id=1, source_target_pairs={{0,1},{1,0},{2,3},{3,2},{4,5},{5,4},{6,7},{7,6},{8,9},{9,8},{10,11... | collective-permute-start | bytes 3145736 | tf_op jit(solution)/shard_map/cond/branch_1_fun/ppermute | solution.py:749
  260.0 23.1 %collective-permute-start.8 = (bf16[512,1024]{1,0:T(8,128)(2,1)}, bf16[512,1024]{1,0:T(8,128)(2,1)}, u32[]{:S(2)}, u32[]{:S(2)}) collective-permute-start(bf16[512,1024]{1,0:T(8,128)(2,1)} %get-tuple-element.422), channel_id=1, source_target_pairs={{0,1},{1,0},{2,3},{3,2},{4,5},{5,4},{6,7},{7,6},{8,9},{9,8},{10,11... | collective-permute-start | bytes 3145736 | tf_op jit(solution)/shard_map/cond/branch_1_fun/ppermute | solution.py:749
  260.1 23.0 %all-to-all-start.1 = ((bf16[4,2,256,128]{3,2,1,0:T(8,128)(2,1)}), bf16[4,2,256,128]{3,2,1,0:T(8,128)(2,1)}, u32[]{:S(2)}, u32[]{:S(2)}) async-start(bf16[4,2,256,128]{3,2,1,0:T(8,128)(2,1)} %get-tuple-element.424), calls=%async_computation.1 | async-start | bytes 1048576 | tf_op jit(solution)/shard_map/cond/branch_1_fun/all_to_all | solution.py:776
  283.2 32.1 %all-to-all-start.2 = ((bf16[4,2,256,128]{3,2,1,0:T(8,128)(2,1)}), bf16[4,2,256,128]{3,2,1,0:T(8,128)(2,1)}, u32[]{:S(2)}, u32[]{:S(2)}) async-start(bf16[4,2,256,128]{3,2,1,0:T(8,128)(2,1)} %get-tuple-element.447), calls=%async_computation.2 | async-start | bytes 1048576 | tf_op jit(solution)/shard_map/cond/branch_1_fun/all_to_all | solution.py:776
  287.3 27.9 %collective-permute-start.10 = (bf16[256,1024]{1,0:T(8,128)(2,1)}, bf16[256,1024]{1,0:T(8,128)(2,1)}, u32[]{:S(2)}, u32[]{:S(2)}) collective-permute-start(bf16[256,1024]{1,0:T(8,128)(2,1)} %get-tuple-element.448), channel_id=1, source_target_pairs={{0,4},{1,5},{2,6},{3,7},{4,0},{5,1},{6,2},{7,3},{8,12},{9,13},{10,... | collective-permute-start | bytes 1572872 | tf_op jit(solution)/shard_map/cond/branch_1_fun/ppermute | solution.py:749
  288.8 26.4 %collective-permute-start.11 = (bf16[512,1024]{1,0:T(8,128)(2,1)}, bf16[512,1024]{1,0:T(8,128)(2,1)}, u32[]{:S(2)}, u32[]{:S(2)}) collective-permute-start(bf16[512,1024]{1,0:T(8,128)(2,1)} %get-tuple-element.449), channel_id=1, source_target_pairs={{0,1},{1,0},{2,3},{3,2},{4,5},{5,4},{6,7},{7,6},{8,9},{9,8},{10,11... | collective-permute-start | bytes 3145736 | tf_op jit(solution)/shard_map/cond/branch_1_fun/ppermute | solution.py:749
  289.0 26.3 %collective-permute-start.12 = (bf16[2,4,64,1024]{3,2,1,0:T(8,128)(2,1)}, bf16[2,4,64,1024]{3,2,1,0:T(8,128)(2,1)}, u32[]{:S(2)}, u32[]{:S(2)}) collective-permute-start(bf16[2,4,64,1024]{3,2,1,0:T(8,128)(2,1)} %get-tuple-element.450), channel_id=1, source_target_pairs={{0,8},{1,9},{2,10},{3,11},{4,12},{5,13},{6,14},{7,15},{8,0},{9,1},... | collective-permute-start | bytes 3145736 | tf_op jit(solution)/shard_map/cond/branch_1_fun/ppermute | solution.py:749
  290.5 25.5 %collective-permute-start.13 = (bf16[2,4,64,1024]{3,2,1,0:T(8,128)(2,1)}, bf16[2,4,64,1024]{3,2,1,0:T(8,128)(2,1)}, u32[]{:S(2)}, u32[]{:S(2)}) collective-permute-start(bf16[2,4,64,1024]{3,2,1,0:T(8,128)(2,1)} %get-tuple-element.451), channel_id=1, source_target_pairs={{0,16},{1,17},{2,18},{3,19},{4,20},{5,21},{6,22},{7,23},{8,24},{9,... | collective-permute-start | bytes 3145736 | tf_op jit(solution)/shard_map/cond/branch_1_fun/ppermute | solution.py:749
  318.1 44.1 %all-to-all-start.3 = ((bf16[4,3,2,256,128]{4,3,2,1,0:T(8,128)(2,1)}), bf16[4,3,2,256,128]{4,3,2,1,0:T(8,128)(2,1)}, u32[]{:S(2)}, u32[]{:S(2)}) async-start(bf16[4,3,2,256,128]{4,3,2,1,0:T(8,128)(2,1)} %get-tuple-element.457), calls=%async_computation.3 | async-start | bytes 3145728 | tf_op jit(solution)/shard_map/cond/branch_1_fun/all_to_all | solution.py:776
  322.5 28.4 %collective-permute-start.14 = (bf16[4,64,1024]{2,1,0:T(8,128)(2,1)}, bf16[4,64,1024]{2,1,0:T(8,128)(2,1)}, u32[]{:S(2)}, u32[]{:S(2)}) collective-permute-start(bf16[4,64,1024]{2,1,0:T(8,128)(2,1)} %get-tuple-element.458), channel_id=1, source_target_pairs={{0,16},{1,17},{2,18},{3,19},{4,20},{5,21},{6,22},{7,23},{8,24},{9,... | collective-permute-start | bytes 1572872 | tf_op jit(solution)/shard_map/cond/branch_1_fun/ppermute | solution.py:749
  325.5 25.4 %collective-permute-start.15 = (bf16[4,64,1024]{2,1,0:T(8,128)(2,1)}, bf16[4,64,1024]{2,1,0:T(8,128)(2,1)}, u32[]{:S(2)}, u32[]{:S(2)}) collective-permute-start(bf16[4,64,1024]{2,1,0:T(8,128)(2,1)} %get-tuple-element.459), channel_id=1, source_target_pairs={{0,8},{1,9},{2,10},{3,11},{4,12},{5,13},{6,14},{7,15},{8,0},{9,1},... | collective-permute-start | bytes 1572872 | tf_op jit(solution)/shard_map/cond/branch_1_fun/ppermute | solution.py:749
  325.5 36.7 %collective-permute-start.16 = (bf16[2,4,64,1024]{3,2,1,0:T(8,128)(2,1)}, bf16[2,4,64,1024]{3,2,1,0:T(8,128)(2,1)}, u32[]{:S(2)}, u32[]{:S(2)}) collective-permute-start(bf16[2,4,64,1024]{3,2,1,0:T(8,128)(2,1)} %get-tuple-element.460), channel_id=1, source_target_pairs={{0,8},{1,9},{2,10},{3,11},{4,12},{5,13},{6,14},{7,15},{8,0},{9,1},... | collective-permute-start | bytes 3145736 | tf_op jit(solution)/shard_map/cond/branch_1_fun/ppermute | solution.py:749
  327.6 34.7 %collective-permute-start.17 = (bf16[2,4,64,1024]{3,2,1,0:T(8,128)(2,1)}, bf16[2,4,64,1024]{3,2,1,0:T(8,128)(2,1)}, u32[]{:S(2)}, u32[]{:S(2)}) collective-permute-start(bf16[2,4,64,1024]{3,2,1,0:T(8,128)(2,1)} %get-tuple-element.461), channel_id=1, source_target_pairs={{0,16},{1,17},{2,18},{3,19},{4,20},{5,21},{6,22},{7,23},{8,24},{9,... | collective-permute-start | bytes 3145736 | tf_op jit(solution)/shard_map/cond/branch_1_fun/ppermute | solution.py:749
  364.5 24.5 %all-to-all-start.4 = ((bf16[4,3,2,256,128]{4,3,2,1,0:T(8,128)(2,1)}), bf16[4,3,2,256,128]{4,3,2,1,0:T(8,128)(2,1)}, u32[]{:S(2)}, u32[]{:S(2)}) async-start(bf16[4,3,2,256,128]{4,3,2,1,0:T(8,128)(2,1)} %get-tuple-element.462), calls=%async_computation.4 | async-start | bytes 3145728 | tf_op jit(solution)/shard_map/cond/branch_1_fun/all_to_all | solution.py:776
  389.0 72.2 %reduce-scatter.6.cloned.1.call-start = ((), (), s32[]{:S(2)}) async-start(), calls=%async_computation.13 | async-start | bytes 2621440 | tf_op jit(solution)/shard_map/cond/branch_1_fun/reduce_scatter | solution.py:1065
  397.2 25.9 %collective-permute-start.21 = (bf16[2,4,64,1024]{3,2,1,0:T(8,128)(2,1)}, bf16[2,4,64,1024]{3,2,1,0:T(8,128)(2,1)}, u32[]{:S(2)}, u32[]{:S(2)}) collective-permute-start(bf16[2,4,64,1024]{3,2,1,0:T(8,128)(2,1)} %get-tuple-element.510), channel_id=1, source_target_pairs={{0,8},{1,9},{2,10},{3,11},{4,12},{5,13},{6,14},{7,15},{8,0},{9,1},... | collective-permute-start | bytes 3145736 | tf_op jit(solution)/shard_map/cond/branch_1_fun/cond/branch_1_fun/ppermute | solution.py:749
  397.5 25.6 %collective-permute-start.22 = (bf16[2,4,64,1024]{3,2,1,0:T(8,128)(2,1)}, bf16[2,4,64,1024]{3,2,1,0:T(8,128)(2,1)}, u32[]{:S(2)}, u32[]{:S(2)}) collective-permute-start(bf16[2,4,64,1024]{3,2,1,0:T(8,128)(2,1)} %get-tuple-element.511), channel_id=1, source_target_pairs={{0,16},{1,17},{2,18},{3,19},{4,20},{5,21},{6,22},{7,23},{8,24},{9,... | collective-permute-start | bytes 3145736 | tf_op jit(solution)/shard_map/cond/branch_1_fun/cond/branch_1_fun/ppermute | solution.py:749
  423.1 21.5 %collective-permute-start.23 = (bf16[512,1024]{1,0:T(8,128)(2,1)S(1)}, bf16[512,1024]{1,0:T(8,128)(2,1)}, u32[]{:S(2)}, u32[]{:S(2)}) collective-permute-start(bf16[512,1024]{1,0:T(8,128)(2,1)S(1)} %get-tuple-element.517), channel_id=1, source_target_pairs={{0,1},{1,0},{2,3},{3,2},{4,5},{5,4},{6,7},{7,6},{8,9},{9,8},{10,11... | collective-permute-start | bytes 3145736 | tf_op jit(solution)/shard_map/cond/branch_1_fun/cond/branch_1_fun/ppermute | solution.py:749
  423.1 20.1 %collective-permute-start.24 = (bf16[2,4,64,768]{3,2,1,0:T(8,128)(2,1)S(1)}, bf16[2,4,64,768]{3,2,1,0:T(8,128)(2,1)}, u32[]{:S(2)}, u32[]{:S(2)}) collective-permute-start(bf16[2,4,64,768]{3,2,1,0:T(8,128)(2,1)S(1)} %get-tuple-element.518), channel_id=1, source_target_pairs={{0,8},{1,9},{2,10},{3,11},{4,12},{5,13},{6,14},{7,15},{8,0},{9,1},... | collective-permute-start | bytes 2359304 | tf_op jit(solution)/shard_map/cond/branch_1_fun/cond/branch_1_fun/ppermute | solution.py:749
  424.8 19.8 %collective-permute-start.25 = (bf16[2,4,64,768]{3,2,1,0:T(8,128)(2,1)S(1)}, bf16[2,4,64,768]{3,2,1,0:T(8,128)(2,1)}, u32[]{:S(2)}, u32[]{:S(2)}) collective-permute-start(bf16[2,4,64,768]{3,2,1,0:T(8,128)(2,1)S(1)} %get-tuple-element.519), channel_id=1, source_target_pairs={{0,16},{1,17},{2,18},{3,19},{4,20},{5,21},{6,22},{7,23},{8,24},{9,... | collective-permute-start | bytes 2359304 | tf_op jit(solution)/shard_map/cond/branch_1_fun/cond/branch_1_fun/ppermute | solution.py:749
  468.1 34.3 %reduce-scatter.8.cloned.1.call-start = ((), (), s32[]{:S(2)}) async-start(), calls=%async_computation.14 | async-start | bytes 1310720 | tf_op jit(solution)/shard_map/cond/branch_1_fun/reduce_scatter | solution.py:1065
  468.8 33.5 %collective-permute-start.29 = (bf16[2,4,64,1024]{3,2,1,0:T(8,128)(2,1)}, bf16[2,4,64,1024]{3,2,1,0:T(8,128)(2,1)}, u32[]{:S(2)}, u32[]{:S(2)}) collective-permute-start(bf16[2,4,64,1024]{3,2,1,0:T(8,128)(2,1)} %get-tuple-element.593), channel_id=1, source_target_pairs={{0,8},{1,9},{2,10},{3,11},{4,12},{5,13},{6,14},{7,15},{8,0},{9,1},... | collective-permute-start | bytes 3145736 | tf_op jit(solution)/shard_map/cond/branch_1_fun/ppermute | solution.py:749
  469.5 32.9 %collective-permute-start.30 = (bf16[2,4,64,1024]{3,2,1,0:T(8,128)(2,1)}, bf16[2,4,64,1024]{3,2,1,0:T(8,128)(2,1)}, u32[]{:S(2)}, u32[]{:S(2)}) collective-permute-start(bf16[2,4,64,1024]{3,2,1,0:T(8,128)(2,1)} %get-tuple-element.594), channel_id=1, source_target_pairs={{0,16},{1,17},{2,18},{3,19},{4,20},{5,21},{6,22},{7,23},{8,24},{9,... | collective-permute-start | bytes 3145736 | tf_op jit(solution)/shard_map/cond/branch_1_fun/ppermute | solution.py:749
  470.6 31.8 %collective-permute-start.31 = (bf16[4,64,768]{2,1,0:T(8,128)(2,1)}, bf16[4,64,768]{2,1,0:T(8,128)(2,1)}, u32[]{:S(2)}, u32[]{:S(2)}) collective-permute-start(bf16[4,64,768]{2,1,0:T(8,128)(2,1)} %get-tuple-element.595), channel_id=1, source_target_pairs={{0,16},{1,17},{2,18},{3,19},{4,20},{5,21},{6,22},{7,23},{8,24},{9,... | collective-permute-start | bytes 1179656 | tf_op jit(solution)/shard_map/cond/branch_1_fun/ppermute | solution.py:749
  471.5 30.8 %collective-permute-start.32 = (bf16[4,64,768]{2,1,0:T(8,128)(2,1)}, bf16[4,64,768]{2,1,0:T(8,128)(2,1)}, u32[]{:S(2)}, u32[]{:S(2)}) collective-permute-start(bf16[4,64,768]{2,1,0:T(8,128)(2,1)} %get-tuple-element.596), channel_id=1, source_target_pairs={{0,8},{1,9},{2,10},{3,11},{4,12},{5,13},{6,14},{7,15},{8,0},{9,1},... | collective-permute-start | bytes 1179656 | tf_op jit(solution)/shard_map/cond/branch_1_fun/ppermute | solution.py:749
  511.3 40.1 %reduce-scatter.10.cloned.1.call-start = ((), (), s32[]{:S(2)}) async-start(), calls=%async_computation.15 | async-start | bytes 983040 | tf_op jit(solution)/shard_map/cond/branch_1_fun/reduce_scatter | solution.py:1065
  512.1 39.4 %collective-permute-start.34 = (bf16[2,4,64,1024]{3,2,1,0:T(8,128)(2,1)}, bf16[2,4,64,1024]{3,2,1,0:T(8,128)(2,1)}, u32[]{:S(2)}, u32[]{:S(2)}) collective-permute-start(bf16[2,4,64,1024]{3,2,1,0:T(8,128)(2,1)} %get-tuple-element.599), channel_id=1, source_target_pairs={{0,8},{1,9},{2,10},{3,11},{4,12},{5,13},{6,14},{7,15},{8,0},{9,1},... | collective-permute-start | bytes 3145736 | tf_op jit(solution)/shard_map/cond/branch_1_fun/ppermute | solution.py:749
  513.5 37.9 %collective-permute-start.35 = (bf16[2,4,64,1024]{3,2,1,0:T(8,128)(2,1)}, bf16[2,4,64,1024]{3,2,1,0:T(8,128)(2,1)}, u32[]{:S(2)}, u32[]{:S(2)}) collective-permute-start(bf16[2,4,64,1024]{3,2,1,0:T(8,128)(2,1)} %get-tuple-element.600), channel_id=1, source_target_pairs={{0,16},{1,17},{2,18},{3,19},{4,20},{5,21},{6,22},{7,23},{8,24},{9,... | collective-permute-start | bytes 3145736 | tf_op jit(solution)/shard_map/cond/branch_1_fun/ppermute | solution.py:749
  515.0 36.5 %collective-permute-start.33 = (bf16[256,1024]{1,0:T(8,128)(2,1)}, bf16[256,1024]{1,0:T(8,128)(2,1)}, u32[]{:S(2)}, u32[]{:S(2)}) collective-permute-start(bf16[256,1024]{1,0:T(8,128)(2,1)} %get-tuple-element.598), channel_id=1, source_target_pairs={{0,4},{1,5},{2,6},{3,7},{4,0},{5,1},{6,2},{7,3},{8,12},{9,13},{10,... | collective-permute-start | bytes 1572872 | tf_op jit(solution)/shard_map/cond/branch_1_fun/ppermute | solution.py:749
  516.6 34.8 %collective-permute-start.36 = (bf16[4,64,1024]{2,1,0:T(8,128)(2,1)}, bf16[4,64,1024]{2,1,0:T(8,128)(2,1)}, u32[]{:S(2)}, u32[]{:S(2)}) collective-permute-start(bf16[4,64,1024]{2,1,0:T(8,128)(2,1)} %get-tuple-element.601), channel_id=1, source_target_pairs={{0,16},{1,17},{2,18},{3,19},{4,20},{5,21},{6,22},{7,23},{8,24},{9,... | collective-permute-start | bytes 1572872 | tf_op jit(solution)/shard_map/cond/branch_1_fun/ppermute | solution.py:749
  518.0 33.4 %collective-permute-start.37 = (bf16[4,64,1024]{2,1,0:T(8,128)(2,1)}, bf16[4,64,1024]{2,1,0:T(8,128)(2,1)}, u32[]{:S(2)}, u32[]{:S(2)}) collective-permute-start(bf16[4,64,1024]{2,1,0:T(8,128)(2,1)} %get-tuple-element.602), channel_id=1, source_target_pairs={{0,8},{1,9},{2,10},{3,11},{4,12},{5,13},{6,14},{7,15},{8,0},{9,1},... | collective-permute-start | bytes 1572872 | tf_op jit(solution)/shard_map/cond/branch_1_fun/ppermute | solution.py:749
  553.6 41.9 %reduce-scatter.12.cloned.1.call-start = ((), (), s32[]{:S(2)}) async-start(), calls=%async_computation.16 | async-start | bytes 1310720 | tf_op jit(solution)/shard_map/cond/branch_1_fun/reduce_scatter | solution.py:1065
  556.5 55.3 %reduce-scatter.14.cloned.1.call-start = ((), (), s32[]{:S(2)}) async-start(), calls=%async_computation.17 | async-start | bytes 1310720 | tf_op jit(solution)/shard_map/cond/branch_1_fun/reduce_scatter | solution.py:1065
  (71 other events, 671.2 us)
Sparse Core Ops, SparseCore 0:
  392.1 42.6 reduce-scatter.5
  471.9 26.7 reduce-scatter.7
  515.0 31.2 reduce-scatter.9
  557.0 26.0 reduce-scatter.11
  586.0 25.7 reduce-scatter.13
where the time goes:
time: 644 us; the launch traced here: 633 us
  Pallas kernels  287 us (45%)
  waiting for transfers between devices  151 us (23%)
  starting transfers between devices  78 us (12%)
  other arithmetic  42.6 us (7%)
  local copies, waits for them, and re-layouts  36.8 us (6%)
  between operations  18 us (3%)
  matrix products  17.8 us (3%)
    ppermute x49, waiting for transfers between devices, swap(): return lax.ppermute(value, EVERY, flipped(axis_bit, count))  107 us
    pallas_call x2, Pallas kernels, attend_backward(): pl.pallas_call(functools.partial(attn_bwd_kernel, heads, size, group), gr...  46.6 us
    pallas_call x4, Pallas kernels, column_grads(): pl.pallas_call(functools.partial(column_grad_kernel, heads, len(lefts)),...  40.8 us
    ppermute x49, starting transfers between devices, swap(): return lax.ppermute(value, EVERY, flipped(axis_bit, count))  40.3 us
    pallas_call x2, Pallas kernels, front(): pl.pallas_call(functools.partial(front_kernel, size, ffn_steps, pieces),...  39.6 us
    all_to_all x8, starting transfers between devices, exchange(): lax.all_to_all(value, 'heads', split_axis=0, concat_axis=0, tiled=True, a...  33.9 us
    pallas_call x2, Pallas kernels, attend_forward(): pl.pallas_call(functools.partial(attn_fwd_kernel, heads, size, group), gr...  32.9 us
    pallas_call x2, Pallas kernels, stream_gradient(): pl.pallas_call(down_kernel, grid=(units // wide,), in_specs=[whole((rows,...  24.5 us
  transfers between devices with their start and end apart: 66, of which 27 were waited for; matrix products, arithmetic and copies ran while one was open for 4% of the time, Pallas kernels for 36%

commit v1 on v0

--- a/solution.py
+++ b/solution.py
@@ -17,6 +17,7 @@
 BLOCK = 512
 INNER_FWD = 1024
 INNER_BWD = 512
+TURNED = 512
 LANES = 128
 BIG = 1e30
 VMEM_LIMIT = 56 << 20
@@ -390,7 +391,7 @@
 def ffn_forward(stream, gain_row, weight_in, weight_out, last_gain, upstream):
     rows, model = stream.shape
     units = weight_in.shape[1]
-    wide = 512
+    wide = min(units, 1024)
     return pl.pallas_call(
         ffn_fwd_kernel,
         grid=(units // wide,),
@@ -447,7 +448,7 @@
 def ffn_backward(upstream, stream, slope, gain_row, weight_in, weight_out):
     rows, model = stream.shape
     units = weight_in.shape[1]
-    wide = 512
+    wide = min(units, 1024)
     return pl.pallas_call(
         ffn_bwd_kernel,
         grid=(units // wide,),
@@ -490,7 +491,7 @@
 def hidden_gradient(upstream, slope, weight_out):
     rows, model = upstream.shape
     units = weight_out.shape[0]
-    wide = 512
+    wide = min(units, 1024)
     return pl.pallas_call(
         hidden_kernel,
         grid=(units // wide,),
@@ -535,7 +536,7 @@
 def stream_gradient(upstream, stream, grad, gain_row, weight, down_type):
     rows, model = stream.shape
     units = weight.shape[1]
-    wide = 512
+    wide = min(units, 1024)
     return pl.pallas_call(
         down_kernel,
         grid=(units // wide,),
@@ -560,6 +561,9 @@
 
 
 def turn(field, cosines, sines, size):
+    repeats = field.shape[1] // cosines.shape[1]
+    cosines = jnp.concatenate([cosines] * repeats, 1)
+    sines = jnp.concatenate([sines] * repeats, 1)
     lane = lax.broadcasted_iota(jnp.int32, field.shape, 1)
     half = size // 2
     width = field.shape[1]
@@ -571,18 +575,15 @@
     return field * cosines + swapped * sines
 
 
-def rope_tables(position, size, width):
+def rope_tables(position, size):
     half = size // 2
+    lane = jnp.arange(LANES, dtype=jnp.int32)
     freqs = jnp.exp(
-        -jnp.log(jnp.float32(ROPE_BASE)) * jnp.arange(half, dtype=jnp.float32) / half
+        -jnp.log(jnp.float32(ROPE_BASE)) * (lane % half).astype(jnp.float32) / half
     )
     angles = position.astype(jnp.float32)[:, None] * freqs[None, :]
-    cosines, sines = jnp.cos(angles), jnp.sin(angles)
-    repeats = width // size
-    return (
-        jnp.tile(jnp.concatenate([cosines, cosines], 1), (1, repeats)),
-        jnp.tile(jnp.concatenate([-sines, sines], 1), (1, repeats)),
-    )
+    signs = jnp.where(lane % size < half, -1.0, 1.0)
+    return (jnp.cos(angles), jnp.sin(angles) * signs[None, :])
 
 
 def front_kernel(
@@ -632,9 +633,9 @@
 ):
     rows, model = frames.shape
     units = weight_in.shape[1]
-    wide = 512
+    wide = min(units, 1024)
     ffn_steps = units // wide
-    turned_wide = cosines.shape[1]
+    turned_wide = TURNED
     turns = model // turned_wide
     pieces = model // (places * LANES)
     each = turns // pieces
@@ -653,7 +654,7 @@
 
     row_block = pl.BlockSpec((rows, model), lambda s, row: (row[0], 0))
     unit_block = pl.BlockSpec((rows, wide), lambda s, row: (row[0], ffn_at(s, row)))
-    angle_block = pl.BlockSpec((rows, turned_wide), lambda s, row: (row[0], 0))
+    angle_block = pl.BlockSpec((rows, LANES), lambda s, row: (row[0], 0))
     out_shape = [
         jax.ShapeDtypeStruct((chunks * rows, model), F32),
         jax.ShapeDtypeStruct((chunks * rows, units), BF16),
@@ -707,7 +708,7 @@
     cosines = jnp.where(rotated, cos_ref[...], 1.0)
     sines = jnp.where(rotated, -sin_ref[...], 0.0)
     places, _, chunks, frames, _ = backs[0].shape
-    wide = cosines.shape[1]
+    wide = TURNED
     per = wide // LANES
     for piece, back in enumerate(backs):
         for first in range(0, places, per):
@@ -1108,10 +1109,10 @@
     where = jnp.stack(
         [place % 2, lax.axis_index("items") if items > 1 else 0 * place]
     ).astype(jnp.int32)
-    always = jnp.min(bucket_counts) >= 0
+    always = bucket_counts[0, 0, 0] >= 0
     first = jnp.arange(chunks, dtype=jnp.int32)[:, None] * span + place % half * here
     position = first + jnp.arange(here, dtype=jnp.int32)[None]
-    cosines, sines = rope_tables(position.reshape(-1), size, 2 * LANES)
+    cosines, sines = rope_tables(position.reshape(-1), size)
     depth_rows = w_depth.astype(F32)
     gain = [gains[i : i + 1] for i in range(6)]
     counts = lax.dynamic_index_in_dim(bucket_counts[:, 0], side, 0, keepdims=False)
@@ -1352,25 +1353,35 @@
     attn.second(second_sums(attn)[0])
     one_out = Scatter(*shares_out)
     middle_columns = [w.shape[1] for w in (w_point_out, w_point_in, w_out)]
-    middle_sum = last_sum(middle, columns=middle_columns)
-
     middle_grad, shares, (grad_zero, _, gain_zero) = fenced(
         always,
         (one_out, attn),
         lambda: (
-            along_z(middle_sum),
+            along_z(last_sum(middle, columns=middle_columns)),
             column_grads([ent_one], [grad_pre], ways, where, items),
             stream_gradient(grad_one, stream, grad_pre[0], gain[0], w_ffn1_in, BF16),
         ),
     )
     one_in = Scatter(*shares)
     one_out.second(second_sums(one_out)[0])
-    attn_sum = last_sum(attn)
     grad_own, grad_theirs = parted(grad_zero, side)
     attn_grad, grad_other = fenced(
-        always, (one_in, one_out), lambda: (along_z(attn_sum), across(grad_theirs))
+        always, (one_in, one_out), lambda: (along_z(last_sum(attn)), across(grad_theirs))
     )
     one_in.second(second_sums(one_in)[0])
+
+    hidden = w_ffn1_in.shape[1]
+
+    def unfolded(share):
+        each, wide = share.shape
+        span = hidden // ways
+        halves = share.reshape(2, each // 2, wide)
+        parts = [
+            halves[half, :, i * span : (i + 1) * span]
+            for i in range(wide // span)
+            for half in range(2)
+        ]
+        return jnp.concatenate(parts, 0).T.astype(F32)
 
     def last_part():
         out_grads = along_z(last_sum(one_out))
@@ -1383,41 +1394,37 @@
                 0,
             )
         )
-        return (out_grads, along_z(last_sum(scatter)), small)
-
-    one_out_grad, one_in_grad, small = fenced(always, (), last_part)
-    hidden = w_ffn1_in.shape[1]
-
-    def unfolded(share):
-        each, wide = share.shape
-        span = hidden // ways
-        halves = share.reshape(2, each // 2, wide)
-        parts = [
-            halves[half, :, i * span : (i + 1) * span]
-            for i in range(wide // span)
-            for half in range(2)
-        ]
-        return jnp.concatenate(parts, 0).T.astype(F32)
-
-    middle_parts = []
-    start = 0
-    for weight in (w_point_out, w_point_in, w_out):
-        each = weight.shape[1] // lax.axis_size("items")
-        middle_parts.append(middle_grad[0][:, start : start + each].astype(F32))
-        start += each
+        middle_parts = []
+        start = 0
+        for columns in middle_columns:
+            each = columns // lax.axis_size("items")
+            middle_parts.append(middle_grad[0][:, start : start + each].astype(F32))
+            start += each
+        ready = (
+            gathered(out_own[None], out_other[None], side),
+            gathered(grad_own[None], grad_other[None], side),
+            attn_grad[0].astype(F32),
+            middle_parts,
+            two_grads[1].astype(F32),
+            unfolded(two_grads[0]),
+        )
+        return (out_grads, along_z(last_sum(scatter)), small, ready)
+
+    one_out_grad, one_in_grad, small, ready = fenced(always, (), last_part)
+    out, grad_in, attn_full, middle_parts, two_in_full, two_out_full = ready
     return (
-        gathered(out_own[None], out_other[None], side),
-        gathered(grad_own[None], grad_other[None], side),
+        out,
+        grad_in,
         small[:6],
         one_in_grad[0].astype(F32),
         unfolded(one_out_grad[0]),
-        attn_grad[0].astype(F32),
+        attn_full,
         middle_parts[2],
         middle_parts[1],
         small[6:],
         middle_parts[0],
-        two_grads[1].astype(F32),
-        unfolded(two_grads[0]),
+        two_in_full,
+        two_out_full,
     )
 
 

time: 644 us -> 620 us (0.963)
  waiting for transfers between devices: 151 us -> 137 us
  Pallas kernels: 287 us -> 274 us
  starting transfers between devices: 78 us -> 85.4 us
    ppermute x49, waiting for transfers between devices: 107 us -> 99.1 us  [swap(): return lax.ppermute(value, EVERY, flipped(axis_bit, count))]
    ppermute x49, starting transfers between devices: 40.3 us -> 47.5 us  [swap(): return lax.ppermute(value, EVERY, flipped(axis_bit, count))]
  transfers between devices with their start and end apart: 66 -> 66, of which waited for: 27 -> 25; matrix products, arithmetic and copies ran while one was open for 4% -> 6% of each run, Pallas kernels for 36% -> 36%
where the time goes in v1:
time: 620 us; the launch traced here: 610 us
  Pallas kernels  274 us (44%)
  waiting for transfers between devices  137 us (22%)
  starting transfers between devices  85.4 us (14%)
  other arithmetic  41.5 us (7%)
  local copies, waits for them, and re-layouts  33.6 us (5%)
  matrix products  18.8 us (3%)
  between operations  18.1 us (3%)
    ppermute x49, waiting for transfers between devices, swap(): return lax.ppermute(value, EVERY, flipped(axis_bit, count))  99.1 us
    ppermute x49, starting transfers between devices, swap(): return lax.ppermute(value, EVERY, flipped(axis_bit, count))  47.5 us
    pallas_call x2, Pallas kernels, attend_backward(): pl.pallas_call(functools.partial(attn_bwd_kernel, heads, size, group), gr...  46.6 us
    pallas_call x4, Pallas kernels, column_grads(): pl.pallas_call(functools.partial(column_grad_kernel, heads, len(lefts)),...  41.3 us
    pallas_call x2, Pallas kernels, front(): pl.pallas_call(functools.partial(front_kernel, size, ffn_steps, pieces),...  33.6 us
    all_to_all x8, starting transfers between devices, exchange(): lax.all_to_all(value, 'heads', split_axis=0, concat_axis=0, tiled=True, a...  33.6 us
    pallas_call x2, Pallas kernels, attend_forward(): pl.pallas_call(functools.partial(attn_fwd_kernel, heads, size, group), gr...  32.9 us
    pallas_call x2, Pallas kernels, stream_gradient(): pl.pallas_call(down_kernel, grid=(units // wide,), in_specs=[whole((rows,...  21.9 us
  transfers between devices with their start and end apart: 66, of which 25 were waited for; matrix products, arithmetic and copies ran while one was open for 6% of the time, Pallas kernels for 36%

profile of v1, /device:TPU:0, one launch (start us, length us, event | category | flops | bytes accessed | tf_op | source)
XLA Modules:
  0.0 610.3 jit_solution(11712054900066138622)
XLA Ops:
  12.9 28.6 %conditional.15 = (f32[512,1024]{1,0:T(8,128)}, bf16[512,4096]{1,0:T(8,128)(2,1)}, bf16[512,4096]{1,0:T(8,128)(2,1)}, bf16[512,1024]{1,0:T(8,128)(2,1)}, bf16[51...) conditional(s32[]{:T(128)} %convert_element_type.152, ...), branch_computations={%region_0.1_spmd, %region_1.2_spmd} | conditional | flops 5905580032 | bytes 34603160 | solution.py:760
  18.2 16.1 %front.2 = (f32[512,1024]{1,0:T(8,128)}, bf16[512,4096]{1,0:T(8,128)(2,1)}, bf16[512,4096]{1,0:T(8,128)(2,1)}, bf16[512,1024]{1,0:T(8,128)(2,1)}, bf16[512,1024]...) custom-call(s32[1]{0:T(128)} %bitcast.row_ref, ...), custom_call_target="tpu_custom_call" | custom-call | flops 5905580032 | bytes 31457280 | tf_op jit(solution)/shard_map/cond/branch_1_fun/front/pallas_call | solution.py:688
  34.3 7.2 %collective-permute-done.38 = bf16[256,1024]{1,0:T(8,128)(2,1)} collective-permute-done((bf16[256,1024]{1,0:T(8,128)(2,1)S(1)}, bf16[256,1024]{1,0:T(8,128)(2,1)}, u32[]{:S(2)}, u32[]{:S(2)}) %collective-permute-start.38) | collective-permute-done | bytes 524320 | tf_op jit(solution)/shard_map/cond/branch_1_fun/ppermute | solution.py:750
  41.5 17.5 %front.3 = (f32[512,1024]{1,0:T(8,128)}, bf16[512,4096]{1,0:T(8,128)(2,1)}, bf16[512,4096]{1,0:T(8,128)(2,1)}, bf16[512,1024]{1,0:T(8,128)(2,1)}, bf16[512,1024]...) custom-call(s32[1]{0:T(128)} %bitcast.26.row_ref, ...), custom_call_target="tpu_custom_call", output_to_operand_aliasing={{0}: (11, {}), {1}: (12, {}), {2}: (13, {}), {3}: (14, {}),... | custom-call | flops 5905580032 | bytes 31457280 | tf_op jit(solution)/shard_map/front/pallas_call | solution.py:688
  59.1 4.5 all-to-all-start.6
  69.8 13.9 %all-to-all-done.6 = bf16[4,3,2,256,128]{4,3,2,1,0:T(8,128)(2,1)} async-done(((bf16[4,3,2,256,128]{4,3,2,1,0:T(8,128)(2,1)}), bf16[4,3,2,256,128]{4,3,2,1,0:T(8,128)(2,1)}, u32[]{:S(2)}, u32[]{:S(2)}) %all-to-all-start.6) | async-done | bytes 1572896 | tf_op jit(solution)/shard_map/all_to_all | solution.py:777
  83.7 25.1 %conditional.16 = (bf16[4,2,256,128]{3,2,1,0:T(8,128)(2,1)}, f32[2048,128]{1,0:T(8,128)}, f32[2,2048,128]{2,1,0:T(8,128)}, bf16[4,3,2,256,128]{4,3,2,1,0:T(8,128...) conditional(s32[]{:T(128)} %convert_element_type.152, () %tuple.134, ...), branch_computations={%region_2.3_spmd, %region_3.4_spmd} | conditional | flops 8589934592 | bytes 36176080 | solution.py:760
  84.2 4.4 all-to-all-start
  89.2 16.4 %attend_forward.2 = (bf16[4,2,256,128]{3,2,1,0:T(8,128)(2,1)}, f32[2048,128]{1,0:T(8,128)}, f32[2,2048,128]{2,1,0:T(8,128)}) custom-call(s32[2]{0:T(128)S(1)} %get-tuple-element.428.counts_ref, bf16[4,3,2,256,128]{4,3,2,1,0:T(8,128)(2,1)} %get-tuple-element.429.qkv_ref), custom_call_target="tpu_custom_call" | custom-call | flops 8589934592 | bytes 6291456 | tf_op jit(solution)/shard_map/cond/branch_1_fun/attend_forward/pallas_call | solution.py:221
  108.8 26.9 %conditional.17 = (bf16[4,2,256,128]{3,2,1,0:T(8,128)(2,1)}, f32[2048,128]{1,0:T(8,128)}, f32[2,2048,128]{2,1,0:T(8,128)}, bf16[4,2,256,128]{3,2,1,0:T(8,128)(2,1)}, bf16[256,1024]{1,0:T(8,128)(2,1)}) conditional(s32[]{:T(128)} %convert_element_type.152, () %tuple.138, (s32[2]{0:T(128)S(1)}, bf16[4,3,2,256,128]{4,3,2,1,0:T(8,128)(2,1)}, ...), branch_computations={%region_4.5_spmd, %region_5.6_spmd} | conditional | flops 8589934592 | bytes 11010210 | solution.py:760
  115.7 16.5 %attend_forward.3 = (bf16[4,2,256,128]{3,2,1,0:T(8,128)(2,1)}, f32[2048,128]{1,0:T(8,128)}, f32[2,2048,128]{2,1,0:T(8,128)}) custom-call(s32[2]{0:T(128)S(1)} %get-tuple-element.437.counts_ref, bf16[4,3,2,256,128]{4,3,2,1,0:T(8,128)(2,1)} %get-tuple-element.438.qkv_ref), custom_call_target="tpu_custom_call" | custom-call | flops 8589934592 | bytes 6291456 | tf_op jit(solution)/shard_map/cond/branch_1_fun/attend_forward/pallas_call | solution.py:221
  143.8 4.1 all-to-all-done.7
  174.2 18.0 %ffn_forward.1 = (bf16[512,1024]{1,0:T(8,128)(2,1)}, f32[512,1024]{1,0:T(8,128)}, f32[1,1024]{1,0:T(1,128)}, bf16[512,4096]{1,0:T(8,128)(2,1)}, bf16[512,4096]{1...) custom-call(f32[512,1024]{1,0:T(8,128)S(1)} %convolution_add_fusion.x_ref, f32[1,1024]{1,0:T(1,128)S(1)} %get-tuple-element.1054.gain_ref, ...), custom_call_target="tpu_custom_call" | custom-call | flops 8589934592 | bytes 25165824 | tf_op jit(solution)/shard_map/ffn_forward/pallas_call | solution.py:395
  193.2 19.2 %conditional.18 = (f32[512,1024]{1,0:T(8,128)S(1)}, f32[1,1024]{1,0:T(1,128)}, bf16[512,1024]{1,0:T(8,128)(2,1)}, bf16[512,4096]{1,0:T(8,128)(2,1)}, bf16[512,40...) conditional(s32[]{:T(128)} %convert_element_type.152, () %tuple.142, (f32[512,1024]{1,0:T(8,128)S(1)}, ...), branch_computations={%region_10.11_spmd, %region_11.12_spmd} | conditional | flops 8589934592 | bytes 58720412 | solution.py:760
  194.7 17.7 %ffn_backward.1 = (f32[512,1024]{1,0:T(8,128)S(1)}, f32[1,1024]{1,0:T(1,128)}, bf16[512,1024]{1,0:T(8,128)(2,1)}, bf16[512,4096]{1,0:T(8,128)(2,1)}) custom-call(f32[512,1024]{1,0:T(8,128)} %copy-done.55, f32[1,1024]{1,0:T(1,128)S(1)} %get-tuple-element.446.gain_ref, f32[512,1024]{1,0:T(8,128)} %get-tuple-element.447.up_ref, ...), custom_call_target="tpu_custom_call" | custom-call | flops 8589934592 | bytes 29360128 | tf_op jit(solution)/shard_map/cond/branch_1_fun/ffn_backward/pallas_call | solution.py:452
  214.4 4.9 multiply_reduce_fusion
  245.9 24.3 %conditional.19 = (bf16[512,1024]{1,0:T(8,128)(2,1)}, bf16[512,1024]{1,0:T(8,128)(2,1)}, bf16[512,1024]{1,0:T(8,128)(2,1)}, bf16[512,1024]{1,0:T(8,128)(2,1)}, b...) conditional(s32[]{:T(128)} %convert_element_type.152, ...), branch_computations={%region_16.17_spmd, %region_17.18_spmd} | conditional | flops 8589934592 | bytes 64487796 | solution.py:760
  247.0 4.1 all-to-all-start.1
  251.2 9.2 %out_grad.2 = (bf16[2,4,64,1024]{3,2,1,0:T(8,128)(2,1)S(1)}, bf16[2,4,64,1024]{3,2,1,0:T(8,128)(2,1)S(1)}, bf16[2,4,64,1024]{3,2,1,0:T(8,128)(2,1)}, bf16[2,4,64,1024]{3,2,1,0:T(8,128)(2,1)}) custom-call(s32[2]{0:T(128)S(1)} %get-tuple-element.463.place_ref, bf16[512,1024]{1,0:T(8,128)(2,1)} %get-tuple-element.464.up_own, ...), custom_call_target="tpu_custom_call" | custom-call | flops 4294967296 | bytes 16777216 | tf_op jit(solution)/shard_map/cond/branch_1_fun/out_grad/pallas_call | solution.py:869
  260.4 9.9 %column_grads.4 = (bf16[2,4,64,1024]{3,2,1,0:T(8,128)(2,1)S(1)}, bf16[2,4,64,1024]{3,2,1,0:T(8,128)(2,1)}, bf16[2,4,64,1024]{3,2,1,0:T(8,128)(2,1)}, bf16[2,4,64,1024]{3,2,1,0:T(8,128)(2,1)}) custom-call(s32[2]{0:T(128)S(1)} %get-tuple-element.463.place_ref, bf16[512,1024]{1,0:T(8,128)(2,1)S(1)} %copy-done.53, bf16[512,1024]{1,0:T(8,128)(2,1)} %get-tuple-element.473.refs_1_, ...), custom_call_target="tpu_custom_call" | custom-call | flops 4294967296 | bytes 16777216 | tf_op jit(solution)/shard_map/cond/branch_1_fun/column_grads/pallas_call | solution.py:946
  270.3 31.4 %conditional.20 = (bf16[4,3,2,256,128]{4,3,2,1,0:T(8,128)(2,1)}, bf16[4,2,256,128]{3,2,1,0:T(8,128)(2,1)}, bf16[256,1024]{1,0:T(8,128)(2,1)}, bf16[512,1024]{1,0...) conditional(s32[]{:T(128)} %convert_element_type.152, () %tuple.140, ...), branch_computations={%region_18.19_spmd, %region_19.20_spmd} | conditional | flops 17179869184 | bytes 25690352 | solution.py:760
  278.4 23.3 %attend_backward.2 = bf16[4,3,2,256,128]{4,3,2,1,0:T(8,128)(2,1)} custom-call(s32[2]{0:T(128)S(1)} %get-tuple-element.480.counts_ref, bf16[4,3,2,256,128]{4,3,2,1,0:T(8,128)(2,1)} %get-tuple-element.481.qkv_ref, f32[2048,128]{1,0:T(8,128)} %get-tuple-element.482.full_ref, f32[2,2048,128]{2,1,0:T(8,128)} %get-tuple-element.483.lse_ref, ...), custom_call_target="tpu_custom_call" | custom-call | flops 17179869184 | bytes 9437184 | tf_op jit(solution)/shard_map/cond/branch_1_fun/attend_backward/pallas_call | solution.py:331
  303.8 44.0 %conditional.21 = (bf16[4,3,2,256,128]{4,3,2,1,0:T(8,128)(2,1)}, bf16[4,3,2,256,128]{4,3,2,1,0:T(8,128)(2,1)}, bf16[4,64,1024]{2,1,0:T(8,128)(2,1)}, bf16[4,64,1...) conditional(s32[]{:T(128)} %convert_element_type.152, () %tuple.133, ...), branch_computations={%region_20.21_spmd, %region_21.22_spmd} | conditional | flops 17179869184 | bytes 26738928 | solution.py:760
  303.8 4.4 all-to-all-start.3
  312.9 23.3 %attend_backward.3 = bf16[4,3,2,256,128]{4,3,2,1,0:T(8,128)(2,1)} custom-call(s32[2]{0:T(128)S(1)} %get-tuple-element.490.counts_ref, bf16[4,3,2,256,128]{4,3,2,1,0:T(8,128)(2,1)} %get-tuple-element.491.qkv_ref, f32[2048,128]{1,0:T(8,128)} %get-tuple-element.492.full_ref, f32[2,2048,128]{2,1,0:T(8,128)} %get-tuple-element.493.lse_ref, ...), custom_call_target="tpu_custom_call" | custom-call | flops 17179869184 | bytes 9437184 | tf_op jit(solution)/shard_map/cond/branch_1_fun/attend_backward/pallas_call | solution.py:331
  336.2 11.6 %collective-permute-done.14 = bf16[4,64,1024]{2,1,0:T(8,128)(2,1)} collective-permute-done((bf16[4,64,1024]{2,1,0:T(8,128)(2,1)}, bf16[4,64,1024]{2,1,0:T(8,128)(2,1)}, u32[]{:S(2)}, u32[]{:S(2)}) %collective-permute-start.14) | collective-permute-done | bytes 524320 | tf_op jit(solution)/shard_map/cond/branch_1_fun/ppermute | solution.py:750
  350.0 25.0 %conditional.22 = (bf16[4,3,2,256,128]{4,3,2,1,0:T(8,128)(2,1)}, bf16[2,4,64,1024]{3,2,1,0:T(8,128)(2,1)}, bf16[2,4,64,1024]{3,2,1,0:T(8,128)(2,1)}, bf16[2,4,64...) conditional(s32[]{:T(128)} %convert_element_type.152, ...), branch_computations={%region_22.23_spmd, %region_23.24_spmd} | conditional | flops 4294967296 | bytes 38273240 | solution.py:760
  350.1 4.5 all-to-all-start.4
  356.8 12.6 %column_grads.5 = (bf16[2,4,64,1024]{3,2,1,0:T(8,128)(2,1)}, bf16[2,4,64,1024]{3,2,1,0:T(8,128)(2,1)}, bf16[2,4,64,1024]{3,2,1,0:T(8,128)(2,1)}, bf16[2,4,64,1024]{3,2,1,0:T(8,128)(2,1)}) custom-call(s32[2]{0:T(128)S(1)} %get-tuple-element.501.place_ref, bf16[512,1024]{1,0:T(8,128)(2,1)} %get-tuple-element.502.refs_0_, ...), custom_call_target="tpu_custom_call" | custom-call | flops 4294967296 | bytes 16777216 | tf_op jit(solution)/shard_map/cond/branch_1_fun/column_grads/pallas_call | solution.py:946
  375.0 74.0 %conditional.23 = (bf16[128,1024]{1,0:T(8,128)(2,1)S(1)}, bf16[128,1024]{1,0:T(8,128)(2,1)S(1)}, bf16[2,4,64,1024]{3,2,1,0:T(8,128)(2,1)}, bf16[2,4,64,1024]{3,2...) conditional(s32[]{:T(128)} %convert_element_type.152, ...), branch_computations={%region_24.25_spmd, %region_25.33_spmd} | conditional | flops 15032385536 | bytes 157811728 | solution.py:760
  376.8 32.4 %conditional = (f32[512,1024]{1,0:T(8,128)}, bf16[512,1024]{1,0:T(8,128)(2,1)S(1)}, f32[1,1024]{1,0:T(1,128)}, bf16[2,4,64,768]{3,2,1,0:T(8,128)(2,1)}, bf16[2,4...) conditional(s32[]{:T(128)} %convert_element_type.113, () %tuple.90, ...), branch_computations={%region_27.27_spmd, %region_28.28_spmd} | conditional | flops 6442450944 | bytes 61866204 | solution.py:760
  376.8 6.1 unturned.1.grad_ref.refs_2_
  384.7 10.2 %stream_gradient.2 = (f32[512,1024]{1,0:T(8,128)}, bf16[512,1024]{1,0:T(8,128)(2,1)S(1)}, f32[1,1024]{1,0:T(1,128)}) custom-call(f32[512,1024]{1,0:T(8,128)} %get-tuple-element.530.x_ref, f32[1,1024]{1,0:T(1,128)S(1)} %get-tuple-element.531.gain_ref, f32[512,1024]{1,0:T(8,128)S(1)} %get-tuple-element.532.up_ref, bf16[512,3072]{1,0:T(8,128)(2,1)} %unturned.1.grad_ref.refs_2_, ...), custom_call_target="tpu_custom_call" | custom-call | flops 3221225472 | bytes 9437184 | tf_op jit(solution)/shard_map/cond/branch_1_fun/cond/branch_1_fun/stream_gradient/pallas_call | solution.py:540
  396.6 8.8 %column_grads.6 = (bf16[2,4,64,768]{3,2,1,0:T(8,128)(2,1)}, bf16[2,4,64,768]{3,2,1,0:T(8,128)(2,1)}, bf16[2,4,64,768]{3,2,1,0:T(8,128)(2,1)S(1)}, bf16[2,4,64,768]{3,2,1,0:T(8,128)(2,1)S(1)}) custom-call(s32[2]{0:T(128)S(1)} %get-tuple-element.541.place_ref, bf16[512,1024]{1,0:T(8,128)(2,1)} %get-tuple-element.542.refs_0_, ...), custom_call_target="tpu_custom_call" | custom-call | flops 3221225472 | bytes 12582912 | tf_op jit(solution)/shard_map/cond/branch_1_fun/cond/branch_1_fun/column_grads/pallas_call | solution.py:946
  409.2 21.2 %conditional.1 = (bf16[512,1024]{1,0:T(8,128)(2,1)S(1)}, bf16[512,4096]{1,0:T(8,128)(2,1)}, bf16[512,1024]{1,0:T(8,128)(2,1)}, bf16[2,4,64,768]{3,2,1,0:T(8,128)(2,1)}, bf16[2,4,64,768]{3,2,1,0:T(8,128)(2,1)}) conditional(s32[]{:T(128)} %convert_element_type.113, () %tuple.93, (f32[512,1024]{1,0:T(8,128)}, bf16[512,4096]{1,0:T(8,128)(2,1)}, ...), branch_computations={%region_29.29_spmd, %region_30.30_spmd} | conditional | flops 4294967296 | bytes 31457440 | solution.py:760
  412.0 10.5 %hidden_gradient.1 = (bf16[512,1024]{1,0:T(8,128)(2,1)S(1)}, bf16[512,4096]{1,0:T(8,128)(2,1)}) custom-call(f32[512,1024]{1,0:T(8,128)} %get-tuple-element.550.up_ref, bf16[512,4096]{1,0:T(8,128)(2,1)} %get-tuple-element.551.slope_ref, bf16[4096,1024]{1,0:T(8,128)(2,1)} %get-tuple-element.552.wout_ref), custom_call_target="tpu_custom_call" | custom-call | flops 4294967296 | bytes 20971520 | tf_op jit(solution)/shard_map/cond/branch_1_fun/cond/branch_1_fun/hidden_gradient/pallas_call | solution.py:495
  422.5 6.8 %collective-permute-done.24 = bf16[2,4,64,768]{3,2,1,0:T(8,128)(2,1)} collective-permute-done((bf16[2,4,64,768]{3,2,1,0:T(8,128)(2,1)S(1)}, bf16[2,4,64,768]{3,2,1,0:T(8,128)(2,1)}, u32[]{:S(2)}, u32[]{:S(2)}) %collective-permute-start.24) | collective-permute-done | bytes 786464 | tf_op jit(solution)/shard_map/cond/branch_1_fun/cond/branch_1_fun/ppermute | solution.py:750
  432.1 15.7 %conditional.2 = (bf16[512,4096]{1,0:T(8,128)(2,1)}, bf16[2,4,64,1024]{3,2,1,0:T(8,128)(2,1)}, bf16[2,4,64,1024]{3,2,1,0:T(8,128)(2,1)}, bf16[2,4,64,1024]{3,2,1...) conditional(s32[]{:T(128)} %convert_element_type.113, () %tuple.92, ...), branch_computations={%region_31.31_spmd, %region_32.32_spmd} | conditional | flops 4294967296 | bytes 37748912 | solution.py:760
  434.0 9.2 %out_grad.3 = (bf16[2,4,64,1024]{3,2,1,0:T(8,128)(2,1)}, bf16[2,4,64,1024]{3,2,1,0:T(8,128)(2,1)}, bf16[2,4,64,1024]{3,2,1,0:T(8,128)(2,1)}, bf16[2,4,64,1024]{3,2,1,0:T(8,128)(2,1)}) custom-call(s32[2]{0:T(128)S(1)} %get-tuple-element.559.place_ref, bf16[512,1024]{1,0:T(8,128)(2,1)S(1)} %get-tuple-element.560.up_own, ...), custom_call_target="tpu_custom_call" | custom-call | flops 4294967296 | bytes 16777216 | tf_op jit(solution)/shard_map/cond/branch_1_fun/cond/branch_1_fun/out_grad/pallas_call | solution.py:869
  451.6 36.2 %conditional.24 = (bf16[128,1024]{1,0:T(8,128)(2,1)}, bf16[2,4,64,1024]{3,2,1,0:T(8,128)(2,1)S(1)}, bf16[2,4,64,1024]{3,2,1,0:T(8,128)(2,1)S(1)}, bf16[2,4,64,10...) conditional(s32[]{:T(128)} %convert_element_type.152, ...), branch_computations={%region_33.34_spmd, %region_34.36_spmd} | conditional | flops 8589934592 | bytes 53215556 | solution.py:760
  458.6 10.0 %column_grads.7 = (bf16[2,4,64,1024]{3,2,1,0:T(8,128)(2,1)S(1)}, bf16[2,4,64,1024]{3,2,1,0:T(8,128)(2,1)S(1)}, bf16[2,4,64,1024]{3,2,1,0:T(8,128)(2,1)}, bf16[2,4,64,1024]{3,2,1,0:T(8,128)(2,1)}) custom-call(s32[2]{0:T(128)S(1)} %get-tuple-element.620.place_ref, bf16[512,1024]{1,0:T(8,128)(2,1)} %get-tuple-element.621.refs_0_, ...), custom_call_target="tpu_custom_call" | custom-call | flops 4294967296 | bytes 16777216 | tf_op jit(solution)/shard_map/cond/branch_1_fun/column_grads/pallas_call | solution.py:946
  468.7 11.7 %stream_gradient.3 = (bf16[512,1024]{1,0:T(8,128)(2,1)}, bf16[512,1024]{1,0:T(8,128)(2,1)}, f32[1,1024]{1,0:T(1,128)}) custom-call(bf16[512,1024]{1,0:T(8,128)(2,1)S(1)} %copy-done.25, f32[1,1024]{1,0:T(1,128)S(1)} %get-tuple-element.630.gain_ref, f32[512,1024]{1,0:T(8,128)} %get-tuple-element.631.up_ref, ...), custom_call_target="tpu_custom_call" | custom-call | flops 4294967296 | bytes 12582912 | tf_op jit(solution)/shard_map/cond/branch_1_fun/stream_gradient/pallas_call | solution.py:540
  480.4 7.4 %collective-permute-done.31 = bf16[4,64,768]{2,1,0:T(8,128)(2,1)} collective-permute-done((bf16[4,64,768]{2,1,0:T(8,128)(2,1)}, bf16[4,64,768]{2,1,0:T(8,128)(2,1)}, u32[]{:S(2)}, u32[]{:S(2)}) %collective-permute-start.31) | collective-permute-done | bytes 393248 | tf_op jit(solution)/shard_map/cond/branch_1_fun/ppermute | solution.py:750
  492.3 41.9 %conditional.25 = (bf16[128,768]{1,0:T(8,128)(2,1)}, bf16[256,1024]{1,0:T(8,128)(2,1)}, bf16[2,4,64,1024]{3,2,1,0:T(8,128)(2,1)}, bf16[2,4,64,1024]{3,2,1,0:T(8,...) conditional(s32[]{:T(128)} %convert_element_type.152, () %tuple.152, ...), branch_computations={%region_36.37_spmd, %region_37.39_spmd} | conditional | bytes 20775200 | solution.py:760
  502.3 31.9 %collective-permute-done.33 = bf16[256,1024]{1,0:T(8,128)(2,1)} collective-permute-done((bf16[256,1024]{1,0:T(8,128)(2,1)}, bf16[256,1024]{1,0:T(8,128)(2,1)}, u32[]{:S(2)}, u32[]{:S(2)}) %collective-permute-start.33) | collective-permute-done | bytes 524320 | tf_op jit(solution)/shard_map/cond/branch_1_fun/ppermute | solution.py:750
  536.3 59.8 %conditional.26 = (bf16[128,1024]{1,0:T(8,128)(2,1)}, bf16[128,1024]{1,0:T(8,128)(2,1)}, f32[11,1024]{1,0:T(8,128)S(1)}, bf16[2,256,1024]{2,1,0:T(8,128)(2,1)}, ...) conditional(s32[]{:T(128)} %convert_element_type.152, ...), branch_computations={%region_46.47_spmd, %region_47.50_spmd} | conditional | flops 3562497 | bytes 39351036 | solution.py:760
  541.4 11.4 %collective-permute-done.40.refs_2_ = bf16[4,64,1024]{2,1,0:T(8,128)(2,1)S(1)} collective-permute-done((bf16[4,64,1024]{2,1,0:T(8,128)(2,1)}, bf16[4,64,1024]{2,1,0:T(8,128)(2,1)S(1)}, u32[]{:S(2)}, u32[]{:S(2)}) %collective-permute-start.40) | collective-permute-done | bytes 524320 | tf_op jit(solution)/shard_map/cond/branch_1_fun/ppermute | solution.py:750
  583.2 12.9 %reduce-scatter.14.cloned.1.call-done = bf16[1,1,2,64,1024]{4,3,2,1,0:T(8,128)(2,1)} async-done(((bf16[4,1,2,64,1024]{4,3,2,1,0:T(8,128)(2,1)}), bf16[1,1,2,64,1024]{4,3,2,1,0:T(8,128)(2,1)}) %reduce-scatter.14.cloned.1.call-update) | async-done | bytes 262160 | tf_op jit(solution)/shard_map/cond/branch_1_fun/reduce_scatter | solution.py:1066
  (339 shorter events, 209.5 us)
Async XLA Ops:
  14.1 27.4 %collective-permute-start.38 = (bf16[256,1024]{1,0:T(8,128)(2,1)S(1)}, bf16[256,1024]{1,0:T(8,128)(2,1)}, u32[]{:S(2)}, u32[]{:S(2)}) collective-permute-start(bf16[256,1024]{1,0:T(8,128)(2,1)S(1)} %dynamic-slice_bitcast_fusion), channel_id=1, source_target_pairs={{0,4},{1,5},{2,6},{3,7},{4,0},{5,1},{6,2},{7,3},{8,12},{9,13},{10,... | collective-permute-start | bytes 1572872 | tf_op jit(solution)/shard_map/cond/branch_1_fun/ppermute | solution.py:750
  59.1 24.6 %all-to-all-start.6 = ((bf16[4,3,2,256,128]{4,3,2,1,0:T(8,128)(2,1)}), bf16[4,3,2,256,128]{4,3,2,1,0:T(8,128)(2,1)}, u32[]{:S(2)}, u32[]{:S(2)}) async-start(bf16[4,3,2,256,128]{4,3,2,1,0:T(8,128)(2,1)} %get-tuple-element.841), calls=%async_computation.11 | async-start | bytes 3145728 | tf_op jit(solution)/shard_map/all_to_all | solution.py:777
  84.1 24.6 %collective-permute-start = (bf16[512,4096]{1,0:T(8,128)(2,1)}, bf16[512,4096]{1,0:T(8,128)(2,1)}, u32[]{:S(2)}, u32[]{:S(2)}) collective-permute-start(bf16[512,4096]{1,0:T(8,128)(2,1)} %get-tuple-element.434), channel_id=1, source_target_pairs={{0,1},{1,0},{2,3},{3,2},{4,5},{5,4},{6,7},{7,6},{8,9},{9,8},{10,11... | collective-permute-start | bytes 12582920 | tf_op jit(solution)/shard_map/cond/branch_1_fun/ppermute | solution.py:750
  84.2 24.5 %all-to-all-start = ((bf16[4,3,2,256,128]{4,3,2,1,0:T(8,128)(2,1)}), bf16[4,3,2,256,128]{4,3,2,1,0:T(8,128)(2,1)}, u32[]{:S(2)}, u32[]{:S(2)}) async-start(bf16[4,3,2,256,128]{4,3,2,1,0:T(8,128)(2,1)} %get-tuple-element.433), calls=%async_computation | async-start | bytes 3145728 | tf_op jit(solution)/shard_map/cond/branch_1_fun/all_to_all | solution.py:777
  88.6 17.0 %collective-permute-start.1 = (bf16[512,1024]{1,0:T(8,128)(2,1)}, bf16[512,1024]{1,0:T(8,128)(2,1)}, u32[]{:S(2)}, u32[]{:S(2)}) collective-permute-start(bf16[512,1024]{1,0:T(8,128)(2,1)} %get-tuple-element.435), channel_id=1, source_target_pairs={{0,1},{1,0},{2,3},{3,2},{4,5},{5,4},{6,7},{7,6},{8,9},{9,8},{10,11... | collective-permute-start | bytes 3145736 | tf_op jit(solution)/shard_map/cond/branch_1_fun/ppermute | solution.py:750
  89.1 16.5 %collective-permute-start.2 = (bf16[512,1024]{1,0:T(8,128)(2,1)}, bf16[512,1024]{1,0:T(8,128)(2,1)}, u32[]{:S(2)}, u32[]{:S(2)}) collective-permute-start(bf16[512,1024]{1,0:T(8,128)(2,1)} %get-tuple-element.436), channel_id=1, source_target_pairs={{0,1},{1,0},{2,3},{3,2},{4,5},{5,4},{6,7},{7,6},{8,9},{9,8},{10,11... | collective-permute-start | bytes 3145736 | tf_op jit(solution)/shard_map/cond/branch_1_fun/ppermute | solution.py:750
  109.6 26.0 %collective-permute-start.39 = (bf16[256,1024]{1,0:T(8,128)(2,1)}, bf16[256,1024]{1,0:T(8,128)(2,1)}, u32[]{:S(2)}, u32[]{:S(2)}) collective-permute-start(bf16[256,1024]{1,0:T(8,128)(2,1)} %dynamic-slice_bitcast_fusion.1), channel_id=1, source_target_pairs={{0,4},{1,5},{2,6},{3,7},{4,0},{5,1},{6,2},{7,3},{8,12},{9,13},{10,... | collective-permute-start | bytes 1572872 | tf_op jit(solution)/shard_map/cond/branch_1_fun/ppermute | solution.py:750
  111.6 24.1 %all-to-all-start.5 = ((bf16[4,2,256,128]{3,2,1,0:T(8,128)(2,1)}), bf16[4,2,256,128]{3,2,1,0:T(8,128)(2,1)}, u32[]{:S(2)}, u32[]{:S(2)}) async-start(bf16[4,2,256,128]{3,2,1,0:T(8,128)(2,1)} %get-tuple-element.442), calls=%async_computation.7 | async-start | bytes 1048576 | tf_op jit(solution)/shard_map/cond/branch_1_fun/all_to_all | solution.py:777
  193.4 19.0 %collective-permute-start.3 = (bf16[512,4096]{1,0:T(8,128)(2,1)}, bf16[512,4096]{1,0:T(8,128)(2,1)}, u32[]{:S(2)}, u32[]{:S(2)}) collective-permute-start(bf16[512,4096]{1,0:T(8,128)(2,1)} %get-tuple-element.455), channel_id=1, source_target_pairs={{0,1},{1,0},{2,3},{3,2},{4,5},{5,4},{6,7},{7,6},{8,9},{9,8},{10,11... | collective-permute-start | bytes 12582920 | tf_op jit(solution)/shard_map/cond/branch_1_fun/ppermute | solution.py:750
  193.9 18.5 %collective-permute-start.4 = (bf16[512,1024]{1,0:T(8,128)(2,1)S(1)}, bf16[512,1024]{1,0:T(8,128)(2,1)}, u32[]{:S(2)}, u32[]{:S(2)}) collective-permute-start(bf16[512,1024]{1,0:T(8,128)(2,1)S(1)} %get-tuple-element.456), channel_id=1, source_target_pairs={{0,1},{1,0},{2,3},{3,2},{4,5},{5,4},{6,7},{7,6},{8,9},{9,8},{10,11... | collective-permute-start | bytes 3145736 | tf_op jit(solution)/shard_map/cond/branch_1_fun/ppermute | solution.py:750
  225.3 20.6 %collective-permute-start.52 = (bf16[512,4096]{1,0:T(8,128)(2,1)}, bf16[512,4096]{1,0:T(8,128)(2,1)}, u32[]{:S(2)}, u32[]{:S(2)}) collective-permute-start(bf16[512,4096]{1,0:T(8,128)(2,1)} %get-tuple-element.864), channel_id=1, source_target_pairs={{0,1},{1,0},{2,3},{3,2},{4,5},{5,4},{6,7},{7,6},{8,9},{9,8},{10,11... | collective-permute-start | bytes 12582920 | tf_op jit(solution)/shard_map/ppermute | solution.py:750
  225.8 20.1 %collective-permute-start.51 = (bf16[512,1024]{1,0:T(8,128)(2,1)}, bf16[512,1024]{1,0:T(8,128)(2,1)}, u32[]{:S(2)}, u32[]{:S(2)}) collective-permute-start(bf16[512,1024]{1,0:T(8,128)(2,1)} %get-tuple-element.861), channel_id=1, source_target_pairs={{0,1},{1,0},{2,3},{3,2},{4,5},{5,4},{6,7},{7,6},{8,9},{9,8},{10,11... | collective-permute-start | bytes 3145736 | tf_op jit(solution)/shard_map/ppermute | solution.py:750
  245.9 24.3 %collective-permute-start.9 = (bf16[512,2048]{1,0:T(8,128)(2,1)}, bf16[512,2048]{1,0:T(8,128)(2,1)}, u32[]{:S(2)}, u32[]{:S(2)}) collective-permute-start(bf16[512,2048]{1,0:T(8,128)(2,1)} %get-tuple-element.461), channel_id=1, source_target_pairs={{0,1},{1,0},{2,3},{3,2},{4,5},{5,4},{6,7},{7,6},{8,9},{9,8},{10,11... | collective-permute-start | bytes 6291464 | tf_op jit(solution)/shard_map/cond/branch_1_fun/ppermute | solution.py:750
  246.0 24.3 %collective-permute-start.5 = (bf16[512,1024]{1,0:T(8,128)(2,1)}, bf16[512,1024]{1,0:T(8,128)(2,1)}, u32[]{:S(2)}, u32[]{:S(2)}) collective-permute-start(bf16[512,1024]{1,0:T(8,128)(2,1)} %get-tuple-element.457), channel_id=1, source_target_pairs={{0,1},{1,0},{2,3},{3,2},{4,5},{5,4},{6,7},{7,6},{8,9},{9,8},{10,11... | collective-permute-start | bytes 3145736 | tf_op jit(solution)/shard_map/cond/branch_1_fun/ppermute | solution.py:750
  246.5 23.8 %collective-permute-start.6 = (bf16[512,1024]{1,0:T(8,128)(2,1)}, bf16[512,1024]{1,0:T(8,128)(2,1)}, u32[]{:S(2)}, u32[]{:S(2)}) collective-permute-start(bf16[512,1024]{1,0:T(8,128)(2,1)} %get-tuple-element.458), channel_id=1, source_target_pairs={{0,1},{1,0},{2,3},{3,2},{4,5},{5,4},{6,7},{7,6},{8,9},{9,8},{10,11... | collective-permute-start | bytes 3145736 | tf_op jit(solution)/shard_map/cond/branch_1_fun/ppermute | solution.py:750
  246.5 23.7 %collective-permute-start.7 = (bf16[512,1024]{1,0:T(8,128)(2,1)}, bf16[512,1024]{1,0:T(8,128)(2,1)}, u32[]{:S(2)}, u32[]{:S(2)}) collective-permute-start(bf16[512,1024]{1,0:T(8,128)(2,1)} %get-tuple-element.459), channel_id=1, source_target_pairs={{0,1},{1,0},{2,3},{3,2},{4,5},{5,4},{6,7},{7,6},{8,9},{9,8},{10,11... | collective-permute-start | bytes 3145736 | tf_op jit(solution)/shard_map/cond/branch_1_fun/ppermute | solution.py:750
  247.0 23.3 %collective-permute-start.8 = (bf16[512,1024]{1,0:T(8,128)(2,1)}, bf16[512,1024]{1,0:T(8,128)(2,1)}, u32[]{:S(2)}, u32[]{:S(2)}) collective-permute-start(bf16[512,1024]{1,0:T(8,128)(2,1)} %get-tuple-element.460), channel_id=1, source_target_pairs={{0,1},{1,0},{2,3},{3,2},{4,5},{5,4},{6,7},{7,6},{8,9},{9,8},{10,11... | collective-permute-start | bytes 3145736 | tf_op jit(solution)/shard_map/cond/branch_1_fun/ppermute | solution.py:750
  247.0 23.2 %all-to-all-start.1 = ((bf16[4,2,256,128]{3,2,1,0:T(8,128)(2,1)}), bf16[4,2,256,128]{3,2,1,0:T(8,128)(2,1)}, u32[]{:S(2)}, u32[]{:S(2)}) async-start(bf16[4,2,256,128]{3,2,1,0:T(8,128)(2,1)} %get-tuple-element.462), calls=%async_computation.1 | async-start | bytes 1048576 | tf_op jit(solution)/shard_map/cond/branch_1_fun/all_to_all | solution.py:777
  270.5 31.2 %collective-permute-start.11 = (bf16[512,1024]{1,0:T(8,128)(2,1)}, bf16[512,1024]{1,0:T(8,128)(2,1)}, u32[]{:S(2)}, u32[]{:S(2)}) collective-permute-start(bf16[512,1024]{1,0:T(8,128)(2,1)} %get-tuple-element.487), channel_id=1, source_target_pairs={{0,1},{1,0},{2,3},{3,2},{4,5},{5,4},{6,7},{7,6},{8,9},{9,8},{10,11... | collective-permute-start | bytes 3145736 | tf_op jit(solution)/shard_map/cond/branch_1_fun/ppermute | solution.py:750
  271.0 30.7 %collective-permute-start.12 = (bf16[2,4,64,1024]{3,2,1,0:T(8,128)(2,1)}, bf16[2,4,64,1024]{3,2,1,0:T(8,128)(2,1)}, u32[]{:S(2)}, u32[]{:S(2)}) collective-permute-start(bf16[2,4,64,1024]{3,2,1,0:T(8,128)(2,1)} %get-tuple-element.488), channel_id=1, source_target_pairs={{0,8},{1,9},{2,10},{3,11},{4,12},{5,13},{6,14},{7,15},{8,0},{9,1},... | collective-permute-start | bytes 3145736 | tf_op jit(solution)/shard_map/cond/branch_1_fun/ppermute | solution.py:750
  272.5 29.2 %collective-permute-start.13 = (bf16[2,4,64,1024]{3,2,1,0:T(8,128)(2,1)}, bf16[2,4,64,1024]{3,2,1,0:T(8,128)(2,1)}, u32[]{:S(2)}, u32[]{:S(2)}) collective-permute-start(bf16[2,4,64,1024]{3,2,1,0:T(8,128)(2,1)} %get-tuple-element.489), channel_id=1, source_target_pairs={{0,16},{1,17},{2,18},{3,19},{4,20},{5,21},{6,22},{7,23},{8,24},{9,... | collective-permute-start | bytes 3145736 | tf_op jit(solution)/shard_map/cond/branch_1_fun/ppermute | solution.py:750
  273.9 27.8 %collective-permute-start.10 = (bf16[256,1024]{1,0:T(8,128)(2,1)}, bf16[256,1024]{1,0:T(8,128)(2,1)}, u32[]{:S(2)}, u32[]{:S(2)}) collective-permute-start(bf16[256,1024]{1,0:T(8,128)(2,1)} %get-tuple-element.486), channel_id=1, source_target_pairs={{0,4},{1,5},{2,6},{3,7},{4,0},{5,1},{6,2},{7,3},{8,12},{9,13},{10,... | collective-permute-start | bytes 1572872 | tf_op jit(solution)/shard_map/cond/branch_1_fun/ppermute | solution.py:750
  274.2 27.5 %all-to-all-start.2 = ((bf16[4,2,256,128]{3,2,1,0:T(8,128)(2,1)}), bf16[4,2,256,128]{3,2,1,0:T(8,128)(2,1)}, u32[]{:S(2)}, u32[]{:S(2)}) async-start(bf16[4,2,256,128]{3,2,1,0:T(8,128)(2,1)} %get-tuple-element.485), calls=%async_computation.2 | async-start | bytes 1048576 | tf_op jit(solution)/shard_map/cond/branch_1_fun/all_to_all | solution.py:777
  303.8 44.0 %all-to-all-start.3 = ((bf16[4,3,2,256,128]{4,3,2,1,0:T(8,128)(2,1)}), bf16[4,3,2,256,128]{4,3,2,1,0:T(8,128)(2,1)}, u32[]{:S(2)}, u32[]{:S(2)}) async-start(bf16[4,3,2,256,128]{4,3,2,1,0:T(8,128)(2,1)} %get-tuple-element.495), calls=%async_computation.3 | async-start | bytes 3145728 | tf_op jit(solution)/shard_map/cond/branch_1_fun/all_to_all | solution.py:777
  308.2 39.6 %collective-permute-start.16 = (bf16[2,4,64,1024]{3,2,1,0:T(8,128)(2,1)}, bf16[2,4,64,1024]{3,2,1,0:T(8,128)(2,1)}, u32[]{:S(2)}, u32[]{:S(2)}) collective-permute-start(bf16[2,4,64,1024]{3,2,1,0:T(8,128)(2,1)} %get-tuple-element.498), channel_id=1, source_target_pairs={{0,8},{1,9},{2,10},{3,11},{4,12},{5,13},{6,14},{7,15},{8,0},{9,1},... | collective-permute-start | bytes 3145736 | tf_op jit(solution)/shard_map/cond/branch_1_fun/ppermute | solution.py:750
  309.3 38.5 %collective-permute-start.17 = (bf16[2,4,64,1024]{3,2,1,0:T(8,128)(2,1)}, bf16[2,4,64,1024]{3,2,1,0:T(8,128)(2,1)}, u32[]{:S(2)}, u32[]{:S(2)}) collective-permute-start(bf16[2,4,64,1024]{3,2,1,0:T(8,128)(2,1)} %get-tuple-element.499), channel_id=1, source_target_pairs={{0,16},{1,17},{2,18},{3,19},{4,20},{5,21},{6,22},{7,23},{8,24},{9,... | collective-permute-start | bytes 3145736 | tf_op jit(solution)/shard_map/cond/branch_1_fun/ppermute | solution.py:750
  312.8 35.0 %collective-permute-start.14 = (bf16[4,64,1024]{2,1,0:T(8,128)(2,1)}, bf16[4,64,1024]{2,1,0:T(8,128)(2,1)}, u32[]{:S(2)}, u32[]{:S(2)}) collective-permute-start(bf16[4,64,1024]{2,1,0:T(8,128)(2,1)} %get-tuple-element.496), channel_id=1, source_target_pairs={{0,16},{1,17},{2,18},{3,19},{4,20},{5,21},{6,22},{7,23},{8,24},{9,... | collective-permute-start | bytes 1572872 | tf_op jit(solution)/shard_map/cond/branch_1_fun/ppermute | solution.py:750
  312.8 35.0 %collective-permute-start.15 = (bf16[4,64,1024]{2,1,0:T(8,128)(2,1)}, bf16[4,64,1024]{2,1,0:T(8,128)(2,1)}, u32[]{:S(2)}, u32[]{:S(2)}) collective-permute-start(bf16[4,64,1024]{2,1,0:T(8,128)(2,1)} %get-tuple-element.497), channel_id=1, source_target_pairs={{0,8},{1,9},{2,10},{3,11},{4,12},{5,13},{6,14},{7,15},{8,0},{9,1},... | collective-permute-start | bytes 1572872 | tf_op jit(solution)/shard_map/cond/branch_1_fun/ppermute | solution.py:750
  350.1 24.9 %all-to-all-start.4 = ((bf16[4,3,2,256,128]{4,3,2,1,0:T(8,128)(2,1)}), bf16[4,3,2,256,128]{4,3,2,1,0:T(8,128)(2,1)}, u32[]{:S(2)}, u32[]{:S(2)}) async-start(bf16[4,3,2,256,128]{4,3,2,1,0:T(8,128)(2,1)} %get-tuple-element.500), calls=%async_computation.4 | async-start | bytes 3145728 | tf_op jit(solution)/shard_map/cond/branch_1_fun/all_to_all | solution.py:777
  375.3 72.5 %reduce-scatter.6.cloned.1.call-start = ((), (), s32[]{:S(2)}) async-start(), calls=%async_computation.13 | async-start | bytes 2621440 | tf_op jit(solution)/shard_map/cond/branch_1_fun/reduce_scatter | solution.py:1066
  382.9 25.9 %collective-permute-start.21 = (bf16[2,4,64,1024]{3,2,1,0:T(8,128)(2,1)}, bf16[2,4,64,1024]{3,2,1,0:T(8,128)(2,1)}, u32[]{:S(2)}, u32[]{:S(2)}) collective-permute-start(bf16[2,4,64,1024]{3,2,1,0:T(8,128)(2,1)} %get-tuple-element.548), channel_id=1, source_target_pairs={{0,8},{1,9},{2,10},{3,11},{4,12},{5,13},{6,14},{7,15},{8,0},{9,1},... | collective-permute-start | bytes 3145736 | tf_op jit(solution)/shard_map/cond/branch_1_fun/cond/branch_1_fun/ppermute | solution.py:750
  383.6 25.6 %collective-permute-start.22 = (bf16[2,4,64,1024]{3,2,1,0:T(8,128)(2,1)}, bf16[2,4,64,1024]{3,2,1,0:T(8,128)(2,1)}, u32[]{:S(2)}, u32[]{:S(2)}) collective-permute-start(bf16[2,4,64,1024]{3,2,1,0:T(8,128)(2,1)} %get-tuple-element.549), channel_id=1, source_target_pairs={{0,16},{1,17},{2,18},{3,19},{4,20},{5,21},{6,22},{7,23},{8,24},{9,... | collective-permute-start | bytes 3145736 | tf_op jit(solution)/shard_map/cond/branch_1_fun/cond/branch_1_fun/ppermute | solution.py:750
  409.2 21.2 %collective-permute-start.23 = (bf16[512,1024]{1,0:T(8,128)(2,1)S(1)}, bf16[512,1024]{1,0:T(8,128)(2,1)}, u32[]{:S(2)}, u32[]{:S(2)}) collective-permute-start(bf16[512,1024]{1,0:T(8,128)(2,1)S(1)} %get-tuple-element.555), channel_id=1, source_target_pairs={{0,1},{1,0},{2,3},{3,2},{4,5},{5,4},{6,7},{7,6},{8,9},{9,8},{10,11... | collective-permute-start | bytes 3145736 | tf_op jit(solution)/shard_map/cond/branch_1_fun/cond/branch_1_fun/ppermute | solution.py:750
  409.2 20.1 %collective-permute-start.24 = (bf16[2,4,64,768]{3,2,1,0:T(8,128)(2,1)S(1)}, bf16[2,4,64,768]{3,2,1,0:T(8,128)(2,1)}, u32[]{:S(2)}, u32[]{:S(2)}) collective-permute-start(bf16[2,4,64,768]{3,2,1,0:T(8,128)(2,1)S(1)} %get-tuple-element.556), channel_id=1, source_target_pairs={{0,8},{1,9},{2,10},{3,11},{4,12},{5,13},{6,14},{7,15},{8,0},{9,1},... | collective-permute-start | bytes 2359304 | tf_op jit(solution)/shard_map/cond/branch_1_fun/cond/branch_1_fun/ppermute | solution.py:750
  410.6 19.8 %collective-permute-start.25 = (bf16[2,4,64,768]{3,2,1,0:T(8,128)(2,1)S(1)}, bf16[2,4,64,768]{3,2,1,0:T(8,128)(2,1)}, u32[]{:S(2)}, u32[]{:S(2)}) collective-permute-start(bf16[2,4,64,768]{3,2,1,0:T(8,128)(2,1)S(1)} %get-tuple-element.557), channel_id=1, source_target_pairs={{0,16},{1,17},{2,18},{3,19},{4,20},{5,21},{6,22},{7,23},{8,24},{9,... | collective-permute-start | bytes 2359304 | tf_op jit(solution)/shard_map/cond/branch_1_fun/cond/branch_1_fun/ppermute | solution.py:750
  451.6 36.2 %reduce-scatter.8.cloned.1.call-start = ((), (), s32[]{:S(2)}) async-start(), calls=%async_computation.14 | async-start | bytes 1310720 | tf_op jit(solution)/shard_map/cond/branch_1_fun/reduce_scatter | solution.py:1066
  454.5 33.3 %collective-permute-start.29 = (bf16[2,4,64,1024]{3,2,1,0:T(8,128)(2,1)}, bf16[2,4,64,1024]{3,2,1,0:T(8,128)(2,1)}, u32[]{:S(2)}, u32[]{:S(2)}) collective-permute-start(bf16[2,4,64,1024]{3,2,1,0:T(8,128)(2,1)} %get-tuple-element.636), channel_id=1, source_target_pairs={{0,8},{1,9},{2,10},{3,11},{4,12},{5,13},{6,14},{7,15},{8,0},{9,1},... | collective-permute-start | bytes 3145736 | tf_op jit(solution)/shard_map/cond/branch_1_fun/ppermute | solution.py:750
  454.9 32.9 %collective-permute-start.30 = (bf16[2,4,64,1024]{3,2,1,0:T(8,128)(2,1)}, bf16[2,4,64,1024]{3,2,1,0:T(8,128)(2,1)}, u32[]{:S(2)}, u32[]{:S(2)}) collective-permute-start(bf16[2,4,64,1024]{3,2,1,0:T(8,128)(2,1)} %get-tuple-element.637), channel_id=1, source_target_pairs={{0,16},{1,17},{2,18},{3,19},{4,20},{5,21},{6,22},{7,23},{8,24},{9,... | collective-permute-start | bytes 3145736 | tf_op jit(solution)/shard_map/cond/branch_1_fun/ppermute | solution.py:750
  455.9 31.9 %collective-permute-start.31 = (bf16[4,64,768]{2,1,0:T(8,128)(2,1)}, bf16[4,64,768]{2,1,0:T(8,128)(2,1)}, u32[]{:S(2)}, u32[]{:S(2)}) collective-permute-start(bf16[4,64,768]{2,1,0:T(8,128)(2,1)} %get-tuple-element.638), channel_id=1, source_target_pairs={{0,16},{1,17},{2,18},{3,19},{4,20},{5,21},{6,22},{7,23},{8,24},{9,... | collective-permute-start | bytes 1179656 | tf_op jit(solution)/shard_map/cond/branch_1_fun/ppermute | solution.py:750
  457.0 30.8 %collective-permute-start.32 = (bf16[4,64,768]{2,1,0:T(8,128)(2,1)}, bf16[4,64,768]{2,1,0:T(8,128)(2,1)}, u32[]{:S(2)}, u32[]{:S(2)}) collective-permute-start(bf16[4,64,768]{2,1,0:T(8,128)(2,1)} %get-tuple-element.639), channel_id=1, source_target_pairs={{0,8},{1,9},{2,10},{3,11},{4,12},{5,13},{6,14},{7,15},{8,0},{9,1},... | collective-permute-start | bytes 1179656 | tf_op jit(solution)/shard_map/cond/branch_1_fun/ppermute | solution.py:750
  492.3 41.9 %reduce-scatter.10.cloned.1.call-start = ((), (), s32[]{:S(2)}) async-start(), calls=%async_computation.15 | async-start | bytes 983040 | tf_op jit(solution)/shard_map/cond/branch_1_fun/reduce_scatter | solution.py:1066
  494.8 39.3 %collective-permute-start.34 = (bf16[2,4,64,1024]{3,2,1,0:T(8,128)(2,1)}, bf16[2,4,64,1024]{3,2,1,0:T(8,128)(2,1)}, u32[]{:S(2)}, u32[]{:S(2)}) collective-permute-start(bf16[2,4,64,1024]{3,2,1,0:T(8,128)(2,1)} %get-tuple-element.647), channel_id=1, source_target_pairs={{0,8},{1,9},{2,10},{3,11},{4,12},{5,13},{6,14},{7,15},{8,0},{9,1},... | collective-permute-start | bytes 3145736 | tf_op jit(solution)/shard_map/cond/branch_1_fun/ppermute | solution.py:750
  496.5 37.6 %collective-permute-start.35 = (bf16[2,4,64,1024]{3,2,1,0:T(8,128)(2,1)}, bf16[2,4,64,1024]{3,2,1,0:T(8,128)(2,1)}, u32[]{:S(2)}, u32[]{:S(2)}) collective-permute-start(bf16[2,4,64,1024]{3,2,1,0:T(8,128)(2,1)} %get-tuple-element.648), channel_id=1, source_target_pairs={{0,16},{1,17},{2,18},{3,19},{4,20},{5,21},{6,22},{7,23},{8,24},{9,... | collective-permute-start | bytes 3145736 | tf_op jit(solution)/shard_map/cond/branch_1_fun/ppermute | solution.py:750
  497.2 37.0 %collective-permute-start.33 = (bf16[256,1024]{1,0:T(8,128)(2,1)}, bf16[256,1024]{1,0:T(8,128)(2,1)}, u32[]{:S(2)}, u32[]{:S(2)}) collective-permute-start(bf16[256,1024]{1,0:T(8,128)(2,1)} %get-tuple-element.646), channel_id=1, source_target_pairs={{0,4},{1,5},{2,6},{3,7},{4,0},{5,1},{6,2},{7,3},{8,12},{9,13},{10,... | collective-permute-start | bytes 1572872 | tf_op jit(solution)/shard_map/cond/branch_1_fun/ppermute | solution.py:750
  500.3 33.9 %collective-permute-start.36 = (bf16[4,64,1024]{2,1,0:T(8,128)(2,1)}, bf16[4,64,1024]{2,1,0:T(8,128)(2,1)}, u32[]{:S(2)}, u32[]{:S(2)}) collective-permute-start(bf16[4,64,1024]{2,1,0:T(8,128)(2,1)} %get-tuple-element.649), channel_id=1, source_target_pairs={{0,16},{1,17},{2,18},{3,19},{4,20},{5,21},{6,22},{7,23},{8,24},{9,... | collective-permute-start | bytes 1572872 | tf_op jit(solution)/shard_map/cond/branch_1_fun/ppermute | solution.py:750
  500.9 33.2 %collective-permute-start.37 = (bf16[4,64,1024]{2,1,0:T(8,128)(2,1)}, bf16[4,64,1024]{2,1,0:T(8,128)(2,1)}, u32[]{:S(2)}, u32[]{:S(2)}) collective-permute-start(bf16[4,64,1024]{2,1,0:T(8,128)(2,1)} %get-tuple-element.650), channel_id=1, source_target_pairs={{0,8},{1,9},{2,10},{3,11},{4,12},{5,13},{6,14},{7,15},{8,0},{9,1},... | collective-permute-start | bytes 1572872 | tf_op jit(solution)/shard_map/cond/branch_1_fun/ppermute | solution.py:750
  536.4 46.8 %reduce-scatter.12.cloned.1.call-start = ((), (), s32[]{:S(2)}) async-start(), calls=%async_computation.16 | async-start | bytes 1310720 | tf_op jit(solution)/shard_map/cond/branch_1_fun/reduce_scatter | solution.py:1066
  539.3 56.9 %reduce-scatter.14.cloned.1.call-start = ((), (), s32[]{:S(2)}) async-start(), calls=%async_computation.17 | async-start | bytes 1310720 | tf_op jit(solution)/shard_map/cond/branch_1_fun/reduce_scatter | solution.py:1066
  (74 other events, 740.9 us)
Sparse Core Ops, SparseCore 0:
  378.4 44.7 reduce-scatter.5
  454.9 27.2 reduce-scatter.7
  496.0 33.1 reduce-scatter.9
  539.4 27.2 reduce-scatter.11
  569.0 27.0 reduce-scatter.13

commit v2 on v1

--- a/solution.py
+++ b/solution.py
@@ -587,7 +587,7 @@
 
 
 def front_kernel(
-    size, ffn_steps, pieces, row_ref, x_ref, gain_ref, next_gain_ref, win_ref, wout_ref,
+    size, ffn_steps, pieces, row_ref, x_ref, gain_ref, win_ref, wout_ref,
     wq_ref, wk_ref, wv_ref, cos_ref, sin_ref, *refs,
 ):
     refs = refs[-(6 + pieces) :]
@@ -597,7 +597,8 @@
 
     @pl.when(step == 0)
     def _():
-        entered_ref[...] = layer_norm(x_ref[...].astype(F32), gain_ref[...])[0].astype(BF16)
+        gain = gain_ref[0:1, :]
+        entered_ref[...] = layer_norm(x_ref[0].astype(F32), gain)[0].astype(BF16)
         total[...] = jnp.zeros_like(total)
 
     @pl.when(step < ffn_steps)
@@ -609,9 +610,9 @@
 
     @pl.when(step == ffn_steps)
     def _():
-        out = x_ref[...].astype(F32) + 0.5 * total[...]
+        out = x_ref[0].astype(F32) + 0.5 * total[...]
         out_ref[...] = out
-        next_ref[...] = layer_norm(out, next_gain_ref[...])[0].astype(BF16)
+        next_ref[...] = layer_norm(out, gain_ref[1:2, :])[0].astype(BF16)
 
     each = (pl.num_programs(0) - ffn_steps) // pieces
     for piece, out in enumerate(outs):
@@ -628,10 +629,10 @@
 
 
 def front(
-    frames, row, gain_row, weight_in, weight_out, next_gain, weight, cosines, sines,
+    frames, row, gains, weight_in, weight_out, weight, cosines, sines,
     places, chunks, size, before=(),
 ):
-    rows, model = frames.shape
+    given, rows, model = frames.shape
     units = weight_in.shape[1]
     wide = min(units, 1024)
     ffn_steps = units // wide
@@ -663,9 +664,8 @@
         jax.ShapeDtypeStruct((chunks * rows, model), BF16),
     ] + [piece] * pieces
     in_specs = [
-        whole((rows, model)),
-        whole((1, model)),
-        whole((1, model)),
+        pl.BlockSpec((1, rows, model), lambda s, row: (row[0] if given > 1 else 0, 0, 0)),
+        whole(gains.shape),
         pl.BlockSpec((model, wide), lambda s, row: (0, ffn_at(s, row))),
         pl.BlockSpec((wide, model), lambda s, row: (ffn_at(s, row), 0)),
         pl.BlockSpec((model, turned_wide), lambda s, row: (0, turn_at(s))),
@@ -697,19 +697,27 @@
         ),
         name="front",
     )(
-        row, frames, gain_row, next_gain, weight_in, weight_out, weight, weight, weight,
+        row, frames, gains, weight_in, weight_out, weight, weight, weight,
         cosines, sines, *before,
     )
 
 
-def unturn_kernel(size, pieces, cos_ref, sin_ref, *refs):
-    backs, out = refs[:pieces], refs[pieces]
-    rotated = pl.program_id(0) < 2
+def projection_kernel(
+    size, pieces, cos_ref, sin_ref, x_ref, gain_ref, up_ref, weight_ref, *refs
+):
+    backs, refs = refs[:pieces], refs[pieces:]
+    grad_ref, down_ref, half_ref, gain_grad_ref, total = refs
+    step = pl.program_id(0)
+
+    @pl.when(step == 0)
+    def _():
+        total[...] = jnp.zeros_like(total)
+
+    rotated = step < 2
     cosines = jnp.where(rotated, cos_ref[...], 1.0)
     sines = jnp.where(rotated, -sin_ref[...], 0.0)
     places, _, chunks, frames, _ = backs[0].shape
-    wide = TURNED
-    per = wide // LANES
+    per = TURNED // LANES
     for piece, back in enumerate(backs):
         for first in range(0, places, per):
             for chunk in range(chunks):
@@ -717,24 +725,54 @@
                 field = jnp.concatenate([back[first + i, 0, chunk] for i in range(per)], 1)
                 made = turn(field.astype(F32), cosines[rows], sines[rows], size).astype(BF16)
                 start = (piece * places + first) * LANES
-                out[rows, start : start + wide] = made
-
-
-def unturned(backs, cosines, sines, size):
+                grad_ref[rows, start : start + TURNED] = made
+    total[...] += dot(grad_ref[...], weight_ref[...], NT)
+
+    @pl.when(step == pl.num_programs(0) - 1)
+    def _():
+        gain = gain_ref[...]
+        normed, inverse = layer_norm(x_ref[...], gain)[1:]
+        through, grad_gain = norm_back(total[...], normed, inverse, gain)
+        down = up_ref[...] + through
+        down_ref[...] = down
+        half_ref[...] = (0.5 * down).astype(BF16)
+        gain_grad_ref[...] = grad_gain
+
+
+def projection_backward(backs, cosines, sines, size, upstream, stream, gain_row, weight):
     places, kinds, chunks, frames, _ = backs[0].shape
     pieces = len(backs)
+    rows, model = stream.shape
     block = pl.BlockSpec((places, 1, chunks, frames, LANES), lambda s: (0, s, 0, 0, 0))
-    model = pieces * places * LANES
     return pl.pallas_call(
-        functools.partial(unturn_kernel, size, pieces),
+        functools.partial(projection_kernel, size, pieces),
         grid=(kinds,),
-        in_specs=[whole(cosines.shape), whole(sines.shape)] + [block] * pieces,
-        out_specs=pl.BlockSpec((chunks * frames, model), lambda s: (0, s)),
-        out_shape=jax.ShapeDtypeStruct((chunks * frames, kinds * model), BF16),
+        in_specs=[
+            whole(cosines.shape),
+            whole(sines.shape),
+            whole((rows, model)),
+            whole((1, model)),
+            whole((rows, model)),
+            pl.BlockSpec((model, model), lambda s: (0, s)),
+        ]
+        + [block] * pieces,
+        out_specs=[
+            pl.BlockSpec((rows, model), lambda s: (0, s)),
+            whole((rows, model)),
+            whole((rows, model)),
+            whole((1, model)),
+        ],
+        out_shape=[
+            jax.ShapeDtypeStruct((rows, kinds * model), BF16),
+            jax.ShapeDtypeStruct((rows, model), F32),
+            jax.ShapeDtypeStruct((rows, model), BF16),
+            jax.ShapeDtypeStruct((1, model), F32),
+        ],
+        scratch_shapes=[pltpu.VMEM((rows, model), F32)],
         compiler_params=compiler_params(),
-        cost_estimate=cost(0, 4 * chunks * frames * kinds * model),
-        name="unturned",
-    )(cosines, sines, *backs)
+        cost_estimate=cost(6 * rows * model * model, 6 * model * model + 22 * rows * model),
+        name="projection_backward",
+    )(cosines, sines, stream, gain_row, upstream, weight, *backs)
 
 
 def flipped(axis_bit, count):
@@ -876,9 +914,10 @@
     )(place, *upstream, *hidden)
 
 
-def column_grad_kernel(heads, count, place_ref, *refs):
+def column_grad_kernel(heads, items, split, place_ref, *refs):
+    count = len(split)
     lefts, refs = refs[: 2 * count], refs[2 * count :]
-    rights, refs = refs[: 2 * count], refs[2 * count :]
+    rights, refs = refs[: 2 * (count + sum(split))], refs[2 * (count + sum(split)) :]
     targets, turned = refs[:-count], refs[-count:]
     r = pl.program_id(0)
     rows = lefts[0].shape[0]
@@ -892,8 +931,14 @@
                 )
 
     made = []
+    at = 0
     for number in range(count):
-        right = jnp.concatenate([rights[2 * number][...], rights[2 * number + 1][...]], 0)
+        right = jnp.concatenate([rights[at][...], rights[at + 1][...]], 0)
+        at += 2
+        if split[number]:
+            second = jnp.concatenate([rights[at][...], rights[at + 1][...]], 0)
+            at += 2
+            right = jnp.where((r ^ place_ref[1]) < items // 2, right, second)
         made.append(dot(turned[number][...], right).astype(BF16))
     made = made[0] if count == 1 else jnp.concatenate(made, 1)
     half = made.shape[0] // 2
@@ -921,10 +966,34 @@
 
 
 def column_grads(lefts, rights, heads, place, items):
+    if items == 1:
+        flat = [
+            (left, part)
+            for left, right in zip(lefts, rights)
+            for part in (right if isinstance(right[0], tuple) else (right,))
+        ]
+        lefts, rights = [left for left, _ in flat], [right for _, right in flat]
+    split = [isinstance(right[0], tuple) for right in rights]
     rows, model = lefts[0][0].shape
-    columns = sum(right[0].shape[1] for right in rights)
+    parts = []
+    for right, two in zip(rights, split):
+        parts += [part for pair in right for part in pair] if two else list(right)
+    columns = sum(part.shape[1] for part in parts) // 2
     shapes = share_shapes(items, heads, model, columns)
     block = (1,) + shapes[0].shape[1:]
+    right_specs = []
+    for right, two in zip(rights, split):
+        if two:
+            share = pl.BlockSpec(
+                (rows, right[0][0].shape[1] * 2 // items),
+                lambda r, place: (0, (r ^ place[1]) % (items // 2)),
+            )
+            right_specs += [share] * 4
+        else:
+            share = pl.BlockSpec(
+                (rows, right[0].shape[1] // items), lambda r, place: (0, r ^ place[1])
+            )
+            right_specs += [share] * 2
     maps = [
         lambda r, place: (r // 2, 0, 0, 0),
         lambda r, place: (jnp.minimum(r, 1), 0, 0, 0),
@@ -934,23 +1003,18 @@
     grid_spec = pltpu.PrefetchScalarGridSpec(
         num_scalar_prefetch=1,
         grid=(items,),
-        in_specs=[whole((rows, model))] * (2 * len(lefts))
-        + [
-            pl.BlockSpec((rows, right[0].shape[1] // items), lambda r, place: (0, r ^ place[1]))
-            for right in rights
-            for _ in range(2)
-        ],
+        in_specs=[whole((rows, model))] * (2 * len(lefts)) + right_specs,
         out_specs=[pl.BlockSpec(block, index) for index in maps[: len(shapes)]],
         scratch_shapes=[pltpu.VMEM((model // 2, 2 * rows), BF16)] * len(lefts),
     )
     return pl.pallas_call(
-        functools.partial(column_grad_kernel, heads, len(lefts)),
+        functools.partial(column_grad_kernel, heads, items, split),
         grid_spec=grid_spec,
         out_shape=shapes,
         compiler_params=compiler_params(),
         cost_estimate=cost(2 * rows * model * columns, 4 * model * columns),
         name="column_grads",
-    )(place, *[part for left in lefts for part in left], *[part for right in rights for part in right])
+    )(place, *[part for left in lefts for part in left], *parts)
 
 
 class Scatter:
@@ -1069,6 +1133,57 @@
     return [made[i].reshape(-1, made.shape[-1]) for i in range(made.shape[0])]
 
 
+def unfold_kernel(share_ref, out_ref):
+    each = share_ref.shape[0]
+    span = out_ref.shape[0]
+    for part in range(share_ref.shape[1] // span):
+        turned = jnp.transpose(share_ref[:, part * span : (part + 1) * span].astype(F32))
+        out_ref[:, part * each : (part + 1) * each] = turned
+
+
+def unfolded(share, span):
+    each, wide = share.shape
+    shape = (span, each * wide // span)
+    return pl.pallas_call(
+        unfold_kernel,
+        out_shape=jax.ShapeDtypeStruct(shape, F32),
+        cost_estimate=cost(0, 6 * each * wide),
+        name="unfolded",
+    )(share)
+
+
+def heads_kernel(grad_ref, weight_ref, *outs):
+    step = pl.program_id(0)
+    made = dot(grad_ref[...], weight_ref[...], NT).astype(BF16)
+    for piece, out in enumerate(outs):
+
+        @pl.when(step == piece)
+        def _():
+            places, chunks, frames, _ = out.shape
+            for place in range(places):
+                for chunk in range(chunks):
+                    out[place, chunk] = made[
+                        chunk * frames : (chunk + 1) * frames, place * LANES : (place + 1) * LANES
+                    ]
+
+
+def heads_gradient(grad, weight, places, chunks):
+    rows, model = grad.shape
+    wide = places * LANES
+    pieces = model // wide
+    shape = (places, chunks, rows // chunks, LANES)
+    return pl.pallas_call(
+        heads_kernel,
+        grid=(pieces,),
+        in_specs=[whole((rows, model)), pl.BlockSpec((wide, model), lambda s: (s, 0))],
+        out_specs=[whole(shape)] * pieces,
+        out_shape=[jax.ShapeDtypeStruct(shape, BF16)] * pieces,
+        compiler_params=compiler_params(),
+        cost_estimate=cost(2 * rows * model * model, 2 * model * model + 4 * rows * model),
+        name="heads_gradient",
+    )(grad, weight)
+
+
 def sum_everywhere(value):
     for axis in EVERY:
         bit = 1
@@ -1109,7 +1224,7 @@
     where = jnp.stack(
         [place % 2, lax.axis_index("items") if items > 1 else 0 * place]
     ).astype(jnp.int32)
-    always = bucket_counts[0, 0, 0] >= 0
+    always = place >= 0
     first = jnp.arange(chunks, dtype=jnp.int32)[:, None] * span + place % half * here
     position = first + jnp.arange(here, dtype=jnp.int32)[None]
     cosines, sines = rope_tables(position.reshape(-1), size)
@@ -1128,18 +1243,17 @@
 
     def begin(chunk, row, before=()):
         return front(
-            chunk, row.reshape(1).astype(jnp.int32), gain[0], w_ffn1_in, w_ffn1_out, gain[1],
-            w_qkv, cosines, sines, half, chunks, size, before,
+            chunk, row.reshape(1).astype(jnp.int32), gains, w_ffn1_in, w_ffn1_out, w_qkv,
+            cosines, sines, half, chunks, size, before,
         )
 
-    own_frames = mine(frames)
     before, other_frames = fenced(
-        always, (), lambda: (begin(own_frames, side), across(theirs(frames)))
-    )
-    stream = gathered(own_frames, other_frames, side)
+        always, (), lambda: (begin(frames, side), across(theirs(frames)))
+    )
     stream_one, slope_one, hid_one, ent_one, ent_att, *sent = begin(
-        other_frames, 1 - side, before
-    )
+        other_frames[None], 1 - side, before
+    )
+    stream = gathered(mine(frames), other_frames, side)
     qkv = [exchange(sent[0])]
     kept, contexts = [], []
     for number in range(pieces):
@@ -1175,10 +1289,12 @@
         cot_other = across(theirs(cotangent))
     fulls = [made[1] for made in kept]
     lses = [made[2] for made in kept]
-    context = jnp.concatenate(
-        [part.transpose(1, 2, 0, 3).reshape(rows, -1) for part in contexts], 1
-    )
-    stream_two = stream_one + dot(context, w_out)
+    contexts = [part.transpose(1, 2, 0, 3).reshape(rows, -1) for part in contexts]
+    context = jnp.concatenate(contexts, 1)
+    stream_two = stream_one
+    for number, part in enumerate(contexts):
+        wide = part.shape[1]
+        stream_two = stream_two + dot(part, w_out[number * wide : (number + 1) * wide])
     shaped, conv_normed, conv_inverse = layer_norm(stream_two, gain[2])
     conv_entered = shaped.astype(BF16)
     pointwise = dot(conv_entered, w_point_in)
@@ -1215,43 +1331,28 @@
     grad_depth, gain_three = norm_back(grad_norm_in, depth_normed, depth_inverse, gain[3])
     grad_depth_low = grad_depth.astype(BF16).reshape(chunks, here, model)
     grad_widened = edges(grad_depth_low, reach)
-    grad_depth_full = grad_depth_low.astype(F32)
-    taps = []
     grad_gated = jnp.zeros((chunks, here, model), F32)
     for offset in range(KERNEL):
-        same = (seg_wide[:, offset : offset + here] == seg_own)[:, :, None]
-        taps.append(
-            jnp.sum(
-                jnp.where(same, grad_depth_full * widened[:, offset : offset + here], 0.0), (0, 1)
-            )
-        )
         mirror = 2 * reach - offset
         same_back = (seg_wide[:, mirror : mirror + here] == seg_own)[:, :, None]
         grad_gated = grad_gated + depth_rows[offset] * jnp.where(
             same_back, grad_widened[:, mirror : mirror + here], 0.0
         )
     grad_gated = grad_gated.reshape(rows, model)
-    grad_point = jnp.concatenate(
-        [grad_gated * sigmoid_gate, grad_gated * linear * sigmoid_gate * (1.0 - sigmoid_gate)], 1
-    ).astype(BF16)
+    grad_a = (grad_gated * sigmoid_gate).astype(BF16)
+    grad_b = (grad_gated * linear * sigmoid_gate * (1.0 - sigmoid_gate)).astype(BF16)
     through, gain_two = norm_back(
-        dot(grad_point, w_point_in, NT), conv_normed, conv_inverse, gain[2]
+        dot(grad_a, w_point_in[:, :model], NT) + dot(grad_b, w_point_in[:, model:], NT),
+        conv_normed, conv_inverse, gain[2],
     )
     grad_two = grad_three + through
     grad_attn_out = grad_two.astype(BF16)
-    grad_context = dot(grad_attn_out, w_out, NT).astype(BF16)
-    grad_heads = []
-    for number in range(pieces):
-        columns = half * LANES
-        part = grad_context[:, number * columns : (number + 1) * columns]
-        grad_heads.append(part.reshape(chunks, here, half, LANES).transpose(2, 0, 1, 3))
-
+    grad_heads = list(heads_gradient(grad_attn_out, w_out, half, chunks))
     lefts = (mixed_low, conv_entered, context)
-    rights = (grad_mix, grad_point, grad_attn_out)
 
     def ffn_grads():
         return (
-            [other_core(part) for part in lefts + rights[:2]],
+            [other_core(part) for part in lefts + (grad_a, grad_b)],
             exchange(grad_heads[0]),
             out_grad((half_two, half_other), (hid_two, hid_other), ways, where, items),
             column_grads(
@@ -1274,7 +1375,7 @@
                 extra.append(exchange(grads[number - 1]))
             if number == 0:
                 extra.append(across(out_theirs))
-                extra.append(other_core(rights[2]))
+                extra += [other_core(grad_mix), other_core(grad_attn_out)]
             return extra
 
         def attend_now():
@@ -1290,8 +1391,7 @@
         if number > 0:
             backs.append(extra.pop(0))
         if number == 0:
-            out_other = extra.pop(0)
-            others.append(extra.pop(0))
+            out_other, *late = extra
             two_out.second(second_sums(two_out)[0])
     two_in.second(second_sums(two_in)[0])
 
@@ -1300,7 +1400,13 @@
         scatter = copy.copy(two_in)
         moved(scatter)
         shares = column_grads(
-            list(zip(lefts, others[:3])), list(zip(rights, others[3:])), ways, where, items
+            list(zip(lefts, others[:3])),
+            [
+                (grad_mix, late[0]),
+                ((grad_a, others[3]), (grad_b, others[4])),
+                (grad_attn_out, late[1]),
+            ],
+            ways, where, items,
         )
         return (back, shares, last_sum(two_out, scatter))
 
@@ -1312,35 +1418,33 @@
         two_grads = along_z(two_sum)
         scatter = copy.copy(middle)
 
-        def qkv_part():
-            grad_proj = unturned(backs, cosines, sines, size)
-            proj_other = other_core(grad_proj)
-            down = stream_gradient(grad_two, stream_one, grad_proj, gain[1], w_qkv, F32)
-            shares = column_grads(
-                [ent_att], [(grad_proj, proj_other)], ways, where, items
-            )
-            return (down, shares)
-
-        (grad_one, half_one, gain_one), shares = fenced(always, (scatter,), qkv_part)
+        grad_proj, grad_one, half_one, gain_one = fenced(
+            always,
+            (scatter,),
+            lambda: projection_backward(
+                backs, cosines, sines, size, grad_two, stream_one, gain[1], w_qkv
+            ),
+        )
         first = scatter.got
         scatter.second(second_sums(scatter)[0])
+
+        def qkv_part():
+            half_other = other_core(half_one)
+            right = (grad_proj, other_core(grad_proj))
+            return (half_other, column_grads([ent_att], [right], ways, where, items))
+
+        half_other, shares = fenced(always, (scatter,), qkv_part)
         attn = Scatter(*shares)
-        (half_own, grad_pre), half_other = fenced(
-            always,
-            (attn,),
-            lambda: (hidden_gradient(grad_one, slope_one, w_ffn1_out), other_core(half_one)),
-        )
-        pre_other, shares_out = fenced(
-            always,
-            (scatter,),
-            lambda: (
-                other_core(grad_pre),
-                out_grad((half_own, half_other), hid_one, ways, where, items),
-            ),
-        )
+
+        def hidden_part():
+            half_own, grad_pre = hidden_gradient(grad_one, slope_one, w_ffn1_out)
+            shares = out_grad((half_own, half_other), hid_one, ways, where, items)
+            return (grad_pre, shares)
+
+        grad_pre, shares_out = fenced(always, (attn,), hidden_part)
         return (
             two_grads, first, scatter.got, (grad_one, gain_one), shares[:2], attn.got,
-            (grad_pre, pre_other), shares_out,
+            grad_pre, shares_out,
         )
 
     two_grads, first, got, (grad_one, gain_one), shares, attn_got, grad_pre, shares_out = fenced(
@@ -1358,8 +1462,8 @@
         (one_out, attn),
         lambda: (
             along_z(last_sum(middle, columns=middle_columns)),
-            column_grads([ent_one], [grad_pre], ways, where, items),
-            stream_gradient(grad_one, stream, grad_pre[0], gain[0], w_ffn1_in, BF16),
+            column_grads([ent_one], [(grad_pre, other_core(grad_pre))], ways, where, items),
+            stream_gradient(grad_one, stream, grad_pre, gain[0], w_ffn1_in, BF16),
         ),
     )
     one_in = Scatter(*shares)
@@ -1372,16 +1476,13 @@
 
     hidden = w_ffn1_in.shape[1]
 
-    def unfolded(share):
-        each, wide = share.shape
-        span = hidden // ways
-        halves = share.reshape(2, each // 2, wide)
-        parts = [
-            halves[half, :, i * span : (i + 1) * span]
-            for i in range(wide // span)
-            for half in range(2)
-        ]
-        return jnp.concatenate(parts, 0).T.astype(F32)
+    def tap_sums_here():
+        rows_of = []
+        for offset in range(KERNEL):
+            same = (seg_wide[:, offset : offset + here] == seg_own)[:, :, None]
+            product = grad_depth_low.astype(F32) * widened[:, offset : offset + here]
+            rows_of.append(jnp.sum(jnp.where(same, product, 0.0), (0, 1))[None])
+        return rows_of
 
     def last_part():
         out_grads = along_z(last_sum(one_out))
@@ -1390,7 +1491,7 @@
         small = sum_everywhere(
             jnp.concatenate(
                 [gain_zero, gain_one, gain_two, gain_three, gain_four, gain_five]
-                + [tap[None] for tap in taps],
+                + tap_sums_here(),
                 0,
             )
         )
@@ -1406,22 +1507,23 @@
             attn_grad[0].astype(F32),
             middle_parts,
             two_grads[1].astype(F32),
-            unfolded(two_grads[0]),
+            unfolded(two_grads[0], hidden // ways),
+            unfolded(out_grads[0], hidden // ways),
         )
-        return (out_grads, along_z(last_sum(scatter)), small, ready)
-
-    one_out_grad, one_in_grad, small, ready = fenced(always, (), last_part)
-    out, grad_in, attn_full, middle_parts, two_in_full, two_out_full = ready
+        return (along_z(last_sum(scatter)), small[:6], small[6:], ready)
+
+    one_in_grad, gain_sums, tap_sums, ready = fenced(always, (), last_part)
+    out, grad_in, attn_full, middle_parts, two_in_full, two_out_full, one_out_full = ready
     return (
         out,
         grad_in,
-        small[:6],
+        gain_sums,
         one_in_grad[0].astype(F32),
-        unfolded(one_out_grad[0]),
+        one_out_full,
         attn_full,
         middle_parts[2],
         middle_parts[1],
-        small[6:],
+        tap_sums,
         middle_parts[0],
         two_in_full,
         two_out_full,

time: 620 us -> 607 us (0.979)
  local copies, waits for them, and re-layouts: 33.6 us -> 19.9 us
    pallas_call x5 -> x8, Pallas kernels: 47.4 us -> 60 us  [the longest x4 41.7 us: column_grads(): pl.pallas_call(functools.partial(column_grad_kernel, heads, items, split)...]
    pallas_call x2 -> x1, Pallas kernels: 21.9 us -> 11.5 us  [stream_gradient(): pl.pallas_call(down_kernel, grid=(units // wide,), in_specs=[whole((rows,...]
    ppermute x49 -> x50, waiting for transfers between devices: 99.1 us -> 106 us  [swap(): return lax.ppermute(value, EVERY, flipped(axis_bit, count))]
    dot_general x6 -> x7, matrix products: 18.8 us -> 21.2 us  [dot(): return lax.dot_general(left, right, dims, preferred_element_type=F32)]
    ppermute x49 -> x50, starting transfers between devices: 47.5 us -> 46.2 us  [swap(): return lax.ppermute(value, EVERY, flipped(axis_bit, count))]
  transfers between devices with their start and end apart: 66 -> 67, of which waited for: 25 -> 22; matrix products, arithmetic and copies ran while one was open for 6% -> 7% of each run, Pallas kernels for 36% -> 38%
where the time goes in v2:
time: 607 us; the launch traced here: 597 us
  Pallas kernels  278 us (46%)
  waiting for transfers between devices  140 us (23%)
  starting transfers between devices  82.3 us (14%)
  other arithmetic  37.5 us (6%)
  matrix products  21.2 us (3%)
  local copies, waits for them, and re-layouts  19.9 us (3%)
  between operations  17.5 us (3%)
    ppermute x50, waiting for transfers between devices, swap(): return lax.ppermute(value, EVERY, flipped(axis_bit, count))  106 us
    pallas_call x2, Pallas kernels, attend_backward(): pl.pallas_call(functools.partial(attn_bwd_kernel, heads, size, group), gr...  46.5 us
    ppermute x50, starting transfers between devices, swap(): return lax.ppermute(value, EVERY, flipped(axis_bit, count))  46.2 us
    pallas_call x4, Pallas kernels, column_grads(): pl.pallas_call(functools.partial(column_grad_kernel, heads, items, split)...  41.7 us
    pallas_call x2, Pallas kernels, front(): pl.pallas_call(functools.partial(front_kernel, size, ffn_steps, pieces),...  34.4 us
    all_to_all x8, starting transfers between devices, exchange(): lax.all_to_all(value, 'heads', split_axis=0, concat_axis=0, tiled=True, a...  34.1 us
    pallas_call x2, Pallas kernels, attend_forward(): pl.pallas_call(functools.partial(attn_fwd_kernel, heads, size, group), gr...  32.9 us
    dot_general x7, matrix products, dot(): return lax.dot_general(left, right, dims, preferred_element_type=F32)  21.2 us
  transfers between devices with their start and end apart: 67, of which 22 were waited for; matrix products, arithmetic and copies ran while one was open for 7% of the time, Pallas kernels for 38%

profile of v2, /device:TPU:0, one launch (start us, length us, event | category | flops | bytes accessed | tf_op | source)
XLA Modules:
  0.0 597.4 jit_solution(16821264731826400400)
XLA Ops:
  8.4 28.6 %conditional.15 = (f32[512,1024]{1,0:T(8,128)}, bf16[512,4096]{1,0:T(8,128)(2,1)}, bf16[512,4096]{1,0:T(8,128)(2,1)}, bf16[512,1024]{1,0:T(8,128)(2,1)}, bf16[51...) conditional(s32[]{:T(128)} %convert_element_type.144, ...), branch_computations={%region_0.1_spmd, %region_1.2_spmd} | conditional | flops 5905580032 | bytes 34603160 | solution.py:798
  13.7 16.9 %front.2 = (f32[512,1024]{1,0:T(8,128)}, bf16[512,4096]{1,0:T(8,128)(2,1)}, bf16[512,4096]{1,0:T(8,128)(2,1)}, bf16[512,1024]{1,0:T(8,128)(2,1)}, bf16[512,1024]...) custom-call(s32[1]{0:T(128)} %bitcast.row_ref, ...), custom_call_target="tpu_custom_call" | custom-call | flops 5905580032 | bytes 31457280 | tf_op jit(solution)/shard_map/cond/branch_1_fun/front/pallas_call | solution.py:688
  30.6 6.3 %collective-permute-done.39 = bf16[256,1024]{1,0:T(8,128)(2,1)} collective-permute-done((bf16[256,1024]{1,0:T(8,128)(2,1)S(1)}, bf16[256,1024]{1,0:T(8,128)(2,1)}, u32[]{:S(2)}, u32[]{:S(2)}) %collective-permute-start.39) | collective-permute-done | bytes 524320 | tf_op jit(solution)/shard_map/cond/branch_1_fun/ppermute | solution.py:788
  37.0 17.5 %front.3 = (f32[512,1024]{1,0:T(8,128)}, bf16[512,4096]{1,0:T(8,128)(2,1)}, bf16[512,4096]{1,0:T(8,128)(2,1)}, bf16[512,1024]{1,0:T(8,128)(2,1)}, bf16[512,1024]...) custom-call(s32[1]{0:T(128)} %bitcast.19.row_ref, ...), custom_call_target="tpu_custom_call", output_to_operand_aliasing={{0}: (10, {}), {1}: (11, {}), {2}: (12, {}), {3}: (13, {}),... | custom-call | flops 5905580032 | bytes 31457280 | tf_op jit(solution)/shard_map/front/pallas_call | solution.py:688
  54.5 4.5 all-to-all-start.6
  66.7 12.5 %all-to-all-done.6 = bf16[4,3,2,256,128]{4,3,2,1,0:T(8,128)(2,1)} async-done(((bf16[4,3,2,256,128]{4,3,2,1,0:T(8,128)(2,1)}), bf16[4,3,2,256,128]{4,3,2,1,0:T(8,128)(2,1)}, u32[]{:S(2)}, u32[]{:S(2)}) %all-to-all-start.6) | async-done | bytes 1572896 | tf_op jit(solution)/shard_map/all_to_all | solution.py:815
  79.1 24.9 %conditional.16 = (bf16[4,2,256,128]{3,2,1,0:T(8,128)(2,1)}, f32[2048,128]{1,0:T(8,128)}, f32[2,2048,128]{2,1,0:T(8,128)}, bf16[4,3,2,256,128]{4,3,2,1,0:T(8,128...) conditional(s32[]{:T(128)} %convert_element_type.144, () %tuple.134, ...), branch_computations={%region_2.3_spmd, %region_3.4_spmd} | conditional | flops 8589934592 | bytes 36176080 | solution.py:798
  79.1 4.7 all-to-all-start
  84.5 16.4 %attend_forward.2 = (bf16[4,2,256,128]{3,2,1,0:T(8,128)(2,1)}, f32[2048,128]{1,0:T(8,128)}, f32[2,2048,128]{2,1,0:T(8,128)}) custom-call(s32[2]{0:T(128)S(1)} %get-tuple-element.425.counts_ref, bf16[4,3,2,256,128]{4,3,2,1,0:T(8,128)(2,1)} %get-tuple-element.426.qkv_ref), custom_call_target="tpu_custom_call" | custom-call | flops 8589934592 | bytes 6291456 | tf_op jit(solution)/shard_map/cond/branch_1_fun/attend_forward/pallas_call | solution.py:221
  104.0 30.8 %conditional.17 = (bf16[4,2,256,128]{3,2,1,0:T(8,128)(2,1)}, f32[2048,128]{1,0:T(8,128)}, f32[2,2048,128]{2,1,0:T(8,128)}, bf16[4,2,256,128]{3,2,1,0:T(8,128)(2,1)}, bf16[256,1024]{1,0:T(8,128)(2,1)}) conditional(s32[]{:T(128)} %convert_element_type.144, () %tuple.138, (s32[2]{0:T(128)S(1)}, bf16[4,3,2,256,128]{4,3,2,1,0:T(8,128)(2,1)}, ...), branch_computations={%region_4.5_spmd, %region_5.6_spmd} | conditional | flops 8589934592 | bytes 11010210 | solution.py:798
  110.2 16.4 %attend_forward.3 = (bf16[4,2,256,128]{3,2,1,0:T(8,128)(2,1)}, f32[2048,128]{1,0:T(8,128)}, f32[2,2048,128]{2,1,0:T(8,128)}) custom-call(s32[2]{0:T(128)S(1)} %get-tuple-element.434.counts_ref, bf16[4,3,2,256,128]{4,3,2,1,0:T(8,128)(2,1)} %get-tuple-element.435.qkv_ref), custom_call_target="tpu_custom_call" | custom-call | flops 8589934592 | bytes 6291456 | tf_op jit(solution)/shard_map/cond/branch_1_fun/attend_forward/pallas_call | solution.py:221
  126.7 8.1 %collective-permute-done.40 = bf16[256,1024]{1,0:T(8,128)(2,1)} collective-permute-done((bf16[256,1024]{1,0:T(8,128)(2,1)S(1)}, bf16[256,1024]{1,0:T(8,128)(2,1)}, u32[]{:S(2)}, u32[]{:S(2)}) %collective-permute-start.40) | collective-permute-done | bytes 524320 | tf_op jit(solution)/shard_map/cond/branch_1_fun/ppermute | solution.py:788
  171.0 18.0 %ffn_forward.1 = (bf16[512,1024]{1,0:T(8,128)(2,1)}, f32[512,1024]{1,0:T(8,128)}, f32[1,1024]{1,0:T(1,128)}, bf16[512,4096]{1,0:T(8,128)(2,1)}, bf16[512,4096]{1...) custom-call(f32[512,1024]{1,0:T(8,128)S(1)} %convolution_add_fusion.x_ref, f32[1,1024]{1,0:T(1,128)S(1)} %get-tuple-element.1023.gain_ref, ...), custom_call_target="tpu_custom_call" | custom-call | flops 8589934592 | bytes 25165824 | tf_op jit(solution)/shard_map/ffn_forward/pallas_call | solution.py:395
  190.0 18.0 %conditional.18 = (f32[512,1024]{1,0:T(8,128)S(1)}, f32[1,1024]{1,0:T(1,128)S(1)}, bf16[512,1024]{1,0:T(8,128)(2,1)}, bf16[512,4096]{1,0:T(8,128)(2,1)}, bf16[51...) conditional(s32[]{:T(128)} %convert_element_type.144, () %tuple.142, (f32[512,1024]{1,0:T(8,128)S(1)}, ...), branch_computations={%region_10.11_spmd, %region_11.12_spmd} | conditional | flops 8589934592 | bytes 50331776 | solution.py:798
  190.5 17.5 %ffn_backward.1 = (f32[512,1024]{1,0:T(8,128)S(1)}, f32[1,1024]{1,0:T(1,128)S(1)}, bf16[512,1024]{1,0:T(8,128)(2,1)}, bf16[512,4096]{1,0:T(8,128)(2,1)}) custom-call(f32[512,1024]{1,0:T(8,128)S(1)} %get-tuple-element.442.x_ref, f32[1,1024]{1,0:T(1,128)S(1)} %get-tuple-element.443.gain_ref, f32[512,1024]{1,0:T(8,128)} %get-tuple-element.444.up_ref, ...), custom_call_target="tpu_custom_call" | custom-call | flops 8589934592 | bytes 29360128 | tf_op jit(solution)/shard_map/cond/branch_1_fun/ffn_backward/pallas_call | solution.py:452
  217.9 4.7 collective-permute-done.50
  239.7 24.9 %conditional.19 = (bf16[512,1024]{1,0:T(8,128)(2,1)}, bf16[512,1024]{1,0:T(8,128)(2,1)}, bf16[512,1024]{1,0:T(8,128)(2,1)}, bf16[512,1024]{1,0:T(8,128)(2,1)}, b...) conditional(s32[]{:T(128)} %convert_element_type.144, ...), branch_computations={%region_16.17_spmd, %region_17.18_spmd} | conditional | flops 8589934592 | bytes 60293492 | solution.py:798
  240.9 4.3 all-to-all-start.1
  245.2 9.2 %out_grad.2 = (bf16[2,4,64,1024]{3,2,1,0:T(8,128)(2,1)S(1)}, bf16[2,4,64,1024]{3,2,1,0:T(8,128)(2,1)S(1)}, bf16[2,4,64,1024]{3,2,1,0:T(8,128)(2,1)}, bf16[2,4,64,1024]{3,2,1,0:T(8,128)(2,1)}) custom-call(s32[2]{0:T(128)S(1)} %get-tuple-element.460.place_ref, bf16[512,1024]{1,0:T(8,128)(2,1)} %get-tuple-element.461.up_own, ...), custom_call_target="tpu_custom_call" | custom-call | flops 4294967296 | bytes 16777216 | tf_op jit(solution)/shard_map/cond/branch_1_fun/out_grad/pallas_call | solution.py:907
  254.4 10.1 %column_grads.4 = (bf16[2,4,64,1024]{3,2,1,0:T(8,128)(2,1)}, bf16[2,4,64,1024]{3,2,1,0:T(8,128)(2,1)}, bf16[2,4,64,1024]{3,2,1,0:T(8,128)(2,1)}, bf16[2,4,64,1024]{3,2,1,0:T(8,128)(2,1)}) custom-call(s32[2]{0:T(128)S(1)} %get-tuple-element.460.place_ref, bf16[512,1024]{1,0:T(8,128)(2,1)S(1)} %copy-done.46, bf16[512,1024]{1,0:T(8,128)(2,1)} %get-tuple-element.470.refs_1_, ...), custom_call_target="tpu_custom_call" | custom-call | flops 4294967296 | bytes 16777216 | tf_op jit(solution)/shard_map/cond/branch_1_fun/column_grads/pallas_call | solution.py:1010
  264.5 32.8 %conditional.20 = (bf16[4,3,2,256,128]{4,3,2,1,0:T(8,128)(2,1)}, bf16[4,2,256,128]{3,2,1,0:T(8,128)(2,1)}, bf16[256,1024]{1,0:T(8,128)(2,1)}, bf16[512,1024]{1,0...) conditional(s32[]{:T(128)} %convert_element_type.144, ...), branch_computations={%region_18.19_spmd, %region_19.20_spmd} | conditional | flops 17179869184 | bytes 29884704 | solution.py:798
  273.6 23.3 %attend_backward.2 = bf16[4,3,2,256,128]{4,3,2,1,0:T(8,128)(2,1)} custom-call(s32[2]{0:T(128)S(1)} %get-tuple-element.477.counts_ref, bf16[4,3,2,256,128]{4,3,2,1,0:T(8,128)(2,1)} %get-tuple-element.478.qkv_ref, f32[2048,128]{1,0:T(8,128)} %get-tuple-element.479.full_ref, f32[2,2048,128]{2,1,0:T(8,128)} %get-tuple-element.480.lse_ref, ...), custom_call_target="tpu_custom_call" | custom-call | flops 17179869184 | bytes 9437184 | tf_op jit(solution)/shard_map/cond/branch_1_fun/attend_backward/pallas_call | solution.py:331
  299.4 43.0 %conditional.21 = (bf16[4,3,2,256,128]{4,3,2,1,0:T(8,128)(2,1)}, bf16[4,3,2,256,128]{4,3,2,1,0:T(8,128)(2,1)}, bf16[4,64,1024]{2,1,0:T(8,128)(2,1)}, bf16[4,64,1...) conditional(s32[]{:T(128)} %convert_element_type.144, () %tuple.133, ...), branch_computations={%region_20.21_spmd, %region_21.22_spmd} | conditional | flops 17179869184 | bytes 26738928 | solution.py:798
  299.4 4.3 all-to-all-start.3
  307.9 23.3 %attend_backward.3 = bf16[4,3,2,256,128]{4,3,2,1,0:T(8,128)(2,1)} custom-call(s32[2]{0:T(128)S(1)} %get-tuple-element.488.counts_ref, bf16[4,3,2,256,128]{4,3,2,1,0:T(8,128)(2,1)} %get-tuple-element.489.qkv_ref, f32[2048,128]{1,0:T(8,128)} %get-tuple-element.490.full_ref, f32[2,2048,128]{2,1,0:T(8,128)} %get-tuple-element.491.lse_ref, ...), custom_call_target="tpu_custom_call" | custom-call | flops 17179869184 | bytes 9437184 | tf_op jit(solution)/shard_map/cond/branch_1_fun/attend_backward/pallas_call | solution.py:331
  331.2 11.3 %collective-permute-done.17 = bf16[2,4,64,1024]{3,2,1,0:T(8,128)(2,1)} collective-permute-done((bf16[2,4,64,1024]{3,2,1,0:T(8,128)(2,1)}, bf16[2,4,64,1024]{3,2,1,0:T(8,128)(2,1)}, u32[]{:S(2)}, u32[]{:S(2)}) %collective-permute-start.17) | collective-permute-done | bytes 1048608 | tf_op jit(solution)/shard_map/cond/branch_1_fun/ppermute | solution.py:788
  344.8 24.7 %conditional.22 = (bf16[4,3,2,256,128]{4,3,2,1,0:T(8,128)(2,1)}, bf16[2,4,64,1024]{3,2,1,0:T(8,128)(2,1)}, bf16[2,4,64,1024]{3,2,1,0:T(8,128)(2,1)}, bf16[2,4,64...) conditional(s32[]{:T(128)} %convert_element_type.144, ...), branch_computations={%region_22.23_spmd, %region_23.24_spmd} | conditional | flops 4294967296 | bytes 38273240 | solution.py:798
  344.8 4.5 all-to-all-start.4
  351.5 13.1 %column_grads.5 = (bf16[2,4,64,1024]{3,2,1,0:T(8,128)(2,1)}, bf16[2,4,64,1024]{3,2,1,0:T(8,128)(2,1)}, bf16[2,4,64,1024]{3,2,1,0:T(8,128)(2,1)}, bf16[2,4,64,1024]{3,2,1,0:T(8,128)(2,1)}) custom-call(s32[2]{0:T(128)S(1)} %get-tuple-element.499.place_ref, bf16[512,1024]{1,0:T(8,128)(2,1)} %get-tuple-element.500.refs_0_, ...), custom_call_target="tpu_custom_call" | custom-call | flops 4294967296 | bytes 16777216 | tf_op jit(solution)/shard_map/cond/branch_1_fun/column_grads/pallas_call | solution.py:1010
  369.5 70.3 %conditional.23 = (bf16[128,1024]{1,0:T(8,128)(2,1)S(1)}, bf16[128,1024]{1,0:T(8,128)(2,1)S(1)}, bf16[2,4,64,1024]{3,2,1,0:T(8,128)(2,1)}, bf16[2,4,64,1024]{3,2...) conditional(s32[]{:T(128)} %convert_element_type.144, ...), branch_computations={%region_24.25_spmd, %region_25.33_spmd} | conditional | flops 15032385536 | bytes 136856480 | solution.py:798
  371.1 26.5 %conditional = (bf16[512,3072]{1,0:T(8,128)(2,1)S(1)}, f32[512,1024]{1,0:T(8,128)}, bf16[512,1024]{1,0:T(8,128)(2,1)S(1)}, f32[1,1024]{1,0:T(1,128)}, bf16[2,4,6...) conditional(s32[]{:T(128)} %convert_element_type.108, () %tuple.90, (f32[512,128]{1,0:T(8,128)}, ...), branch_computations={%region_27.27_spmd, %region_28.28_spmd} | conditional | flops 3221225472 | bytes 26214528 | solution.py:798
  373.6 11.4 %projection_backward.1 = (bf16[512,3072]{1,0:T(8,128)(2,1)S(1)}, f32[512,1024]{1,0:T(8,128)}, bf16[512,1024]{1,0:T(8,128)(2,1)S(1)}, f32[1,1024]{1,0:T(1,128)}) custom-call(f32[512,128]{1,0:T(8,128)} %get-tuple-element.530.cos_ref, f32[512,128]{1,0:T(8,128)S(1)} %get-tuple-element.531.sin_ref, f32[512,1024]{1,0:T(8,128)} %get-tuple-element.532.x_ref, ...), custom_call_target="tpu_custom_call" | custom-call | flops 3221225472 | bytes 17825792 | tf_op jit(solution)/shard_map/cond/branch_1_fun/cond/branch_1_fun/projection_backward/pallas_call | solution.py:747
  385.0 11.2 %collective-permute-done.21 = bf16[2,4,64,1024]{3,2,1,0:T(8,128)(2,1)} collective-permute-done((bf16[2,4,64,1024]{3,2,1,0:T(8,128)(2,1)}, bf16[2,4,64,1024]{3,2,1,0:T(8,128)(2,1)}, u32[]{:S(2)}, u32[]{:S(2)}) %collective-permute-start.21) | collective-permute-done | bytes 1048608 | tf_op jit(solution)/shard_map/cond/branch_1_fun/cond/branch_1_fun/ppermute | solution.py:788
  399.2 17.2 %conditional.1 = (bf16[512,1024]{1,0:T(8,128)(2,1)}, bf16[2,4,64,768]{3,2,1,0:T(8,128)(2,1)}, bf16[2,4,64,768]{3,2,1,0:T(8,128)(2,1)}, bf16[2,4,64,768]{3,2,1,0:...) conditional(s32[]{:T(128)} %convert_element_type.108, () %tuple.92, ...), branch_computations={%region_29.29_spmd, %region_30.30_spmd} | conditional | flops 3221225472 | bytes 46137588 | solution.py:798
  402.0 4.5 collective-permute-done.24.refs_3_
  408.1 8.2 %column_grads.6 = (bf16[2,4,64,768]{3,2,1,0:T(8,128)(2,1)}, bf16[2,4,64,768]{3,2,1,0:T(8,128)(2,1)}, bf16[2,4,64,768]{3,2,1,0:T(8,128)(2,1)S(1)}, bf16[2,4,64,768]{3,2,1,0:T(8,128)(2,1)S(1)}) custom-call(s32[2]{0:T(128)S(1)} %get-tuple-element.545.place_ref, bf16[512,1024]{1,0:T(8,128)(2,1)} %get-tuple-element.546.refs_0_, ...), custom_call_target="tpu_custom_call" | custom-call | flops 3221225472 | bytes 12582912 | tf_op jit(solution)/shard_map/cond/branch_1_fun/cond/branch_1_fun/column_grads/pallas_call | solution.py:1010
  416.4 22.2 %conditional.2 = (bf16[512,4096]{1,0:T(8,128)(2,1)}, bf16[2,4,64,1024]{3,2,1,0:T(8,128)(2,1)}, bf16[2,4,64,1024]{3,2,1,0:T(8,128)(2,1)}, bf16[2,4,64,1024]{3,2,1...) conditional(s32[]{:T(128)} %convert_element_type.108, () %tuple.94, ...), branch_computations={%region_31.31_spmd, %region_32.32_spmd} | conditional | flops 8589934592 | bytes 44040328 | solution.py:798
  418.7 10.5 %hidden_gradient.1 = (bf16[512,1024]{1,0:T(8,128)(2,1)}, bf16[512,4096]{1,0:T(8,128)(2,1)}) custom-call(f32[512,1024]{1,0:T(8,128)} %get-tuple-element.555.up_ref, bf16[512,4096]{1,0:T(8,128)(2,1)} %get-tuple-element.556.slope_ref, bf16[4096,1024]{1,0:T(8,128)(2,1)} %get-tuple-element.557.wout_ref), custom_call_target="tpu_custom_call" | custom-call | flops 4294967296 | bytes 20971520 | tf_op jit(solution)/shard_map/cond/branch_1_fun/cond/branch_1_fun/hidden_gradient/pallas_call | solution.py:495
  429.1 9.5 %out_grad.3 = (bf16[2,4,64,1024]{3,2,1,0:T(8,128)(2,1)}, bf16[2,4,64,1024]{3,2,1,0:T(8,128)(2,1)}, bf16[2,4,64,1024]{3,2,1,0:T(8,128)(2,1)}, bf16[2,4,64,1024]{3,2,1,0:T(8,128)(2,1)}) custom-call(s32[2]{0:T(128)S(1)} %get-tuple-element.559.place_ref, bf16[512,1024]{1,0:T(8,128)(2,1)} %get-tuple-element.560.up_own, ...), custom_call_target="tpu_custom_call" | custom-call | flops 4294967296 | bytes 16777216 | tf_op jit(solution)/shard_map/cond/branch_1_fun/cond/branch_1_fun/out_grad/pallas_call | solution.py:907
  442.3 37.7 %conditional.24 = (bf16[128,1024]{1,0:T(8,128)(2,1)}, bf16[2,4,64,1024]{3,2,1,0:T(8,128)(2,1)}, bf16[2,4,64,1024]{3,2,1,0:T(8,128)(2,1)}, bf16[2,4,64,1024]{3,2,...) conditional(s32[]{:T(128)} %convert_element_type.144, ...), branch_computations={%region_33.34_spmd, %region_34.36_spmd} | conditional | flops 8589934592 | bytes 65806672 | solution.py:798
  451.0 11.5 %stream_gradient.1 = (bf16[512,1024]{1,0:T(8,128)(2,1)S(1)}, bf16[512,1024]{1,0:T(8,128)(2,1)}, f32[1,1024]{1,0:T(1,128)S(1)}) custom-call(bf16[512,1024]{1,0:T(8,128)(2,1)S(1)} %get-tuple-element.627.x_ref, f32[1,1024]{1,0:T(1,128)} %slice.150.gain_ref, f32[512,1024]{1,0:T(8,128)} %get-tuple-element.629.up_ref, ...), custom_call_target="tpu_custom_call" | custom-call | flops 4294967296 | bytes 12582912 | tf_op jit(solution)/shard_map/cond/branch_1_fun/stream_gradient/pallas_call | solution.py:540
  462.6 10.3 %column_grads.7 = (bf16[2,4,64,1024]{3,2,1,0:T(8,128)(2,1)}, bf16[2,4,64,1024]{3,2,1,0:T(8,128)(2,1)}, bf16[2,4,64,1024]{3,2,1,0:T(8,128)(2,1)S(1)}, bf16[2,4,64,1024]{3,2,1,0:T(8,128)(2,1)}) custom-call(s32[2]{0:T(128)S(1)} %get-tuple-element.619.place_ref, bf16[512,1024]{1,0:T(8,128)(2,1)} %get-tuple-element.620.refs_0_, ...), custom_call_target="tpu_custom_call" | custom-call | flops 4294967296 | bytes 16777216 | tf_op jit(solution)/shard_map/cond/branch_1_fun/column_grads/pallas_call | solution.py:1010
  472.9 7.1 %collective-permute-done.32 = bf16[4,64,768]{2,1,0:T(8,128)(2,1)} collective-permute-done((bf16[4,64,768]{2,1,0:T(8,128)(2,1)}, bf16[4,64,768]{2,1,0:T(8,128)(2,1)}, u32[]{:S(2)}, u32[]{:S(2)}) %collective-permute-start.32) | collective-permute-done | bytes 393248 | tf_op jit(solution)/shard_map/cond/branch_1_fun/ppermute | solution.py:788
  483.4 42.5 %conditional.25 = (bf16[128,768]{1,0:T(8,128)(2,1)}, bf16[256,1024]{1,0:T(8,128)(2,1)}, bf16[2,4,64,1024]{3,2,1,0:T(8,128)(2,1)}, bf16[2,4,64,1024]{3,2,1,0:T(8,...) conditional(s32[]{:T(128)} %convert_element_type.144, () %tuple.152, ...), branch_computations={%region_36.37_spmd, %region_37.39_spmd} | conditional | bytes 20775200 | solution.py:798
  493.0 33.0 %collective-permute-done.34 = bf16[256,1024]{1,0:T(8,128)(2,1)} collective-permute-done((bf16[256,1024]{1,0:T(8,128)(2,1)S(1)}, bf16[256,1024]{1,0:T(8,128)(2,1)}, u32[]{:S(2)}, u32[]{:S(2)}) %collective-permute-start.34) | collective-permute-done | bytes 524320 | tf_op jit(solution)/shard_map/cond/branch_1_fun/ppermute | solution.py:788
  528.7 59.8 %conditional.26 = (bf16[128,1024]{1,0:T(8,128)(2,1)}, f32[6,1024]{1,0:T(8,128)S(1)}, f32[5,1024]{1,0:T(8,128)S(1)}, bf16[2,256,1024]{2,1,0:T(8,128)(2,1)}, bf16[...) conditional(s32[]{:T(128)} %convert_element_type.144, ...), branch_computations={%region_41.42_spmd, %region_42.50_spmd} | conditional | flops 13521409 | bytes 45901348 | solution.py:798
  533.8 10.8 %collective-permute-done.41.refs_2_ = bf16[4,64,1024]{2,1,0:T(8,128)(2,1)S(1)} collective-permute-done((bf16[4,64,1024]{2,1,0:T(8,128)(2,1)}, bf16[4,64,1024]{2,1,0:T(8,128)(2,1)S(1)}, u32[]{:S(2)}, u32[]{:S(2)}) %collective-permute-start.41) | collective-permute-done | bytes 524320 | tf_op jit(solution)/shard_map/cond/branch_1_fun/ppermute | solution.py:788
  579.5 8.9 %reduce-scatter.12.cloned.1.call-done = bf16[1,1,2,64,1024]{4,3,2,1,0:T(8,128)(2,1)} async-done(((bf16[4,1,2,64,1024]{4,3,2,1,0:T(8,128)(2,1)}), bf16[1,1,2,64,1024]{4,3,2,1,0:T(8,128)(2,1)}) %reduce-scatter.12.cloned.1.call-update) | async-done | bytes 262160 | tf_op jit(solution)/shard_map/cond/branch_1_fun/reduce_scatter | solution.py:1130
  (319 shorter events, 195.4 us)
Async XLA Ops:
  9.6 27.4 %collective-permute-start.39 = (bf16[256,1024]{1,0:T(8,128)(2,1)S(1)}, bf16[256,1024]{1,0:T(8,128)(2,1)}, u32[]{:S(2)}, u32[]{:S(2)}) collective-permute-start(bf16[256,1024]{1,0:T(8,128)(2,1)S(1)} %dynamic-slice_bitcast_fusion), channel_id=1, source_target_pairs={{0,4},{1,5},{2,6},{3,7},{4,0},{5,1},{6,2},{7,3},{8,12},{9,13},{10,... | collective-permute-start | bytes 1572872 | tf_op jit(solution)/shard_map/cond/branch_1_fun/ppermute | solution.py:788
  54.5 24.6 %all-to-all-start.6 = ((bf16[4,3,2,256,128]{4,3,2,1,0:T(8,128)(2,1)}), bf16[4,3,2,256,128]{4,3,2,1,0:T(8,128)(2,1)}, u32[]{:S(2)}, u32[]{:S(2)}) async-start(bf16[4,3,2,256,128]{4,3,2,1,0:T(8,128)(2,1)} %get-tuple-element.842), calls=%async_computation.11 | async-start | bytes 3145728 | tf_op jit(solution)/shard_map/all_to_all | solution.py:815
  79.1 24.9 %collective-permute-start = (bf16[512,4096]{1,0:T(8,128)(2,1)}, bf16[512,4096]{1,0:T(8,128)(2,1)}, u32[]{:S(2)}, u32[]{:S(2)}) collective-permute-start(bf16[512,4096]{1,0:T(8,128)(2,1)} %get-tuple-element.431), channel_id=1, source_target_pairs={{0,1},{1,0},{2,3},{3,2},{4,5},{5,4},{6,7},{7,6},{8,9},{9,8},{10,11... | collective-permute-start | bytes 12582920 | tf_op jit(solution)/shard_map/cond/branch_1_fun/ppermute | solution.py:788
  79.1 24.8 %all-to-all-start = ((bf16[4,3,2,256,128]{4,3,2,1,0:T(8,128)(2,1)}), bf16[4,3,2,256,128]{4,3,2,1,0:T(8,128)(2,1)}, u32[]{:S(2)}, u32[]{:S(2)}) async-start(bf16[4,3,2,256,128]{4,3,2,1,0:T(8,128)(2,1)} %get-tuple-element.430), calls=%async_computation | async-start | bytes 3145728 | tf_op jit(solution)/shard_map/cond/branch_1_fun/all_to_all | solution.py:815
  104.0 30.8 %all-to-all-start.5 = ((bf16[4,2,256,128]{3,2,1,0:T(8,128)(2,1)}), bf16[4,2,256,128]{3,2,1,0:T(8,128)(2,1)}, u32[]{:S(2)}, u32[]{:S(2)}) async-start(bf16[4,2,256,128]{3,2,1,0:T(8,128)(2,1)} %get-tuple-element.439), calls=%async_computation.7 | async-start | bytes 1048576 | tf_op jit(solution)/shard_map/cond/branch_1_fun/all_to_all | solution.py:815
  108.2 26.6 %collective-permute-start.40 = (bf16[256,1024]{1,0:T(8,128)(2,1)S(1)}, bf16[256,1024]{1,0:T(8,128)(2,1)}, u32[]{:S(2)}, u32[]{:S(2)}) collective-permute-start(bf16[256,1024]{1,0:T(8,128)(2,1)S(1)} %dynamic-slice_bitcast_fusion.1), channel_id=1, source_target_pairs={{0,4},{1,5},{2,6},{3,7},{4,0},{5,1},{6,2},{7,3},{8,12},{9,13},{10,... | collective-permute-start | bytes 1572872 | tf_op jit(solution)/shard_map/cond/branch_1_fun/ppermute | solution.py:788
  190.0 18.0 %collective-permute-start.3 = (bf16[512,4096]{1,0:T(8,128)(2,1)}, bf16[512,4096]{1,0:T(8,128)(2,1)}, u32[]{:S(2)}, u32[]{:S(2)}) collective-permute-start(bf16[512,4096]{1,0:T(8,128)(2,1)} %get-tuple-element.452), channel_id=1, source_target_pairs={{0,1},{1,0},{2,3},{3,2},{4,5},{5,4},{6,7},{7,6},{8,9},{9,8},{10,11... | collective-permute-start | bytes 12582920 | tf_op jit(solution)/shard_map/cond/branch_1_fun/ppermute | solution.py:788
  190.0 18.0 %collective-permute-start.4 = (bf16[512,1024]{1,0:T(8,128)(2,1)S(1)}, bf16[512,1024]{1,0:T(8,128)(2,1)}, u32[]{:S(2)}, u32[]{:S(2)}) collective-permute-start(bf16[512,1024]{1,0:T(8,128)(2,1)S(1)} %get-tuple-element.453), channel_id=1, source_target_pairs={{0,1},{1,0},{2,3},{3,2},{4,5},{5,4},{6,7},{7,6},{8,9},{9,8},{10,11... | collective-permute-start | bytes 3145736 | tf_op jit(solution)/shard_map/cond/branch_1_fun/ppermute | solution.py:788
  214.7 25.0 %collective-permute-start.53 = (bf16[512,4096]{1,0:T(8,128)(2,1)}, bf16[512,4096]{1,0:T(8,128)(2,1)}, u32[]{:S(2)}, u32[]{:S(2)}) collective-permute-start(bf16[512,4096]{1,0:T(8,128)(2,1)} %get-tuple-element.866), channel_id=1, source_target_pairs={{0,1},{1,0},{2,3},{3,2},{4,5},{5,4},{6,7},{7,6},{8,9},{9,8},{10,11... | collective-permute-start | bytes 12582920 | tf_op jit(solution)/shard_map/ppermute | solution.py:788
  217.9 21.8 %collective-permute-start.52 = (bf16[512,1024]{1,0:T(8,128)(2,1)}, bf16[512,1024]{1,0:T(8,128)(2,1)}, u32[]{:S(2)}, u32[]{:S(2)}) collective-permute-start(bf16[512,1024]{1,0:T(8,128)(2,1)} %get-tuple-element.863), channel_id=1, source_target_pairs={{0,1},{1,0},{2,3},{3,2},{4,5},{5,4},{6,7},{7,6},{8,9},{9,8},{10,11... | collective-permute-start | bytes 3145736 | tf_op jit(solution)/shard_map/ppermute | solution.py:788
  239.7 24.8 %collective-permute-start.5 = (bf16[512,1024]{1,0:T(8,128)(2,1)}, bf16[512,1024]{1,0:T(8,128)(2,1)}, u32[]{:S(2)}, u32[]{:S(2)}) collective-permute-start(bf16[512,1024]{1,0:T(8,128)(2,1)} %get-tuple-element.454), channel_id=1, source_target_pairs={{0,1},{1,0},{2,3},{3,2},{4,5},{5,4},{6,7},{7,6},{8,9},{9,8},{10,11... | collective-permute-start | bytes 3145736 | tf_op jit(solution)/shard_map/cond/branch_1_fun/ppermute | solution.py:788
  239.9 24.6 %collective-permute-start.6 = (bf16[512,1024]{1,0:T(8,128)(2,1)}, bf16[512,1024]{1,0:T(8,128)(2,1)}, u32[]{:S(2)}, u32[]{:S(2)}) collective-permute-start(bf16[512,1024]{1,0:T(8,128)(2,1)} %get-tuple-element.455), channel_id=1, source_target_pairs={{0,1},{1,0},{2,3},{3,2},{4,5},{5,4},{6,7},{7,6},{8,9},{9,8},{10,11... | collective-permute-start | bytes 3145736 | tf_op jit(solution)/shard_map/cond/branch_1_fun/ppermute | solution.py:788
  240.3 24.3 %collective-permute-start.7 = (bf16[512,1024]{1,0:T(8,128)(2,1)}, bf16[512,1024]{1,0:T(8,128)(2,1)}, u32[]{:S(2)}, u32[]{:S(2)}) collective-permute-start(bf16[512,1024]{1,0:T(8,128)(2,1)} %get-tuple-element.456), channel_id=1, source_target_pairs={{0,1},{1,0},{2,3},{3,2},{4,5},{5,4},{6,7},{7,6},{8,9},{9,8},{10,11... | collective-permute-start | bytes 3145736 | tf_op jit(solution)/shard_map/cond/branch_1_fun/ppermute | solution.py:788
  240.4 24.1 %collective-permute-start.8 = (bf16[512,1024]{1,0:T(8,128)(2,1)}, bf16[512,1024]{1,0:T(8,128)(2,1)}, u32[]{:S(2)}, u32[]{:S(2)}) collective-permute-start(bf16[512,1024]{1,0:T(8,128)(2,1)} %get-tuple-element.457), channel_id=1, source_target_pairs={{0,1},{1,0},{2,3},{3,2},{4,5},{5,4},{6,7},{7,6},{8,9},{9,8},{10,11... | collective-permute-start | bytes 3145736 | tf_op jit(solution)/shard_map/cond/branch_1_fun/ppermute | solution.py:788
  240.8 23.8 %collective-permute-start.9 = (bf16[512,1024]{1,0:T(8,128)(2,1)}, bf16[512,1024]{1,0:T(8,128)(2,1)}, u32[]{:S(2)}, u32[]{:S(2)}) collective-permute-start(bf16[512,1024]{1,0:T(8,128)(2,1)} %get-tuple-element.458), channel_id=1, source_target_pairs={{0,1},{1,0},{2,3},{3,2},{4,5},{5,4},{6,7},{7,6},{8,9},{9,8},{10,11... | collective-permute-start | bytes 3145736 | tf_op jit(solution)/shard_map/cond/branch_1_fun/ppermute | solution.py:788
  240.9 23.6 %all-to-all-start.1 = ((bf16[4,2,256,128]{3,2,1,0:T(8,128)(2,1)}), bf16[4,2,256,128]{3,2,1,0:T(8,128)(2,1)}, u32[]{:S(2)}, u32[]{:S(2)}) async-start(bf16[4,2,256,128]{3,2,1,0:T(8,128)(2,1)} %get-tuple-element.459), calls=%async_computation.1 | async-start | bytes 1048576 | tf_op jit(solution)/shard_map/cond/branch_1_fun/all_to_all | solution.py:815
  264.6 32.3 %all-to-all-start.2 = ((bf16[4,2,256,128]{3,2,1,0:T(8,128)(2,1)}), bf16[4,2,256,128]{3,2,1,0:T(8,128)(2,1)}, u32[]{:S(2)}, u32[]{:S(2)}) async-start(bf16[4,2,256,128]{3,2,1,0:T(8,128)(2,1)} %get-tuple-element.482), calls=%async_computation.2 | async-start | bytes 1048576 | tf_op jit(solution)/shard_map/cond/branch_1_fun/all_to_all | solution.py:815
  268.7 28.1 %collective-permute-start.10 = (bf16[256,1024]{1,0:T(8,128)(2,1)}, bf16[256,1024]{1,0:T(8,128)(2,1)}, u32[]{:S(2)}, u32[]{:S(2)}) collective-permute-start(bf16[256,1024]{1,0:T(8,128)(2,1)} %get-tuple-element.483), channel_id=1, source_target_pairs={{0,4},{1,5},{2,6},{3,7},{4,0},{5,1},{6,2},{7,3},{8,12},{9,13},{10,... | collective-permute-start | bytes 1572872 | tf_op jit(solution)/shard_map/cond/branch_1_fun/ppermute | solution.py:788
  270.1 26.8 %collective-permute-start.11 = (bf16[512,1024]{1,0:T(8,128)(2,1)}, bf16[512,1024]{1,0:T(8,128)(2,1)}, u32[]{:S(2)}, u32[]{:S(2)}) collective-permute-start(bf16[512,1024]{1,0:T(8,128)(2,1)} %get-tuple-element.484), channel_id=1, source_target_pairs={{0,1},{1,0},{2,3},{3,2},{4,5},{5,4},{6,7},{7,6},{8,9},{9,8},{10,11... | collective-permute-start | bytes 3145736 | tf_op jit(solution)/shard_map/cond/branch_1_fun/ppermute | solution.py:788
  270.3 26.6 %collective-permute-start.12 = (bf16[512,1024]{1,0:T(8,128)(2,1)}, bf16[512,1024]{1,0:T(8,128)(2,1)}, u32[]{:S(2)}, u32[]{:S(2)}) collective-permute-start(bf16[512,1024]{1,0:T(8,128)(2,1)} %get-tuple-element.485), channel_id=1, source_target_pairs={{0,1},{1,0},{2,3},{3,2},{4,5},{5,4},{6,7},{7,6},{8,9},{9,8},{10,11... | collective-permute-start | bytes 3145736 | tf_op jit(solution)/shard_map/cond/branch_1_fun/ppermute | solution.py:788
  270.6 26.3 %collective-permute-start.13 = (bf16[2,4,64,1024]{3,2,1,0:T(8,128)(2,1)}, bf16[2,4,64,1024]{3,2,1,0:T(8,128)(2,1)}, u32[]{:S(2)}, u32[]{:S(2)}) collective-permute-start(bf16[2,4,64,1024]{3,2,1,0:T(8,128)(2,1)} %get-tuple-element.486), channel_id=1, source_target_pairs={{0,8},{1,9},{2,10},{3,11},{4,12},{5,13},{6,14},{7,15},{8,0},{9,1},... | collective-permute-start | bytes 3145736 | tf_op jit(solution)/shard_map/cond/branch_1_fun/ppermute | solution.py:788
  272.1 25.3 %collective-permute-start.14 = (bf16[2,4,64,1024]{3,2,1,0:T(8,128)(2,1)}, bf16[2,4,64,1024]{3,2,1,0:T(8,128)(2,1)}, u32[]{:S(2)}, u32[]{:S(2)}) collective-permute-start(bf16[2,4,64,1024]{3,2,1,0:T(8,128)(2,1)} %get-tuple-element.487), channel_id=1, source_target_pairs={{0,16},{1,17},{2,18},{3,19},{4,20},{5,21},{6,22},{7,23},{8,24},{9,... | collective-permute-start | bytes 3145736 | tf_op jit(solution)/shard_map/cond/branch_1_fun/ppermute | solution.py:788
  299.4 43.0 %all-to-all-start.3 = ((bf16[4,3,2,256,128]{4,3,2,1,0:T(8,128)(2,1)}), bf16[4,3,2,256,128]{4,3,2,1,0:T(8,128)(2,1)}, u32[]{:S(2)}, u32[]{:S(2)}) async-start(bf16[4,3,2,256,128]{4,3,2,1,0:T(8,128)(2,1)} %get-tuple-element.493), calls=%async_computation.3 | async-start | bytes 3145728 | tf_op jit(solution)/shard_map/cond/branch_1_fun/all_to_all | solution.py:815
  303.8 27.4 %collective-permute-start.15 = (bf16[4,64,1024]{2,1,0:T(8,128)(2,1)}, bf16[4,64,1024]{2,1,0:T(8,128)(2,1)}, u32[]{:S(2)}, u32[]{:S(2)}) collective-permute-start(bf16[4,64,1024]{2,1,0:T(8,128)(2,1)} %get-tuple-element.494), channel_id=1, source_target_pairs={{0,16},{1,17},{2,18},{3,19},{4,20},{5,21},{6,22},{7,23},{8,24},{9,... | collective-permute-start | bytes 1572872 | tf_op jit(solution)/shard_map/cond/branch_1_fun/ppermute | solution.py:788
  305.4 25.8 %collective-permute-start.16 = (bf16[4,64,1024]{2,1,0:T(8,128)(2,1)}, bf16[4,64,1024]{2,1,0:T(8,128)(2,1)}, u32[]{:S(2)}, u32[]{:S(2)}) collective-permute-start(bf16[4,64,1024]{2,1,0:T(8,128)(2,1)} %get-tuple-element.495), channel_id=1, source_target_pairs={{0,8},{1,9},{2,10},{3,11},{4,12},{5,13},{6,14},{7,15},{8,0},{9,1},... | collective-permute-start | bytes 1572872 | tf_op jit(solution)/shard_map/cond/branch_1_fun/ppermute | solution.py:788
  307.5 35.0 %collective-permute-start.17 = (bf16[2,4,64,1024]{3,2,1,0:T(8,128)(2,1)}, bf16[2,4,64,1024]{3,2,1,0:T(8,128)(2,1)}, u32[]{:S(2)}, u32[]{:S(2)}) collective-permute-start(bf16[2,4,64,1024]{3,2,1,0:T(8,128)(2,1)} %get-tuple-element.496), channel_id=1, source_target_pairs={{0,8},{1,9},{2,10},{3,11},{4,12},{5,13},{6,14},{7,15},{8,0},{9,1},... | collective-permute-start | bytes 3145736 | tf_op jit(solution)/shard_map/cond/branch_1_fun/ppermute | solution.py:788
  307.5 34.9 %collective-permute-start.18 = (bf16[2,4,64,1024]{3,2,1,0:T(8,128)(2,1)}, bf16[2,4,64,1024]{3,2,1,0:T(8,128)(2,1)}, u32[]{:S(2)}, u32[]{:S(2)}) collective-permute-start(bf16[2,4,64,1024]{3,2,1,0:T(8,128)(2,1)} %get-tuple-element.497), channel_id=1, source_target_pairs={{0,16},{1,17},{2,18},{3,19},{4,20},{5,21},{6,22},{7,23},{8,24},{9,... | collective-permute-start | bytes 3145736 | tf_op jit(solution)/shard_map/cond/branch_1_fun/ppermute | solution.py:788
  344.8 24.7 %all-to-all-start.4 = ((bf16[4,3,2,256,128]{4,3,2,1,0:T(8,128)(2,1)}), bf16[4,3,2,256,128]{4,3,2,1,0:T(8,128)(2,1)}, u32[]{:S(2)}, u32[]{:S(2)}) async-start(bf16[4,3,2,256,128]{4,3,2,1,0:T(8,128)(2,1)} %get-tuple-element.498), calls=%async_computation.4 | async-start | bytes 3145728 | tf_op jit(solution)/shard_map/cond/branch_1_fun/all_to_all | solution.py:815
  369.5 69.2 %reduce-scatter.6.cloned.1.call-start = ((), (), s32[]{:S(2)}) async-start(), calls=%async_computation.13 | async-start | bytes 2621440 | tf_op jit(solution)/shard_map/cond/branch_1_fun/reduce_scatter | solution.py:1130
  371.1 25.1 %collective-permute-start.21 = (bf16[2,4,64,1024]{3,2,1,0:T(8,128)(2,1)}, bf16[2,4,64,1024]{3,2,1,0:T(8,128)(2,1)}, u32[]{:S(2)}, u32[]{:S(2)}) collective-permute-start(bf16[2,4,64,1024]{3,2,1,0:T(8,128)(2,1)} %get-tuple-element.542), channel_id=1, source_target_pairs={{0,8},{1,9},{2,10},{3,11},{4,12},{5,13},{6,14},{7,15},{8,0},{9,1},... | collective-permute-start | bytes 3145736 | tf_op jit(solution)/shard_map/cond/branch_1_fun/cond/branch_1_fun/ppermute | solution.py:788
  372.8 24.7 %collective-permute-start.22 = (bf16[2,4,64,1024]{3,2,1,0:T(8,128)(2,1)}, bf16[2,4,64,1024]{3,2,1,0:T(8,128)(2,1)}, u32[]{:S(2)}, u32[]{:S(2)}) collective-permute-start(bf16[2,4,64,1024]{3,2,1,0:T(8,128)(2,1)} %get-tuple-element.543), channel_id=1, source_target_pairs={{0,16},{1,17},{2,18},{3,19},{4,20},{5,21},{6,22},{7,23},{8,24},{9,... | collective-permute-start | bytes 3145736 | tf_op jit(solution)/shard_map/cond/branch_1_fun/cond/branch_1_fun/ppermute | solution.py:788
  399.3 17.1 %collective-permute-start.23 = (bf16[512,1024]{1,0:T(8,128)(2,1)S(1)}, bf16[512,1024]{1,0:T(8,128)(2,1)}, u32[]{:S(2)}, u32[]{:S(2)}) collective-permute-start(bf16[512,1024]{1,0:T(8,128)(2,1)S(1)} %get-tuple-element.544), channel_id=1, source_target_pairs={{0,1},{1,0},{2,3},{3,2},{4,5},{5,4},{6,7},{7,6},{8,9},{9,8},{10,11... | collective-permute-start | bytes 3145736 | tf_op jit(solution)/shard_map/cond/branch_1_fun/cond/branch_1_fun/ppermute | solution.py:788
  416.4 22.2 %collective-permute-start.27 = (bf16[2,4,64,768]{3,2,1,0:T(8,128)(2,1)S(1)}, bf16[2,4,64,768]{3,2,1,0:T(8,128)(2,1)}, u32[]{:S(2)}, u32[]{:S(2)}) collective-permute-start(bf16[2,4,64,768]{3,2,1,0:T(8,128)(2,1)S(1)} %get-tuple-element.568), channel_id=1, source_target_pairs={{0,8},{1,9},{2,10},{3,11},{4,12},{5,13},{6,14},{7,15},{8,0},{9,1},... | collective-permute-start | bytes 2359304 | tf_op jit(solution)/shard_map/cond/branch_1_fun/cond/branch_1_fun/ppermute | solution.py:788
  416.9 21.8 %collective-permute-start.28 = (bf16[2,4,64,768]{3,2,1,0:T(8,128)(2,1)S(1)}, bf16[2,4,64,768]{3,2,1,0:T(8,128)(2,1)}, u32[]{:S(2)}, u32[]{:S(2)}) collective-permute-start(bf16[2,4,64,768]{3,2,1,0:T(8,128)(2,1)S(1)} %get-tuple-element.569), channel_id=1, source_target_pairs={{0,16},{1,17},{2,18},{3,19},{4,20},{5,21},{6,22},{7,23},{8,24},{9,... | collective-permute-start | bytes 2359304 | tf_op jit(solution)/shard_map/cond/branch_1_fun/cond/branch_1_fun/ppermute | solution.py:788
  442.3 37.7 %reduce-scatter.8.cloned.1.call-start = ((), (), s32[]{:S(2)}) async-start(), calls=%async_computation.14 | async-start | bytes 1310720 | tf_op jit(solution)/shard_map/cond/branch_1_fun/reduce_scatter | solution.py:1130
  442.6 20.0 %collective-permute-start.29 = (bf16[512,4096]{1,0:T(8,128)(2,1)}, bf16[512,4096]{1,0:T(8,128)(2,1)}, u32[]{:S(2)}, u32[]{:S(2)}) collective-permute-start(bf16[512,4096]{1,0:T(8,128)(2,1)} %get-tuple-element.622.refs_2_.grad_ref), channel_id=1, source_target_pairs={{0,1},{1,0},{2,3},{3,2},{4,5},{5,4},{6,7},{7,6},{8,9},{9,8},{10,11... | collective-permute-start | bytes 12582920 | tf_op jit(solution)/shard_map/cond/branch_1_fun/ppermute | solution.py:788
  445.6 34.4 %collective-permute-start.30 = (bf16[2,4,64,1024]{3,2,1,0:T(8,128)(2,1)}, bf16[2,4,64,1024]{3,2,1,0:T(8,128)(2,1)}, u32[]{:S(2)}, u32[]{:S(2)}) collective-permute-start(bf16[2,4,64,1024]{3,2,1,0:T(8,128)(2,1)} %get-tuple-element.634), channel_id=1, source_target_pairs={{0,8},{1,9},{2,10},{3,11},{4,12},{5,13},{6,14},{7,15},{8,0},{9,1},... | collective-permute-start | bytes 3145736 | tf_op jit(solution)/shard_map/cond/branch_1_fun/ppermute | solution.py:788
  446.0 34.0 %collective-permute-start.31 = (bf16[2,4,64,1024]{3,2,1,0:T(8,128)(2,1)}, bf16[2,4,64,1024]{3,2,1,0:T(8,128)(2,1)}, u32[]{:S(2)}, u32[]{:S(2)}) collective-permute-start(bf16[2,4,64,1024]{3,2,1,0:T(8,128)(2,1)} %get-tuple-element.635), channel_id=1, source_target_pairs={{0,16},{1,17},{2,18},{3,19},{4,20},{5,21},{6,22},{7,23},{8,24},{9,... | collective-permute-start | bytes 3145736 | tf_op jit(solution)/shard_map/cond/branch_1_fun/ppermute | solution.py:788
  447.5 32.5 %collective-permute-start.32 = (bf16[4,64,768]{2,1,0:T(8,128)(2,1)}, bf16[4,64,768]{2,1,0:T(8,128)(2,1)}, u32[]{:S(2)}, u32[]{:S(2)}) collective-permute-start(bf16[4,64,768]{2,1,0:T(8,128)(2,1)} %get-tuple-element.636), channel_id=1, source_target_pairs={{0,16},{1,17},{2,18},{3,19},{4,20},{5,21},{6,22},{7,23},{8,24},{9,... | collective-permute-start | bytes 1179656 | tf_op jit(solution)/shard_map/cond/branch_1_fun/ppermute | solution.py:788
  448.0 32.0 %collective-permute-start.33 = (bf16[4,64,768]{2,1,0:T(8,128)(2,1)}, bf16[4,64,768]{2,1,0:T(8,128)(2,1)}, u32[]{:S(2)}, u32[]{:S(2)}) collective-permute-start(bf16[4,64,768]{2,1,0:T(8,128)(2,1)} %get-tuple-element.637), channel_id=1, source_target_pairs={{0,8},{1,9},{2,10},{3,11},{4,12},{5,13},{6,14},{7,15},{8,0},{9,1},... | collective-permute-start | bytes 1179656 | tf_op jit(solution)/shard_map/cond/branch_1_fun/ppermute | solution.py:788
  483.4 42.5 %reduce-scatter.10.cloned.1.call-start = ((), (), s32[]{:S(2)}) async-start(), calls=%async_computation.15 | async-start | bytes 983040 | tf_op jit(solution)/shard_map/cond/branch_1_fun/reduce_scatter | solution.py:1130
  486.1 39.8 %collective-permute-start.35 = (bf16[2,4,64,1024]{3,2,1,0:T(8,128)(2,1)S(1)}, bf16[2,4,64,1024]{3,2,1,0:T(8,128)(2,1)}, u32[]{:S(2)}, u32[]{:S(2)}) collective-permute-start(bf16[2,4,64,1024]{3,2,1,0:T(8,128)(2,1)S(1)} %get-tuple-element.645), channel_id=1, source_target_pairs={{0,8},{1,9},{2,10},{3,11},{4,12},{5,13},{6,14},{7,15},{8,0},{9,1},... | collective-permute-start | bytes 3145736 | tf_op jit(solution)/shard_map/cond/branch_1_fun/ppermute | solution.py:788
  487.8 38.1 %collective-permute-start.36 = (bf16[2,4,64,1024]{3,2,1,0:T(8,128)(2,1)}, bf16[2,4,64,1024]{3,2,1,0:T(8,128)(2,1)}, u32[]{:S(2)}, u32[]{:S(2)}) collective-permute-start(bf16[2,4,64,1024]{3,2,1,0:T(8,128)(2,1)} %get-tuple-element.646), channel_id=1, source_target_pairs={{0,16},{1,17},{2,18},{3,19},{4,20},{5,21},{6,22},{7,23},{8,24},{9,... | collective-permute-start | bytes 3145736 | tf_op jit(solution)/shard_map/cond/branch_1_fun/ppermute | solution.py:788
  488.1 37.8 %collective-permute-start.34 = (bf16[256,1024]{1,0:T(8,128)(2,1)S(1)}, bf16[256,1024]{1,0:T(8,128)(2,1)}, u32[]{:S(2)}, u32[]{:S(2)}) collective-permute-start(bf16[256,1024]{1,0:T(8,128)(2,1)S(1)} %get-tuple-element.644), channel_id=1, source_target_pairs={{0,4},{1,5},{2,6},{3,7},{4,0},{5,1},{6,2},{7,3},{8,12},{9,13},{10,... | collective-permute-start | bytes 1572872 | tf_op jit(solution)/shard_map/cond/branch_1_fun/ppermute | solution.py:788
  491.0 35.0 %collective-permute-start.37 = (bf16[4,64,1024]{2,1,0:T(8,128)(2,1)S(1)}, bf16[4,64,1024]{2,1,0:T(8,128)(2,1)}, u32[]{:S(2)}, u32[]{:S(2)}) collective-permute-start(bf16[4,64,1024]{2,1,0:T(8,128)(2,1)S(1)} %get-tuple-element.647), channel_id=1, source_target_pairs={{0,16},{1,17},{2,18},{3,19},{4,20},{5,21},{6,22},{7,23},{8,24},{9,... | collective-permute-start | bytes 1572872 | tf_op jit(solution)/shard_map/cond/branch_1_fun/ppermute | solution.py:788
  492.4 33.5 %collective-permute-start.38 = (bf16[4,64,1024]{2,1,0:T(8,128)(2,1)}, bf16[4,64,1024]{2,1,0:T(8,128)(2,1)}, u32[]{:S(2)}, u32[]{:S(2)}) collective-permute-start(bf16[4,64,1024]{2,1,0:T(8,128)(2,1)} %get-tuple-element.648), channel_id=1, source_target_pairs={{0,8},{1,9},{2,10},{3,11},{4,12},{5,13},{6,14},{7,15},{8,0},{9,1},... | collective-permute-start | bytes 1572872 | tf_op jit(solution)/shard_map/cond/branch_1_fun/ppermute | solution.py:788
  528.7 49.0 %reduce-scatter.14.cloned.1.call-start = ((), (), s32[]{:S(2)}) async-start(), calls=%async_computation.17 | async-start | bytes 1310720 | tf_op jit(solution)/shard_map/cond/branch_1_fun/reduce_scatter | solution.py:1130
  531.6 56.8 %reduce-scatter.12.cloned.1.call-start = ((), (), s32[]{:S(2)}) async-start(), calls=%async_computation.16 | async-start | bytes 1310720 | tf_op jit(solution)/shard_map/cond/branch_1_fun/reduce_scatter | solution.py:1130
  (67 other events, 644.5 us)
Sparse Core Ops, SparseCore 0:
  372.6 44.7 reduce-scatter.5
  445.7 27.6 reduce-scatter.7
  487.1 34.2 reduce-scatter.9
  531.7 27.2 reduce-scatter.13
  561.2 27.1 reduce-scatter.11

commit v3 on v2

--- a/solution.py
+++ b/solution.py
@@ -788,15 +788,20 @@
     return lax.ppermute(value, EVERY, flipped(axis_bit, count))
 
 
+def branched(always, work):
+    def empty():
+        return jax.tree.map(lambda leaf: jnp.zeros(leaf.shape, leaf.dtype), jax.eval_shape(work))
+
+    return lax.optimization_barrier(lax.cond(always, work, empty))
+
+
 def fenced(always, scatters, work):
     def run():
-        return (work(), [scatter.move() for scatter in scatters])
-
-    def empty():
-        return jax.tree.map(lambda leaf: jnp.zeros(leaf.shape, leaf.dtype), jax.eval_shape(run))
-
-    result, moved = lax.optimization_barrier(lax.cond(always, run, empty))
-    for scatter, parts in zip(scatters, moved):
+        moves = [scatter.move() for scatter in scatters]
+        return (branched(always, work) if any(moves) else work(), moves)
+
+    result, moves = branched(always, run)
+    for scatter, parts in zip(scatters, moves):
         scatter.take(parts)
     return result
 
@@ -1418,20 +1423,19 @@
         two_grads = along_z(two_sum)
         scatter = copy.copy(middle)
 
-        grad_proj, grad_one, half_one, gain_one = fenced(
-            always,
-            (scatter,),
-            lambda: projection_backward(
+        def projection_part():
+            grad_proj, *down = projection_backward(
                 backs, cosines, sines, size, grad_two, stream_one, gain[1], w_qkv
-            ),
-        )
+            )
+            return ((grad_proj, other_core(grad_proj)), down)
+
+        grad_proj, (grad_one, half_one, gain_one) = fenced(always, (scatter,), projection_part)
         first = scatter.got
         scatter.second(second_sums(scatter)[0])
 
         def qkv_part():
             half_other = other_core(half_one)
-            right = (grad_proj, other_core(grad_proj))
-            return (half_other, column_grads([ent_att], [right], ways, where, items))
+            return (half_other, column_grads([ent_att], [grad_proj], ways, where, items))
 
         half_other, shares = fenced(always, (scatter,), qkv_part)
         attn = Scatter(*shares)

time: 607 us -> 596 us (0.982)
  waiting for transfers between devices: 140 us -> 123 us
  Pallas kernels: 278 us -> 289 us
    ppermute x50, waiting for transfers between devices: 106 us -> 91.1 us  [swap(): return lax.ppermute(value, EVERY, flipped(axis_bit, count))]
    pallas_call x2, Pallas kernels: 46.5 us -> 52.7 us  [attend_backward(): pl.pallas_call(functools.partial(attn_bwd_kernel, heads, size, group), gr...]
  transfers between devices with their start and end apart: 67 -> 67, of which waited for: 22 -> 23; matrix products, arithmetic and copies ran while one was open for 7% -> 7% of each run, Pallas kernels for 38% -> 41%
where the time goes in v3:
time: 596 us; the launch traced here: 587 us
  Pallas kernels  289 us (48%)
  waiting for transfers between devices  123 us (21%)
  starting transfers between devices  78.2 us (13%)
  other arithmetic  38.5 us (6%)
  matrix products  21.3 us (4%)
  local copies, waits for them, and re-layouts  18.6 us (3%)
  between operations  17.5 us (3%)
    ppermute x50, waiting for transfers between devices, swap(): return lax.ppermute(value, EVERY, flipped(axis_bit, count))  91.1 us
    pallas_call x2, Pallas kernels, attend_backward(): pl.pallas_call(functools.partial(attn_bwd_kernel, heads, size, group), gr...  52.7 us
    pallas_call x4, Pallas kernels, column_grads(): pl.pallas_call(functools.partial(column_grad_kernel, heads, items, split)...  42.9 us
    ppermute x50, starting transfers between devices, swap(): return lax.ppermute(value, EVERY, flipped(axis_bit, count))  42.2 us
    pallas_call x2, Pallas kernels, attend_forward(): pl.pallas_call(functools.partial(attn_fwd_kernel, heads, size, group), gr...  36.4 us
    pallas_call x2, Pallas kernels, front(): pl.pallas_call(functools.partial(front_kernel, size, ffn_steps, pieces),...  34.4 us
    all_to_all x8, starting transfers between devices, exchange(): lax.all_to_all(value, 'heads', split_axis=0, concat_axis=0, tiled=True, a...  34.1 us
    dot_general x7, matrix products, dot(): return lax.dot_general(left, right, dims, preferred_element_type=F32)  21.3 us
  transfers between devices with their start and end apart: 67, of which 23 were waited for; matrix products, arithmetic and copies ran while one was open for 7% of the time, Pallas kernels for 41%

profile of v3, /device:TPU:0, one launch (start us, length us, event | category | flops | bytes accessed | tf_op | source)
XLA Modules:
  0.0 586.7 jit_solution(10603987723631471806)
XLA Ops:
  8.4 28.6 %conditional.22 = (f32[512,1024]{1,0:T(8,128)}, bf16[512,4096]{1,0:T(8,128)(2,1)}, bf16[512,4096]{1,0:T(8,128)(2,1)}, bf16[512,1024]{1,0:T(8,128)(2,1)}, bf16[51...) conditional(s32[]{:T(128)} %convert_element_type.165, ...), branch_computations={%region_0.1_spmd, %region_1.2_spmd} | conditional | flops 5905580032 | bytes 34603160 | solution.py:795
  13.7 16.9 %front.2 = (f32[512,1024]{1,0:T(8,128)}, bf16[512,4096]{1,0:T(8,128)(2,1)}, bf16[512,4096]{1,0:T(8,128)(2,1)}, bf16[512,1024]{1,0:T(8,128)(2,1)}, bf16[512,1024]...) custom-call(s32[1]{0:T(128)} %bitcast.row_ref, ...), custom_call_target="tpu_custom_call" | custom-call | flops 5905580032 | bytes 31457280 | tf_op jit(solution)/shard_map/cond/branch_1_fun/front/pallas_call | solution.py:688
  30.6 6.3 %collective-permute-done.39 = bf16[256,1024]{1,0:T(8,128)(2,1)} collective-permute-done((bf16[256,1024]{1,0:T(8,128)(2,1)S(1)}, bf16[256,1024]{1,0:T(8,128)(2,1)}, u32[]{:S(2)}, u32[]{:S(2)}) %collective-permute-start.39) | collective-permute-done | bytes 524320 | tf_op jit(solution)/shard_map/cond/branch_1_fun/ppermute | solution.py:788
  37.0 17.4 %front.3 = (f32[512,1024]{1,0:T(8,128)}, bf16[512,4096]{1,0:T(8,128)(2,1)}, bf16[512,4096]{1,0:T(8,128)(2,1)}, bf16[512,1024]{1,0:T(8,128)(2,1)}, bf16[512,1024]...) custom-call(s32[1]{0:T(128)} %bitcast.19.row_ref, ...), custom_call_target="tpu_custom_call", output_to_operand_aliasing={{0}: (10, {}), {1}: (11, {}), {2}: (12, {}), {3}: (13, {}),... | custom-call | flops 5905580032 | bytes 31457280 | tf_op jit(solution)/shard_map/front/pallas_call | solution.py:688
  66.6 12.5 %all-to-all-done.6 = bf16[4,3,2,256,128]{4,3,2,1,0:T(8,128)(2,1)} async-done(((bf16[4,3,2,256,128]{4,3,2,1,0:T(8,128)(2,1)}), bf16[4,3,2,256,128]{4,3,2,1,0:T(8,128)(2,1)}, u32[]{:S(2)}, u32[]{:S(2)}) %all-to-all-start.6) | async-done | bytes 1572896 | tf_op jit(solution)/shard_map/all_to_all | solution.py:820
  79.1 24.8 %conditional.23 = (bf16[4,2,256,128]{3,2,1,0:T(8,128)(2,1)}, f32[2048,128]{1,0:T(8,128)}, f32[2,2048,128]{2,1,0:T(8,128)}, bf16[4,3,2,256,128]{4,3,2,1,0:T(8,128...) conditional(s32[]{:T(128)} %convert_element_type.165, () %tuple.190, ...), branch_computations={%region_2.3_spmd, %region_3.4_spmd} | conditional | flops 8589934592 | bytes 36176080 | solution.py:795
  84.4 18.2 %attend_forward.2 = (bf16[4,2,256,128]{3,2,1,0:T(8,128)(2,1)}, f32[2048,128]{1,0:T(8,128)}, f32[2,2048,128]{2,1,0:T(8,128)}) custom-call(s32[2]{0:T(128)S(1)} %get-tuple-element.555.counts_ref, bf16[4,3,2,256,128]{4,3,2,1,0:T(8,128)(2,1)} %get-tuple-element.556.qkv_ref), custom_call_target="tpu_custom_call" | custom-call | flops 8589934592 | bytes 6291456 | tf_op jit(solution)/shard_map/cond/branch_1_fun/attend_forward/pallas_call | solution.py:221
  103.9 30.8 %conditional.24 = (bf16[4,2,256,128]{3,2,1,0:T(8,128)(2,1)}, f32[2048,128]{1,0:T(8,128)}, f32[2,2048,128]{2,1,0:T(8,128)}, bf16[4,2,256,128]{3,2,1,0:T(8,128)(2,1)}, bf16[256,1024]{1,0:T(8,128)(2,1)}) conditional(s32[]{:T(128)} %convert_element_type.165, () %tuple.194, (s32[2]{0:T(128)S(1)}, bf16[4,3,2,256,128]{4,3,2,1,0:T(8,128)(2,1)}, ...), branch_computations={%region_4.5_spmd, %region_5.6_spmd} | conditional | flops 8589934592 | bytes 11010210 | solution.py:795
  110.2 18.2 %attend_forward.3 = (bf16[4,2,256,128]{3,2,1,0:T(8,128)(2,1)}, f32[2048,128]{1,0:T(8,128)}, f32[2,2048,128]{2,1,0:T(8,128)}) custom-call(s32[2]{0:T(128)S(1)} %get-tuple-element.564.counts_ref, bf16[4,3,2,256,128]{4,3,2,1,0:T(8,128)(2,1)} %get-tuple-element.565.qkv_ref), custom_call_target="tpu_custom_call" | custom-call | flops 8589934592 | bytes 6291456 | tf_op jit(solution)/shard_map/cond/branch_1_fun/attend_forward/pallas_call | solution.py:221
  128.4 6.4 %collective-permute-done.40 = bf16[256,1024]{1,0:T(8,128)(2,1)} collective-permute-done((bf16[256,1024]{1,0:T(8,128)(2,1)S(1)}, bf16[256,1024]{1,0:T(8,128)(2,1)}, u32[]{:S(2)}, u32[]{:S(2)}) %collective-permute-start.40) | collective-permute-done | bytes 524320 | tf_op jit(solution)/shard_map/cond/branch_1_fun/ppermute | solution.py:788
  171.1 18.0 %ffn_forward.1 = (bf16[512,1024]{1,0:T(8,128)(2,1)}, f32[512,1024]{1,0:T(8,128)}, f32[1,1024]{1,0:T(1,128)}, bf16[512,4096]{1,0:T(8,128)(2,1)}, bf16[512,4096]{1...) custom-call(f32[512,1024]{1,0:T(8,128)S(1)} %convolution_add_fusion.x_ref, f32[1,1024]{1,0:T(1,128)S(1)} %get-tuple-element.1251.gain_ref, ...), custom_call_target="tpu_custom_call" | custom-call | flops 8589934592 | bytes 25165824 | tf_op jit(solution)/shard_map/ffn_forward/pallas_call | solution.py:395
  190.0 18.0 %conditional.25 = (f32[512,1024]{1,0:T(8,128)S(1)}, f32[1,1024]{1,0:T(1,128)}, bf16[512,1024]{1,0:T(8,128)(2,1)}, bf16[512,4096]{1,0:T(8,128)(2,1)}, bf16[512,40...) conditional(s32[]{:T(128)} %convert_element_type.165, () %tuple.198, (f32[512,1024]{1,0:T(8,128)S(1)}, ...), branch_computations={%region_10.11_spmd, %region_11.12_spmd} | conditional | flops 8589934592 | bytes 50331776 | solution.py:795
  190.5 17.5 %ffn_backward.1 = (f32[512,1024]{1,0:T(8,128)S(1)}, f32[1,1024]{1,0:T(1,128)}, bf16[512,1024]{1,0:T(8,128)(2,1)}, bf16[512,4096]{1,0:T(8,128)(2,1)}) custom-call(f32[512,1024]{1,0:T(8,128)S(1)} %get-tuple-element.572.x_ref, f32[1,1024]{1,0:T(1,128)S(1)} %get-tuple-element.573.gain_ref, f32[512,1024]{1,0:T(8,128)} %get-tuple-element.574.up_ref, ...), custom_call_target="tpu_custom_call" | custom-call | flops 8589934592 | bytes 29360128 | tf_op jit(solution)/shard_map/cond/branch_1_fun/ffn_backward/pallas_call | solution.py:452
  239.7 24.9 %conditional.26 = (bf16[512,1024]{1,0:T(8,128)(2,1)}, bf16[512,1024]{1,0:T(8,128)(2,1)}, bf16[512,1024]{1,0:T(8,128)(2,1)}, bf16[512,1024]{1,0:T(8,128)(2,1)}, b...) conditional(s32[]{:T(128)} %convert_element_type.165, ...), branch_computations={%region_16.17_spmd, %region_17.18_spmd} | conditional | flops 8589934592 | bytes 60293492 | solution.py:795
  245.3 9.1 %out_grad.2 = (bf16[2,4,64,1024]{3,2,1,0:T(8,128)(2,1)S(1)}, bf16[2,4,64,1024]{3,2,1,0:T(8,128)(2,1)S(1)}, bf16[2,4,64,1024]{3,2,1,0:T(8,128)(2,1)}, bf16[2,4,64,1024]{3,2,1,0:T(8,128)(2,1)}) custom-call(s32[2]{0:T(128)S(1)} %get-tuple-element.590.place_ref, bf16[512,1024]{1,0:T(8,128)(2,1)} %get-tuple-element.591.up_own, ...), custom_call_target="tpu_custom_call" | custom-call | flops 4294967296 | bytes 16777216 | tf_op jit(solution)/shard_map/cond/branch_1_fun/out_grad/pallas_call | solution.py:912
  254.4 10.2 %column_grads.4 = (bf16[2,4,64,1024]{3,2,1,0:T(8,128)(2,1)}, bf16[2,4,64,1024]{3,2,1,0:T(8,128)(2,1)}, bf16[2,4,64,1024]{3,2,1,0:T(8,128)(2,1)}, bf16[2,4,64,1024]{3,2,1,0:T(8,128)(2,1)}) custom-call(s32[2]{0:T(128)S(1)} %get-tuple-element.590.place_ref, bf16[512,1024]{1,0:T(8,128)(2,1)S(1)} %copy-done.44, bf16[512,1024]{1,0:T(8,128)(2,1)} %get-tuple-element.600.refs_1_, ...), custom_call_target="tpu_custom_call" | custom-call | flops 4294967296 | bytes 16777216 | tf_op jit(solution)/shard_map/cond/branch_1_fun/column_grads/pallas_call | solution.py:1015
  264.6 35.6 %conditional.27 = (bf16[4,3,2,256,128]{4,3,2,1,0:T(8,128)(2,1)}, bf16[4,2,256,128]{3,2,1,0:T(8,128)(2,1)}, bf16[256,1024]{1,0:T(8,128)(2,1)}, bf16[512,1024]{1,0...) conditional(s32[]{:T(128)} %convert_element_type.165, ...), branch_computations={%region_18.19_spmd, %region_19.22_spmd} | conditional | flops 17179869184 | bytes 29884820 | solution.py:795
  267.7 32.4 %conditional = (bf16[4,3,2,256,128]{4,3,2,1,0:T(8,128)(2,1)}, bf16[4,2,256,128]{3,2,1,0:T(8,128)(2,1)}, bf16[256,1024]{1,0:T(8,128)(2,1)}, bf16[512,1024]{1,0:T(8,128)(2,1)}, bf16[512,1024]{1,0:T(8,128)(2,1)}) conditional(s32[]{:T(128)} %convert_element_type.122, () %tuple.108, (s32[2]{0:T(128)S(1)}, bf16[4,3,2,256,128]{4,3,2,1,0:T(8,128)(2,1)}, ...), branch_computations={%region_20.20_spmd, %region_21.21_spmd} | conditional | flops 17179869184 | bytes 21496000 | solution.py:795
  273.8 26.4 %attend_backward.2 = bf16[4,3,2,256,128]{4,3,2,1,0:T(8,128)(2,1)} custom-call(s32[2]{0:T(128)S(1)} %get-tuple-element.607.counts_ref, bf16[4,3,2,256,128]{4,3,2,1,0:T(8,128)(2,1)} %get-tuple-element.608.qkv_ref, f32[2048,128]{1,0:T(8,128)} %get-tuple-element.609.full_ref, f32[2,2048,128]{2,1,0:T(8,128)} %get-tuple-element.610.lse_ref, ...), custom_call_target="tpu_custom_call" | custom-call | flops 17179869184 | bytes 9437184 | tf_op jit(solution)/shard_map/cond/branch_1_fun/cond/branch_1_fun/attend_backward/pallas_call | solution.py:331
  302.3 37.0 %conditional.28 = (bf16[4,3,2,256,128]{4,3,2,1,0:T(8,128)(2,1)}, bf16[4,3,2,256,128]{4,3,2,1,0:T(8,128)(2,1)}, bf16[4,64,1024]{2,1,0:T(8,128)(2,1)}, bf16[4,64,1...) conditional(s32[]{:T(128)} %convert_element_type.165, () %tuple.189, ...), branch_computations={%region_22.23_spmd, %region_23.26_spmd} | conditional | flops 17179869184 | bytes 26738996 | solution.py:795
  306.3 30.7 %conditional.1 = (bf16[4,3,2,256,128]{4,3,2,1,0:T(8,128)(2,1)}, bf16[4,3,2,256,128]{4,3,2,1,0:T(8,128)(2,1)}) conditional(s32[]{:T(128)} %convert_element_type.123, () %tuple.114, (s32[2]{0:T(128)S(1)}, bf16[4,3,2,256,128]{4,3,2,1,0:T(8,128)(2,1)}, f32[2048,128]{1,0:T(8,128)}, f32[2,2048,128]{2,1,0:T(8,128)}, bf16[4,2,256,128]{3,2,1,0:T(8,128)(2,1)}, ...), branch_computations={%region_24.24_spmd, %region_25.25_spmd} | conditional | flops 17179869184 | bytes 14155824 | solution.py:795
  310.7 26.3 %attend_backward.3 = bf16[4,3,2,256,128]{4,3,2,1,0:T(8,128)(2,1)} custom-call(s32[2]{0:T(128)S(1)} %get-tuple-element.633.counts_ref, bf16[4,3,2,256,128]{4,3,2,1,0:T(8,128)(2,1)} %get-tuple-element.634.qkv_ref, f32[2048,128]{1,0:T(8,128)} %get-tuple-element.635.full_ref, f32[2,2048,128]{2,1,0:T(8,128)} %get-tuple-element.636.lse_ref, ...), custom_call_target="tpu_custom_call" | custom-call | flops 17179869184 | bytes 9437184 | tf_op jit(solution)/shard_map/cond/branch_1_fun/cond/branch_1_fun/attend_backward/pallas_call | solution.py:331
  341.6 24.6 %conditional.29 = (bf16[4,3,2,256,128]{4,3,2,1,0:T(8,128)(2,1)}, bf16[2,4,64,1024]{3,2,1,0:T(8,128)(2,1)}, bf16[2,4,64,1024]{3,2,1,0:T(8,128)(2,1)}, bf16[2,4,64...) conditional(s32[]{:T(128)} %convert_element_type.165, ...), branch_computations={%region_26.27_spmd, %region_27.28_spmd} | conditional | flops 4294967296 | bytes 38273240 | solution.py:795
  348.2 13.2 %column_grads.5 = (bf16[2,4,64,1024]{3,2,1,0:T(8,128)(2,1)}, bf16[2,4,64,1024]{3,2,1,0:T(8,128)(2,1)}, bf16[2,4,64,1024]{3,2,1,0:T(8,128)(2,1)}, bf16[2,4,64,1024]{3,2,1,0:T(8,128)(2,1)}) custom-call(s32[2]{0:T(128)S(1)} %get-tuple-element.653.place_ref, bf16[512,1024]{1,0:T(8,128)(2,1)} %get-tuple-element.654.refs_0_, ...), custom_call_target="tpu_custom_call" | custom-call | flops 4294967296 | bytes 16777216 | tf_op jit(solution)/shard_map/cond/branch_1_fun/column_grads/pallas_call | solution.py:1015
  366.3 65.6 %conditional.30 = (bf16[128,1024]{1,0:T(8,128)(2,1)S(1)}, bf16[128,1024]{1,0:T(8,128)(2,1)S(1)}, bf16[2,4,64,1024]{3,2,1,0:T(8,128)(2,1)}, bf16[2,4,64,1024]{3,2...) conditional(s32[]{:T(128)} %convert_element_type.165, ...), branch_computations={%region_28.29_spmd, %region_29.43_spmd} | conditional | flops 15032385536 | bytes 124257496 | solution.py:795
  367.9 26.2 %conditional.5 = (bf16[512,3072]{1,0:T(8,128)(2,1)}, bf16[512,3072]{1,0:T(8,128)(2,1)}, f32[512,1024]{1,0:T(8,128)}, bf16[512,1024]{1,0:T(8,128)(2,1)}, f32[1,10...) conditional(s32[]{:T(128)} %convert_element_type.127, () %tuple.138, ...), branch_computations={%region_31.31_spmd, %region_32.34_spmd} | conditional | flops 3221225472 | bytes 38797596 | solution.py:795
  370.1 18.1 %conditional.2 = (bf16[512,3072]{1,0:T(8,128)(2,1)}, bf16[512,3072]{1,0:T(8,128)(2,1)}, f32[512,1024]{1,0:T(8,128)}, bf16[512,1024]{1,0:T(8,128)(2,1)}, f32[1,1024]{1,0:T(1,128)}) conditional(s32[]{:T(128)} %convert_element_type.124, () %tuple.123, (f32[512,128]{1,0:T(8,128)}, f32[512,128]{1,0:T(8,128)S(1)}, f32[512,1024]{1,0:T(8,128)}, ...), branch_computations={%region_33.32_spmd, %region_34.33_spmd} | conditional | flops 3221225472 | bytes 30408784 | solution.py:795
  370.1 12.0 %projection_backward.1 = (bf16[512,3072]{1,0:T(8,128)(2,1)}, f32[512,1024]{1,0:T(8,128)}, bf16[512,1024]{1,0:T(8,128)(2,1)}, f32[1,1024]{1,0:T(1,128)}) custom-call(f32[512,128]{1,0:T(8,128)} %get-tuple-element.684.cos_ref, f32[512,128]{1,0:T(8,128)S(1)} %get-tuple-element.685.sin_ref, f32[512,1024]{1,0:T(8,128)} %get-tuple-element.686.x_ref, ...), custom_call_target="tpu_custom_call" | custom-call | flops 3221225472 | bytes 17825792 | tf_op jit(solution)/shard_map/cond/branch_1_fun/cond/branch_1_fun/cond/branch_1_fun/projection_backward/pallas_call | solution.py:747
  382.2 6.0 %collective-permute-done.21 = bf16[512,3072]{1,0:T(8,128)(2,1)} collective-permute-done((bf16[512,3072]{1,0:T(8,128)(2,1)}, bf16[512,3072]{1,0:T(8,128)(2,1)}, u32[]{:S(2)}, u32[]{:S(2)}) %collective-permute-start.21) | collective-permute-done | bytes 3145760 | tf_op jit(solution)/shard_map/cond/branch_1_fun/cond/branch_1_fun/cond/branch_1_fun/ppermute | solution.py:788
  388.2 4.8 collective-permute-done.22
  395.8 13.1 %conditional.6 = (bf16[512,1024]{1,0:T(8,128)(2,1)}, bf16[2,4,64,768]{3,2,1,0:T(8,128)(2,1)}, bf16[2,4,64,768]{3,2,1,0:T(8,128)(2,1)}, bf16[2,4,64,768]{3,2,1,0:...) conditional(s32[]{:T(128)} %convert_element_type.127, ...), branch_computations={%region_35.35_spmd, %region_36.38_spmd} | conditional | flops 3221225472 | bytes 20971788 | solution.py:795
  398.0 9.1 %conditional.3 = (bf16[512,1024]{1,0:T(8,128)(2,1)}, bf16[2,4,64,768]{3,2,1,0:T(8,128)(2,1)}, bf16[2,4,64,768]{3,2,1,0:T(8,128)(2,1)}, bf16[2,4,64,768]{3,2,1,0:T(8,128)(2,1)}, bf16[2,4,64,768]{3,2,1,0:T(8,128)(2,1)}) conditional(s32[]{:T(128)} %convert_element_type.125, () %tuple.129, (bf16[512,1024]{1,0:T(8,128)(2,1)}, s32[2]{0:T(128)S(1)}, ...), branch_computations={%region_37.36_spmd, %region_38.37_spmd} | conditional | flops 3221225472 | bytes 16777296 | solution.py:795
  398.0 9.1 %column_grads.6 = (bf16[2,4,64,768]{3,2,1,0:T(8,128)(2,1)}, bf16[2,4,64,768]{3,2,1,0:T(8,128)(2,1)}, bf16[2,4,64,768]{3,2,1,0:T(8,128)(2,1)}, bf16[2,4,64,768]{3,2,1,0:T(8,128)(2,1)}) custom-call(s32[2]{0:T(128)S(1)} %get-tuple-element.713.place_ref, bf16[512,1024]{1,0:T(8,128)(2,1)} %get-tuple-element.714.refs_0_, ...), custom_call_target="tpu_custom_call" | custom-call | flops 3221225472 | bytes 12582912 | tf_op jit(solution)/shard_map/cond/branch_1_fun/cond/branch_1_fun/cond/branch_1_fun/column_grads/pallas_call | solution.py:1015
  408.9 21.9 %conditional.7 = (bf16[512,4096]{1,0:T(8,128)(2,1)}, bf16[2,4,64,1024]{3,2,1,0:T(8,128)(2,1)}, bf16[2,4,64,1024]{3,2,1,0:T(8,128)(2,1)}, bf16[2,4,64,1024]{3,2,1...) conditional(s32[]{:T(128)} %convert_element_type.127, ...), branch_computations={%region_39.39_spmd, %region_40.42_spmd} | conditional | flops 8589934592 | bytes 44040428 | solution.py:795
  410.8 20.0 %conditional.4 = (bf16[512,4096]{1,0:T(8,128)(2,1)}, bf16[2,4,64,1024]{3,2,1,0:T(8,128)(2,1)}, bf16[2,4,64,1024]{3,2,1,0:T(8,128)(2,1)}, bf16[2,4,64,1024]{3,2,1,0:T(8,128)(2,1)}, bf16[2,4,64,1024]{3,2,1,0:T(8,128)(2,1)}) conditional(s32[]{:T(128)} %convert_element_type.126, () %tuple.135, (f32[512,1024]{1,0:T(8,128)}, ...), branch_computations={%region_41.40_spmd, %region_42.41_spmd} | conditional | flops 8589934592 | bytes 37748776 | solution.py:795
  410.8 10.5 %hidden_gradient.1 = (bf16[512,1024]{1,0:T(8,128)(2,1)}, bf16[512,4096]{1,0:T(8,128)(2,1)}) custom-call(f32[512,1024]{1,0:T(8,128)} %get-tuple-element.736.up_ref, bf16[512,4096]{1,0:T(8,128)(2,1)} %get-tuple-element.737.slope_ref, bf16[4096,1024]{1,0:T(8,128)(2,1)} %get-tuple-element.738.wout_ref), custom_call_target="tpu_custom_call" | custom-call | flops 4294967296 | bytes 20971520 | tf_op jit(solution)/shard_map/cond/branch_1_fun/cond/branch_1_fun/cond/branch_1_fun/hidden_gradient/pallas_call | solution.py:495
  421.2 9.5 %out_grad.3 = (bf16[2,4,64,1024]{3,2,1,0:T(8,128)(2,1)}, bf16[2,4,64,1024]{3,2,1,0:T(8,128)(2,1)}, bf16[2,4,64,1024]{3,2,1,0:T(8,128)(2,1)}, bf16[2,4,64,1024]{3,2,1,0:T(8,128)(2,1)}) custom-call(s32[2]{0:T(128)S(1)} %get-tuple-element.740.place_ref, bf16[512,1024]{1,0:T(8,128)(2,1)} %get-tuple-element.741.up_own, ...), custom_call_target="tpu_custom_call" | custom-call | flops 4294967296 | bytes 16777216 | tf_op jit(solution)/shard_map/cond/branch_1_fun/cond/branch_1_fun/cond/branch_1_fun/out_grad/pallas_call | solution.py:912
  434.4 34.8 %conditional.31 = (bf16[128,1024]{1,0:T(8,128)(2,1)}, bf16[2,4,64,1024]{3,2,1,0:T(8,128)(2,1)}, bf16[2,4,64,1024]{3,2,1,0:T(8,128)(2,1)}, bf16[2,4,64,1024]{3,2,...) conditional(s32[]{:T(128)} %convert_element_type.165, ...), branch_computations={%region_43.44_spmd, %region_44.48_spmd} | conditional | flops 8589934592 | bytes 65806852 | solution.py:795
  439.2 29.9 %conditional.8 = (bf16[128,1024]{1,0:T(8,128)(2,1)}, bf16[2,4,64,1024]{3,2,1,0:T(8,128)(2,1)}, bf16[2,4,64,1024]{3,2,1,0:T(8,128)(2,1)}, bf16[2,4,64,1024]{3,2,1...) conditional(s32[]{:T(128)} %convert_element_type.128, ...), branch_computations={%region_45.45_spmd, %region_46.47_spmd} | conditional | flops 8589934592 | bytes 54263952 | solution.py:795
  442.4 11.7 %stream_gradient.1 = (bf16[512,1024]{1,0:T(8,128)(2,1)}, bf16[512,1024]{1,0:T(8,128)(2,1)}, f32[1,1024]{1,0:T(1,128)}) custom-call(bf16[512,1024]{1,0:T(8,128)(2,1)S(1)} %get-tuple-element.822.x_ref, f32[1,1024]{1,0:T(1,128)S(1)} %get-tuple-element.823.gain_ref, f32[512,1024]{1,0:T(8,128)} %get-tuple-element.824.up_ref, ...), custom_call_target="tpu_custom_call" | custom-call | flops 4294967296 | bytes 12582912 | tf_op jit(solution)/shard_map/cond/branch_1_fun/cond/branch_1_fun/stream_gradient/pallas_call | solution.py:540
  454.1 10.5 %column_grads.7 = (bf16[2,4,64,1024]{3,2,1,0:T(8,128)(2,1)}, bf16[2,4,64,1024]{3,2,1,0:T(8,128)(2,1)}, bf16[2,4,64,1024]{3,2,1,0:T(8,128)(2,1)}, bf16[2,4,64,1024]{3,2,1,0:T(8,128)(2,1)}) custom-call(s32[2]{0:T(128)S(1)} %get-tuple-element.814.place_ref, bf16[512,1024]{1,0:T(8,128)(2,1)} %get-tuple-element.815.refs_0_, ...), custom_call_target="tpu_custom_call" | custom-call | flops 4294967296 | bytes 16777216 | tf_op jit(solution)/shard_map/cond/branch_1_fun/cond/branch_1_fun/column_grads/pallas_call | solution.py:1015
  472.9 43.2 %conditional.32 = (bf16[128,768]{1,0:T(8,128)(2,1)}, bf16[256,1024]{1,0:T(8,128)(2,1)}, bf16[2,4,64,1024]{3,2,1,0:T(8,128)(2,1)}, bf16[2,4,64,1024]{3,2,1,0:T(8,...) conditional(s32[]{:T(128)} %convert_element_type.165, () %tuple.208, (pred[]{:T(512)}, ...), branch_computations={%region_48.49_spmd, %region_49.53_spmd} | conditional | flops 1 | bytes 20775276 | solution.py:795
  477.0 39.0 %conditional.9 = (bf16[128,768]{1,0:T(8,128)(2,1)}, bf16[256,1024]{1,0:T(8,128)(2,1)}) conditional(s32[]{:T(128)} %convert_element_type.129, () %tuple.154, (bf16[2,4,64,768]{3,2,1,0:T(8,128)(2,1)}, bf16[2,4,64,768]{3,2,1,0:T(8,128)(2,1)}, bf16[4,64,768]{2,1,0:T(8,128)(2,1)}, bf16[2,4,64,768]{3,2,1,0:T(8,128)(2,1)}, ...), branch_computations={%region_50.50_spmd, %region_51.52_spmd} | conditional | bytes 8192096 | solution.py:795
  480.8 35.3 %collective-permute-done.34 = bf16[256,1024]{1,0:T(8,128)(2,1)} collective-permute-done((bf16[256,1024]{1,0:T(8,128)(2,1)S(1)}, bf16[256,1024]{1,0:T(8,128)(2,1)}, u32[]{:S(2)}, u32[]{:S(2)}) %collective-permute-start.34) | collective-permute-done | bytes 524320 | tf_op jit(solution)/shard_map/cond/branch_1_fun/cond/branch_1_fun/ppermute | solution.py:788
  518.8 59.0 %conditional.33 = (bf16[128,1024]{1,0:T(8,128)(2,1)}, f32[6,1024]{1,0:T(8,128)S(1)}, f32[5,1024]{1,0:T(8,128)S(1)}, bf16[2,256,1024]{2,1,0:T(8,128)(2,1)}, bf16[...) conditional(s32[]{:T(128)} %convert_element_type.165, ...), branch_computations={%region_55.56_spmd, %region_56.64_spmd} | conditional | flops 13521409 | bytes 45901348 | solution.py:795
  524.8 11.1 %collective-permute-done.41.refs_2_ = bf16[4,64,1024]{2,1,0:T(8,128)(2,1)S(1)} collective-permute-done((bf16[4,64,1024]{2,1,0:T(8,128)(2,1)}, bf16[4,64,1024]{2,1,0:T(8,128)(2,1)S(1)}, u32[]{:S(2)}, u32[]{:S(2)}) %collective-permute-start.41) | collective-permute-done | bytes 524320 | tf_op jit(solution)/shard_map/cond/branch_1_fun/ppermute | solution.py:788
  555.0 6.1 %collective-permute-done.46 = f32[11,1024]{1,0:T(8,128)S(1)} collective-permute-done((f32[11,1024]{1,0:T(8,128)S(1)}, f32[11,1024]{1,0:T(8,128)S(1)}, u32[]{:S(2)}, u32[]{:S(2)}) %collective-permute-start.46) | collective-permute-done | bytes 45088 | tf_op jit(solution)/shard_map/cond/branch_1_fun/ppermute | solution.py:788
  565.7 5.6 collective-permute-done.47
  (322 shorter events, 220.0 us)
Async XLA Ops:
  9.6 27.4 %collective-permute-start.39 = (bf16[256,1024]{1,0:T(8,128)(2,1)S(1)}, bf16[256,1024]{1,0:T(8,128)(2,1)}, u32[]{:S(2)}, u32[]{:S(2)}) collective-permute-start(bf16[256,1024]{1,0:T(8,128)(2,1)S(1)} %dynamic-slice_bitcast_fusion), channel_id=1, source_target_pairs={{0,4},{1,5},{2,6},{3,7},{4,0},{5,1},{6,2},{7,3},{8,12},{9,13},{10,... | collective-permute-start | bytes 1572872 | tf_op jit(solution)/shard_map/cond/branch_1_fun/ppermute | solution.py:788
  54.5 24.6 %all-to-all-start.6 = ((bf16[4,3,2,256,128]{4,3,2,1,0:T(8,128)(2,1)}), bf16[4,3,2,256,128]{4,3,2,1,0:T(8,128)(2,1)}, u32[]{:S(2)}, u32[]{:S(2)}) async-start(bf16[4,3,2,256,128]{4,3,2,1,0:T(8,128)(2,1)} %get-tuple-element.1070), calls=%async_computation.11 | async-start | bytes 3145728 | tf_op jit(solution)/shard_map/all_to_all | solution.py:820
  79.1 24.8 %collective-permute-start = (bf16[512,4096]{1,0:T(8,128)(2,1)}, bf16[512,4096]{1,0:T(8,128)(2,1)}, u32[]{:S(2)}, u32[]{:S(2)}) collective-permute-start(bf16[512,4096]{1,0:T(8,128)(2,1)} %get-tuple-element.561), channel_id=1, source_target_pairs={{0,1},{1,0},{2,3},{3,2},{4,5},{5,4},{6,7},{7,6},{8,9},{9,8},{10,11... | collective-permute-start | bytes 12582920 | tf_op jit(solution)/shard_map/cond/branch_1_fun/ppermute | solution.py:788
  79.1 24.8 %all-to-all-start = ((bf16[4,3,2,256,128]{4,3,2,1,0:T(8,128)(2,1)}), bf16[4,3,2,256,128]{4,3,2,1,0:T(8,128)(2,1)}, u32[]{:S(2)}, u32[]{:S(2)}) async-start(bf16[4,3,2,256,128]{4,3,2,1,0:T(8,128)(2,1)} %get-tuple-element.560), calls=%async_computation | async-start | bytes 3145728 | tf_op jit(solution)/shard_map/cond/branch_1_fun/all_to_all | solution.py:820
  83.8 18.8 %collective-permute-start.1 = (bf16[512,1024]{1,0:T(8,128)(2,1)}, bf16[512,1024]{1,0:T(8,128)(2,1)}, u32[]{:S(2)}, u32[]{:S(2)}) collective-permute-start(bf16[512,1024]{1,0:T(8,128)(2,1)} %get-tuple-element.562), channel_id=1, source_target_pairs={{0,1},{1,0},{2,3},{3,2},{4,5},{5,4},{6,7},{7,6},{8,9},{9,8},{10,11... | collective-permute-start | bytes 3145736 | tf_op jit(solution)/shard_map/cond/branch_1_fun/ppermute | solution.py:788
  84.3 18.3 %collective-permute-start.2 = (bf16[512,1024]{1,0:T(8,128)(2,1)}, bf16[512,1024]{1,0:T(8,128)(2,1)}, u32[]{:S(2)}, u32[]{:S(2)}) collective-permute-start(bf16[512,1024]{1,0:T(8,128)(2,1)} %get-tuple-element.563), channel_id=1, source_target_pairs={{0,1},{1,0},{2,3},{3,2},{4,5},{5,4},{6,7},{7,6},{8,9},{9,8},{10,11... | collective-permute-start | bytes 3145736 | tf_op jit(solution)/shard_map/cond/branch_1_fun/ppermute | solution.py:788
  103.9 30.8 %all-to-all-start.5 = ((bf16[4,2,256,128]{3,2,1,0:T(8,128)(2,1)}), bf16[4,2,256,128]{3,2,1,0:T(8,128)(2,1)}, u32[]{:S(2)}, u32[]{:S(2)}) async-start(bf16[4,2,256,128]{3,2,1,0:T(8,128)(2,1)} %get-tuple-element.569), calls=%async_computation.7 | async-start | bytes 1048576 | tf_op jit(solution)/shard_map/cond/branch_1_fun/all_to_all | solution.py:820
  108.1 26.6 %collective-permute-start.40 = (bf16[256,1024]{1,0:T(8,128)(2,1)S(1)}, bf16[256,1024]{1,0:T(8,128)(2,1)}, u32[]{:S(2)}, u32[]{:S(2)}) collective-permute-start(bf16[256,1024]{1,0:T(8,128)(2,1)S(1)} %dynamic-slice_bitcast_fusion.1), channel_id=1, source_target_pairs={{0,4},{1,5},{2,6},{3,7},{4,0},{5,1},{6,2},{7,3},{8,12},{9,13},{10,... | collective-permute-start | bytes 1572872 | tf_op jit(solution)/shard_map/cond/branch_1_fun/ppermute | solution.py:788
  190.0 18.0 %collective-permute-start.3 = (bf16[512,4096]{1,0:T(8,128)(2,1)}, bf16[512,4096]{1,0:T(8,128)(2,1)}, u32[]{:S(2)}, u32[]{:S(2)}) collective-permute-start(bf16[512,4096]{1,0:T(8,128)(2,1)} %get-tuple-element.582), channel_id=1, source_target_pairs={{0,1},{1,0},{2,3},{3,2},{4,5},{5,4},{6,7},{7,6},{8,9},{9,8},{10,11... | collective-permute-start | bytes 12582920 | tf_op jit(solution)/shard_map/cond/branch_1_fun/ppermute | solution.py:788
  190.0 18.0 %collective-permute-start.4 = (bf16[512,1024]{1,0:T(8,128)(2,1)S(1)}, bf16[512,1024]{1,0:T(8,128)(2,1)}, u32[]{:S(2)}, u32[]{:S(2)}) collective-permute-start(bf16[512,1024]{1,0:T(8,128)(2,1)S(1)} %get-tuple-element.583), channel_id=1, source_target_pairs={{0,1},{1,0},{2,3},{3,2},{4,5},{5,4},{6,7},{7,6},{8,9},{9,8},{10,11... | collective-permute-start | bytes 3145736 | tf_op jit(solution)/shard_map/cond/branch_1_fun/ppermute | solution.py:788
  214.8 24.9 %collective-permute-start.53 = (bf16[512,4096]{1,0:T(8,128)(2,1)}, bf16[512,4096]{1,0:T(8,128)(2,1)}, u32[]{:S(2)}, u32[]{:S(2)}) collective-permute-start(bf16[512,4096]{1,0:T(8,128)(2,1)} %get-tuple-element.1094), channel_id=1, source_target_pairs={{0,1},{1,0},{2,3},{3,2},{4,5},{5,4},{6,7},{7,6},{8,9},{9,8},{10,11... | collective-permute-start | bytes 12582920 | tf_op jit(solution)/shard_map/ppermute | solution.py:788
  217.9 21.8 %collective-permute-start.52 = (bf16[512,1024]{1,0:T(8,128)(2,1)}, bf16[512,1024]{1,0:T(8,128)(2,1)}, u32[]{:S(2)}, u32[]{:S(2)}) collective-permute-start(bf16[512,1024]{1,0:T(8,128)(2,1)} %get-tuple-element.1091), channel_id=1, source_target_pairs={{0,1},{1,0},{2,3},{3,2},{4,5},{5,4},{6,7},{7,6},{8,9},{9,8},{10,11... | collective-permute-start | bytes 3145736 | tf_op jit(solution)/shard_map/ppermute | solution.py:788
  239.7 24.8 %collective-permute-start.5 = (bf16[512,1024]{1,0:T(8,128)(2,1)}, bf16[512,1024]{1,0:T(8,128)(2,1)}, u32[]{:S(2)}, u32[]{:S(2)}) collective-permute-start(bf16[512,1024]{1,0:T(8,128)(2,1)} %get-tuple-element.584), channel_id=1, source_target_pairs={{0,1},{1,0},{2,3},{3,2},{4,5},{5,4},{6,7},{7,6},{8,9},{9,8},{10,11... | collective-permute-start | bytes 3145736 | tf_op jit(solution)/shard_map/cond/branch_1_fun/ppermute | solution.py:788
  239.9 24.7 %collective-permute-start.6 = (bf16[512,1024]{1,0:T(8,128)(2,1)}, bf16[512,1024]{1,0:T(8,128)(2,1)}, u32[]{:S(2)}, u32[]{:S(2)}) collective-permute-start(bf16[512,1024]{1,0:T(8,128)(2,1)} %get-tuple-element.585), channel_id=1, source_target_pairs={{0,1},{1,0},{2,3},{3,2},{4,5},{5,4},{6,7},{7,6},{8,9},{9,8},{10,11... | collective-permute-start | bytes 3145736 | tf_op jit(solution)/shard_map/cond/branch_1_fun/ppermute | solution.py:788
  240.3 24.3 %collective-permute-start.7 = (bf16[512,1024]{1,0:T(8,128)(2,1)}, bf16[512,1024]{1,0:T(8,128)(2,1)}, u32[]{:S(2)}, u32[]{:S(2)}) collective-permute-start(bf16[512,1024]{1,0:T(8,128)(2,1)} %get-tuple-element.586), channel_id=1, source_target_pairs={{0,1},{1,0},{2,3},{3,2},{4,5},{5,4},{6,7},{7,6},{8,9},{9,8},{10,11... | collective-permute-start | bytes 3145736 | tf_op jit(solution)/shard_map/cond/branch_1_fun/ppermute | solution.py:788
  240.4 24.2 %collective-permute-start.8 = (bf16[512,1024]{1,0:T(8,128)(2,1)}, bf16[512,1024]{1,0:T(8,128)(2,1)}, u32[]{:S(2)}, u32[]{:S(2)}) collective-permute-start(bf16[512,1024]{1,0:T(8,128)(2,1)} %get-tuple-element.587), channel_id=1, source_target_pairs={{0,1},{1,0},{2,3},{3,2},{4,5},{5,4},{6,7},{7,6},{8,9},{9,8},{10,11... | collective-permute-start | bytes 3145736 | tf_op jit(solution)/shard_map/cond/branch_1_fun/ppermute | solution.py:788
  240.8 23.8 %collective-permute-start.9 = (bf16[512,1024]{1,0:T(8,128)(2,1)}, bf16[512,1024]{1,0:T(8,128)(2,1)}, u32[]{:S(2)}, u32[]{:S(2)}) collective-permute-start(bf16[512,1024]{1,0:T(8,128)(2,1)} %get-tuple-element.588), channel_id=1, source_target_pairs={{0,1},{1,0},{2,3},{3,2},{4,5},{5,4},{6,7},{7,6},{8,9},{9,8},{10,11... | collective-permute-start | bytes 3145736 | tf_op jit(solution)/shard_map/cond/branch_1_fun/ppermute | solution.py:788
  240.9 23.6 %all-to-all-start.1 = ((bf16[4,2,256,128]{3,2,1,0:T(8,128)(2,1)}), bf16[4,2,256,128]{3,2,1,0:T(8,128)(2,1)}, u32[]{:S(2)}, u32[]{:S(2)}) async-start(bf16[4,2,256,128]{3,2,1,0:T(8,128)(2,1)} %get-tuple-element.589), calls=%async_computation.1 | async-start | bytes 1048576 | tf_op jit(solution)/shard_map/cond/branch_1_fun/all_to_all | solution.py:820
  264.6 35.6 %collective-permute-start.13 = (bf16[2,4,64,1024]{3,2,1,0:T(8,128)(2,1)}, bf16[2,4,64,1024]{3,2,1,0:T(8,128)(2,1)}, u32[]{:S(2)}, u32[]{:S(2)}) collective-permute-start(bf16[2,4,64,1024]{3,2,1,0:T(8,128)(2,1)} %get-tuple-element.631), channel_id=1, source_target_pairs={{0,8},{1,9},{2,10},{3,11},{4,12},{5,13},{6,14},{7,15},{8,0},{9,1},... | collective-permute-start | bytes 3145736 | tf_op jit(solution)/shard_map/cond/branch_1_fun/ppermute | solution.py:788
  266.2 34.0 %collective-permute-start.14 = (bf16[2,4,64,1024]{3,2,1,0:T(8,128)(2,1)}, bf16[2,4,64,1024]{3,2,1,0:T(8,128)(2,1)}, u32[]{:S(2)}, u32[]{:S(2)}) collective-permute-start(bf16[2,4,64,1024]{3,2,1,0:T(8,128)(2,1)} %get-tuple-element.632), channel_id=1, source_target_pairs={{0,16},{1,17},{2,18},{3,19},{4,20},{5,21},{6,22},{7,23},{8,24},{9,... | collective-permute-start | bytes 3145736 | tf_op jit(solution)/shard_map/cond/branch_1_fun/ppermute | solution.py:788
  267.7 32.4 %all-to-all-start.2 = ((bf16[4,2,256,128]{3,2,1,0:T(8,128)(2,1)}), bf16[4,2,256,128]{3,2,1,0:T(8,128)(2,1)}, u32[]{:S(2)}, u32[]{:S(2)}) async-start(bf16[4,2,256,128]{3,2,1,0:T(8,128)(2,1)} %get-tuple-element.612), calls=%async_computation.2 | async-start | bytes 1048576 | tf_op jit(solution)/shard_map/cond/branch_1_fun/cond/branch_1_fun/all_to_all | solution.py:820
  271.9 28.3 %collective-permute-start.10 = (bf16[256,1024]{1,0:T(8,128)(2,1)}, bf16[256,1024]{1,0:T(8,128)(2,1)}, u32[]{:S(2)}, u32[]{:S(2)}) collective-permute-start(bf16[256,1024]{1,0:T(8,128)(2,1)} %get-tuple-element.613), channel_id=1, source_target_pairs={{0,4},{1,5},{2,6},{3,7},{4,0},{5,1},{6,2},{7,3},{8,12},{9,13},{10,... | collective-permute-start | bytes 1572872 | tf_op jit(solution)/shard_map/cond/branch_1_fun/cond/branch_1_fun/ppermute | solution.py:788
  273.2 26.9 %collective-permute-start.11 = (bf16[512,1024]{1,0:T(8,128)(2,1)}, bf16[512,1024]{1,0:T(8,128)(2,1)}, u32[]{:S(2)}, u32[]{:S(2)}) collective-permute-start(bf16[512,1024]{1,0:T(8,128)(2,1)} %get-tuple-element.614), channel_id=1, source_target_pairs={{0,1},{1,0},{2,3},{3,2},{4,5},{5,4},{6,7},{7,6},{8,9},{9,8},{10,11... | collective-permute-start | bytes 3145736 | tf_op jit(solution)/shard_map/cond/branch_1_fun/cond/branch_1_fun/ppermute | solution.py:788
  273.3 26.8 %collective-permute-start.12 = (bf16[512,1024]{1,0:T(8,128)(2,1)}, bf16[512,1024]{1,0:T(8,128)(2,1)}, u32[]{:S(2)}, u32[]{:S(2)}) collective-permute-start(bf16[512,1024]{1,0:T(8,128)(2,1)} %get-tuple-element.615), channel_id=1, source_target_pairs={{0,1},{1,0},{2,3},{3,2},{4,5},{5,4},{6,7},{7,6},{8,9},{9,8},{10,11... | collective-permute-start | bytes 3145736 | tf_op jit(solution)/shard_map/cond/branch_1_fun/cond/branch_1_fun/ppermute | solution.py:788
  302.3 37.0 %collective-permute-start.17 = (bf16[2,4,64,1024]{3,2,1,0:T(8,128)(2,1)}, bf16[2,4,64,1024]{3,2,1,0:T(8,128)(2,1)}, u32[]{:S(2)}, u32[]{:S(2)}) collective-permute-start(bf16[2,4,64,1024]{3,2,1,0:T(8,128)(2,1)} %get-tuple-element.650), channel_id=1, source_target_pairs={{0,8},{1,9},{2,10},{3,11},{4,12},{5,13},{6,14},{7,15},{8,0},{9,1},... | collective-permute-start | bytes 3145736 | tf_op jit(solution)/shard_map/cond/branch_1_fun/ppermute | solution.py:788
  302.8 36.5 %collective-permute-start.18 = (bf16[2,4,64,1024]{3,2,1,0:T(8,128)(2,1)}, bf16[2,4,64,1024]{3,2,1,0:T(8,128)(2,1)}, u32[]{:S(2)}, u32[]{:S(2)}) collective-permute-start(bf16[2,4,64,1024]{3,2,1,0:T(8,128)(2,1)} %get-tuple-element.651), channel_id=1, source_target_pairs={{0,16},{1,17},{2,18},{3,19},{4,20},{5,21},{6,22},{7,23},{8,24},{9,... | collective-permute-start | bytes 3145736 | tf_op jit(solution)/shard_map/cond/branch_1_fun/ppermute | solution.py:788
  303.3 35.9 %collective-permute-start.15 = (bf16[4,64,1024]{2,1,0:T(8,128)(2,1)}, bf16[4,64,1024]{2,1,0:T(8,128)(2,1)}, u32[]{:S(2)}, u32[]{:S(2)}) collective-permute-start(bf16[4,64,1024]{2,1,0:T(8,128)(2,1)} %get-tuple-element.648), channel_id=1, source_target_pairs={{0,16},{1,17},{2,18},{3,19},{4,20},{5,21},{6,22},{7,23},{8,24},{9,... | collective-permute-start | bytes 1572872 | tf_op jit(solution)/shard_map/cond/branch_1_fun/ppermute | solution.py:788
  304.8 34.4 %collective-permute-start.16 = (bf16[4,64,1024]{2,1,0:T(8,128)(2,1)}, bf16[4,64,1024]{2,1,0:T(8,128)(2,1)}, u32[]{:S(2)}, u32[]{:S(2)}) collective-permute-start(bf16[4,64,1024]{2,1,0:T(8,128)(2,1)} %get-tuple-element.649), channel_id=1, source_target_pairs={{0,8},{1,9},{2,10},{3,11},{4,12},{5,13},{6,14},{7,15},{8,0},{9,1},... | collective-permute-start | bytes 1572872 | tf_op jit(solution)/shard_map/cond/branch_1_fun/ppermute | solution.py:788
  306.3 30.7 %all-to-all-start.3 = ((bf16[4,3,2,256,128]{4,3,2,1,0:T(8,128)(2,1)}), bf16[4,3,2,256,128]{4,3,2,1,0:T(8,128)(2,1)}, u32[]{:S(2)}, u32[]{:S(2)}) async-start(bf16[4,3,2,256,128]{4,3,2,1,0:T(8,128)(2,1)} %get-tuple-element.638), calls=%async_computation.3 | async-start | bytes 3145728 | tf_op jit(solution)/shard_map/cond/branch_1_fun/cond/branch_1_fun/all_to_all | solution.py:820
  341.6 24.6 %all-to-all-start.4 = ((bf16[4,3,2,256,128]{4,3,2,1,0:T(8,128)(2,1)}), bf16[4,3,2,256,128]{4,3,2,1,0:T(8,128)(2,1)}, u32[]{:S(2)}, u32[]{:S(2)}) async-start(bf16[4,3,2,256,128]{4,3,2,1,0:T(8,128)(2,1)} %get-tuple-element.652), calls=%async_computation.4 | async-start | bytes 3145728 | tf_op jit(solution)/shard_map/cond/branch_1_fun/all_to_all | solution.py:820
  366.3 64.5 %reduce-scatter.6.cloned.1.call-start = ((), (), s32[]{:S(2)}) async-start(), calls=%async_computation.13 | async-start | bytes 2621440 | tf_op jit(solution)/shard_map/cond/branch_1_fun/reduce_scatter | solution.py:1135
  367.9 25.1 %collective-permute-start.22 = (bf16[2,4,64,1024]{3,2,1,0:T(8,128)(2,1)}, bf16[2,4,64,1024]{3,2,1,0:T(8,128)(2,1)}, u32[]{:S(2)}, u32[]{:S(2)}) collective-permute-start(bf16[2,4,64,1024]{3,2,1,0:T(8,128)(2,1)} %get-tuple-element.710), channel_id=1, source_target_pairs={{0,8},{1,9},{2,10},{3,11},{4,12},{5,13},{6,14},{7,15},{8,0},{9,1},... | collective-permute-start | bytes 3145736 | tf_op jit(solution)/shard_map/cond/branch_1_fun/cond/branch_1_fun/ppermute | solution.py:788
  369.4 24.7 %collective-permute-start.23 = (bf16[2,4,64,1024]{3,2,1,0:T(8,128)(2,1)}, bf16[2,4,64,1024]{3,2,1,0:T(8,128)(2,1)}, u32[]{:S(2)}, u32[]{:S(2)}) collective-permute-start(bf16[2,4,64,1024]{3,2,1,0:T(8,128)(2,1)} %get-tuple-element.711), channel_id=1, source_target_pairs={{0,16},{1,17},{2,18},{3,19},{4,20},{5,21},{6,22},{7,23},{8,24},{9,... | collective-permute-start | bytes 3145736 | tf_op jit(solution)/shard_map/cond/branch_1_fun/cond/branch_1_fun/ppermute | solution.py:788
  408.9 21.9 %collective-permute-start.27 = (bf16[2,4,64,768]{3,2,1,0:T(8,128)(2,1)}, bf16[2,4,64,768]{3,2,1,0:T(8,128)(2,1)}, u32[]{:S(2)}, u32[]{:S(2)}) collective-permute-start(bf16[2,4,64,768]{3,2,1,0:T(8,128)(2,1)} %get-tuple-element.762), channel_id=1, source_target_pairs={{0,8},{1,9},{2,10},{3,11},{4,12},{5,13},{6,14},{7,15},{8,0},{9,1},... | collective-permute-start | bytes 2359304 | tf_op jit(solution)/shard_map/cond/branch_1_fun/cond/branch_1_fun/ppermute | solution.py:788
  410.3 20.5 %collective-permute-start.28 = (bf16[2,4,64,768]{3,2,1,0:T(8,128)(2,1)}, bf16[2,4,64,768]{3,2,1,0:T(8,128)(2,1)}, u32[]{:S(2)}, u32[]{:S(2)}) collective-permute-start(bf16[2,4,64,768]{3,2,1,0:T(8,128)(2,1)} %get-tuple-element.763), channel_id=1, source_target_pairs={{0,16},{1,17},{2,18},{3,19},{4,20},{5,21},{6,22},{7,23},{8,24},{9,... | collective-permute-start | bytes 2359304 | tf_op jit(solution)/shard_map/cond/branch_1_fun/cond/branch_1_fun/ppermute | solution.py:788
  434.4 34.8 %collective-permute-start.30 = (bf16[2,4,64,1024]{3,2,1,0:T(8,128)(2,1)}, bf16[2,4,64,1024]{3,2,1,0:T(8,128)(2,1)}, u32[]{:S(2)}, u32[]{:S(2)}) collective-permute-start(bf16[2,4,64,1024]{3,2,1,0:T(8,128)(2,1)} %get-tuple-element.852), channel_id=1, source_target_pairs={{0,8},{1,9},{2,10},{3,11},{4,12},{5,13},{6,14},{7,15},{8,0},{9,1},... | collective-permute-start | bytes 3145736 | tf_op jit(solution)/shard_map/cond/branch_1_fun/ppermute | solution.py:788
  435.7 33.5 %collective-permute-start.31 = (bf16[2,4,64,1024]{3,2,1,0:T(8,128)(2,1)}, bf16[2,4,64,1024]{3,2,1,0:T(8,128)(2,1)}, u32[]{:S(2)}, u32[]{:S(2)}) collective-permute-start(bf16[2,4,64,1024]{3,2,1,0:T(8,128)(2,1)} %get-tuple-element.853), channel_id=1, source_target_pairs={{0,16},{1,17},{2,18},{3,19},{4,20},{5,21},{6,22},{7,23},{8,24},{9,... | collective-permute-start | bytes 3145736 | tf_op jit(solution)/shard_map/cond/branch_1_fun/ppermute | solution.py:788
  436.6 32.6 %collective-permute-start.32 = (bf16[4,64,768]{2,1,0:T(8,128)(2,1)S(1)}, bf16[4,64,768]{2,1,0:T(8,128)(2,1)}, u32[]{:S(2)}, u32[]{:S(2)}) collective-permute-start(bf16[4,64,768]{2,1,0:T(8,128)(2,1)S(1)} %get-tuple-element.854), channel_id=1, source_target_pairs={{0,16},{1,17},{2,18},{3,19},{4,20},{5,21},{6,22},{7,23},{8,24},{9,... | collective-permute-start | bytes 1179656 | tf_op jit(solution)/shard_map/cond/branch_1_fun/ppermute | solution.py:788
  437.7 31.5 %collective-permute-start.33 = (bf16[4,64,768]{2,1,0:T(8,128)(2,1)}, bf16[4,64,768]{2,1,0:T(8,128)(2,1)}, u32[]{:S(2)}, u32[]{:S(2)}) collective-permute-start(bf16[4,64,768]{2,1,0:T(8,128)(2,1)} %get-tuple-element.855), channel_id=1, source_target_pairs={{0,8},{1,9},{2,10},{3,11},{4,12},{5,13},{6,14},{7,15},{8,0},{9,1},... | collective-permute-start | bytes 1179656 | tf_op jit(solution)/shard_map/cond/branch_1_fun/ppermute | solution.py:788
  439.2 29.9 %reduce-scatter.8.cloned.1.call-start = ((), (), s32[]{:S(2)}) async-start(), calls=%async_computation.14 | async-start | bytes 1310720 | tf_op jit(solution)/shard_map/cond/branch_1_fun/cond/branch_1_fun/reduce_scatter | solution.py:1135
  472.9 43.2 %collective-permute-start.35 = (bf16[2,4,64,1024]{3,2,1,0:T(8,128)(2,1)}, bf16[2,4,64,1024]{3,2,1,0:T(8,128)(2,1)}, u32[]{:S(2)}, u32[]{:S(2)}) collective-permute-start(bf16[2,4,64,1024]{3,2,1,0:T(8,128)(2,1)} %get-tuple-element.873), channel_id=1, source_target_pairs={{0,8},{1,9},{2,10},{3,11},{4,12},{5,13},{6,14},{7,15},{8,0},{9,1},... | collective-permute-start | bytes 3145736 | tf_op jit(solution)/shard_map/cond/branch_1_fun/ppermute | solution.py:788
  474.4 41.6 %collective-permute-start.36 = (bf16[2,4,64,1024]{3,2,1,0:T(8,128)(2,1)}, bf16[2,4,64,1024]{3,2,1,0:T(8,128)(2,1)}, u32[]{:S(2)}, u32[]{:S(2)}) collective-permute-start(bf16[2,4,64,1024]{3,2,1,0:T(8,128)(2,1)} %get-tuple-element.874), channel_id=1, source_target_pairs={{0,16},{1,17},{2,18},{3,19},{4,20},{5,21},{6,22},{7,23},{8,24},{9,... | collective-permute-start | bytes 3145736 | tf_op jit(solution)/shard_map/cond/branch_1_fun/ppermute | solution.py:788
  475.9 40.1 %collective-permute-start.37 = (bf16[4,64,1024]{2,1,0:T(8,128)(2,1)S(1)}, bf16[4,64,1024]{2,1,0:T(8,128)(2,1)}, u32[]{:S(2)}, u32[]{:S(2)}) collective-permute-start(bf16[4,64,1024]{2,1,0:T(8,128)(2,1)S(1)} %get-tuple-element.875), channel_id=1, source_target_pairs={{0,16},{1,17},{2,18},{3,19},{4,20},{5,21},{6,22},{7,23},{8,24},{9,... | collective-permute-start | bytes 1572872 | tf_op jit(solution)/shard_map/cond/branch_1_fun/ppermute | solution.py:788
  476.5 39.6 %collective-permute-start.38 = (bf16[4,64,1024]{2,1,0:T(8,128)(2,1)S(1)}, bf16[4,64,1024]{2,1,0:T(8,128)(2,1)}, u32[]{:S(2)}, u32[]{:S(2)}) collective-permute-start(bf16[4,64,1024]{2,1,0:T(8,128)(2,1)S(1)} %get-tuple-element.876), channel_id=1, source_target_pairs={{0,8},{1,9},{2,10},{3,11},{4,12},{5,13},{6,14},{7,15},{8,0},{9,1},... | collective-permute-start | bytes 1572872 | tf_op jit(solution)/shard_map/cond/branch_1_fun/ppermute | solution.py:788
  477.0 39.0 %reduce-scatter.10.cloned.1.call-start = ((), (), s32[]{:S(2)}) async-start(), calls=%async_computation.15 | async-start | bytes 983040 | tf_op jit(solution)/shard_map/cond/branch_1_fun/cond/branch_1_fun/reduce_scatter | solution.py:1135
  479.7 36.4 %collective-permute-start.34 = (bf16[256,1024]{1,0:T(8,128)(2,1)S(1)}, bf16[256,1024]{1,0:T(8,128)(2,1)}, u32[]{:S(2)}, u32[]{:S(2)}) collective-permute-start(bf16[256,1024]{1,0:T(8,128)(2,1)S(1)} %get-tuple-element.862), channel_id=1, source_target_pairs={{0,4},{1,5},{2,6},{3,7},{4,0},{5,1},{6,2},{7,3},{8,12},{9,13},{10,... | collective-permute-start | bytes 1572872 | tf_op jit(solution)/shard_map/cond/branch_1_fun/cond/branch_1_fun/ppermute | solution.py:788
  518.8 52.5 %reduce-scatter.14.cloned.1.call-start = ((), (), s32[]{:S(2)}) async-start(), calls=%async_computation.17 | async-start | bytes 1310720 | tf_op jit(solution)/shard_map/cond/branch_1_fun/reduce_scatter | solution.py:1135
  521.8 56.0 %reduce-scatter.12.cloned.1.call-start = ((), (), s32[]{:S(2)}) async-start(), calls=%async_computation.16 | async-start | bytes 1310720 | tf_op jit(solution)/shard_map/cond/branch_1_fun/reduce_scatter | solution.py:1135
  (65 other events, 606.1 us)
Sparse Core Ops, SparseCore 0:
  369.4 43.5 reduce-scatter.5
  442.6 26.5 reduce-scatter.7
  480.7 29.7 reduce-scatter.9
  521.9 26.4 reduce-scatter.13
  550.5 27.1 reduce-scatter.11

commit v4 on v3

--- a/solution.py
+++ b/solution.py
@@ -1461,23 +1461,19 @@
     attn.second(second_sums(attn)[0])
     one_out = Scatter(*shares_out)
     middle_columns = [w.shape[1] for w in (w_point_out, w_point_in, w_out)]
-    middle_grad, shares, (grad_zero, _, gain_zero) = fenced(
-        always,
-        (one_out, attn),
-        lambda: (
-            along_z(last_sum(middle, columns=middle_columns)),
-            column_grads([ent_one], [(grad_pre, other_core(grad_pre))], ways, where, items),
-            stream_gradient(grad_one, stream, grad_pre, gain[0], w_ffn1_in, BF16),
-        ),
+    def input_part():
+        middle_grad = along_z(last_sum(middle, columns=middle_columns))
+        grad_zero, _, gain_zero = stream_gradient(
+            grad_one, stream, grad_pre, gain[0], w_ffn1_in, BF16
+        )
+        shares = column_grads([ent_one], [(grad_pre, other_core(grad_pre))], ways, where, items)
+        return (middle_grad, shares, parted(grad_zero, side), gain_zero)
+
+    middle_grad, shares, (grad_own, grad_theirs), gain_zero = fenced(
+        always, (one_out, attn), input_part
     )
     one_in = Scatter(*shares)
     one_out.second(second_sums(one_out)[0])
-    grad_own, grad_theirs = parted(grad_zero, side)
-    attn_grad, grad_other = fenced(
-        always, (one_in, one_out), lambda: (along_z(last_sum(attn)), across(grad_theirs))
-    )
-    one_in.second(second_sums(one_in)[0])
-
     hidden = w_ffn1_in.shape[1]
 
     def tap_sums_here():
@@ -1489,9 +1485,18 @@
         return rows_of
 
     def last_part():
-        out_grads = along_z(last_sum(one_out))
-        scatter = copy.copy(one_in)
-        moved(scatter)
+        grad_other = across(grad_theirs)
+        attn_grad = along_z(last_sum(attn))
+        out, scatter = copy.copy(one_out), copy.copy(one_in)
+        fenced(always, (out,), lambda: ())
+        out_grads = along_z(last_sum(out))
+        fenced(always, (scatter,), lambda: ())
+        scatter.second(second_sums(scatter)[0])
+        fenced(always, (scatter,), lambda: ())
+        last, grad_other = branched(
+            always,
+            lambda: (last_sum(scatter), grad_other),
+        )
         small = sum_everywhere(
             jnp.concatenate(
                 [gain_zero, gain_one, gain_two, gain_three, gain_four, gain_five]
@@ -1514,7 +1519,7 @@
             unfolded(two_grads[0], hidden // ways),
             unfolded(out_grads[0], hidden // ways),
         )
-        return (along_z(last_sum(scatter)), small[:6], small[6:], ready)
+        return (along_z(last), small[:6], small[6:], ready)
 
     one_in_grad, gain_sums, tap_sums, ready = fenced(always, (), last_part)
     out, grad_in, attn_full, middle_parts, two_in_full, two_out_full, one_out_full = ready

time: 596 us -> 591 us (level)
    reduce_scatter x5, waiting for transfers between devices: 9.11 us -> 1.72 us  [along_z(): lax.psum_scatter(value, 'heads', scatter_dimension=0, tiled=False, axis_i...]
  transfers between devices with their start and end apart: 67 -> 67, of which waited for: 23 -> 26; matrix products, arithmetic and copies ran while one was open for 7% -> 7% of each run, Pallas kernels for 41% -> 41%
where the time goes in v4:
time: 591 us; the launch traced here: 582 us
  Pallas kernels  289 us (49%)
  waiting for transfers between devices  118 us (20%)
  starting transfers between devices  78.2 us (13%)
  other arithmetic  38.9 us (7%)
  matrix products  21.3 us (4%)
  local copies, waits for them, and re-layouts  18.8 us (3%)
  between operations  17.5 us (3%)
    ppermute x50, waiting for transfers between devices, swap(): return lax.ppermute(value, EVERY, flipped(axis_bit, count))  93.4 us
    pallas_call x2, Pallas kernels, attend_backward(): pl.pallas_call(functools.partial(attn_bwd_kernel, heads, size, group), gr...  52.6 us
    pallas_call x4, Pallas kernels, column_grads(): pl.pallas_call(functools.partial(column_grad_kernel, heads, items, split)...  42.8 us
    ppermute x50, starting transfers between devices, swap(): return lax.ppermute(value, EVERY, flipped(axis_bit, count))  42.2 us
    pallas_call x2, Pallas kernels, attend_forward(): pl.pallas_call(functools.partial(attn_fwd_kernel, heads, size, group), gr...  36.4 us
    pallas_call x2, Pallas kernels, front(): pl.pallas_call(functools.partial(front_kernel, size, ffn_steps, pieces),...  34.4 us
    all_to_all x8, starting transfers between devices, exchange(): lax.all_to_all(value, 'heads', split_axis=0, concat_axis=0, tiled=True, a...  34.1 us
    dot_general x7, matrix products, dot(): return lax.dot_general(left, right, dims, preferred_element_type=F32)  21.3 us
  transfers between devices with their start and end apart: 67, of which 26 were waited for; matrix products, arithmetic and copies ran while one was open for 7% of the time, Pallas kernels for 41%

profile of v4, /device:TPU:0, one launch (start us, length us, event | category | flops | bytes accessed | tf_op | source)
XLA Modules:
  0.0 582.2 jit_solution(3115209373526330650)
XLA Ops:
  8.4 28.6 %conditional.24 = (f32[512,1024]{1,0:T(8,128)}, bf16[512,4096]{1,0:T(8,128)(2,1)}, bf16[512,4096]{1,0:T(8,128)(2,1)}, bf16[512,1024]{1,0:T(8,128)(2,1)}, bf16[51...) conditional(s32[]{:T(128)} %convert_element_type.170, ...), branch_computations={%region_0.1_spmd, %region_1.2_spmd} | conditional | flops 5905580032 | bytes 34603160 | solution.py:795
  13.7 16.9 %front.2 = (f32[512,1024]{1,0:T(8,128)}, bf16[512,4096]{1,0:T(8,128)(2,1)}, bf16[512,4096]{1,0:T(8,128)(2,1)}, bf16[512,1024]{1,0:T(8,128)(2,1)}, bf16[512,1024]...) custom-call(s32[1]{0:T(128)} %bitcast.row_ref, ...), custom_call_target="tpu_custom_call" | custom-call | flops 5905580032 | bytes 31457280 | tf_op jit(solution)/shard_map/cond/branch_1_fun/front/pallas_call | solution.py:688
  30.6 6.4 %collective-permute-done.35 = bf16[256,1024]{1,0:T(8,128)(2,1)} collective-permute-done((bf16[256,1024]{1,0:T(8,128)(2,1)S(1)}, bf16[256,1024]{1,0:T(8,128)(2,1)}, u32[]{:S(2)}, u32[]{:S(2)}) %collective-permute-start.35) | collective-permute-done | bytes 524320 | tf_op jit(solution)/shard_map/cond/branch_1_fun/ppermute | solution.py:788
  37.0 17.5 %front.3 = (f32[512,1024]{1,0:T(8,128)}, bf16[512,4096]{1,0:T(8,128)(2,1)}, bf16[512,4096]{1,0:T(8,128)(2,1)}, bf16[512,1024]{1,0:T(8,128)(2,1)}, bf16[512,1024]...) custom-call(s32[1]{0:T(128)} %bitcast.19.row_ref, ...), custom_call_target="tpu_custom_call", output_to_operand_aliasing={{0}: (10, {}), {1}: (11, {}), {2}: (12, {}), {3}: (13, {}),... | custom-call | flops 5905580032 | bytes 31457280 | tf_op jit(solution)/shard_map/front/pallas_call | solution.py:688
  66.7 12.5 %all-to-all-done.6 = bf16[4,3,2,256,128]{4,3,2,1,0:T(8,128)(2,1)} async-done(((bf16[4,3,2,256,128]{4,3,2,1,0:T(8,128)(2,1)}), bf16[4,3,2,256,128]{4,3,2,1,0:T(8,128)(2,1)}, u32[]{:S(2)}, u32[]{:S(2)}) %all-to-all-start.6) | async-done | bytes 1572896 | tf_op jit(solution)/shard_map/all_to_all | solution.py:820
  79.1 24.8 %conditional.25 = (bf16[4,2,256,128]{3,2,1,0:T(8,128)(2,1)}, f32[2048,128]{1,0:T(8,128)}, f32[2,2048,128]{2,1,0:T(8,128)}, bf16[4,3,2,256,128]{4,3,2,1,0:T(8,128...) conditional(s32[]{:T(128)} %convert_element_type.170, () %tuple.203, ...), branch_computations={%region_2.3_spmd, %region_3.4_spmd} | conditional | flops 8589934592 | bytes 36176080 | solution.py:795
  84.4 18.2 %attend_forward.2 = (bf16[4,2,256,128]{3,2,1,0:T(8,128)(2,1)}, f32[2048,128]{1,0:T(8,128)}, f32[2,2048,128]{2,1,0:T(8,128)}) custom-call(s32[2]{0:T(128)S(1)} %get-tuple-element.543.counts_ref, bf16[4,3,2,256,128]{4,3,2,1,0:T(8,128)(2,1)} %get-tuple-element.544.qkv_ref), custom_call_target="tpu_custom_call" | custom-call | flops 8589934592 | bytes 6291456 | tf_op jit(solution)/shard_map/cond/branch_1_fun/attend_forward/pallas_call | solution.py:221
  104.0 30.8 %conditional.26 = (bf16[4,2,256,128]{3,2,1,0:T(8,128)(2,1)}, f32[2048,128]{1,0:T(8,128)}, f32[2,2048,128]{2,1,0:T(8,128)}, bf16[4,2,256,128]{3,2,1,0:T(8,128)(2,1)}, bf16[256,1024]{1,0:T(8,128)(2,1)}) conditional(s32[]{:T(128)} %convert_element_type.170, () %tuple.207, (s32[2]{0:T(128)S(1)}, bf16[4,3,2,256,128]{4,3,2,1,0:T(8,128)(2,1)}, ...), branch_computations={%region_4.5_spmd, %region_5.6_spmd} | conditional | flops 8589934592 | bytes 11010210 | solution.py:795
  110.2 18.2 %attend_forward.3 = (bf16[4,2,256,128]{3,2,1,0:T(8,128)(2,1)}, f32[2048,128]{1,0:T(8,128)}, f32[2,2048,128]{2,1,0:T(8,128)}) custom-call(s32[2]{0:T(128)S(1)} %get-tuple-element.552.counts_ref, bf16[4,3,2,256,128]{4,3,2,1,0:T(8,128)(2,1)} %get-tuple-element.553.qkv_ref), custom_call_target="tpu_custom_call" | custom-call | flops 8589934592 | bytes 6291456 | tf_op jit(solution)/shard_map/cond/branch_1_fun/attend_forward/pallas_call | solution.py:221
  128.3 6.5 %collective-permute-done.36 = bf16[256,1024]{1,0:T(8,128)(2,1)} collective-permute-done((bf16[256,1024]{1,0:T(8,128)(2,1)S(1)}, bf16[256,1024]{1,0:T(8,128)(2,1)}, u32[]{:S(2)}, u32[]{:S(2)}) %collective-permute-start.36) | collective-permute-done | bytes 524320 | tf_op jit(solution)/shard_map/cond/branch_1_fun/ppermute | solution.py:788
  171.1 18.0 %ffn_forward.1 = (bf16[512,1024]{1,0:T(8,128)(2,1)}, f32[512,1024]{1,0:T(8,128)}, f32[1,1024]{1,0:T(1,128)}, bf16[512,4096]{1,0:T(8,128)(2,1)}, bf16[512,4096]{1...) custom-call(f32[512,1024]{1,0:T(8,128)S(1)} %convolution_add_fusion.x_ref, f32[1,1024]{1,0:T(1,128)S(1)} %get-tuple-element.1208.gain_ref, ...), custom_call_target="tpu_custom_call" | custom-call | flops 8589934592 | bytes 25165824 | tf_op jit(solution)/shard_map/ffn_forward/pallas_call | solution.py:395
  190.1 18.0 %conditional.27 = (f32[512,1024]{1,0:T(8,128)S(1)}, f32[1,1024]{1,0:T(1,128)}, bf16[512,1024]{1,0:T(8,128)(2,1)}, bf16[512,4096]{1,0:T(8,128)(2,1)}, bf16[512,40...) conditional(s32[]{:T(128)} %convert_element_type.170, () %tuple.211, (f32[512,1024]{1,0:T(8,128)S(1)}, ...), branch_computations={%region_10.11_spmd, %region_11.12_spmd} | conditional | flops 8589934592 | bytes 50331776 | solution.py:795
  190.6 17.4 %ffn_backward.1 = (f32[512,1024]{1,0:T(8,128)S(1)}, f32[1,1024]{1,0:T(1,128)}, bf16[512,1024]{1,0:T(8,128)(2,1)}, bf16[512,4096]{1,0:T(8,128)(2,1)}) custom-call(f32[512,1024]{1,0:T(8,128)S(1)} %get-tuple-element.560.x_ref, f32[1,1024]{1,0:T(1,128)S(1)} %get-tuple-element.561.gain_ref, f32[512,1024]{1,0:T(8,128)} %get-tuple-element.562.up_ref, ...), custom_call_target="tpu_custom_call" | custom-call | flops 8589934592 | bytes 29360128 | tf_op jit(solution)/shard_map/cond/branch_1_fun/ffn_backward/pallas_call | solution.py:452
  239.6 25.0 %conditional.28 = (bf16[512,1024]{1,0:T(8,128)(2,1)}, bf16[512,1024]{1,0:T(8,128)(2,1)}, bf16[512,1024]{1,0:T(8,128)(2,1)}, bf16[512,1024]{1,0:T(8,128)(2,1)}, b...) conditional(s32[]{:T(128)} %convert_element_type.170, ...), branch_computations={%region_16.17_spmd, %region_17.18_spmd} | conditional | flops 8589934592 | bytes 60293492 | solution.py:795
  245.2 9.2 %out_grad.2 = (bf16[2,4,64,1024]{3,2,1,0:T(8,128)(2,1)S(1)}, bf16[2,4,64,1024]{3,2,1,0:T(8,128)(2,1)S(1)}, bf16[2,4,64,1024]{3,2,1,0:T(8,128)(2,1)}, bf16[2,4,64,1024]{3,2,1,0:T(8,128)(2,1)}) custom-call(s32[2]{0:T(128)S(1)} %get-tuple-element.578.place_ref, bf16[512,1024]{1,0:T(8,128)(2,1)} %get-tuple-element.579.up_own, ...), custom_call_target="tpu_custom_call" | custom-call | flops 4294967296 | bytes 16777216 | tf_op jit(solution)/shard_map/cond/branch_1_fun/out_grad/pallas_call | solution.py:912
  254.4 10.2 %column_grads.4 = (bf16[2,4,64,1024]{3,2,1,0:T(8,128)(2,1)}, bf16[2,4,64,1024]{3,2,1,0:T(8,128)(2,1)}, bf16[2,4,64,1024]{3,2,1,0:T(8,128)(2,1)}, bf16[2,4,64,1024]{3,2,1,0:T(8,128)(2,1)}) custom-call(s32[2]{0:T(128)S(1)} %get-tuple-element.578.place_ref, bf16[512,1024]{1,0:T(8,128)(2,1)S(1)} %copy-done.43, bf16[512,1024]{1,0:T(8,128)(2,1)} %get-tuple-element.588.refs_1_, ...), custom_call_target="tpu_custom_call" | custom-call | flops 4294967296 | bytes 16777216 | tf_op jit(solution)/shard_map/cond/branch_1_fun/column_grads/pallas_call | solution.py:1015
  264.6 35.4 %conditional.29 = (bf16[4,3,2,256,128]{4,3,2,1,0:T(8,128)(2,1)}, bf16[4,2,256,128]{3,2,1,0:T(8,128)(2,1)}, bf16[256,1024]{1,0:T(8,128)(2,1)}, bf16[512,1024]{1,0...) conditional(s32[]{:T(128)} %convert_element_type.170, ...), branch_computations={%region_18.19_spmd, %region_19.22_spmd} | conditional | flops 17179869184 | bytes 29884820 | solution.py:795
  267.7 32.2 %conditional = (bf16[4,3,2,256,128]{4,3,2,1,0:T(8,128)(2,1)}, bf16[4,2,256,128]{3,2,1,0:T(8,128)(2,1)}, bf16[256,1024]{1,0:T(8,128)(2,1)}, bf16[512,1024]{1,0:T(8,128)(2,1)}, bf16[512,1024]{1,0:T(8,128)(2,1)}) conditional(s32[]{:T(128)} %convert_element_type.126, () %tuple.115, (s32[2]{0:T(128)S(1)}, bf16[4,3,2,256,128]{4,3,2,1,0:T(8,128)(2,1)}, ...), branch_computations={%region_20.20_spmd, %region_21.21_spmd} | conditional | flops 17179869184 | bytes 21496000 | solution.py:795
  273.7 26.3 %attend_backward.2 = bf16[4,3,2,256,128]{4,3,2,1,0:T(8,128)(2,1)} custom-call(s32[2]{0:T(128)S(1)} %get-tuple-element.595.counts_ref, bf16[4,3,2,256,128]{4,3,2,1,0:T(8,128)(2,1)} %get-tuple-element.596.qkv_ref, f32[2048,128]{1,0:T(8,128)} %get-tuple-element.597.full_ref, f32[2,2048,128]{2,1,0:T(8,128)} %get-tuple-element.598.lse_ref, ...), custom_call_target="tpu_custom_call" | custom-call | flops 17179869184 | bytes 9437184 | tf_op jit(solution)/shard_map/cond/branch_1_fun/cond/branch_1_fun/attend_backward/pallas_call | solution.py:331
  302.1 37.0 %conditional.30 = (bf16[4,3,2,256,128]{4,3,2,1,0:T(8,128)(2,1)}, bf16[4,3,2,256,128]{4,3,2,1,0:T(8,128)(2,1)}, bf16[4,64,1024]{2,1,0:T(8,128)(2,1)}, bf16[4,64,1...) conditional(s32[]{:T(128)} %convert_element_type.170, () %tuple.202, ...), branch_computations={%region_22.23_spmd, %region_23.26_spmd} | conditional | flops 17179869184 | bytes 26738996 | solution.py:795
  306.1 30.7 %conditional.1 = (bf16[4,3,2,256,128]{4,3,2,1,0:T(8,128)(2,1)}, bf16[4,3,2,256,128]{4,3,2,1,0:T(8,128)(2,1)}) conditional(s32[]{:T(128)} %convert_element_type.127, () %tuple.121, (s32[2]{0:T(128)S(1)}, bf16[4,3,2,256,128]{4,3,2,1,0:T(8,128)(2,1)}, f32[2048,128]{1,0:T(8,128)}, f32[2,2048,128]{2,1,0:T(8,128)}, bf16[4,2,256,128]{3,2,1,0:T(8,128)(2,1)}, ...), branch_computations={%region_24.24_spmd, %region_25.25_spmd} | conditional | flops 17179869184 | bytes 14155824 | solution.py:795
  310.5 26.4 %attend_backward.3 = bf16[4,3,2,256,128]{4,3,2,1,0:T(8,128)(2,1)} custom-call(s32[2]{0:T(128)S(1)} %get-tuple-element.621.counts_ref, bf16[4,3,2,256,128]{4,3,2,1,0:T(8,128)(2,1)} %get-tuple-element.622.qkv_ref, f32[2048,128]{1,0:T(8,128)} %get-tuple-element.623.full_ref, f32[2,2048,128]{2,1,0:T(8,128)} %get-tuple-element.624.lse_ref, ...), custom_call_target="tpu_custom_call" | custom-call | flops 17179869184 | bytes 9437184 | tf_op jit(solution)/shard_map/cond/branch_1_fun/cond/branch_1_fun/attend_backward/pallas_call | solution.py:331
  341.4 24.6 %conditional.31 = (bf16[4,3,2,256,128]{4,3,2,1,0:T(8,128)(2,1)}, bf16[2,4,64,1024]{3,2,1,0:T(8,128)(2,1)}, bf16[2,4,64,1024]{3,2,1,0:T(8,128)(2,1)}, bf16[2,4,64...) conditional(s32[]{:T(128)} %convert_element_type.170, ...), branch_computations={%region_26.27_spmd, %region_27.28_spmd} | conditional | flops 4294967296 | bytes 38273240 | solution.py:795
  348.0 13.1 %column_grads.5 = (bf16[2,4,64,1024]{3,2,1,0:T(8,128)(2,1)}, bf16[2,4,64,1024]{3,2,1,0:T(8,128)(2,1)}, bf16[2,4,64,1024]{3,2,1,0:T(8,128)(2,1)}, bf16[2,4,64,1024]{3,2,1,0:T(8,128)(2,1)}) custom-call(s32[2]{0:T(128)S(1)} %get-tuple-element.641.place_ref, bf16[512,1024]{1,0:T(8,128)(2,1)} %get-tuple-element.642.refs_0_, ...), custom_call_target="tpu_custom_call" | custom-call | flops 4294967296 | bytes 16777216 | tf_op jit(solution)/shard_map/cond/branch_1_fun/column_grads/pallas_call | solution.py:1015
  366.1 65.5 %conditional.32 = (bf16[128,1024]{1,0:T(8,128)(2,1)S(1)}, bf16[128,1024]{1,0:T(8,128)(2,1)S(1)}, bf16[2,4,64,1024]{3,2,1,0:T(8,128)(2,1)}, bf16[2,4,64,1024]{3,2...) conditional(s32[]{:T(128)} %convert_element_type.170, ...), branch_computations={%region_28.29_spmd, %region_29.43_spmd} | conditional | flops 15032385536 | bytes 124257496 | solution.py:795
  367.7 26.2 %conditional.5 = (bf16[512,3072]{1,0:T(8,128)(2,1)}, bf16[512,3072]{1,0:T(8,128)(2,1)}, f32[512,1024]{1,0:T(8,128)}, bf16[512,1024]{1,0:T(8,128)(2,1)}, f32[1,10...) conditional(s32[]{:T(128)} %convert_element_type.131, () %tuple.145, ...), branch_computations={%region_31.31_spmd, %region_32.34_spmd} | conditional | flops 3221225472 | bytes 38797596 | solution.py:795
  370.0 18.0 %conditional.2 = (bf16[512,3072]{1,0:T(8,128)(2,1)}, bf16[512,3072]{1,0:T(8,128)(2,1)}, f32[512,1024]{1,0:T(8,128)}, bf16[512,1024]{1,0:T(8,128)(2,1)}, f32[1,1024]{1,0:T(1,128)}) conditional(s32[]{:T(128)} %convert_element_type.128, () %tuple.130, (f32[512,128]{1,0:T(8,128)}, f32[512,128]{1,0:T(8,128)S(1)}, f32[512,1024]{1,0:T(8,128)}, ...), branch_computations={%region_33.32_spmd, %region_34.33_spmd} | conditional | flops 3221225472 | bytes 30408784 | solution.py:795
  370.0 11.9 %projection_backward.1 = (bf16[512,3072]{1,0:T(8,128)(2,1)}, f32[512,1024]{1,0:T(8,128)}, bf16[512,1024]{1,0:T(8,128)(2,1)}, f32[1,1024]{1,0:T(1,128)}) custom-call(f32[512,128]{1,0:T(8,128)} %get-tuple-element.672.cos_ref, f32[512,128]{1,0:T(8,128)S(1)} %get-tuple-element.673.sin_ref, f32[512,1024]{1,0:T(8,128)} %get-tuple-element.674.x_ref, ...), custom_call_target="tpu_custom_call" | custom-call | flops 3221225472 | bytes 17825792 | tf_op jit(solution)/shard_map/cond/branch_1_fun/cond/branch_1_fun/cond/branch_1_fun/projection_backward/pallas_call | solution.py:747
  382.0 6.0 %collective-permute-done.21 = bf16[512,3072]{1,0:T(8,128)(2,1)} collective-permute-done((bf16[512,3072]{1,0:T(8,128)(2,1)}, bf16[512,3072]{1,0:T(8,128)(2,1)}, u32[]{:S(2)}, u32[]{:S(2)}) %collective-permute-start.21) | collective-permute-done | bytes 3145760 | tf_op jit(solution)/shard_map/cond/branch_1_fun/cond/branch_1_fun/cond/branch_1_fun/ppermute | solution.py:788
  395.6 13.0 %conditional.6 = (bf16[512,1024]{1,0:T(8,128)(2,1)}, bf16[2,4,64,768]{3,2,1,0:T(8,128)(2,1)}, bf16[2,4,64,768]{3,2,1,0:T(8,128)(2,1)}, bf16[2,4,64,768]{3,2,1,0:...) conditional(s32[]{:T(128)} %convert_element_type.131, ...), branch_computations={%region_35.35_spmd, %region_36.38_spmd} | conditional | flops 3221225472 | bytes 20971788 | solution.py:795
  397.8 9.0 %conditional.3 = (bf16[512,1024]{1,0:T(8,128)(2,1)}, bf16[2,4,64,768]{3,2,1,0:T(8,128)(2,1)}, bf16[2,4,64,768]{3,2,1,0:T(8,128)(2,1)}, bf16[2,4,64,768]{3,2,1,0:T(8,128)(2,1)}, bf16[2,4,64,768]{3,2,1,0:T(8,128)(2,1)}) conditional(s32[]{:T(128)} %convert_element_type.129, () %tuple.136, (bf16[512,1024]{1,0:T(8,128)(2,1)}, s32[2]{0:T(128)S(1)}, ...), branch_computations={%region_37.36_spmd, %region_38.37_spmd} | conditional | flops 3221225472 | bytes 16777296 | solution.py:795
  397.8 9.0 %column_grads.6 = (bf16[2,4,64,768]{3,2,1,0:T(8,128)(2,1)}, bf16[2,4,64,768]{3,2,1,0:T(8,128)(2,1)}, bf16[2,4,64,768]{3,2,1,0:T(8,128)(2,1)}, bf16[2,4,64,768]{3,2,1,0:T(8,128)(2,1)}) custom-call(s32[2]{0:T(128)S(1)} %get-tuple-element.701.place_ref, bf16[512,1024]{1,0:T(8,128)(2,1)} %get-tuple-element.702.refs_0_, ...), custom_call_target="tpu_custom_call" | custom-call | flops 3221225472 | bytes 12582912 | tf_op jit(solution)/shard_map/cond/branch_1_fun/cond/branch_1_fun/cond/branch_1_fun/column_grads/pallas_call | solution.py:1015
  408.7 21.8 %conditional.7 = (bf16[512,4096]{1,0:T(8,128)(2,1)}, bf16[2,4,64,1024]{3,2,1,0:T(8,128)(2,1)}, bf16[2,4,64,1024]{3,2,1,0:T(8,128)(2,1)}, bf16[2,4,64,1024]{3,2,1...) conditional(s32[]{:T(128)} %convert_element_type.131, ...), branch_computations={%region_39.39_spmd, %region_40.42_spmd} | conditional | flops 8589934592 | bytes 44040428 | solution.py:795
  410.5 20.0 %conditional.4 = (bf16[512,4096]{1,0:T(8,128)(2,1)}, bf16[2,4,64,1024]{3,2,1,0:T(8,128)(2,1)}, bf16[2,4,64,1024]{3,2,1,0:T(8,128)(2,1)}, bf16[2,4,64,1024]{3,2,1,0:T(8,128)(2,1)}, bf16[2,4,64,1024]{3,2,1,0:T(8,128)(2,1)}) conditional(s32[]{:T(128)} %convert_element_type.130, () %tuple.142, (f32[512,1024]{1,0:T(8,128)}, ...), branch_computations={%region_41.40_spmd, %region_42.41_spmd} | conditional | flops 8589934592 | bytes 37748776 | solution.py:795
  410.5 10.5 %hidden_gradient.1 = (bf16[512,1024]{1,0:T(8,128)(2,1)}, bf16[512,4096]{1,0:T(8,128)(2,1)}) custom-call(f32[512,1024]{1,0:T(8,128)} %get-tuple-element.724.up_ref, bf16[512,4096]{1,0:T(8,128)(2,1)} %get-tuple-element.725.slope_ref, bf16[4096,1024]{1,0:T(8,128)(2,1)} %get-tuple-element.726.wout_ref), custom_call_target="tpu_custom_call" | custom-call | flops 4294967296 | bytes 20971520 | tf_op jit(solution)/shard_map/cond/branch_1_fun/cond/branch_1_fun/cond/branch_1_fun/hidden_gradient/pallas_call | solution.py:495
  420.9 9.5 %out_grad.3 = (bf16[2,4,64,1024]{3,2,1,0:T(8,128)(2,1)}, bf16[2,4,64,1024]{3,2,1,0:T(8,128)(2,1)}, bf16[2,4,64,1024]{3,2,1,0:T(8,128)(2,1)}, bf16[2,4,64,1024]{3,2,1,0:T(8,128)(2,1)}) custom-call(s32[2]{0:T(128)S(1)} %get-tuple-element.728.place_ref, bf16[512,1024]{1,0:T(8,128)(2,1)} %get-tuple-element.729.up_own, ...), custom_call_target="tpu_custom_call" | custom-call | flops 4294967296 | bytes 16777216 | tf_op jit(solution)/shard_map/cond/branch_1_fun/cond/branch_1_fun/cond/branch_1_fun/out_grad/pallas_call | solution.py:912
  434.1 33.4 %conditional.33 = (bf16[128,1024]{1,0:T(8,128)(2,1)}, bf16[2,4,64,1024]{3,2,1,0:T(8,128)(2,1)}, bf16[2,4,64,1024]{3,2,1,0:T(8,128)(2,1)}, bf16[2,4,64,1024]{3,2,...) conditional(s32[]{:T(128)} %convert_element_type.170, ...), branch_computations={%region_43.44_spmd, %region_44.48_spmd} | conditional | flops 8590458880 | bytes 67895824 | solution.py:795
  438.2 29.3 %conditional.8 = (bf16[128,1024]{1,0:T(8,128)(2,1)}, bf16[2,4,64,1024]{3,2,1,0:T(8,128)(2,1)}, bf16[2,4,64,1024]{3,2,1,0:T(8,128)(2,1)}, bf16[2,4,64,1024]{3,2,1...) conditional(s32[]{:T(128)} %convert_element_type.132, ...), branch_computations={%region_45.45_spmd, %region_46.47_spmd} | conditional | flops 8590458880 | bytes 56361112 | solution.py:795
  441.4 11.7 %stream_gradient.1 = (bf16[512,1024]{1,0:T(8,128)(2,1)}, bf16[512,1024]{1,0:T(8,128)(2,1)}, f32[1,1024]{1,0:T(1,128)}) custom-call(bf16[512,1024]{1,0:T(8,128)(2,1)S(1)} %get-tuple-element.811.x_ref, f32[1,1024]{1,0:T(1,128)S(1)} %get-tuple-element.812.gain_ref, f32[512,1024]{1,0:T(8,128)} %get-tuple-element.813.up_ref, ...), custom_call_target="tpu_custom_call" | custom-call | flops 4294967296 | bytes 12582912 | tf_op jit(solution)/shard_map/cond/branch_1_fun/cond/branch_1_fun/stream_gradient/pallas_call | solution.py:540
  455.3 10.5 %column_grads.7 = (bf16[2,4,64,1024]{3,2,1,0:T(8,128)(2,1)}, bf16[2,4,64,1024]{3,2,1,0:T(8,128)(2,1)}, bf16[2,4,64,1024]{3,2,1,0:T(8,128)(2,1)}, bf16[2,4,64,1024]{3,2,1,0:T(8,128)(2,1)}) custom-call(s32[2]{0:T(128)S(1)} %get-tuple-element.802.place_ref, bf16[512,1024]{1,0:T(8,128)(2,1)} %get-tuple-element.803.refs_0_, ...), custom_call_target="tpu_custom_call" | custom-call | flops 4294967296 | bytes 16777216 | tf_op jit(solution)/shard_map/cond/branch_1_fun/cond/branch_1_fun/column_grads/pallas_call | solution.py:1015
  470.2 103.1 %conditional.34 = (bf16[128,1024]{1,0:T(8,128)(2,1)}, f32[6,1024]{1,0:T(8,128)S(1)}, f32[5,1024]{1,0:T(8,128)S(1)}, bf16[2,256,1024]{2,1,0:T(8,128)(2,1)}, bf16[...) conditional(s32[]{:T(128)} %convert_element_type.170, ...), branch_computations={%region_50.51_spmd, %region_51.68_spmd} | conditional | flops 13521410 | bytes 66676600 | solution.py:795
  472.9 15.1 %conditional.12 = (bf16[4,64,1024]{2,1,0:T(8,128)(2,1)}, bf16[4,64,1024]{2,1,0:T(8,128)(2,1)}) conditional(s32[]{:T(128)} %convert_element_type.133, () %tuple.172, (bf16[4,64,1024]{2,1,0:T(8,128)(2,1)}, bf16[4,64,1024]{2,1,0:T(8,128)(2,1)}) %tuple.173), branch_computations={%region_65.65_spmd, %region_66.66_spmd} | conditional | bytes 4194400 | solution.py:795
  475.9 10.9 %collective-permute-done.33 = bf16[4,64,1024]{2,1,0:T(8,128)(2,1)} collective-permute-done((bf16[4,64,1024]{2,1,0:T(8,128)(2,1)}, bf16[4,64,1024]{2,1,0:T(8,128)(2,1)}, u32[]{:S(2)}, u32[]{:S(2)}) %collective-permute-start.33) | collective-permute-done | bytes 524320 | tf_op jit(solution)/shard_map/cond/branch_1_fun/cond/branch_1_fun/ppermute | solution.py:788
  492.3 25.0 %conditional.9 = (bf16[2,4,64,1024]{3,2,1,0:T(8,128)(2,1)}, bf16[2,4,64,1024]{3,2,1,0:T(8,128)(2,1)}) conditional(s32[]{:T(128)} %convert_element_type.133, () %tuple.168, (bf16[2,4,64,1024]{3,2,1,0:T(8,128)(2,1)}, bf16[2,4,64,1024]{3,2,1,0:T(8,128)(2,1)}) %tuple.169), branch_computations={%region_52.52_spmd, %region_53.53_spmd} | conditional | bytes 8388704 | solution.py:795
  494.3 21.8 %collective-permute-done.29 = bf16[2,4,64,1024]{3,2,1,0:T(8,128)(2,1)} collective-permute-done((bf16[2,4,64,1024]{3,2,1,0:T(8,128)(2,1)}, bf16[2,4,64,1024]{3,2,1,0:T(8,128)(2,1)}, u32[]{:S(2)}, u32[]{:S(2)}) %collective-permute-start.29) | collective-permute-done | bytes 1048608 | tf_op jit(solution)/shard_map/cond/branch_1_fun/cond/branch_1_fun/ppermute | solution.py:788
  518.9 11.7 %conditional.10 = (bf16[4,64,1024]{2,1,0:T(8,128)(2,1)}, bf16[4,64,1024]{2,1,0:T(8,128)(2,1)}) conditional(s32[]{:T(128)} %convert_element_type.133, () %tuple.170, (bf16[4,64,1024]{2,1,0:T(8,128)(2,1)S(1)}, bf16[4,64,1024]{2,1,0:T(8,128)(2,1)S(1)}) %second_sums.7), branch_computations={%region_54.54_spmd, %region_55.55_spmd} | conditional | bytes 4194400 | solution.py:795
  520.1 10.1 %collective-permute-done.31 = bf16[4,64,1024]{2,1,0:T(8,128)(2,1)} collective-permute-done((bf16[4,64,1024]{2,1,0:T(8,128)(2,1)S(1)}, bf16[4,64,1024]{2,1,0:T(8,128)(2,1)}, u32[]{:S(2)}, u32[]{:S(2)}) %collective-permute-start.31) | collective-permute-done | bytes 524320 | tf_op jit(solution)/shard_map/cond/branch_1_fun/cond/branch_1_fun/ppermute | solution.py:788
  552.6 6.5 %collective-permute-done.46 = f32[11,1024]{1,0:T(8,128)S(1)} collective-permute-done((f32[11,1024]{1,0:T(8,128)S(1)}, f32[11,1024]{1,0:T(8,128)S(1)}, u32[]{:S(2)}, u32[]{:S(2)}) %collective-permute-start.46) | collective-permute-done | bytes 45088 | tf_op jit(solution)/shard_map/cond/branch_1_fun/ppermute | solution.py:788
  (322 shorter events, 234.0 us)
Async XLA Ops:
  9.6 27.4 %collective-permute-start.35 = (bf16[256,1024]{1,0:T(8,128)(2,1)S(1)}, bf16[256,1024]{1,0:T(8,128)(2,1)}, u32[]{:S(2)}, u32[]{:S(2)}) collective-permute-start(bf16[256,1024]{1,0:T(8,128)(2,1)S(1)} %dynamic-slice_bitcast_fusion), channel_id=1, source_target_pairs={{0,4},{1,5},{2,6},{3,7},{4,0},{5,1},{6,2},{7,3},{8,12},{9,13},{10,... | collective-permute-start | bytes 1572872 | tf_op jit(solution)/shard_map/cond/branch_1_fun/ppermute | solution.py:788
  54.5 24.6 %all-to-all-start.6 = ((bf16[4,3,2,256,128]{4,3,2,1,0:T(8,128)(2,1)}), bf16[4,3,2,256,128]{4,3,2,1,0:T(8,128)(2,1)}, u32[]{:S(2)}, u32[]{:S(2)}) async-start(bf16[4,3,2,256,128]{4,3,2,1,0:T(8,128)(2,1)} %get-tuple-element.1045), calls=%async_computation.11 | async-start | bytes 3145728 | tf_op jit(solution)/shard_map/all_to_all | solution.py:820
  79.1 24.8 %collective-permute-start = (bf16[512,4096]{1,0:T(8,128)(2,1)}, bf16[512,4096]{1,0:T(8,128)(2,1)}, u32[]{:S(2)}, u32[]{:S(2)}) collective-permute-start(bf16[512,4096]{1,0:T(8,128)(2,1)} %get-tuple-element.549), channel_id=1, source_target_pairs={{0,1},{1,0},{2,3},{3,2},{4,5},{5,4},{6,7},{7,6},{8,9},{9,8},{10,11... | collective-permute-start | bytes 12582920 | tf_op jit(solution)/shard_map/cond/branch_1_fun/ppermute | solution.py:788
  79.1 24.8 %all-to-all-start = ((bf16[4,3,2,256,128]{4,3,2,1,0:T(8,128)(2,1)}), bf16[4,3,2,256,128]{4,3,2,1,0:T(8,128)(2,1)}, u32[]{:S(2)}, u32[]{:S(2)}) async-start(bf16[4,3,2,256,128]{4,3,2,1,0:T(8,128)(2,1)} %get-tuple-element.548), calls=%async_computation | async-start | bytes 3145728 | tf_op jit(solution)/shard_map/cond/branch_1_fun/all_to_all | solution.py:820
  83.8 18.8 %collective-permute-start.1 = (bf16[512,1024]{1,0:T(8,128)(2,1)}, bf16[512,1024]{1,0:T(8,128)(2,1)}, u32[]{:S(2)}, u32[]{:S(2)}) collective-permute-start(bf16[512,1024]{1,0:T(8,128)(2,1)} %get-tuple-element.550), channel_id=1, source_target_pairs={{0,1},{1,0},{2,3},{3,2},{4,5},{5,4},{6,7},{7,6},{8,9},{9,8},{10,11... | collective-permute-start | bytes 3145736 | tf_op jit(solution)/shard_map/cond/branch_1_fun/ppermute | solution.py:788
  84.4 18.3 %collective-permute-start.2 = (bf16[512,1024]{1,0:T(8,128)(2,1)}, bf16[512,1024]{1,0:T(8,128)(2,1)}, u32[]{:S(2)}, u32[]{:S(2)}) collective-permute-start(bf16[512,1024]{1,0:T(8,128)(2,1)} %get-tuple-element.551), channel_id=1, source_target_pairs={{0,1},{1,0},{2,3},{3,2},{4,5},{5,4},{6,7},{7,6},{8,9},{9,8},{10,11... | collective-permute-start | bytes 3145736 | tf_op jit(solution)/shard_map/cond/branch_1_fun/ppermute | solution.py:788
  104.0 30.8 %all-to-all-start.5 = ((bf16[4,2,256,128]{3,2,1,0:T(8,128)(2,1)}), bf16[4,2,256,128]{3,2,1,0:T(8,128)(2,1)}, u32[]{:S(2)}, u32[]{:S(2)}) async-start(bf16[4,2,256,128]{3,2,1,0:T(8,128)(2,1)} %get-tuple-element.557), calls=%async_computation.5 | async-start | bytes 1048576 | tf_op jit(solution)/shard_map/cond/branch_1_fun/all_to_all | solution.py:820
  108.2 26.6 %collective-permute-start.36 = (bf16[256,1024]{1,0:T(8,128)(2,1)S(1)}, bf16[256,1024]{1,0:T(8,128)(2,1)}, u32[]{:S(2)}, u32[]{:S(2)}) collective-permute-start(bf16[256,1024]{1,0:T(8,128)(2,1)S(1)} %dynamic-slice_bitcast_fusion.1), channel_id=1, source_target_pairs={{0,4},{1,5},{2,6},{3,7},{4,0},{5,1},{6,2},{7,3},{8,12},{9,13},{10,... | collective-permute-start | bytes 1572872 | tf_op jit(solution)/shard_map/cond/branch_1_fun/ppermute | solution.py:788
  190.1 17.9 %collective-permute-start.3 = (bf16[512,4096]{1,0:T(8,128)(2,1)}, bf16[512,4096]{1,0:T(8,128)(2,1)}, u32[]{:S(2)}, u32[]{:S(2)}) collective-permute-start(bf16[512,4096]{1,0:T(8,128)(2,1)} %get-tuple-element.570), channel_id=1, source_target_pairs={{0,1},{1,0},{2,3},{3,2},{4,5},{5,4},{6,7},{7,6},{8,9},{9,8},{10,11... | collective-permute-start | bytes 12582920 | tf_op jit(solution)/shard_map/cond/branch_1_fun/ppermute | solution.py:788
  190.1 17.9 %collective-permute-start.4 = (bf16[512,1024]{1,0:T(8,128)(2,1)S(1)}, bf16[512,1024]{1,0:T(8,128)(2,1)}, u32[]{:S(2)}, u32[]{:S(2)}) collective-permute-start(bf16[512,1024]{1,0:T(8,128)(2,1)S(1)} %get-tuple-element.571), channel_id=1, source_target_pairs={{0,1},{1,0},{2,3},{3,2},{4,5},{5,4},{6,7},{7,6},{8,9},{9,8},{10,11... | collective-permute-start | bytes 3145736 | tf_op jit(solution)/shard_map/cond/branch_1_fun/ppermute | solution.py:788
  214.8 24.9 %collective-permute-start.53 = (bf16[512,4096]{1,0:T(8,128)(2,1)}, bf16[512,4096]{1,0:T(8,128)(2,1)}, u32[]{:S(2)}, u32[]{:S(2)}) collective-permute-start(bf16[512,4096]{1,0:T(8,128)(2,1)} %get-tuple-element.1069), channel_id=1, source_target_pairs={{0,1},{1,0},{2,3},{3,2},{4,5},{5,4},{6,7},{7,6},{8,9},{9,8},{10,11... | collective-permute-start | bytes 12582920 | tf_op jit(solution)/shard_map/ppermute | solution.py:788
  217.9 21.7 %collective-permute-start.52 = (bf16[512,1024]{1,0:T(8,128)(2,1)}, bf16[512,1024]{1,0:T(8,128)(2,1)}, u32[]{:S(2)}, u32[]{:S(2)}) collective-permute-start(bf16[512,1024]{1,0:T(8,128)(2,1)} %get-tuple-element.1066), channel_id=1, source_target_pairs={{0,1},{1,0},{2,3},{3,2},{4,5},{5,4},{6,7},{7,6},{8,9},{9,8},{10,11... | collective-permute-start | bytes 3145736 | tf_op jit(solution)/shard_map/ppermute | solution.py:788
  239.6 24.9 %collective-permute-start.5 = (bf16[512,1024]{1,0:T(8,128)(2,1)}, bf16[512,1024]{1,0:T(8,128)(2,1)}, u32[]{:S(2)}, u32[]{:S(2)}) collective-permute-start(bf16[512,1024]{1,0:T(8,128)(2,1)} %get-tuple-element.572), channel_id=1, source_target_pairs={{0,1},{1,0},{2,3},{3,2},{4,5},{5,4},{6,7},{7,6},{8,9},{9,8},{10,11... | collective-permute-start | bytes 3145736 | tf_op jit(solution)/shard_map/cond/branch_1_fun/ppermute | solution.py:788
  239.8 24.7 %collective-permute-start.6 = (bf16[512,1024]{1,0:T(8,128)(2,1)}, bf16[512,1024]{1,0:T(8,128)(2,1)}, u32[]{:S(2)}, u32[]{:S(2)}) collective-permute-start(bf16[512,1024]{1,0:T(8,128)(2,1)} %get-tuple-element.573), channel_id=1, source_target_pairs={{0,1},{1,0},{2,3},{3,2},{4,5},{5,4},{6,7},{7,6},{8,9},{9,8},{10,11... | collective-permute-start | bytes 3145736 | tf_op jit(solution)/shard_map/cond/branch_1_fun/ppermute | solution.py:788
  240.2 24.3 %collective-permute-start.7 = (bf16[512,1024]{1,0:T(8,128)(2,1)}, bf16[512,1024]{1,0:T(8,128)(2,1)}, u32[]{:S(2)}, u32[]{:S(2)}) collective-permute-start(bf16[512,1024]{1,0:T(8,128)(2,1)} %get-tuple-element.574), channel_id=1, source_target_pairs={{0,1},{1,0},{2,3},{3,2},{4,5},{5,4},{6,7},{7,6},{8,9},{9,8},{10,11... | collective-permute-start | bytes 3145736 | tf_op jit(solution)/shard_map/cond/branch_1_fun/ppermute | solution.py:788
  240.3 24.2 %collective-permute-start.8 = (bf16[512,1024]{1,0:T(8,128)(2,1)}, bf16[512,1024]{1,0:T(8,128)(2,1)}, u32[]{:S(2)}, u32[]{:S(2)}) collective-permute-start(bf16[512,1024]{1,0:T(8,128)(2,1)} %get-tuple-element.575), channel_id=1, source_target_pairs={{0,1},{1,0},{2,3},{3,2},{4,5},{5,4},{6,7},{7,6},{8,9},{9,8},{10,11... | collective-permute-start | bytes 3145736 | tf_op jit(solution)/shard_map/cond/branch_1_fun/ppermute | solution.py:788
  240.7 23.9 %collective-permute-start.9 = (bf16[512,1024]{1,0:T(8,128)(2,1)}, bf16[512,1024]{1,0:T(8,128)(2,1)}, u32[]{:S(2)}, u32[]{:S(2)}) collective-permute-start(bf16[512,1024]{1,0:T(8,128)(2,1)} %get-tuple-element.576), channel_id=1, source_target_pairs={{0,1},{1,0},{2,3},{3,2},{4,5},{5,4},{6,7},{7,6},{8,9},{9,8},{10,11... | collective-permute-start | bytes 3145736 | tf_op jit(solution)/shard_map/cond/branch_1_fun/ppermute | solution.py:788
  240.8 23.7 %all-to-all-start.1 = ((bf16[4,2,256,128]{3,2,1,0:T(8,128)(2,1)}), bf16[4,2,256,128]{3,2,1,0:T(8,128)(2,1)}, u32[]{:S(2)}, u32[]{:S(2)}) async-start(bf16[4,2,256,128]{3,2,1,0:T(8,128)(2,1)} %get-tuple-element.577), calls=%async_computation.1 | async-start | bytes 1048576 | tf_op jit(solution)/shard_map/cond/branch_1_fun/all_to_all | solution.py:820
  264.6 35.4 %collective-permute-start.13 = (bf16[2,4,64,1024]{3,2,1,0:T(8,128)(2,1)}, bf16[2,4,64,1024]{3,2,1,0:T(8,128)(2,1)}, u32[]{:S(2)}, u32[]{:S(2)}) collective-permute-start(bf16[2,4,64,1024]{3,2,1,0:T(8,128)(2,1)} %get-tuple-element.619), channel_id=1, source_target_pairs={{0,8},{1,9},{2,10},{3,11},{4,12},{5,13},{6,14},{7,15},{8,0},{9,1},... | collective-permute-start | bytes 3145736 | tf_op jit(solution)/shard_map/cond/branch_1_fun/ppermute | solution.py:788
  266.2 33.8 %collective-permute-start.14 = (bf16[2,4,64,1024]{3,2,1,0:T(8,128)(2,1)}, bf16[2,4,64,1024]{3,2,1,0:T(8,128)(2,1)}, u32[]{:S(2)}, u32[]{:S(2)}) collective-permute-start(bf16[2,4,64,1024]{3,2,1,0:T(8,128)(2,1)} %get-tuple-element.620), channel_id=1, source_target_pairs={{0,16},{1,17},{2,18},{3,19},{4,20},{5,21},{6,22},{7,23},{8,24},{9,... | collective-permute-start | bytes 3145736 | tf_op jit(solution)/shard_map/cond/branch_1_fun/ppermute | solution.py:788
  267.7 32.2 %all-to-all-start.2 = ((bf16[4,2,256,128]{3,2,1,0:T(8,128)(2,1)}), bf16[4,2,256,128]{3,2,1,0:T(8,128)(2,1)}, u32[]{:S(2)}, u32[]{:S(2)}) async-start(bf16[4,2,256,128]{3,2,1,0:T(8,128)(2,1)} %get-tuple-element.600), calls=%async_computation.2 | async-start | bytes 1048576 | tf_op jit(solution)/shard_map/cond/branch_1_fun/cond/branch_1_fun/all_to_all | solution.py:820
  271.9 28.1 %collective-permute-start.10 = (bf16[256,1024]{1,0:T(8,128)(2,1)}, bf16[256,1024]{1,0:T(8,128)(2,1)}, u32[]{:S(2)}, u32[]{:S(2)}) collective-permute-start(bf16[256,1024]{1,0:T(8,128)(2,1)} %get-tuple-element.601), channel_id=1, source_target_pairs={{0,4},{1,5},{2,6},{3,7},{4,0},{5,1},{6,2},{7,3},{8,12},{9,13},{10,... | collective-permute-start | bytes 1572872 | tf_op jit(solution)/shard_map/cond/branch_1_fun/cond/branch_1_fun/ppermute | solution.py:788
  273.2 26.8 %collective-permute-start.11 = (bf16[512,1024]{1,0:T(8,128)(2,1)}, bf16[512,1024]{1,0:T(8,128)(2,1)}, u32[]{:S(2)}, u32[]{:S(2)}) collective-permute-start(bf16[512,1024]{1,0:T(8,128)(2,1)} %get-tuple-element.602), channel_id=1, source_target_pairs={{0,1},{1,0},{2,3},{3,2},{4,5},{5,4},{6,7},{7,6},{8,9},{9,8},{10,11... | collective-permute-start | bytes 3145736 | tf_op jit(solution)/shard_map/cond/branch_1_fun/cond/branch_1_fun/ppermute | solution.py:788
  273.2 26.7 %collective-permute-start.12 = (bf16[512,1024]{1,0:T(8,128)(2,1)}, bf16[512,1024]{1,0:T(8,128)(2,1)}, u32[]{:S(2)}, u32[]{:S(2)}) collective-permute-start(bf16[512,1024]{1,0:T(8,128)(2,1)} %get-tuple-element.603), channel_id=1, source_target_pairs={{0,1},{1,0},{2,3},{3,2},{4,5},{5,4},{6,7},{7,6},{8,9},{9,8},{10,11... | collective-permute-start | bytes 3145736 | tf_op jit(solution)/shard_map/cond/branch_1_fun/cond/branch_1_fun/ppermute | solution.py:788
  302.1 37.0 %collective-permute-start.17 = (bf16[2,4,64,1024]{3,2,1,0:T(8,128)(2,1)}, bf16[2,4,64,1024]{3,2,1,0:T(8,128)(2,1)}, u32[]{:S(2)}, u32[]{:S(2)}) collective-permute-start(bf16[2,4,64,1024]{3,2,1,0:T(8,128)(2,1)} %get-tuple-element.638), channel_id=1, source_target_pairs={{0,8},{1,9},{2,10},{3,11},{4,12},{5,13},{6,14},{7,15},{8,0},{9,1},... | collective-permute-start | bytes 3145736 | tf_op jit(solution)/shard_map/cond/branch_1_fun/ppermute | solution.py:788
  302.6 36.4 %collective-permute-start.18 = (bf16[2,4,64,1024]{3,2,1,0:T(8,128)(2,1)}, bf16[2,4,64,1024]{3,2,1,0:T(8,128)(2,1)}, u32[]{:S(2)}, u32[]{:S(2)}) collective-permute-start(bf16[2,4,64,1024]{3,2,1,0:T(8,128)(2,1)} %get-tuple-element.639), channel_id=1, source_target_pairs={{0,16},{1,17},{2,18},{3,19},{4,20},{5,21},{6,22},{7,23},{8,24},{9,... | collective-permute-start | bytes 3145736 | tf_op jit(solution)/shard_map/cond/branch_1_fun/ppermute | solution.py:788
  303.1 35.9 %collective-permute-start.15 = (bf16[4,64,1024]{2,1,0:T(8,128)(2,1)}, bf16[4,64,1024]{2,1,0:T(8,128)(2,1)}, u32[]{:S(2)}, u32[]{:S(2)}) collective-permute-start(bf16[4,64,1024]{2,1,0:T(8,128)(2,1)} %get-tuple-element.636), channel_id=1, source_target_pairs={{0,16},{1,17},{2,18},{3,19},{4,20},{5,21},{6,22},{7,23},{8,24},{9,... | collective-permute-start | bytes 1572872 | tf_op jit(solution)/shard_map/cond/branch_1_fun/ppermute | solution.py:788
  304.6 34.4 %collective-permute-start.16 = (bf16[4,64,1024]{2,1,0:T(8,128)(2,1)}, bf16[4,64,1024]{2,1,0:T(8,128)(2,1)}, u32[]{:S(2)}, u32[]{:S(2)}) collective-permute-start(bf16[4,64,1024]{2,1,0:T(8,128)(2,1)} %get-tuple-element.637), channel_id=1, source_target_pairs={{0,8},{1,9},{2,10},{3,11},{4,12},{5,13},{6,14},{7,15},{8,0},{9,1},... | collective-permute-start | bytes 1572872 | tf_op jit(solution)/shard_map/cond/branch_1_fun/ppermute | solution.py:788
  306.1 30.7 %all-to-all-start.3 = ((bf16[4,3,2,256,128]{4,3,2,1,0:T(8,128)(2,1)}), bf16[4,3,2,256,128]{4,3,2,1,0:T(8,128)(2,1)}, u32[]{:S(2)}, u32[]{:S(2)}) async-start(bf16[4,3,2,256,128]{4,3,2,1,0:T(8,128)(2,1)} %get-tuple-element.626), calls=%async_computation.3 | async-start | bytes 3145728 | tf_op jit(solution)/shard_map/cond/branch_1_fun/cond/branch_1_fun/all_to_all | solution.py:820
  341.4 24.6 %all-to-all-start.4 = ((bf16[4,3,2,256,128]{4,3,2,1,0:T(8,128)(2,1)}), bf16[4,3,2,256,128]{4,3,2,1,0:T(8,128)(2,1)}, u32[]{:S(2)}, u32[]{:S(2)}) async-start(bf16[4,3,2,256,128]{4,3,2,1,0:T(8,128)(2,1)} %get-tuple-element.640), calls=%async_computation.4 | async-start | bytes 3145728 | tf_op jit(solution)/shard_map/cond/branch_1_fun/all_to_all | solution.py:820
  345.9 15.2 %collective-permute-start.19 = (bf16[4,64,1024]{2,1,0:T(8,128)(2,1)}, bf16[4,64,1024]{2,1,0:T(8,128)(2,1)S(1)}, u32[]{:S(2)}, u32[]{:S(2)}) collective-permute-start(bf16[4,64,1024]{2,1,0:T(8,128)(2,1)} %get-tuple-element.668), channel_id=1, source_target_pairs={{0,16},{1,17},{2,18},{3,19},{4,20},{5,21},{6,22},{7,23},{8,24},{9,... | collective-permute-start | bytes 1572872 | tf_op jit(solution)/shard_map/cond/branch_1_fun/ppermute | solution.py:788
  366.1 64.4 %reduce-scatter.6.cloned.1.call-start = ((), (), s32[]{:S(2)}) async-start(), calls=%async_computation.13 | async-start | bytes 2621440 | tf_op jit(solution)/shard_map/cond/branch_1_fun/reduce_scatter | solution.py:1135
  367.7 25.1 %collective-permute-start.22 = (bf16[2,4,64,1024]{3,2,1,0:T(8,128)(2,1)}, bf16[2,4,64,1024]{3,2,1,0:T(8,128)(2,1)}, u32[]{:S(2)}, u32[]{:S(2)}) collective-permute-start(bf16[2,4,64,1024]{3,2,1,0:T(8,128)(2,1)} %get-tuple-element.698), channel_id=1, source_target_pairs={{0,8},{1,9},{2,10},{3,11},{4,12},{5,13},{6,14},{7,15},{8,0},{9,1},... | collective-permute-start | bytes 3145736 | tf_op jit(solution)/shard_map/cond/branch_1_fun/cond/branch_1_fun/ppermute | solution.py:788
  369.2 24.7 %collective-permute-start.23 = (bf16[2,4,64,1024]{3,2,1,0:T(8,128)(2,1)}, bf16[2,4,64,1024]{3,2,1,0:T(8,128)(2,1)}, u32[]{:S(2)}, u32[]{:S(2)}) collective-permute-start(bf16[2,4,64,1024]{3,2,1,0:T(8,128)(2,1)} %get-tuple-element.699), channel_id=1, source_target_pairs={{0,16},{1,17},{2,18},{3,19},{4,20},{5,21},{6,22},{7,23},{8,24},{9,... | collective-permute-start | bytes 3145736 | tf_op jit(solution)/shard_map/cond/branch_1_fun/cond/branch_1_fun/ppermute | solution.py:788
  408.7 21.8 %collective-permute-start.27 = (bf16[2,4,64,768]{3,2,1,0:T(8,128)(2,1)}, bf16[2,4,64,768]{3,2,1,0:T(8,128)(2,1)}, u32[]{:S(2)}, u32[]{:S(2)}) collective-permute-start(bf16[2,4,64,768]{3,2,1,0:T(8,128)(2,1)} %get-tuple-element.750), channel_id=1, source_target_pairs={{0,8},{1,9},{2,10},{3,11},{4,12},{5,13},{6,14},{7,15},{8,0},{9,1},... | collective-permute-start | bytes 2359304 | tf_op jit(solution)/shard_map/cond/branch_1_fun/cond/branch_1_fun/ppermute | solution.py:788
  410.1 20.4 %collective-permute-start.28 = (bf16[2,4,64,768]{3,2,1,0:T(8,128)(2,1)}, bf16[2,4,64,768]{3,2,1,0:T(8,128)(2,1)}, u32[]{:S(2)}, u32[]{:S(2)}) collective-permute-start(bf16[2,4,64,768]{3,2,1,0:T(8,128)(2,1)} %get-tuple-element.751), channel_id=1, source_target_pairs={{0,16},{1,17},{2,18},{3,19},{4,20},{5,21},{6,22},{7,23},{8,24},{9,... | collective-permute-start | bytes 2359304 | tf_op jit(solution)/shard_map/cond/branch_1_fun/cond/branch_1_fun/ppermute | solution.py:788
  434.1 33.4 %collective-permute-start.38 = (bf16[2,4,64,1024]{3,2,1,0:T(8,128)(2,1)}, bf16[2,4,64,1024]{3,2,1,0:T(8,128)(2,1)}, u32[]{:S(2)}, u32[]{:S(2)}) collective-permute-start(bf16[2,4,64,1024]{3,2,1,0:T(8,128)(2,1)} %get-tuple-element.841), channel_id=1, source_target_pairs={{0,8},{1,9},{2,10},{3,11},{4,12},{5,13},{6,14},{7,15},{8,0},{9,1},... | collective-permute-start | bytes 3145736 | tf_op jit(solution)/shard_map/cond/branch_1_fun/ppermute | solution.py:788
  435.5 32.0 %collective-permute-start.39 = (bf16[2,4,64,1024]{3,2,1,0:T(8,128)(2,1)}, bf16[2,4,64,1024]{3,2,1,0:T(8,128)(2,1)}, u32[]{:S(2)}, u32[]{:S(2)}) collective-permute-start(bf16[2,4,64,1024]{3,2,1,0:T(8,128)(2,1)} %get-tuple-element.842), channel_id=1, source_target_pairs={{0,16},{1,17},{2,18},{3,19},{4,20},{5,21},{6,22},{7,23},{8,24},{9,... | collective-permute-start | bytes 3145736 | tf_op jit(solution)/shard_map/cond/branch_1_fun/ppermute | solution.py:788
  436.4 31.1 %collective-permute-start.40 = (bf16[4,64,768]{2,1,0:T(8,128)(2,1)S(1)}, bf16[4,64,768]{2,1,0:T(8,128)(2,1)}, u32[]{:S(2)}, u32[]{:S(2)}) collective-permute-start(bf16[4,64,768]{2,1,0:T(8,128)(2,1)S(1)} %get-tuple-element.843), channel_id=1, source_target_pairs={{0,16},{1,17},{2,18},{3,19},{4,20},{5,21},{6,22},{7,23},{8,24},{9,... | collective-permute-start | bytes 1179656 | tf_op jit(solution)/shard_map/cond/branch_1_fun/ppermute | solution.py:788
  437.5 30.0 %collective-permute-start.41 = (bf16[4,64,768]{2,1,0:T(8,128)(2,1)}, bf16[4,64,768]{2,1,0:T(8,128)(2,1)}, u32[]{:S(2)}, u32[]{:S(2)}) collective-permute-start(bf16[4,64,768]{2,1,0:T(8,128)(2,1)} %get-tuple-element.844), channel_id=1, source_target_pairs={{0,8},{1,9},{2,10},{3,11},{4,12},{5,13},{6,14},{7,15},{8,0},{9,1},... | collective-permute-start | bytes 1179656 | tf_op jit(solution)/shard_map/cond/branch_1_fun/ppermute | solution.py:788
  438.2 29.3 %reduce-scatter.8.cloned.1.call-start = ((), (), s32[]{:S(2)}) async-start(), calls=%async_computation.14 | async-start | bytes 1310720 | tf_op jit(solution)/shard_map/cond/branch_1_fun/cond/branch_1_fun/reduce_scatter | solution.py:1135
  438.4 16.8 %collective-permute-start.37 = (bf16[512,4096]{1,0:T(8,128)(2,1)}, bf16[512,4096]{1,0:T(8,128)(2,1)}, u32[]{:S(2)}, u32[]{:S(2)}) collective-permute-start(bf16[512,4096]{1,0:T(8,128)(2,1)} %get-tuple-element.805.refs_2_.grad_ref), channel_id=1, source_target_pairs={{0,1},{1,0},{2,3},{3,2},{4,5},{5,4},{6,7},{7,6},{8,9},{9,8},{10,11... | collective-permute-start | bytes 12582920 | tf_op jit(solution)/shard_map/cond/branch_1_fun/cond/branch_1_fun/ppermute | solution.py:788
  470.2 99.5 %reduce-scatter.12.cloned.1.call-start = ((), (), s32[]{:S(2)}) async-start(), calls=%async_computation.16 | async-start | bytes 983040 | tf_op jit(solution)/shard_map/cond/branch_1_fun/reduce_scatter | solution.py:1135
  472.9 98.5 %reduce-scatter.14.cloned.1.call-start = ((), (), s32[]{:S(2)}) async-start(), calls=%async_computation.17 | async-start | bytes 1310720 | tf_op jit(solution)/shard_map/cond/branch_1_fun/reduce_scatter | solution.py:1135
  490.9 82.4 %reduce-scatter.10.cloned.1.call-start = ((), (), s32[]{:S(2)}) async-start(), calls=%async_computation.15 | async-start | bytes 1310720 | tf_op jit(solution)/shard_map/cond/branch_1_fun/reduce_scatter | solution.py:1135
  490.9 42.4 %collective-permute-start.42 = (bf16[256,1024]{1,0:T(8,128)(2,1)}, bf16[256,1024]{1,0:T(8,128)(2,1)}, u32[]{:S(2)}, u32[]{:S(2)}) collective-permute-start(bf16[256,1024]{1,0:T(8,128)(2,1)} %get-tuple-element.867), channel_id=1, source_target_pairs={{0,4},{1,5},{2,6},{3,7},{4,0},{5,1},{6,2},{7,3},{8,12},{9,13},{10,... | collective-permute-start | bytes 1572872 | tf_op jit(solution)/shard_map/cond/branch_1_fun/ppermute | solution.py:788
  492.3 23.8 %collective-permute-start.29 = (bf16[2,4,64,1024]{3,2,1,0:T(8,128)(2,1)}, bf16[2,4,64,1024]{3,2,1,0:T(8,128)(2,1)}, u32[]{:S(2)}, u32[]{:S(2)}) collective-permute-start(bf16[2,4,64,1024]{3,2,1,0:T(8,128)(2,1)} %get-tuple-element.845), channel_id=1, source_target_pairs={{0,8},{1,9},{2,10},{3,11},{4,12},{5,13},{6,14},{7,15},{8,0},{9,1},... | collective-permute-start | bytes 3145736 | tf_op jit(solution)/shard_map/cond/branch_1_fun/cond/branch_1_fun/ppermute | solution.py:788
  493.7 23.5 %collective-permute-start.30 = (bf16[2,4,64,1024]{3,2,1,0:T(8,128)(2,1)}, bf16[2,4,64,1024]{3,2,1,0:T(8,128)(2,1)}, u32[]{:S(2)}, u32[]{:S(2)}) collective-permute-start(bf16[2,4,64,1024]{3,2,1,0:T(8,128)(2,1)} %get-tuple-element.846), channel_id=1, source_target_pairs={{0,16},{1,17},{2,18},{3,19},{4,20},{5,21},{6,22},{7,23},{8,24},{9,... | collective-permute-start | bytes 3145736 | tf_op jit(solution)/shard_map/cond/branch_1_fun/cond/branch_1_fun/ppermute | solution.py:788
  (64 other events, 607.2 us)
Sparse Core Ops, SparseCore 0:
  369.2 42.4 reduce-scatter.5
  442.0 25.4 reduce-scatter.7
  473.4 22.5 reduce-scatter.11
  498.3 35.5 reduce-scatter.13
  538.2 29.0 reduce-scatter.9

commit v5 on v4

--- a/solution.py
+++ b/solution.py
@@ -200,6 +200,8 @@
     zeros = tuple(jnp.zeros((BLOCK, LANES), F32) for _ in range(heads))
     sums, accs = lax.fori_loop(low, high, weigh, (zeros, zeros))
     result = None
+    lane = lax.broadcasted_iota(jnp.int32, (BLOCK, LANES), 1)
+    shifted = jnp.where(member_lanes(counts, step * BLOCK, BLOCK, group, 3), 1.0, 0.0)
     for head in range(heads):
         total = jnp.sum(sums[head], 1, keepdims=True)
         mine = accs[head] / total
@@ -207,7 +209,9 @@
             result = mine
         else:
             result = jnp.where(head_lanes(mine.shape, head, size), mine, result)
-        lse_ref[head] = tops[head] + jnp.log(jnp.broadcast_to(total, (BLOCK, LANES)))
+        lse = tops[head] + jnp.log(jnp.broadcast_to(total, (BLOCK, LANES)))
+        spread = spread_columns(split_three(lse), (BLOCK, LANES))
+        lse_ref[head] = jnp.where(lane < 3, -spread, shifted).astype(BF16)
     full_ref[...] = result
     out_ref[...] = result.astype(BF16).reshape(out_ref.shape)
 
@@ -230,7 +234,7 @@
         out_shape=[
             jax.ShapeDtypeStruct((places, chunks, frames, LANES), BF16),
             jax.ShapeDtypeStruct((group, LANES), F32),
-            jax.ShapeDtypeStruct((heads, group, LANES), F32),
+            jax.ShapeDtypeStruct((heads, group, LANES), BF16),
         ],
         scratch_shapes=[
             pltpu.VMEM((group, 2 * LANES), BF16),
@@ -265,19 +269,15 @@
 
         def prepare(j, _):
             rows = pl.ds(pl.multiple_of(j * BLOCK, BLOCK), BLOCK)
-            lane = lax.broadcasted_iota(jnp.int32, (BLOCK, LANES), 1)
             q = chunk_rows(qkv_ref, (0,), j).astype(F32) * (size ** -0.5)
             g = chunk_rows(grad_ref, (), j).astype(F32)
             product = g * full_ref[rows, :]
-            member = jnp.where(member_lanes(counts, j * BLOCK, BLOCK, group, 3), 1.0, 0.0)
             for head in range(heads):
                 own = head_lanes((BLOCK, LANES), head, size)
-                lse = lse_ref[head, rows, :]
-                spread = spread_columns(split_three(lse), (BLOCK, LANES))
                 delta = jnp.sum(jnp.where(own, product, 0.0), 1, keepdims=True)
                 delta = jnp.broadcast_to(delta, (BLOCK, LANES))
                 qcat[head, rows, :LANES] = jnp.where(own, q, 0.0).astype(BF16)
-                qcat[head, rows, LANES:] = jnp.where(lane < 3, -spread, member).astype(BF16)
+                qcat[head, rows, LANES:] = lse_ref[head, rows, :]
                 gcat[head, rows, :LANES] = jnp.where(own, g, 0.0).astype(BF16)
                 spread = spread_columns(split_three(delta), (BLOCK, LANES))
                 gcat[head, rows, LANES:] = (-spread).astype(BF16)

time: 591 us -> 590 us (level)
  no operation moved by 1% of the time
where the time goes in v5:
time: 590 us; the launch traced here: 580 us
  Pallas kernels  288 us (49%)
  waiting for transfers between devices  118 us (20%)
  starting transfers between devices  76.8 us (13%)
  other arithmetic  38.8 us (7%)
  matrix products  21.3 us (4%)
  local copies, waits for them, and re-layouts  18.7 us (3%)
  between operations  17.5 us (3%)
    ppermute x50, waiting for transfers between devices, swap(): return lax.ppermute(value, EVERY, flipped(axis_bit, count))  93 us
    pallas_call x2, Pallas kernels, attend_backward(): pl.pallas_call(functools.partial(attn_bwd_kernel, heads, size, group), gr...  49.5 us
    pallas_call x4, Pallas kernels, column_grads(): pl.pallas_call(functools.partial(column_grad_kernel, heads, items, split)...  42.8 us
    ppermute x50, starting transfers between devices, swap(): return lax.ppermute(value, EVERY, flipped(axis_bit, count))  41.2 us
    pallas_call x2, Pallas kernels, attend_forward(): pl.pallas_call(functools.partial(attn_fwd_kernel, heads, size, group), gr...  37.7 us
    pallas_call x2, Pallas kernels, front(): pl.pallas_call(functools.partial(front_kernel, size, ffn_steps, pieces),...  34.4 us
    all_to_all x8, starting transfers between devices, exchange(): lax.all_to_all(value, 'heads', split_axis=0, concat_axis=0, tiled=True, a...  34.1 us
    dot_general x7, matrix products, dot(): return lax.dot_general(left, right, dims, preferred_element_type=F32)  21.3 us
  transfers between devices with their start and end apart: 67, of which 26 were waited for; matrix products, arithmetic and copies ran while one was open for 7% of the time, Pallas kernels for 41%

profile of v5, /device:TPU:0, one launch (start us, length us, event | category | flops | bytes accessed | tf_op | source)
XLA Modules:
  0.0 579.7 jit_solution(11476635556716698072)
XLA Ops:
  8.4 28.6 %conditional.24 = (f32[512,1024]{1,0:T(8,128)}, bf16[512,4096]{1,0:T(8,128)(2,1)}, bf16[512,4096]{1,0:T(8,128)(2,1)}, bf16[512,1024]{1,0:T(8,128)(2,1)}, bf16[51...) conditional(s32[]{:T(128)} %convert_element_type.170, ...), branch_computations={%region_0.1_spmd, %region_1.2_spmd} | conditional | flops 5905580032 | bytes 34603160 | solution.py:795
  13.7 16.9 %front.2 = (f32[512,1024]{1,0:T(8,128)}, bf16[512,4096]{1,0:T(8,128)(2,1)}, bf16[512,4096]{1,0:T(8,128)(2,1)}, bf16[512,1024]{1,0:T(8,128)(2,1)}, bf16[512,1024]...) custom-call(s32[1]{0:T(128)} %bitcast.row_ref, ...), custom_call_target="tpu_custom_call" | custom-call | flops 5905580032 | bytes 31457280 | tf_op jit(solution)/shard_map/cond/branch_1_fun/front/pallas_call | solution.py:688
  30.6 6.4 %collective-permute-done.35 = bf16[256,1024]{1,0:T(8,128)(2,1)} collective-permute-done((bf16[256,1024]{1,0:T(8,128)(2,1)S(1)}, bf16[256,1024]{1,0:T(8,128)(2,1)}, u32[]{:S(2)}, u32[]{:S(2)}) %collective-permute-start.35) | collective-permute-done | bytes 524320 | tf_op jit(solution)/shard_map/cond/branch_1_fun/ppermute | solution.py:788
  37.0 17.5 %front.3 = (f32[512,1024]{1,0:T(8,128)}, bf16[512,4096]{1,0:T(8,128)(2,1)}, bf16[512,4096]{1,0:T(8,128)(2,1)}, bf16[512,1024]{1,0:T(8,128)(2,1)}, bf16[512,1024]...) custom-call(s32[1]{0:T(128)} %bitcast.19.row_ref, ...), custom_call_target="tpu_custom_call", output_to_operand_aliasing={{0}: (10, {}), {1}: (11, {}), {2}: (12, {}), {3}: (13, {}),... | custom-call | flops 5905580032 | bytes 31457280 | tf_op jit(solution)/shard_map/front/pallas_call | solution.py:688
  66.7 12.5 %all-to-all-done.6 = bf16[4,3,2,256,128]{4,3,2,1,0:T(8,128)(2,1)} async-done(((bf16[4,3,2,256,128]{4,3,2,1,0:T(8,128)(2,1)}), bf16[4,3,2,256,128]{4,3,2,1,0:T(8,128)(2,1)}, u32[]{:S(2)}, u32[]{:S(2)}) %all-to-all-start.6) | async-done | bytes 1572896 | tf_op jit(solution)/shard_map/all_to_all | solution.py:820
  79.1 24.8 %conditional.25 = (bf16[4,2,256,128]{3,2,1,0:T(8,128)(2,1)}, f32[2048,128]{1,0:T(8,128)}, bf16[2,2048,128]{2,1,0:T(8,128)(2,1)}, bf16[4,3,2,256,128]{4,3,2,1,0:T...) conditional(s32[]{:T(128)} %convert_element_type.170, ...), branch_computations={%region_2.3_spmd, %region_3.4_spmd} | conditional | flops 8589934592 | bytes 36176080 | solution.py:795
  84.4 18.8 %attend_forward.2 = (bf16[4,2,256,128]{3,2,1,0:T(8,128)(2,1)}, f32[2048,128]{1,0:T(8,128)}, bf16[2,2048,128]{2,1,0:T(8,128)(2,1)}) custom-call(s32[2]{0:T(128)S(1)} %get-tuple-element.543.counts_ref, bf16[4,3,2,256,128]{4,3,2,1,0:T(8,128)(2,1)} %get-tuple-element.544.qkv_ref), custom_call_target="tpu_custom_call" | custom-call | flops 8589934592 | bytes 6291456 | tf_op jit(solution)/shard_map/cond/branch_1_fun/attend_forward/pallas_call | solution.py:225
  104.0 30.8 %conditional.26 = (bf16[4,2,256,128]{3,2,1,0:T(8,128)(2,1)}, f32[2048,128]{1,0:T(8,128)}, bf16[2,2048,128]{2,1,0:T(8,128)(2,1)}, bf16[4,2,256,128]{3,2,1,0:T(8,128)(2,1)}, bf16[256,1024]{1,0:T(8,128)(2,1)}) conditional(s32[]{:T(128)} %convert_element_type.170, () %tuple.207, (s32[2]{0:T(128)S(1)}, bf16[4,3,2,256,128]{4,3,2,1,0:T(8,128)(2,1)}, ...), branch_computations={%region_4.5_spmd, %region_5.6_spmd} | conditional | flops 8589934592 | bytes 11010210 | solution.py:795
  110.1 18.9 %attend_forward.3 = (bf16[4,2,256,128]{3,2,1,0:T(8,128)(2,1)}, f32[2048,128]{1,0:T(8,128)}, bf16[2,2048,128]{2,1,0:T(8,128)(2,1)}) custom-call(s32[2]{0:T(128)S(1)} %get-tuple-element.552.counts_ref, bf16[4,3,2,256,128]{4,3,2,1,0:T(8,128)(2,1)} %get-tuple-element.553.qkv_ref), custom_call_target="tpu_custom_call" | custom-call | flops 8589934592 | bytes 6291456 | tf_op jit(solution)/shard_map/cond/branch_1_fun/attend_forward/pallas_call | solution.py:225
  129.0 5.8 collective-permute-done.36
  170.9 18.1 %ffn_forward.1 = (bf16[512,1024]{1,0:T(8,128)(2,1)}, f32[512,1024]{1,0:T(8,128)}, f32[1,1024]{1,0:T(1,128)}, bf16[512,4096]{1,0:T(8,128)(2,1)}, bf16[512,4096]{1...) custom-call(f32[512,1024]{1,0:T(8,128)S(1)} %convolution_add_fusion.x_ref, f32[1,1024]{1,0:T(1,128)S(1)} %get-tuple-element.1208.gain_ref, ...), custom_call_target="tpu_custom_call" | custom-call | flops 8589934592 | bytes 25165824 | tf_op jit(solution)/shard_map/ffn_forward/pallas_call | solution.py:395
  190.0 18.0 %conditional.27 = (f32[512,1024]{1,0:T(8,128)S(1)}, f32[1,1024]{1,0:T(1,128)}, bf16[512,1024]{1,0:T(8,128)(2,1)}, bf16[512,4096]{1,0:T(8,128)(2,1)}, bf16[512,40...) conditional(s32[]{:T(128)} %convert_element_type.170, () %tuple.211, (f32[512,1024]{1,0:T(8,128)S(1)}, ...), branch_computations={%region_10.11_spmd, %region_11.12_spmd} | conditional | flops 8589934592 | bytes 50331776 | solution.py:795
  190.5 17.5 %ffn_backward.1 = (f32[512,1024]{1,0:T(8,128)S(1)}, f32[1,1024]{1,0:T(1,128)}, bf16[512,1024]{1,0:T(8,128)(2,1)}, bf16[512,4096]{1,0:T(8,128)(2,1)}) custom-call(f32[512,1024]{1,0:T(8,128)S(1)} %get-tuple-element.560.x_ref, f32[1,1024]{1,0:T(1,128)S(1)} %get-tuple-element.561.gain_ref, f32[512,1024]{1,0:T(8,128)} %get-tuple-element.562.up_ref, ...), custom_call_target="tpu_custom_call" | custom-call | flops 8589934592 | bytes 29360128 | tf_op jit(solution)/shard_map/cond/branch_1_fun/ffn_backward/pallas_call | solution.py:452
  239.6 24.9 %conditional.28 = (bf16[512,1024]{1,0:T(8,128)(2,1)}, bf16[512,1024]{1,0:T(8,128)(2,1)}, bf16[512,1024]{1,0:T(8,128)(2,1)}, bf16[512,1024]{1,0:T(8,128)(2,1)}, b...) conditional(s32[]{:T(128)} %convert_element_type.170, ...), branch_computations={%region_16.17_spmd, %region_17.18_spmd} | conditional | flops 8589934592 | bytes 60293492 | solution.py:795
  245.2 9.2 %out_grad.2 = (bf16[2,4,64,1024]{3,2,1,0:T(8,128)(2,1)S(1)}, bf16[2,4,64,1024]{3,2,1,0:T(8,128)(2,1)S(1)}, bf16[2,4,64,1024]{3,2,1,0:T(8,128)(2,1)}, bf16[2,4,64,1024]{3,2,1,0:T(8,128)(2,1)}) custom-call(s32[2]{0:T(128)S(1)} %get-tuple-element.578.place_ref, bf16[512,1024]{1,0:T(8,128)(2,1)} %get-tuple-element.579.up_own, ...), custom_call_target="tpu_custom_call" | custom-call | flops 4294967296 | bytes 16777216 | tf_op jit(solution)/shard_map/cond/branch_1_fun/out_grad/pallas_call | solution.py:912
  254.3 10.2 %column_grads.4 = (bf16[2,4,64,1024]{3,2,1,0:T(8,128)(2,1)}, bf16[2,4,64,1024]{3,2,1,0:T(8,128)(2,1)}, bf16[2,4,64,1024]{3,2,1,0:T(8,128)(2,1)}, bf16[2,4,64,1024]{3,2,1,0:T(8,128)(2,1)}) custom-call(s32[2]{0:T(128)S(1)} %get-tuple-element.578.place_ref, bf16[512,1024]{1,0:T(8,128)(2,1)S(1)} %copy-done.43, bf16[512,1024]{1,0:T(8,128)(2,1)} %get-tuple-element.588.refs_1_, ...), custom_call_target="tpu_custom_call" | custom-call | flops 4294967296 | bytes 16777216 | tf_op jit(solution)/shard_map/cond/branch_1_fun/column_grads/pallas_call | solution.py:1015
  264.5 34.1 %conditional.29 = (bf16[4,3,2,256,128]{4,3,2,1,0:T(8,128)(2,1)}, bf16[4,2,256,128]{3,2,1,0:T(8,128)(2,1)}, bf16[256,1024]{1,0:T(8,128)(2,1)}, bf16[512,1024]{1,0...) conditional(s32[]{:T(128)} %convert_element_type.170, ...), branch_computations={%region_18.19_spmd, %region_19.22_spmd} | conditional | flops 17179869184 | bytes 29884820 | solution.py:795
  267.7 30.9 %conditional = (bf16[4,3,2,256,128]{4,3,2,1,0:T(8,128)(2,1)}, bf16[4,2,256,128]{3,2,1,0:T(8,128)(2,1)}, bf16[256,1024]{1,0:T(8,128)(2,1)}, bf16[512,1024]{1,0:T(8,128)(2,1)}, bf16[512,1024]{1,0:T(8,128)(2,1)}) conditional(s32[]{:T(128)} %convert_element_type.126, () %tuple.115, (s32[2]{0:T(128)S(1)}, bf16[4,3,2,256,128]{4,3,2,1,0:T(8,128)(2,1)}, ...), branch_computations={%region_20.20_spmd, %region_21.21_spmd} | conditional | flops 17179869184 | bytes 21496000 | solution.py:795
  273.6 24.7 %attend_backward.2 = bf16[4,3,2,256,128]{4,3,2,1,0:T(8,128)(2,1)} custom-call(s32[2]{0:T(128)S(1)} %get-tuple-element.595.counts_ref, bf16[4,3,2,256,128]{4,3,2,1,0:T(8,128)(2,1)} %get-tuple-element.596.qkv_ref, f32[2048,128]{1,0:T(8,128)} %get-tuple-element.597.full_ref, bf16[2,2048,128]{2,1,0:T(8,128)(2,1)} %get-tuple-element.598.lse_ref, ...), custom_call_target="tpu_custom_call" | custom-call | flops 17179869184 | bytes 9437184 | tf_op jit(solution)/shard_map/cond/branch_1_fun/cond/branch_1_fun/attend_backward/pallas_call | solution.py:331
  300.7 36.7 %conditional.30 = (bf16[4,3,2,256,128]{4,3,2,1,0:T(8,128)(2,1)}, bf16[4,3,2,256,128]{4,3,2,1,0:T(8,128)(2,1)}, bf16[4,64,1024]{2,1,0:T(8,128)(2,1)}, bf16[4,64,1...) conditional(s32[]{:T(128)} %convert_element_type.170, () %tuple.202, ...), branch_computations={%region_22.23_spmd, %region_23.26_spmd} | conditional | flops 17179869184 | bytes 26738996 | solution.py:795
  304.8 29.1 %conditional.1 = (bf16[4,3,2,256,128]{4,3,2,1,0:T(8,128)(2,1)}, bf16[4,3,2,256,128]{4,3,2,1,0:T(8,128)(2,1)}) conditional(s32[]{:T(128)} %convert_element_type.127, () %tuple.121, (s32[2]{0:T(128)S(1)}, bf16[4,3,2,256,128]{4,3,2,1,0:T(8,128)(2,1)}, f32[2048,128]{1,0:T(8,128)}, bf16[2,2048,128]{2,1,0:T(8,128)(2,1)}, ...), branch_computations={%region_24.24_spmd, %region_25.25_spmd} | conditional | flops 17179869184 | bytes 14155824 | solution.py:795
  309.1 24.7 %attend_backward.3 = bf16[4,3,2,256,128]{4,3,2,1,0:T(8,128)(2,1)} custom-call(s32[2]{0:T(128)S(1)} %get-tuple-element.621.counts_ref, bf16[4,3,2,256,128]{4,3,2,1,0:T(8,128)(2,1)} %get-tuple-element.622.qkv_ref, f32[2048,128]{1,0:T(8,128)} %get-tuple-element.623.full_ref, bf16[2,2048,128]{2,1,0:T(8,128)(2,1)} %get-tuple-element.624.lse_ref, ...), custom_call_target="tpu_custom_call" | custom-call | flops 17179869184 | bytes 9437184 | tf_op jit(solution)/shard_map/cond/branch_1_fun/cond/branch_1_fun/attend_backward/pallas_call | solution.py:331
  339.8 24.6 %conditional.31 = (bf16[4,3,2,256,128]{4,3,2,1,0:T(8,128)(2,1)}, bf16[2,4,64,1024]{3,2,1,0:T(8,128)(2,1)}, bf16[2,4,64,1024]{3,2,1,0:T(8,128)(2,1)}, bf16[2,4,64...) conditional(s32[]{:T(128)} %convert_element_type.170, ...), branch_computations={%region_26.27_spmd, %region_27.28_spmd} | conditional | flops 4294967296 | bytes 38273240 | solution.py:795
  346.4 13.1 %column_grads.5 = (bf16[2,4,64,1024]{3,2,1,0:T(8,128)(2,1)}, bf16[2,4,64,1024]{3,2,1,0:T(8,128)(2,1)}, bf16[2,4,64,1024]{3,2,1,0:T(8,128)(2,1)}, bf16[2,4,64,1024]{3,2,1,0:T(8,128)(2,1)}) custom-call(s32[2]{0:T(128)S(1)} %get-tuple-element.641.place_ref, bf16[512,1024]{1,0:T(8,128)(2,1)} %get-tuple-element.642.refs_0_, ...), custom_call_target="tpu_custom_call" | custom-call | flops 4294967296 | bytes 16777216 | tf_op jit(solution)/shard_map/cond/branch_1_fun/column_grads/pallas_call | solution.py:1015
  364.4 65.5 %conditional.32 = (bf16[128,1024]{1,0:T(8,128)(2,1)S(1)}, bf16[128,1024]{1,0:T(8,128)(2,1)S(1)}, bf16[2,4,64,1024]{3,2,1,0:T(8,128)(2,1)}, bf16[2,4,64,1024]{3,2...) conditional(s32[]{:T(128)} %convert_element_type.170, ...), branch_computations={%region_28.29_spmd, %region_29.43_spmd} | conditional | flops 15032385536 | bytes 124257496 | solution.py:795
  366.0 26.2 %conditional.5 = (bf16[512,3072]{1,0:T(8,128)(2,1)}, bf16[512,3072]{1,0:T(8,128)(2,1)}, f32[512,1024]{1,0:T(8,128)}, bf16[512,1024]{1,0:T(8,128)(2,1)}, f32[1,10...) conditional(s32[]{:T(128)} %convert_element_type.131, () %tuple.145, ...), branch_computations={%region_31.31_spmd, %region_32.34_spmd} | conditional | flops 3221225472 | bytes 38797596 | solution.py:795
  368.3 18.3 %conditional.2 = (bf16[512,3072]{1,0:T(8,128)(2,1)}, bf16[512,3072]{1,0:T(8,128)(2,1)}, f32[512,1024]{1,0:T(8,128)}, bf16[512,1024]{1,0:T(8,128)(2,1)}, f32[1,1024]{1,0:T(1,128)}) conditional(s32[]{:T(128)} %convert_element_type.128, () %tuple.130, (f32[512,128]{1,0:T(8,128)}, f32[512,128]{1,0:T(8,128)S(1)}, f32[512,1024]{1,0:T(8,128)}, ...), branch_computations={%region_33.32_spmd, %region_34.33_spmd} | conditional | flops 3221225472 | bytes 30408784 | solution.py:795
  368.3 12.2 %projection_backward.1 = (bf16[512,3072]{1,0:T(8,128)(2,1)}, f32[512,1024]{1,0:T(8,128)}, bf16[512,1024]{1,0:T(8,128)(2,1)}, f32[1,1024]{1,0:T(1,128)}) custom-call(f32[512,128]{1,0:T(8,128)} %get-tuple-element.672.cos_ref, f32[512,128]{1,0:T(8,128)S(1)} %get-tuple-element.673.sin_ref, f32[512,1024]{1,0:T(8,128)} %get-tuple-element.674.x_ref, ...), custom_call_target="tpu_custom_call" | custom-call | flops 3221225472 | bytes 17825792 | tf_op jit(solution)/shard_map/cond/branch_1_fun/cond/branch_1_fun/cond/branch_1_fun/projection_backward/pallas_call | solution.py:747
  380.6 6.0 %collective-permute-done.21 = bf16[512,3072]{1,0:T(8,128)(2,1)} collective-permute-done((bf16[512,3072]{1,0:T(8,128)(2,1)}, bf16[512,3072]{1,0:T(8,128)(2,1)}, u32[]{:S(2)}, u32[]{:S(2)}) %collective-permute-start.21) | collective-permute-done | bytes 3145760 | tf_op jit(solution)/shard_map/cond/branch_1_fun/cond/branch_1_fun/cond/branch_1_fun/ppermute | solution.py:788
  393.9 13.1 %conditional.6 = (bf16[512,1024]{1,0:T(8,128)(2,1)}, bf16[2,4,64,768]{3,2,1,0:T(8,128)(2,1)}, bf16[2,4,64,768]{3,2,1,0:T(8,128)(2,1)}, bf16[2,4,64,768]{3,2,1,0:...) conditional(s32[]{:T(128)} %convert_element_type.131, ...), branch_computations={%region_35.35_spmd, %region_36.38_spmd} | conditional | flops 3221225472 | bytes 20971788 | solution.py:795
  396.2 9.1 %conditional.3 = (bf16[512,1024]{1,0:T(8,128)(2,1)}, bf16[2,4,64,768]{3,2,1,0:T(8,128)(2,1)}, bf16[2,4,64,768]{3,2,1,0:T(8,128)(2,1)}, bf16[2,4,64,768]{3,2,1,0:T(8,128)(2,1)}, bf16[2,4,64,768]{3,2,1,0:T(8,128)(2,1)}) conditional(s32[]{:T(128)} %convert_element_type.129, () %tuple.136, (bf16[512,1024]{1,0:T(8,128)(2,1)}, s32[2]{0:T(128)S(1)}, ...), branch_computations={%region_37.36_spmd, %region_38.37_spmd} | conditional | flops 3221225472 | bytes 16777296 | solution.py:795
  396.2 9.1 %column_grads.6 = (bf16[2,4,64,768]{3,2,1,0:T(8,128)(2,1)}, bf16[2,4,64,768]{3,2,1,0:T(8,128)(2,1)}, bf16[2,4,64,768]{3,2,1,0:T(8,128)(2,1)}, bf16[2,4,64,768]{3,2,1,0:T(8,128)(2,1)}) custom-call(s32[2]{0:T(128)S(1)} %get-tuple-element.701.place_ref, bf16[512,1024]{1,0:T(8,128)(2,1)} %get-tuple-element.702.refs_0_, ...), custom_call_target="tpu_custom_call" | custom-call | flops 3221225472 | bytes 12582912 | tf_op jit(solution)/shard_map/cond/branch_1_fun/cond/branch_1_fun/cond/branch_1_fun/column_grads/pallas_call | solution.py:1015
  407.0 21.8 %conditional.7 = (bf16[512,4096]{1,0:T(8,128)(2,1)}, bf16[2,4,64,1024]{3,2,1,0:T(8,128)(2,1)}, bf16[2,4,64,1024]{3,2,1,0:T(8,128)(2,1)}, bf16[2,4,64,1024]{3,2,1...) conditional(s32[]{:T(128)} %convert_element_type.131, ...), branch_computations={%region_39.39_spmd, %region_40.42_spmd} | conditional | flops 8589934592 | bytes 44040428 | solution.py:795
  408.9 20.0 %conditional.4 = (bf16[512,4096]{1,0:T(8,128)(2,1)}, bf16[2,4,64,1024]{3,2,1,0:T(8,128)(2,1)}, bf16[2,4,64,1024]{3,2,1,0:T(8,128)(2,1)}, bf16[2,4,64,1024]{3,2,1,0:T(8,128)(2,1)}, bf16[2,4,64,1024]{3,2,1,0:T(8,128)(2,1)}) conditional(s32[]{:T(128)} %convert_element_type.130, () %tuple.142, (f32[512,1024]{1,0:T(8,128)}, ...), branch_computations={%region_41.40_spmd, %region_42.41_spmd} | conditional | flops 8589934592 | bytes 37748776 | solution.py:795
  408.9 10.4 %hidden_gradient.1 = (bf16[512,1024]{1,0:T(8,128)(2,1)}, bf16[512,4096]{1,0:T(8,128)(2,1)}) custom-call(f32[512,1024]{1,0:T(8,128)} %get-tuple-element.724.up_ref, bf16[512,4096]{1,0:T(8,128)(2,1)} %get-tuple-element.725.slope_ref, bf16[4096,1024]{1,0:T(8,128)(2,1)} %get-tuple-element.726.wout_ref), custom_call_target="tpu_custom_call" | custom-call | flops 4294967296 | bytes 20971520 | tf_op jit(solution)/shard_map/cond/branch_1_fun/cond/branch_1_fun/cond/branch_1_fun/hidden_gradient/pallas_call | solution.py:495
  419.3 9.5 %out_grad.3 = (bf16[2,4,64,1024]{3,2,1,0:T(8,128)(2,1)}, bf16[2,4,64,1024]{3,2,1,0:T(8,128)(2,1)}, bf16[2,4,64,1024]{3,2,1,0:T(8,128)(2,1)}, bf16[2,4,64,1024]{3,2,1,0:T(8,128)(2,1)}) custom-call(s32[2]{0:T(128)S(1)} %get-tuple-element.728.place_ref, bf16[512,1024]{1,0:T(8,128)(2,1)} %get-tuple-element.729.up_own, ...), custom_call_target="tpu_custom_call" | custom-call | flops 4294967296 | bytes 16777216 | tf_op jit(solution)/shard_map/cond/branch_1_fun/cond/branch_1_fun/cond/branch_1_fun/out_grad/pallas_call | solution.py:912
  432.4 34.6 %conditional.33 = (bf16[128,1024]{1,0:T(8,128)(2,1)}, bf16[2,4,64,1024]{3,2,1,0:T(8,128)(2,1)}, bf16[2,4,64,1024]{3,2,1,0:T(8,128)(2,1)}, bf16[2,4,64,1024]{3,2,...) conditional(s32[]{:T(128)} %convert_element_type.170, ...), branch_computations={%region_43.44_spmd, %region_44.48_spmd} | conditional | flops 8590458880 | bytes 67895824 | solution.py:795
  436.6 30.4 %conditional.8 = (bf16[128,1024]{1,0:T(8,128)(2,1)}, bf16[2,4,64,1024]{3,2,1,0:T(8,128)(2,1)}, bf16[2,4,64,1024]{3,2,1,0:T(8,128)(2,1)}, bf16[2,4,64,1024]{3,2,1...) conditional(s32[]{:T(128)} %convert_element_type.132, ...), branch_computations={%region_45.45_spmd, %region_46.47_spmd} | conditional | flops 8590458880 | bytes 56361112 | solution.py:795
  439.7 11.8 %stream_gradient.1 = (bf16[512,1024]{1,0:T(8,128)(2,1)}, bf16[512,1024]{1,0:T(8,128)(2,1)}, f32[1,1024]{1,0:T(1,128)}) custom-call(bf16[512,1024]{1,0:T(8,128)(2,1)S(1)} %get-tuple-element.811.x_ref, f32[1,1024]{1,0:T(1,128)S(1)} %get-tuple-element.812.gain_ref, f32[512,1024]{1,0:T(8,128)} %get-tuple-element.813.up_ref, ...), custom_call_target="tpu_custom_call" | custom-call | flops 4294967296 | bytes 12582912 | tf_op jit(solution)/shard_map/cond/branch_1_fun/cond/branch_1_fun/stream_gradient/pallas_call | solution.py:540
  453.7 10.5 %column_grads.7 = (bf16[2,4,64,1024]{3,2,1,0:T(8,128)(2,1)}, bf16[2,4,64,1024]{3,2,1,0:T(8,128)(2,1)}, bf16[2,4,64,1024]{3,2,1,0:T(8,128)(2,1)}, bf16[2,4,64,1024]{3,2,1,0:T(8,128)(2,1)}) custom-call(s32[2]{0:T(128)S(1)} %get-tuple-element.802.place_ref, bf16[512,1024]{1,0:T(8,128)(2,1)} %get-tuple-element.803.refs_0_, ...), custom_call_target="tpu_custom_call" | custom-call | flops 4294967296 | bytes 16777216 | tf_op jit(solution)/shard_map/cond/branch_1_fun/cond/branch_1_fun/column_grads/pallas_call | solution.py:1015
  469.7 101.1 %conditional.34 = (bf16[128,1024]{1,0:T(8,128)(2,1)}, f32[6,1024]{1,0:T(8,128)S(1)}, f32[5,1024]{1,0:T(8,128)S(1)}, bf16[2,256,1024]{2,1,0:T(8,128)(2,1)}, bf16[...) conditional(s32[]{:T(128)} %convert_element_type.170, ...), branch_computations={%region_50.51_spmd, %region_51.68_spmd} | conditional | flops 13521410 | bytes 66676600 | solution.py:795
  472.4 15.1 %conditional.12 = (bf16[4,64,1024]{2,1,0:T(8,128)(2,1)}, bf16[4,64,1024]{2,1,0:T(8,128)(2,1)}) conditional(s32[]{:T(128)} %convert_element_type.133, () %tuple.172, (bf16[4,64,1024]{2,1,0:T(8,128)(2,1)}, bf16[4,64,1024]{2,1,0:T(8,128)(2,1)}) %tuple.173), branch_computations={%region_65.65_spmd, %region_66.66_spmd} | conditional | bytes 4194400 | solution.py:795
  475.5 10.9 %collective-permute-done.33 = bf16[4,64,1024]{2,1,0:T(8,128)(2,1)} collective-permute-done((bf16[4,64,1024]{2,1,0:T(8,128)(2,1)}, bf16[4,64,1024]{2,1,0:T(8,128)(2,1)}, u32[]{:S(2)}, u32[]{:S(2)}) %collective-permute-start.33) | collective-permute-done | bytes 524320 | tf_op jit(solution)/shard_map/cond/branch_1_fun/cond/branch_1_fun/ppermute | solution.py:788
  491.8 25.0 %conditional.9 = (bf16[2,4,64,1024]{3,2,1,0:T(8,128)(2,1)}, bf16[2,4,64,1024]{3,2,1,0:T(8,128)(2,1)}) conditional(s32[]{:T(128)} %convert_element_type.133, () %tuple.168, (bf16[2,4,64,1024]{3,2,1,0:T(8,128)(2,1)}, bf16[2,4,64,1024]{3,2,1,0:T(8,128)(2,1)}) %tuple.169), branch_computations={%region_52.52_spmd, %region_53.53_spmd} | conditional | bytes 8388704 | solution.py:795
  493.8 21.8 %collective-permute-done.29 = bf16[2,4,64,1024]{3,2,1,0:T(8,128)(2,1)} collective-permute-done((bf16[2,4,64,1024]{3,2,1,0:T(8,128)(2,1)}, bf16[2,4,64,1024]{3,2,1,0:T(8,128)(2,1)}, u32[]{:S(2)}, u32[]{:S(2)}) %collective-permute-start.29) | collective-permute-done | bytes 1048608 | tf_op jit(solution)/shard_map/cond/branch_1_fun/cond/branch_1_fun/ppermute | solution.py:788
  518.4 11.6 %conditional.10 = (bf16[4,64,1024]{2,1,0:T(8,128)(2,1)}, bf16[4,64,1024]{2,1,0:T(8,128)(2,1)}) conditional(s32[]{:T(128)} %convert_element_type.133, () %tuple.170, (bf16[4,64,1024]{2,1,0:T(8,128)(2,1)S(1)}, bf16[4,64,1024]{2,1,0:T(8,128)(2,1)S(1)}) %second_sums.7), branch_computations={%region_54.54_spmd, %region_55.55_spmd} | conditional | bytes 4194400 | solution.py:795
  519.6 10.0 %collective-permute-done.31 = bf16[4,64,1024]{2,1,0:T(8,128)(2,1)} collective-permute-done((bf16[4,64,1024]{2,1,0:T(8,128)(2,1)S(1)}, bf16[4,64,1024]{2,1,0:T(8,128)(2,1)}, u32[]{:S(2)}, u32[]{:S(2)}) %collective-permute-start.31) | collective-permute-done | bytes 524320 | tf_op jit(solution)/shard_map/cond/branch_1_fun/cond/branch_1_fun/ppermute | solution.py:788
  549.4 6.1 %collective-permute-done.46 = f32[11,1024]{1,0:T(8,128)S(1)} collective-permute-done((f32[11,1024]{1,0:T(8,128)S(1)}, f32[11,1024]{1,0:T(8,128)S(1)}, u32[]{:S(2)}, u32[]{:S(2)}) %collective-permute-start.46) | collective-permute-done | bytes 45088 | tf_op jit(solution)/shard_map/cond/branch_1_fun/ppermute | solution.py:788
  (322 shorter events, 234.2 us)
Async XLA Ops:
  9.6 27.4 %collective-permute-start.35 = (bf16[256,1024]{1,0:T(8,128)(2,1)S(1)}, bf16[256,1024]{1,0:T(8,128)(2,1)}, u32[]{:S(2)}, u32[]{:S(2)}) collective-permute-start(bf16[256,1024]{1,0:T(8,128)(2,1)S(1)} %dynamic-slice_bitcast_fusion), channel_id=1, source_target_pairs={{0,4},{1,5},{2,6},{3,7},{4,0},{5,1},{6,2},{7,3},{8,12},{9,13},{10,... | collective-permute-start | bytes 1572872 | tf_op jit(solution)/shard_map/cond/branch_1_fun/ppermute | solution.py:788
  54.5 24.6 %all-to-all-start.6 = ((bf16[4,3,2,256,128]{4,3,2,1,0:T(8,128)(2,1)}), bf16[4,3,2,256,128]{4,3,2,1,0:T(8,128)(2,1)}, u32[]{:S(2)}, u32[]{:S(2)}) async-start(bf16[4,3,2,256,128]{4,3,2,1,0:T(8,128)(2,1)} %get-tuple-element.1045), calls=%async_computation.11 | async-start | bytes 3145728 | tf_op jit(solution)/shard_map/all_to_all | solution.py:820
  79.1 24.8 %collective-permute-start = (bf16[512,4096]{1,0:T(8,128)(2,1)}, bf16[512,4096]{1,0:T(8,128)(2,1)}, u32[]{:S(2)}, u32[]{:S(2)}) collective-permute-start(bf16[512,4096]{1,0:T(8,128)(2,1)} %get-tuple-element.549), channel_id=1, source_target_pairs={{0,1},{1,0},{2,3},{3,2},{4,5},{5,4},{6,7},{7,6},{8,9},{9,8},{10,11... | collective-permute-start | bytes 12582920 | tf_op jit(solution)/shard_map/cond/branch_1_fun/ppermute | solution.py:788
  79.1 24.8 %all-to-all-start = ((bf16[4,3,2,256,128]{4,3,2,1,0:T(8,128)(2,1)}), bf16[4,3,2,256,128]{4,3,2,1,0:T(8,128)(2,1)}, u32[]{:S(2)}, u32[]{:S(2)}) async-start(bf16[4,3,2,256,128]{4,3,2,1,0:T(8,128)(2,1)} %get-tuple-element.548), calls=%async_computation | async-start | bytes 3145728 | tf_op jit(solution)/shard_map/cond/branch_1_fun/all_to_all | solution.py:820
  83.8 19.4 %collective-permute-start.1 = (bf16[512,1024]{1,0:T(8,128)(2,1)}, bf16[512,1024]{1,0:T(8,128)(2,1)}, u32[]{:S(2)}, u32[]{:S(2)}) collective-permute-start(bf16[512,1024]{1,0:T(8,128)(2,1)} %get-tuple-element.550), channel_id=1, source_target_pairs={{0,1},{1,0},{2,3},{3,2},{4,5},{5,4},{6,7},{7,6},{8,9},{9,8},{10,11... | collective-permute-start | bytes 3145736 | tf_op jit(solution)/shard_map/cond/branch_1_fun/ppermute | solution.py:788
  84.4 18.9 %collective-permute-start.2 = (bf16[512,1024]{1,0:T(8,128)(2,1)}, bf16[512,1024]{1,0:T(8,128)(2,1)}, u32[]{:S(2)}, u32[]{:S(2)}) collective-permute-start(bf16[512,1024]{1,0:T(8,128)(2,1)} %get-tuple-element.551), channel_id=1, source_target_pairs={{0,1},{1,0},{2,3},{3,2},{4,5},{5,4},{6,7},{7,6},{8,9},{9,8},{10,11... | collective-permute-start | bytes 3145736 | tf_op jit(solution)/shard_map/cond/branch_1_fun/ppermute | solution.py:788
  104.0 30.8 %all-to-all-start.5 = ((bf16[4,2,256,128]{3,2,1,0:T(8,128)(2,1)}), bf16[4,2,256,128]{3,2,1,0:T(8,128)(2,1)}, u32[]{:S(2)}, u32[]{:S(2)}) async-start(bf16[4,2,256,128]{3,2,1,0:T(8,128)(2,1)} %get-tuple-element.557), calls=%async_computation.5 | async-start | bytes 1048576 | tf_op jit(solution)/shard_map/cond/branch_1_fun/all_to_all | solution.py:820
  108.2 26.6 %collective-permute-start.36 = (bf16[256,1024]{1,0:T(8,128)(2,1)S(1)}, bf16[256,1024]{1,0:T(8,128)(2,1)}, u32[]{:S(2)}, u32[]{:S(2)}) collective-permute-start(bf16[256,1024]{1,0:T(8,128)(2,1)S(1)} %dynamic-slice_bitcast_fusion.1), channel_id=1, source_target_pairs={{0,4},{1,5},{2,6},{3,7},{4,0},{5,1},{6,2},{7,3},{8,12},{9,13},{10,... | collective-permute-start | bytes 1572872 | tf_op jit(solution)/shard_map/cond/branch_1_fun/ppermute | solution.py:788
  190.0 18.0 %collective-permute-start.3 = (bf16[512,4096]{1,0:T(8,128)(2,1)}, bf16[512,4096]{1,0:T(8,128)(2,1)}, u32[]{:S(2)}, u32[]{:S(2)}) collective-permute-start(bf16[512,4096]{1,0:T(8,128)(2,1)} %get-tuple-element.570), channel_id=1, source_target_pairs={{0,1},{1,0},{2,3},{3,2},{4,5},{5,4},{6,7},{7,6},{8,9},{9,8},{10,11... | collective-permute-start | bytes 12582920 | tf_op jit(solution)/shard_map/cond/branch_1_fun/ppermute | solution.py:788
  190.0 18.0 %collective-permute-start.4 = (bf16[512,1024]{1,0:T(8,128)(2,1)S(1)}, bf16[512,1024]{1,0:T(8,128)(2,1)}, u32[]{:S(2)}, u32[]{:S(2)}) collective-permute-start(bf16[512,1024]{1,0:T(8,128)(2,1)S(1)} %get-tuple-element.571), channel_id=1, source_target_pairs={{0,1},{1,0},{2,3},{3,2},{4,5},{5,4},{6,7},{7,6},{8,9},{9,8},{10,11... | collective-permute-start | bytes 3145736 | tf_op jit(solution)/shard_map/cond/branch_1_fun/ppermute | solution.py:788
  214.7 24.9 %collective-permute-start.53 = (bf16[512,4096]{1,0:T(8,128)(2,1)}, bf16[512,4096]{1,0:T(8,128)(2,1)}, u32[]{:S(2)}, u32[]{:S(2)}) collective-permute-start(bf16[512,4096]{1,0:T(8,128)(2,1)} %get-tuple-element.1069), channel_id=1, source_target_pairs={{0,1},{1,0},{2,3},{3,2},{4,5},{5,4},{6,7},{7,6},{8,9},{9,8},{10,11... | collective-permute-start | bytes 12582920 | tf_op jit(solution)/shard_map/ppermute | solution.py:788
  217.9 21.7 %collective-permute-start.52 = (bf16[512,1024]{1,0:T(8,128)(2,1)}, bf16[512,1024]{1,0:T(8,128)(2,1)}, u32[]{:S(2)}, u32[]{:S(2)}) collective-permute-start(bf16[512,1024]{1,0:T(8,128)(2,1)} %get-tuple-element.1066), channel_id=1, source_target_pairs={{0,1},{1,0},{2,3},{3,2},{4,5},{5,4},{6,7},{7,6},{8,9},{9,8},{10,11... | collective-permute-start | bytes 3145736 | tf_op jit(solution)/shard_map/ppermute | solution.py:788
  239.6 24.9 %collective-permute-start.5 = (bf16[512,1024]{1,0:T(8,128)(2,1)}, bf16[512,1024]{1,0:T(8,128)(2,1)}, u32[]{:S(2)}, u32[]{:S(2)}) collective-permute-start(bf16[512,1024]{1,0:T(8,128)(2,1)} %get-tuple-element.572), channel_id=1, source_target_pairs={{0,1},{1,0},{2,3},{3,2},{4,5},{5,4},{6,7},{7,6},{8,9},{9,8},{10,11... | collective-permute-start | bytes 3145736 | tf_op jit(solution)/shard_map/cond/branch_1_fun/ppermute | solution.py:788
  239.8 24.7 %collective-permute-start.6 = (bf16[512,1024]{1,0:T(8,128)(2,1)}, bf16[512,1024]{1,0:T(8,128)(2,1)}, u32[]{:S(2)}, u32[]{:S(2)}) collective-permute-start(bf16[512,1024]{1,0:T(8,128)(2,1)} %get-tuple-element.573), channel_id=1, source_target_pairs={{0,1},{1,0},{2,3},{3,2},{4,5},{5,4},{6,7},{7,6},{8,9},{9,8},{10,11... | collective-permute-start | bytes 3145736 | tf_op jit(solution)/shard_map/cond/branch_1_fun/ppermute | solution.py:788
  240.2 24.3 %collective-permute-start.7 = (bf16[512,1024]{1,0:T(8,128)(2,1)}, bf16[512,1024]{1,0:T(8,128)(2,1)}, u32[]{:S(2)}, u32[]{:S(2)}) collective-permute-start(bf16[512,1024]{1,0:T(8,128)(2,1)} %get-tuple-element.574), channel_id=1, source_target_pairs={{0,1},{1,0},{2,3},{3,2},{4,5},{5,4},{6,7},{7,6},{8,9},{9,8},{10,11... | collective-permute-start | bytes 3145736 | tf_op jit(solution)/shard_map/cond/branch_1_fun/ppermute | solution.py:788
  240.3 24.2 %collective-permute-start.8 = (bf16[512,1024]{1,0:T(8,128)(2,1)}, bf16[512,1024]{1,0:T(8,128)(2,1)}, u32[]{:S(2)}, u32[]{:S(2)}) collective-permute-start(bf16[512,1024]{1,0:T(8,128)(2,1)} %get-tuple-element.575), channel_id=1, source_target_pairs={{0,1},{1,0},{2,3},{3,2},{4,5},{5,4},{6,7},{7,6},{8,9},{9,8},{10,11... | collective-permute-start | bytes 3145736 | tf_op jit(solution)/shard_map/cond/branch_1_fun/ppermute | solution.py:788
  240.7 23.8 %collective-permute-start.9 = (bf16[512,1024]{1,0:T(8,128)(2,1)}, bf16[512,1024]{1,0:T(8,128)(2,1)}, u32[]{:S(2)}, u32[]{:S(2)}) collective-permute-start(bf16[512,1024]{1,0:T(8,128)(2,1)} %get-tuple-element.576), channel_id=1, source_target_pairs={{0,1},{1,0},{2,3},{3,2},{4,5},{5,4},{6,7},{7,6},{8,9},{9,8},{10,11... | collective-permute-start | bytes 3145736 | tf_op jit(solution)/shard_map/cond/branch_1_fun/ppermute | solution.py:788
  240.8 23.6 %all-to-all-start.1 = ((bf16[4,2,256,128]{3,2,1,0:T(8,128)(2,1)}), bf16[4,2,256,128]{3,2,1,0:T(8,128)(2,1)}, u32[]{:S(2)}, u32[]{:S(2)}) async-start(bf16[4,2,256,128]{3,2,1,0:T(8,128)(2,1)} %get-tuple-element.577), calls=%async_computation.1 | async-start | bytes 1048576 | tf_op jit(solution)/shard_map/cond/branch_1_fun/all_to_all | solution.py:820
  264.5 34.1 %collective-permute-start.13 = (bf16[2,4,64,1024]{3,2,1,0:T(8,128)(2,1)}, bf16[2,4,64,1024]{3,2,1,0:T(8,128)(2,1)}, u32[]{:S(2)}, u32[]{:S(2)}) collective-permute-start(bf16[2,4,64,1024]{3,2,1,0:T(8,128)(2,1)} %get-tuple-element.619), channel_id=1, source_target_pairs={{0,8},{1,9},{2,10},{3,11},{4,12},{5,13},{6,14},{7,15},{8,0},{9,1},... | collective-permute-start | bytes 3145736 | tf_op jit(solution)/shard_map/cond/branch_1_fun/ppermute | solution.py:788
  266.2 32.5 %collective-permute-start.14 = (bf16[2,4,64,1024]{3,2,1,0:T(8,128)(2,1)}, bf16[2,4,64,1024]{3,2,1,0:T(8,128)(2,1)}, u32[]{:S(2)}, u32[]{:S(2)}) collective-permute-start(bf16[2,4,64,1024]{3,2,1,0:T(8,128)(2,1)} %get-tuple-element.620), channel_id=1, source_target_pairs={{0,16},{1,17},{2,18},{3,19},{4,20},{5,21},{6,22},{7,23},{8,24},{9,... | collective-permute-start | bytes 3145736 | tf_op jit(solution)/shard_map/cond/branch_1_fun/ppermute | solution.py:788
  267.7 30.9 %all-to-all-start.2 = ((bf16[4,2,256,128]{3,2,1,0:T(8,128)(2,1)}), bf16[4,2,256,128]{3,2,1,0:T(8,128)(2,1)}, u32[]{:S(2)}, u32[]{:S(2)}) async-start(bf16[4,2,256,128]{3,2,1,0:T(8,128)(2,1)} %get-tuple-element.600), calls=%async_computation.2 | async-start | bytes 1048576 | tf_op jit(solution)/shard_map/cond/branch_1_fun/cond/branch_1_fun/all_to_all | solution.py:820
  271.8 26.8 %collective-permute-start.10 = (bf16[256,1024]{1,0:T(8,128)(2,1)}, bf16[256,1024]{1,0:T(8,128)(2,1)}, u32[]{:S(2)}, u32[]{:S(2)}) collective-permute-start(bf16[256,1024]{1,0:T(8,128)(2,1)} %get-tuple-element.601), channel_id=1, source_target_pairs={{0,4},{1,5},{2,6},{3,7},{4,0},{5,1},{6,2},{7,3},{8,12},{9,13},{10,... | collective-permute-start | bytes 1572872 | tf_op jit(solution)/shard_map/cond/branch_1_fun/cond/branch_1_fun/ppermute | solution.py:788
  273.1 25.5 %collective-permute-start.11 = (bf16[512,1024]{1,0:T(8,128)(2,1)}, bf16[512,1024]{1,0:T(8,128)(2,1)}, u32[]{:S(2)}, u32[]{:S(2)}) collective-permute-start(bf16[512,1024]{1,0:T(8,128)(2,1)} %get-tuple-element.602), channel_id=1, source_target_pairs={{0,1},{1,0},{2,3},{3,2},{4,5},{5,4},{6,7},{7,6},{8,9},{9,8},{10,11... | collective-permute-start | bytes 3145736 | tf_op jit(solution)/shard_map/cond/branch_1_fun/cond/branch_1_fun/ppermute | solution.py:788
  273.2 25.4 %collective-permute-start.12 = (bf16[512,1024]{1,0:T(8,128)(2,1)}, bf16[512,1024]{1,0:T(8,128)(2,1)}, u32[]{:S(2)}, u32[]{:S(2)}) collective-permute-start(bf16[512,1024]{1,0:T(8,128)(2,1)} %get-tuple-element.603), channel_id=1, source_target_pairs={{0,1},{1,0},{2,3},{3,2},{4,5},{5,4},{6,7},{7,6},{8,9},{9,8},{10,11... | collective-permute-start | bytes 3145736 | tf_op jit(solution)/shard_map/cond/branch_1_fun/cond/branch_1_fun/ppermute | solution.py:788
  300.7 36.7 %collective-permute-start.17 = (bf16[2,4,64,1024]{3,2,1,0:T(8,128)(2,1)}, bf16[2,4,64,1024]{3,2,1,0:T(8,128)(2,1)}, u32[]{:S(2)}, u32[]{:S(2)}) collective-permute-start(bf16[2,4,64,1024]{3,2,1,0:T(8,128)(2,1)} %get-tuple-element.638), channel_id=1, source_target_pairs={{0,8},{1,9},{2,10},{3,11},{4,12},{5,13},{6,14},{7,15},{8,0},{9,1},... | collective-permute-start | bytes 3145736 | tf_op jit(solution)/shard_map/cond/branch_1_fun/ppermute | solution.py:788
  301.2 36.1 %collective-permute-start.18 = (bf16[2,4,64,1024]{3,2,1,0:T(8,128)(2,1)}, bf16[2,4,64,1024]{3,2,1,0:T(8,128)(2,1)}, u32[]{:S(2)}, u32[]{:S(2)}) collective-permute-start(bf16[2,4,64,1024]{3,2,1,0:T(8,128)(2,1)} %get-tuple-element.639), channel_id=1, source_target_pairs={{0,16},{1,17},{2,18},{3,19},{4,20},{5,21},{6,22},{7,23},{8,24},{9,... | collective-permute-start | bytes 3145736 | tf_op jit(solution)/shard_map/cond/branch_1_fun/ppermute | solution.py:788
  301.7 35.7 %collective-permute-start.15 = (bf16[4,64,1024]{2,1,0:T(8,128)(2,1)}, bf16[4,64,1024]{2,1,0:T(8,128)(2,1)}, u32[]{:S(2)}, u32[]{:S(2)}) collective-permute-start(bf16[4,64,1024]{2,1,0:T(8,128)(2,1)} %get-tuple-element.636), channel_id=1, source_target_pairs={{0,16},{1,17},{2,18},{3,19},{4,20},{5,21},{6,22},{7,23},{8,24},{9,... | collective-permute-start | bytes 1572872 | tf_op jit(solution)/shard_map/cond/branch_1_fun/ppermute | solution.py:788
  303.3 34.1 %collective-permute-start.16 = (bf16[4,64,1024]{2,1,0:T(8,128)(2,1)}, bf16[4,64,1024]{2,1,0:T(8,128)(2,1)}, u32[]{:S(2)}, u32[]{:S(2)}) collective-permute-start(bf16[4,64,1024]{2,1,0:T(8,128)(2,1)} %get-tuple-element.637), channel_id=1, source_target_pairs={{0,8},{1,9},{2,10},{3,11},{4,12},{5,13},{6,14},{7,15},{8,0},{9,1},... | collective-permute-start | bytes 1572872 | tf_op jit(solution)/shard_map/cond/branch_1_fun/ppermute | solution.py:788
  304.8 29.1 %all-to-all-start.3 = ((bf16[4,3,2,256,128]{4,3,2,1,0:T(8,128)(2,1)}), bf16[4,3,2,256,128]{4,3,2,1,0:T(8,128)(2,1)}, u32[]{:S(2)}, u32[]{:S(2)}) async-start(bf16[4,3,2,256,128]{4,3,2,1,0:T(8,128)(2,1)} %get-tuple-element.626), calls=%async_computation.3 | async-start | bytes 3145728 | tf_op jit(solution)/shard_map/cond/branch_1_fun/cond/branch_1_fun/all_to_all | solution.py:820
  339.8 24.6 %all-to-all-start.4 = ((bf16[4,3,2,256,128]{4,3,2,1,0:T(8,128)(2,1)}), bf16[4,3,2,256,128]{4,3,2,1,0:T(8,128)(2,1)}, u32[]{:S(2)}, u32[]{:S(2)}) async-start(bf16[4,3,2,256,128]{4,3,2,1,0:T(8,128)(2,1)} %get-tuple-element.640), calls=%async_computation.4 | async-start | bytes 3145728 | tf_op jit(solution)/shard_map/cond/branch_1_fun/all_to_all | solution.py:820
  344.3 15.2 %collective-permute-start.19 = (bf16[4,64,1024]{2,1,0:T(8,128)(2,1)}, bf16[4,64,1024]{2,1,0:T(8,128)(2,1)S(1)}, u32[]{:S(2)}, u32[]{:S(2)}) collective-permute-start(bf16[4,64,1024]{2,1,0:T(8,128)(2,1)} %get-tuple-element.668), channel_id=1, source_target_pairs={{0,16},{1,17},{2,18},{3,19},{4,20},{5,21},{6,22},{7,23},{8,24},{9,... | collective-permute-start | bytes 1572872 | tf_op jit(solution)/shard_map/cond/branch_1_fun/ppermute | solution.py:788
  364.4 64.4 %reduce-scatter.6.cloned.1.call-start = ((), (), s32[]{:S(2)}) async-start(), calls=%async_computation.13 | async-start | bytes 2621440 | tf_op jit(solution)/shard_map/cond/branch_1_fun/reduce_scatter | solution.py:1135
  366.0 25.1 %collective-permute-start.22 = (bf16[2,4,64,1024]{3,2,1,0:T(8,128)(2,1)}, bf16[2,4,64,1024]{3,2,1,0:T(8,128)(2,1)}, u32[]{:S(2)}, u32[]{:S(2)}) collective-permute-start(bf16[2,4,64,1024]{3,2,1,0:T(8,128)(2,1)} %get-tuple-element.698), channel_id=1, source_target_pairs={{0,8},{1,9},{2,10},{3,11},{4,12},{5,13},{6,14},{7,15},{8,0},{9,1},... | collective-permute-start | bytes 3145736 | tf_op jit(solution)/shard_map/cond/branch_1_fun/cond/branch_1_fun/ppermute | solution.py:788
  367.5 24.7 %collective-permute-start.23 = (bf16[2,4,64,1024]{3,2,1,0:T(8,128)(2,1)}, bf16[2,4,64,1024]{3,2,1,0:T(8,128)(2,1)}, u32[]{:S(2)}, u32[]{:S(2)}) collective-permute-start(bf16[2,4,64,1024]{3,2,1,0:T(8,128)(2,1)} %get-tuple-element.699), channel_id=1, source_target_pairs={{0,16},{1,17},{2,18},{3,19},{4,20},{5,21},{6,22},{7,23},{8,24},{9,... | collective-permute-start | bytes 3145736 | tf_op jit(solution)/shard_map/cond/branch_1_fun/cond/branch_1_fun/ppermute | solution.py:788
  407.0 21.8 %collective-permute-start.27 = (bf16[2,4,64,768]{3,2,1,0:T(8,128)(2,1)}, bf16[2,4,64,768]{3,2,1,0:T(8,128)(2,1)}, u32[]{:S(2)}, u32[]{:S(2)}) collective-permute-start(bf16[2,4,64,768]{3,2,1,0:T(8,128)(2,1)} %get-tuple-element.750), channel_id=1, source_target_pairs={{0,8},{1,9},{2,10},{3,11},{4,12},{5,13},{6,14},{7,15},{8,0},{9,1},... | collective-permute-start | bytes 2359304 | tf_op jit(solution)/shard_map/cond/branch_1_fun/cond/branch_1_fun/ppermute | solution.py:788
  408.4 20.4 %collective-permute-start.28 = (bf16[2,4,64,768]{3,2,1,0:T(8,128)(2,1)}, bf16[2,4,64,768]{3,2,1,0:T(8,128)(2,1)}, u32[]{:S(2)}, u32[]{:S(2)}) collective-permute-start(bf16[2,4,64,768]{3,2,1,0:T(8,128)(2,1)} %get-tuple-element.751), channel_id=1, source_target_pairs={{0,16},{1,17},{2,18},{3,19},{4,20},{5,21},{6,22},{7,23},{8,24},{9,... | collective-permute-start | bytes 2359304 | tf_op jit(solution)/shard_map/cond/branch_1_fun/cond/branch_1_fun/ppermute | solution.py:788
  432.4 34.5 %collective-permute-start.38 = (bf16[2,4,64,1024]{3,2,1,0:T(8,128)(2,1)}, bf16[2,4,64,1024]{3,2,1,0:T(8,128)(2,1)}, u32[]{:S(2)}, u32[]{:S(2)}) collective-permute-start(bf16[2,4,64,1024]{3,2,1,0:T(8,128)(2,1)} %get-tuple-element.841), channel_id=1, source_target_pairs={{0,8},{1,9},{2,10},{3,11},{4,12},{5,13},{6,14},{7,15},{8,0},{9,1},... | collective-permute-start | bytes 3145736 | tf_op jit(solution)/shard_map/cond/branch_1_fun/ppermute | solution.py:788
  433.8 33.2 %collective-permute-start.39 = (bf16[2,4,64,1024]{3,2,1,0:T(8,128)(2,1)}, bf16[2,4,64,1024]{3,2,1,0:T(8,128)(2,1)}, u32[]{:S(2)}, u32[]{:S(2)}) collective-permute-start(bf16[2,4,64,1024]{3,2,1,0:T(8,128)(2,1)} %get-tuple-element.842), channel_id=1, source_target_pairs={{0,16},{1,17},{2,18},{3,19},{4,20},{5,21},{6,22},{7,23},{8,24},{9,... | collective-permute-start | bytes 3145736 | tf_op jit(solution)/shard_map/cond/branch_1_fun/ppermute | solution.py:788
  434.7 32.3 %collective-permute-start.40 = (bf16[4,64,768]{2,1,0:T(8,128)(2,1)S(1)}, bf16[4,64,768]{2,1,0:T(8,128)(2,1)}, u32[]{:S(2)}, u32[]{:S(2)}) collective-permute-start(bf16[4,64,768]{2,1,0:T(8,128)(2,1)S(1)} %get-tuple-element.843), channel_id=1, source_target_pairs={{0,16},{1,17},{2,18},{3,19},{4,20},{5,21},{6,22},{7,23},{8,24},{9,... | collective-permute-start | bytes 1179656 | tf_op jit(solution)/shard_map/cond/branch_1_fun/ppermute | solution.py:788
  435.8 31.1 %collective-permute-start.41 = (bf16[4,64,768]{2,1,0:T(8,128)(2,1)}, bf16[4,64,768]{2,1,0:T(8,128)(2,1)}, u32[]{:S(2)}, u32[]{:S(2)}) collective-permute-start(bf16[4,64,768]{2,1,0:T(8,128)(2,1)} %get-tuple-element.844), channel_id=1, source_target_pairs={{0,8},{1,9},{2,10},{3,11},{4,12},{5,13},{6,14},{7,15},{8,0},{9,1},... | collective-permute-start | bytes 1179656 | tf_op jit(solution)/shard_map/cond/branch_1_fun/ppermute | solution.py:788
  436.6 30.4 %reduce-scatter.8.cloned.1.call-start = ((), (), s32[]{:S(2)}) async-start(), calls=%async_computation.14 | async-start | bytes 1310720 | tf_op jit(solution)/shard_map/cond/branch_1_fun/cond/branch_1_fun/reduce_scatter | solution.py:1135
  436.6 17.1 %collective-permute-start.37 = (bf16[512,4096]{1,0:T(8,128)(2,1)}, bf16[512,4096]{1,0:T(8,128)(2,1)}, u32[]{:S(2)}, u32[]{:S(2)}) collective-permute-start(bf16[512,4096]{1,0:T(8,128)(2,1)} %get-tuple-element.805.refs_2_.grad_ref), channel_id=1, source_target_pairs={{0,1},{1,0},{2,3},{3,2},{4,5},{5,4},{6,7},{7,6},{8,9},{9,8},{10,11... | collective-permute-start | bytes 12582920 | tf_op jit(solution)/shard_map/cond/branch_1_fun/cond/branch_1_fun/ppermute | solution.py:788
  469.7 97.5 %reduce-scatter.12.cloned.1.call-start = ((), (), s32[]{:S(2)}) async-start(), calls=%async_computation.16 | async-start | bytes 983040 | tf_op jit(solution)/shard_map/cond/branch_1_fun/reduce_scatter | solution.py:1135
  472.4 96.5 %reduce-scatter.14.cloned.1.call-start = ((), (), s32[]{:S(2)}) async-start(), calls=%async_computation.17 | async-start | bytes 1310720 | tf_op jit(solution)/shard_map/cond/branch_1_fun/reduce_scatter | solution.py:1135
  490.4 80.4 %reduce-scatter.10.cloned.1.call-start = ((), (), s32[]{:S(2)}) async-start(), calls=%async_computation.15 | async-start | bytes 1310720 | tf_op jit(solution)/shard_map/cond/branch_1_fun/reduce_scatter | solution.py:1135
  490.4 39.7 %collective-permute-start.42 = (bf16[256,1024]{1,0:T(8,128)(2,1)}, bf16[256,1024]{1,0:T(8,128)(2,1)}, u32[]{:S(2)}, u32[]{:S(2)}) collective-permute-start(bf16[256,1024]{1,0:T(8,128)(2,1)} %get-tuple-element.867), channel_id=1, source_target_pairs={{0,4},{1,5},{2,6},{3,7},{4,0},{5,1},{6,2},{7,3},{8,12},{9,13},{10,... | collective-permute-start | bytes 1572872 | tf_op jit(solution)/shard_map/cond/branch_1_fun/ppermute | solution.py:788
  491.8 23.8 %collective-permute-start.29 = (bf16[2,4,64,1024]{3,2,1,0:T(8,128)(2,1)}, bf16[2,4,64,1024]{3,2,1,0:T(8,128)(2,1)}, u32[]{:S(2)}, u32[]{:S(2)}) collective-permute-start(bf16[2,4,64,1024]{3,2,1,0:T(8,128)(2,1)} %get-tuple-element.845), channel_id=1, source_target_pairs={{0,8},{1,9},{2,10},{3,11},{4,12},{5,13},{6,14},{7,15},{8,0},{9,1},... | collective-permute-start | bytes 3145736 | tf_op jit(solution)/shard_map/cond/branch_1_fun/cond/branch_1_fun/ppermute | solution.py:788
  493.2 23.5 %collective-permute-start.30 = (bf16[2,4,64,1024]{3,2,1,0:T(8,128)(2,1)}, bf16[2,4,64,1024]{3,2,1,0:T(8,128)(2,1)}, u32[]{:S(2)}, u32[]{:S(2)}) collective-permute-start(bf16[2,4,64,1024]{3,2,1,0:T(8,128)(2,1)} %get-tuple-element.846), channel_id=1, source_target_pairs={{0,16},{1,17},{2,18},{3,19},{4,20},{5,21},{6,22},{7,23},{8,24},{9,... | collective-permute-start | bytes 3145736 | tf_op jit(solution)/shard_map/cond/branch_1_fun/cond/branch_1_fun/ppermute | solution.py:788
  (64 other events, 606.9 us)
Sparse Core Ops, SparseCore 0:
  367.6 43.6 reduce-scatter.5
  440.4 26.5 reduce-scatter.7
  472.9 23.4 reduce-scatter.11
  498.6 34.9 reduce-scatter.13
  535.8 29.0 reduce-scatter.9

commit v6 on v5

--- a/solution.py
+++ b/solution.py
@@ -211,7 +211,8 @@
             result = jnp.where(head_lanes(mine.shape, head, size), mine, result)
         lse = tops[head] + jnp.log(jnp.broadcast_to(total, (BLOCK, LANES)))
         spread = spread_columns(split_three(lse), (BLOCK, LANES))
-        lse_ref[head] = jnp.where(lane < 3, -spread, shifted).astype(BF16)
+        lse_ref[head, :, :LANES] = queries[head][:, :LANES]
+        lse_ref[head, :, LANES:] = jnp.where(lane < 3, -spread, shifted).astype(BF16)
     full_ref[...] = result
     out_ref[...] = result.astype(BF16).reshape(out_ref.shape)
 
@@ -229,12 +230,12 @@
         out_specs=[
             pl.BlockSpec((per, 1, frames, LANES), lambda i: (i % each, i // each, 0, 0)),
             pl.BlockSpec((BLOCK, LANES), lambda i: (i, 0)),
-            pl.BlockSpec((heads, BLOCK, LANES), lambda i: (0, i, 0)),
+            pl.BlockSpec((heads, BLOCK, 2 * LANES), lambda i: (0, i, 0)),
         ],
         out_shape=[
             jax.ShapeDtypeStruct((places, chunks, frames, LANES), BF16),
             jax.ShapeDtypeStruct((group, LANES), F32),
-            jax.ShapeDtypeStruct((heads, group, LANES), BF16),
+            jax.ShapeDtypeStruct((heads, group, 2 * LANES), BF16),
         ],
         scratch_shapes=[
             pltpu.VMEM((group, 2 * LANES), BF16),
@@ -248,8 +249,8 @@
 
 
 def attn_bwd_kernel(
-    heads, size, group, counts_ref, qkv_ref, full_ref, lse_ref, grad_ref, out_ref,
-    qcat, gcat, k_turned, dq_turned,
+    heads, size, group, counts_ref, qkv_ref, full_ref, qcat, grad_ref, out_ref,
+    gcat, k_turned, dq_turned,
 ):
     step = pl.program_id(0)
     counts = (counts_ref[0], counts_ref[1])
@@ -269,15 +270,12 @@
 
         def prepare(j, _):
             rows = pl.ds(pl.multiple_of(j * BLOCK, BLOCK), BLOCK)
-            q = chunk_rows(qkv_ref, (0,), j).astype(F32) * (size ** -0.5)
             g = chunk_rows(grad_ref, (), j).astype(F32)
             product = g * full_ref[rows, :]
             for head in range(heads):
                 own = head_lanes((BLOCK, LANES), head, size)
                 delta = jnp.sum(jnp.where(own, product, 0.0), 1, keepdims=True)
                 delta = jnp.broadcast_to(delta, (BLOCK, LANES))
-                qcat[head, rows, :LANES] = jnp.where(own, q, 0.0).astype(BF16)
-                qcat[head, rows, LANES:] = lse_ref[head, rows, :]
                 gcat[head, rows, :LANES] = jnp.where(own, g, 0.0).astype(BF16)
                 spread = spread_columns(split_three(delta), (BLOCK, LANES))
                 gcat[head, rows, LANES:] = (-spread).astype(BF16)
@@ -341,7 +339,6 @@
         out_specs=whole(qkv.shape),
         out_shape=jax.ShapeDtypeStruct(qkv.shape, BF16),
         scratch_shapes=[
-            pltpu.VMEM((heads, group, 2 * LANES), BF16),
             pltpu.VMEM((heads, group, 2 * LANES), BF16),
             pltpu.VMEM((steps, LANES, BLOCK), BF16),
             pltpu.VMEM((group // INNER_BWD, LANES, INNER_BWD), F32),

time: 590 us -> 591 us (level)
  transfers between devices with their start and end apart: 67 -> 67, of which waited for: 26 -> 27; matrix products, arithmetic and copies ran while one was open for 7% -> 7% of each run, Pallas kernels for 41% -> 41%
where the time goes in v6:
time: 591 us; the launch traced here: 582 us
  Pallas kernels  288 us (49%)
  waiting for transfers between devices  118 us (20%)
  starting transfers between devices  77.9 us (13%)
  other arithmetic  38.9 us (7%)
  matrix products  21.3 us (4%)
  local copies, waits for them, and re-layouts  18.8 us (3%)
  between operations  17.5 us (3%)
    ppermute x50, waiting for transfers between devices, swap(): return lax.ppermute(value, EVERY, flipped(axis_bit, count))  93.5 us
    pallas_call x2, Pallas kernels, attend_backward(): pl.pallas_call(functools.partial(attn_bwd_kernel, heads, size, group), gr...  49.6 us
    pallas_call x4, Pallas kernels, column_grads(): pl.pallas_call(functools.partial(column_grad_kernel, heads, items, split)...  42.8 us
    ppermute x50, starting transfers between devices, swap(): return lax.ppermute(value, EVERY, flipped(axis_bit, count))  42.3 us
    pallas_call x2, Pallas kernels, attend_forward(): pl.pallas_call(functools.partial(attn_fwd_kernel, heads, size, group), gr...  38.2 us
    pallas_call x2, Pallas kernels, front(): pl.pallas_call(functools.partial(front_kernel, size, ffn_steps, pieces),...  34.4 us
    all_to_all x8, starting transfers between devices, exchange(): lax.all_to_all(value, 'heads', split_axis=0, concat_axis=0, tiled=True, a...  34.1 us
    dot_general x7, matrix products, dot(): return lax.dot_general(left, right, dims, preferred_element_type=F32)  21.3 us
  transfers between devices with their start and end apart: 67, of which 27 were waited for; matrix products, arithmetic and copies ran while one was open for 7% of the time, Pallas kernels for 41%

profile of v6, /device:TPU:0, one launch (start us, length us, event | category | flops | bytes accessed | tf_op | source)
XLA Modules:
  0.0 581.8 jit_solution(12066595825567088539)
XLA Ops:
  8.4 28.6 %conditional.24 = (f32[512,1024]{1,0:T(8,128)}, bf16[512,4096]{1,0:T(8,128)(2,1)}, bf16[512,4096]{1,0:T(8,128)(2,1)}, bf16[512,1024]{1,0:T(8,128)(2,1)}, bf16[51...) conditional(s32[]{:T(128)} %convert_element_type.170, ...), branch_computations={%region_0.1_spmd, %region_1.2_spmd} | conditional | flops 5905580032 | bytes 34603160 | solution.py:792
  13.7 16.9 %front.2 = (f32[512,1024]{1,0:T(8,128)}, bf16[512,4096]{1,0:T(8,128)(2,1)}, bf16[512,4096]{1,0:T(8,128)(2,1)}, bf16[512,1024]{1,0:T(8,128)(2,1)}, bf16[512,1024]...) custom-call(s32[1]{0:T(128)} %bitcast.row_ref, ...), custom_call_target="tpu_custom_call" | custom-call | flops 5905580032 | bytes 31457280 | tf_op jit(solution)/shard_map/cond/branch_1_fun/front/pallas_call | solution.py:685
  30.6 6.4 %collective-permute-done.35 = bf16[256,1024]{1,0:T(8,128)(2,1)} collective-permute-done((bf16[256,1024]{1,0:T(8,128)(2,1)S(1)}, bf16[256,1024]{1,0:T(8,128)(2,1)}, u32[]{:S(2)}, u32[]{:S(2)}) %collective-permute-start.35) | collective-permute-done | bytes 524320 | tf_op jit(solution)/shard_map/cond/branch_1_fun/ppermute | solution.py:785
  37.0 17.5 %front.3 = (f32[512,1024]{1,0:T(8,128)}, bf16[512,4096]{1,0:T(8,128)(2,1)}, bf16[512,4096]{1,0:T(8,128)(2,1)}, bf16[512,1024]{1,0:T(8,128)(2,1)}, bf16[512,1024]...) custom-call(s32[1]{0:T(128)} %bitcast.19.row_ref, ...), custom_call_target="tpu_custom_call", output_to_operand_aliasing={{0}: (10, {}), {1}: (11, {}), {2}: (12, {}), {3}: (13, {}),... | custom-call | flops 5905580032 | bytes 31457280 | tf_op jit(solution)/shard_map/front/pallas_call | solution.py:685
  66.7 12.5 %all-to-all-done.6 = bf16[4,3,2,256,128]{4,3,2,1,0:T(8,128)(2,1)} async-done(((bf16[4,3,2,256,128]{4,3,2,1,0:T(8,128)(2,1)}), bf16[4,3,2,256,128]{4,3,2,1,0:T(8,128)(2,1)}, u32[]{:S(2)}, u32[]{:S(2)}) %all-to-all-start.6) | async-done | bytes 1572896 | tf_op jit(solution)/shard_map/all_to_all | solution.py:817
  79.1 24.8 %conditional.25 = (bf16[4,2,256,128]{3,2,1,0:T(8,128)(2,1)}, f32[2048,128]{1,0:T(8,128)}, bf16[2,2048,256]{2,1,0:T(8,128)(2,1)}, bf16[4,3,2,256,128]{4,3,2,1,0:T...) conditional(s32[]{:T(128)} %convert_element_type.170, ...), branch_computations={%region_2.3_spmd, %region_3.4_spmd} | conditional | flops 8589934592 | bytes 36176080 | solution.py:792
  84.4 19.1 %attend_forward.2 = (bf16[4,2,256,128]{3,2,1,0:T(8,128)(2,1)}, f32[2048,128]{1,0:T(8,128)}, bf16[2,2048,256]{2,1,0:T(8,128)(2,1)}) custom-call(s32[2]{0:T(128)S(1)} %get-tuple-element.543.counts_ref, bf16[4,3,2,256,128]{4,3,2,1,0:T(8,128)(2,1)} %get-tuple-element.544.qkv_ref), custom_call_target="tpu_custom_call" | custom-call | flops 8589934592 | bytes 6291456 | tf_op jit(solution)/shard_map/cond/branch_1_fun/attend_forward/pallas_call | solution.py:226
  104.0 30.8 %conditional.26 = (bf16[4,2,256,128]{3,2,1,0:T(8,128)(2,1)}, f32[2048,128]{1,0:T(8,128)}, bf16[2,2048,256]{2,1,0:T(8,128)(2,1)}, bf16[4,2,256,128]{3,2,1,0:T(8,128)(2,1)}, bf16[256,1024]{1,0:T(8,128)(2,1)}) conditional(s32[]{:T(128)} %convert_element_type.170, () %tuple.207, (s32[2]{0:T(128)S(1)}, bf16[4,3,2,256,128]{4,3,2,1,0:T(8,128)(2,1)}, ...), branch_computations={%region_4.5_spmd, %region_5.6_spmd} | conditional | flops 8589934592 | bytes 11010210 | solution.py:792
  110.2 19.1 %attend_forward.3 = (bf16[4,2,256,128]{3,2,1,0:T(8,128)(2,1)}, f32[2048,128]{1,0:T(8,128)}, bf16[2,2048,256]{2,1,0:T(8,128)(2,1)}) custom-call(s32[2]{0:T(128)S(1)} %get-tuple-element.552.counts_ref, bf16[4,3,2,256,128]{4,3,2,1,0:T(8,128)(2,1)} %get-tuple-element.553.qkv_ref), custom_call_target="tpu_custom_call" | custom-call | flops 8589934592 | bytes 6291456 | tf_op jit(solution)/shard_map/cond/branch_1_fun/attend_forward/pallas_call | solution.py:226
  129.3 5.5 collective-permute-done.36
  171.1 18.0 %ffn_forward.1 = (bf16[512,1024]{1,0:T(8,128)(2,1)}, f32[512,1024]{1,0:T(8,128)}, f32[1,1024]{1,0:T(1,128)}, bf16[512,4096]{1,0:T(8,128)(2,1)}, bf16[512,4096]{1...) custom-call(f32[512,1024]{1,0:T(8,128)S(1)} %convolution_add_fusion.x_ref, f32[1,1024]{1,0:T(1,128)S(1)} %get-tuple-element.1208.gain_ref, ...), custom_call_target="tpu_custom_call" | custom-call | flops 8589934592 | bytes 25165824 | tf_op jit(solution)/shard_map/ffn_forward/pallas_call | solution.py:392
  190.1 18.0 %conditional.27 = (f32[512,1024]{1,0:T(8,128)S(1)}, f32[1,1024]{1,0:T(1,128)}, bf16[512,1024]{1,0:T(8,128)(2,1)}, bf16[512,4096]{1,0:T(8,128)(2,1)}, bf16[512,40...) conditional(s32[]{:T(128)} %convert_element_type.170, () %tuple.211, (f32[512,1024]{1,0:T(8,128)S(1)}, ...), branch_computations={%region_10.11_spmd, %region_11.12_spmd} | conditional | flops 8589934592 | bytes 50331776 | solution.py:792
  190.6 17.4 %ffn_backward.1 = (f32[512,1024]{1,0:T(8,128)S(1)}, f32[1,1024]{1,0:T(1,128)}, bf16[512,1024]{1,0:T(8,128)(2,1)}, bf16[512,4096]{1,0:T(8,128)(2,1)}) custom-call(f32[512,1024]{1,0:T(8,128)S(1)} %get-tuple-element.560.x_ref, f32[1,1024]{1,0:T(1,128)S(1)} %get-tuple-element.561.gain_ref, f32[512,1024]{1,0:T(8,128)} %get-tuple-element.562.up_ref, ...), custom_call_target="tpu_custom_call" | custom-call | flops 8589934592 | bytes 29360128 | tf_op jit(solution)/shard_map/cond/branch_1_fun/ffn_backward/pallas_call | solution.py:449
  239.6 25.0 %conditional.28 = (bf16[512,1024]{1,0:T(8,128)(2,1)}, bf16[512,1024]{1,0:T(8,128)(2,1)}, bf16[512,1024]{1,0:T(8,128)(2,1)}, bf16[512,1024]{1,0:T(8,128)(2,1)}, b...) conditional(s32[]{:T(128)} %convert_element_type.170, ...), branch_computations={%region_16.17_spmd, %region_17.18_spmd} | conditional | flops 8589934592 | bytes 60293492 | solution.py:792
  245.2 9.2 %out_grad.2 = (bf16[2,4,64,1024]{3,2,1,0:T(8,128)(2,1)S(1)}, bf16[2,4,64,1024]{3,2,1,0:T(8,128)(2,1)S(1)}, bf16[2,4,64,1024]{3,2,1,0:T(8,128)(2,1)}, bf16[2,4,64,1024]{3,2,1,0:T(8,128)(2,1)}) custom-call(s32[2]{0:T(128)S(1)} %get-tuple-element.578.place_ref, bf16[512,1024]{1,0:T(8,128)(2,1)} %get-tuple-element.579.up_own, ...), custom_call_target="tpu_custom_call" | custom-call | flops 4294967296 | bytes 16777216 | tf_op jit(solution)/shard_map/cond/branch_1_fun/out_grad/pallas_call | solution.py:909
  254.4 10.2 %column_grads.4 = (bf16[2,4,64,1024]{3,2,1,0:T(8,128)(2,1)}, bf16[2,4,64,1024]{3,2,1,0:T(8,128)(2,1)}, bf16[2,4,64,1024]{3,2,1,0:T(8,128)(2,1)}, bf16[2,4,64,1024]{3,2,1,0:T(8,128)(2,1)}) custom-call(s32[2]{0:T(128)S(1)} %get-tuple-element.578.place_ref, bf16[512,1024]{1,0:T(8,128)(2,1)S(1)} %copy-done.43, bf16[512,1024]{1,0:T(8,128)(2,1)} %get-tuple-element.588.refs_1_, ...), custom_call_target="tpu_custom_call" | custom-call | flops 4294967296 | bytes 16777216 | tf_op jit(solution)/shard_map/cond/branch_1_fun/column_grads/pallas_call | solution.py:1012
  264.6 34.1 %conditional.29 = (bf16[4,3,2,256,128]{4,3,2,1,0:T(8,128)(2,1)}, bf16[4,2,256,128]{3,2,1,0:T(8,128)(2,1)}, bf16[256,1024]{1,0:T(8,128)(2,1)}, bf16[512,1024]{1,0...) conditional(s32[]{:T(128)} %convert_element_type.170, ...), branch_computations={%region_18.19_spmd, %region_19.22_spmd} | conditional | flops 17179869184 | bytes 29884820 | solution.py:792
  267.7 30.9 %conditional = (bf16[4,3,2,256,128]{4,3,2,1,0:T(8,128)(2,1)}, bf16[4,2,256,128]{3,2,1,0:T(8,128)(2,1)}, bf16[256,1024]{1,0:T(8,128)(2,1)}, bf16[512,1024]{1,0:T(8,128)(2,1)}, bf16[512,1024]{1,0:T(8,128)(2,1)}) conditional(s32[]{:T(128)} %convert_element_type.126, () %tuple.115, (s32[2]{0:T(128)S(1)}, bf16[4,3,2,256,128]{4,3,2,1,0:T(8,128)(2,1)}, ...), branch_computations={%region_20.20_spmd, %region_21.21_spmd} | conditional | flops 17179869184 | bytes 21496000 | solution.py:792
  273.7 24.7 %attend_backward.2 = bf16[4,3,2,256,128]{4,3,2,1,0:T(8,128)(2,1)} custom-call(s32[2]{0:T(128)S(1)} %get-tuple-element.595.counts_ref, bf16[4,3,2,256,128]{4,3,2,1,0:T(8,128)(2,1)} %get-tuple-element.596.qkv_ref, f32[2048,128]{1,0:T(8,128)} %get-tuple-element.597.full_ref, bf16[2,2048,256]{2,1,0:T(8,128)(2,1)} %get-tuple-element.598.qcat, ...), custom_call_target="tpu_custom_call" | custom-call | flops 17179869184 | bytes 9437184 | tf_op jit(solution)/shard_map/cond/branch_1_fun/cond/branch_1_fun/attend_backward/pallas_call | solution.py:329
  300.8 36.5 %conditional.30 = (bf16[4,3,2,256,128]{4,3,2,1,0:T(8,128)(2,1)}, bf16[4,3,2,256,128]{4,3,2,1,0:T(8,128)(2,1)}, bf16[4,64,1024]{2,1,0:T(8,128)(2,1)}, bf16[4,64,1...) conditional(s32[]{:T(128)} %convert_element_type.170, () %tuple.202, ...), branch_computations={%region_22.23_spmd, %region_23.26_spmd} | conditional | flops 17179869184 | bytes 26738996 | solution.py:792
  304.8 29.2 %conditional.1 = (bf16[4,3,2,256,128]{4,3,2,1,0:T(8,128)(2,1)}, bf16[4,3,2,256,128]{4,3,2,1,0:T(8,128)(2,1)}) conditional(s32[]{:T(128)} %convert_element_type.127, () %tuple.121, (s32[2]{0:T(128)S(1)}, bf16[4,3,2,256,128]{4,3,2,1,0:T(8,128)(2,1)}, f32[2048,128]{1,0:T(8,128)}, bf16[2,2048,256]{2,1,0:T(8,128)(2,1)}, ...), branch_computations={%region_24.24_spmd, %region_25.25_spmd} | conditional | flops 17179869184 | bytes 14155824 | solution.py:792
  309.2 24.8 %attend_backward.3 = bf16[4,3,2,256,128]{4,3,2,1,0:T(8,128)(2,1)} custom-call(s32[2]{0:T(128)S(1)} %get-tuple-element.621.counts_ref, bf16[4,3,2,256,128]{4,3,2,1,0:T(8,128)(2,1)} %get-tuple-element.622.qkv_ref, f32[2048,128]{1,0:T(8,128)} %get-tuple-element.623.full_ref, bf16[2,2048,256]{2,1,0:T(8,128)(2,1)} %get-tuple-element.624.qcat, ...), custom_call_target="tpu_custom_call" | custom-call | flops 17179869184 | bytes 9437184 | tf_op jit(solution)/shard_map/cond/branch_1_fun/cond/branch_1_fun/attend_backward/pallas_call | solution.py:329
  339.7 24.6 %conditional.31 = (bf16[4,3,2,256,128]{4,3,2,1,0:T(8,128)(2,1)}, bf16[2,4,64,1024]{3,2,1,0:T(8,128)(2,1)}, bf16[2,4,64,1024]{3,2,1,0:T(8,128)(2,1)}, bf16[2,4,64...) conditional(s32[]{:T(128)} %convert_element_type.170, ...), branch_computations={%region_26.27_spmd, %region_27.28_spmd} | conditional | flops 4294967296 | bytes 38273240 | solution.py:792
  346.3 13.1 %column_grads.5 = (bf16[2,4,64,1024]{3,2,1,0:T(8,128)(2,1)}, bf16[2,4,64,1024]{3,2,1,0:T(8,128)(2,1)}, bf16[2,4,64,1024]{3,2,1,0:T(8,128)(2,1)}, bf16[2,4,64,1024]{3,2,1,0:T(8,128)(2,1)}) custom-call(s32[2]{0:T(128)S(1)} %get-tuple-element.641.place_ref, bf16[512,1024]{1,0:T(8,128)(2,1)} %get-tuple-element.642.refs_0_, ...), custom_call_target="tpu_custom_call" | custom-call | flops 4294967296 | bytes 16777216 | tf_op jit(solution)/shard_map/cond/branch_1_fun/column_grads/pallas_call | solution.py:1012
  364.3 65.7 %conditional.32 = (bf16[128,1024]{1,0:T(8,128)(2,1)S(1)}, bf16[128,1024]{1,0:T(8,128)(2,1)S(1)}, bf16[2,4,64,1024]{3,2,1,0:T(8,128)(2,1)}, bf16[2,4,64,1024]{3,2...) conditional(s32[]{:T(128)} %convert_element_type.170, ...), branch_computations={%region_28.29_spmd, %region_29.43_spmd} | conditional | flops 15032385536 | bytes 124257496 | solution.py:792
  365.9 26.4 %conditional.5 = (bf16[512,3072]{1,0:T(8,128)(2,1)}, bf16[512,3072]{1,0:T(8,128)(2,1)}, f32[512,1024]{1,0:T(8,128)}, bf16[512,1024]{1,0:T(8,128)(2,1)}, f32[1,10...) conditional(s32[]{:T(128)} %convert_element_type.131, () %tuple.145, ...), branch_computations={%region_31.31_spmd, %region_32.34_spmd} | conditional | flops 3221225472 | bytes 38797596 | solution.py:792
  368.4 18.3 %conditional.2 = (bf16[512,3072]{1,0:T(8,128)(2,1)}, bf16[512,3072]{1,0:T(8,128)(2,1)}, f32[512,1024]{1,0:T(8,128)}, bf16[512,1024]{1,0:T(8,128)(2,1)}, f32[1,1024]{1,0:T(1,128)}) conditional(s32[]{:T(128)} %convert_element_type.128, () %tuple.130, (f32[512,128]{1,0:T(8,128)}, f32[512,128]{1,0:T(8,128)S(1)}, f32[512,1024]{1,0:T(8,128)}, ...), branch_computations={%region_33.32_spmd, %region_34.33_spmd} | conditional | flops 3221225472 | bytes 30408784 | solution.py:792
  368.4 12.2 %projection_backward.1 = (bf16[512,3072]{1,0:T(8,128)(2,1)}, f32[512,1024]{1,0:T(8,128)}, bf16[512,1024]{1,0:T(8,128)(2,1)}, f32[1,1024]{1,0:T(1,128)}) custom-call(f32[512,128]{1,0:T(8,128)} %get-tuple-element.672.cos_ref, f32[512,128]{1,0:T(8,128)S(1)} %get-tuple-element.673.sin_ref, f32[512,1024]{1,0:T(8,128)} %get-tuple-element.674.x_ref, ...), custom_call_target="tpu_custom_call" | custom-call | flops 3221225472 | bytes 17825792 | tf_op jit(solution)/shard_map/cond/branch_1_fun/cond/branch_1_fun/cond/branch_1_fun/projection_backward/pallas_call | solution.py:744
  380.7 6.0 %collective-permute-done.21 = bf16[512,3072]{1,0:T(8,128)(2,1)} collective-permute-done((bf16[512,3072]{1,0:T(8,128)(2,1)}, bf16[512,3072]{1,0:T(8,128)(2,1)}, u32[]{:S(2)}, u32[]{:S(2)}) %collective-permute-start.21) | collective-permute-done | bytes 3145760 | tf_op jit(solution)/shard_map/cond/branch_1_fun/cond/branch_1_fun/cond/branch_1_fun/ppermute | solution.py:785
  394.0 13.1 %conditional.6 = (bf16[512,1024]{1,0:T(8,128)(2,1)}, bf16[2,4,64,768]{3,2,1,0:T(8,128)(2,1)}, bf16[2,4,64,768]{3,2,1,0:T(8,128)(2,1)}, bf16[2,4,64,768]{3,2,1,0:...) conditional(s32[]{:T(128)} %convert_element_type.131, ...), branch_computations={%region_35.35_spmd, %region_36.38_spmd} | conditional | flops 3221225472 | bytes 20971788 | solution.py:792
  396.3 9.1 %conditional.3 = (bf16[512,1024]{1,0:T(8,128)(2,1)}, bf16[2,4,64,768]{3,2,1,0:T(8,128)(2,1)}, bf16[2,4,64,768]{3,2,1,0:T(8,128)(2,1)}, bf16[2,4,64,768]{3,2,1,0:T(8,128)(2,1)}, bf16[2,4,64,768]{3,2,1,0:T(8,128)(2,1)}) conditional(s32[]{:T(128)} %convert_element_type.129, () %tuple.136, (bf16[512,1024]{1,0:T(8,128)(2,1)}, s32[2]{0:T(128)S(1)}, ...), branch_computations={%region_37.36_spmd, %region_38.37_spmd} | conditional | flops 3221225472 | bytes 16777296 | solution.py:792
  396.3 9.1 %column_grads.6 = (bf16[2,4,64,768]{3,2,1,0:T(8,128)(2,1)}, bf16[2,4,64,768]{3,2,1,0:T(8,128)(2,1)}, bf16[2,4,64,768]{3,2,1,0:T(8,128)(2,1)}, bf16[2,4,64,768]{3,2,1,0:T(8,128)(2,1)}) custom-call(s32[2]{0:T(128)S(1)} %get-tuple-element.701.place_ref, bf16[512,1024]{1,0:T(8,128)(2,1)} %get-tuple-element.702.refs_0_, ...), custom_call_target="tpu_custom_call" | custom-call | flops 3221225472 | bytes 12582912 | tf_op jit(solution)/shard_map/cond/branch_1_fun/cond/branch_1_fun/cond/branch_1_fun/column_grads/pallas_call | solution.py:1012
  407.1 21.7 %conditional.7 = (bf16[512,4096]{1,0:T(8,128)(2,1)}, bf16[2,4,64,1024]{3,2,1,0:T(8,128)(2,1)}, bf16[2,4,64,1024]{3,2,1,0:T(8,128)(2,1)}, bf16[2,4,64,1024]{3,2,1...) conditional(s32[]{:T(128)} %convert_element_type.131, ...), branch_computations={%region_39.39_spmd, %region_40.42_spmd} | conditional | flops 8589934592 | bytes 44040428 | solution.py:792
  408.9 20.0 %conditional.4 = (bf16[512,4096]{1,0:T(8,128)(2,1)}, bf16[2,4,64,1024]{3,2,1,0:T(8,128)(2,1)}, bf16[2,4,64,1024]{3,2,1,0:T(8,128)(2,1)}, bf16[2,4,64,1024]{3,2,1,0:T(8,128)(2,1)}, bf16[2,4,64,1024]{3,2,1,0:T(8,128)(2,1)}) conditional(s32[]{:T(128)} %convert_element_type.130, () %tuple.142, (f32[512,1024]{1,0:T(8,128)}, ...), branch_computations={%region_41.40_spmd, %region_42.41_spmd} | conditional | flops 8589934592 | bytes 37748776 | solution.py:792
  408.9 10.4 %hidden_gradient.1 = (bf16[512,1024]{1,0:T(8,128)(2,1)}, bf16[512,4096]{1,0:T(8,128)(2,1)}) custom-call(f32[512,1024]{1,0:T(8,128)} %get-tuple-element.724.up_ref, bf16[512,4096]{1,0:T(8,128)(2,1)} %get-tuple-element.725.slope_ref, bf16[4096,1024]{1,0:T(8,128)(2,1)} %get-tuple-element.726.wout_ref), custom_call_target="tpu_custom_call" | custom-call | flops 4294967296 | bytes 20971520 | tf_op jit(solution)/shard_map/cond/branch_1_fun/cond/branch_1_fun/cond/branch_1_fun/hidden_gradient/pallas_call | solution.py:492
  419.4 9.5 %out_grad.3 = (bf16[2,4,64,1024]{3,2,1,0:T(8,128)(2,1)}, bf16[2,4,64,1024]{3,2,1,0:T(8,128)(2,1)}, bf16[2,4,64,1024]{3,2,1,0:T(8,128)(2,1)}, bf16[2,4,64,1024]{3,2,1,0:T(8,128)(2,1)}) custom-call(s32[2]{0:T(128)S(1)} %get-tuple-element.728.place_ref, bf16[512,1024]{1,0:T(8,128)(2,1)} %get-tuple-element.729.up_own, ...), custom_call_target="tpu_custom_call" | custom-call | flops 4294967296 | bytes 16777216 | tf_op jit(solution)/shard_map/cond/branch_1_fun/cond/branch_1_fun/cond/branch_1_fun/out_grad/pallas_call | solution.py:909
  432.5 34.6 %conditional.33 = (bf16[128,1024]{1,0:T(8,128)(2,1)}, bf16[2,4,64,1024]{3,2,1,0:T(8,128)(2,1)}, bf16[2,4,64,1024]{3,2,1,0:T(8,128)(2,1)}, bf16[2,4,64,1024]{3,2,...) conditional(s32[]{:T(128)} %convert_element_type.170, ...), branch_computations={%region_43.44_spmd, %region_44.48_spmd} | conditional | flops 8590458880 | bytes 67895824 | solution.py:792
  436.6 30.5 %conditional.8 = (bf16[128,1024]{1,0:T(8,128)(2,1)}, bf16[2,4,64,1024]{3,2,1,0:T(8,128)(2,1)}, bf16[2,4,64,1024]{3,2,1,0:T(8,128)(2,1)}, bf16[2,4,64,1024]{3,2,1...) conditional(s32[]{:T(128)} %convert_element_type.132, ...), branch_computations={%region_45.45_spmd, %region_46.47_spmd} | conditional | flops 8590458880 | bytes 56361112 | solution.py:792
  439.7 11.8 %stream_gradient.1 = (bf16[512,1024]{1,0:T(8,128)(2,1)}, bf16[512,1024]{1,0:T(8,128)(2,1)}, f32[1,1024]{1,0:T(1,128)}) custom-call(bf16[512,1024]{1,0:T(8,128)(2,1)S(1)} %get-tuple-element.811.x_ref, f32[1,1024]{1,0:T(1,128)S(1)} %get-tuple-element.812.gain_ref, f32[512,1024]{1,0:T(8,128)} %get-tuple-element.813.up_ref, ...), custom_call_target="tpu_custom_call" | custom-call | flops 4294967296 | bytes 12582912 | tf_op jit(solution)/shard_map/cond/branch_1_fun/cond/branch_1_fun/stream_gradient/pallas_call | solution.py:537
  453.8 10.5 %column_grads.7 = (bf16[2,4,64,1024]{3,2,1,0:T(8,128)(2,1)}, bf16[2,4,64,1024]{3,2,1,0:T(8,128)(2,1)}, bf16[2,4,64,1024]{3,2,1,0:T(8,128)(2,1)}, bf16[2,4,64,1024]{3,2,1,0:T(8,128)(2,1)}) custom-call(s32[2]{0:T(128)S(1)} %get-tuple-element.802.place_ref, bf16[512,1024]{1,0:T(8,128)(2,1)} %get-tuple-element.803.refs_0_, ...), custom_call_target="tpu_custom_call" | custom-call | flops 4294967296 | bytes 16777216 | tf_op jit(solution)/shard_map/cond/branch_1_fun/cond/branch_1_fun/column_grads/pallas_call | solution.py:1012
  469.8 103.1 %conditional.34 = (bf16[128,1024]{1,0:T(8,128)(2,1)}, f32[6,1024]{1,0:T(8,128)S(1)}, f32[5,1024]{1,0:T(8,128)S(1)}, bf16[2,256,1024]{2,1,0:T(8,128)(2,1)}, bf16[...) conditional(s32[]{:T(128)} %convert_element_type.170, ...), branch_computations={%region_50.51_spmd, %region_51.68_spmd} | conditional | flops 13521410 | bytes 66676600 | solution.py:792
  472.6 15.1 %conditional.12 = (bf16[4,64,1024]{2,1,0:T(8,128)(2,1)}, bf16[4,64,1024]{2,1,0:T(8,128)(2,1)}) conditional(s32[]{:T(128)} %convert_element_type.133, () %tuple.172, (bf16[4,64,1024]{2,1,0:T(8,128)(2,1)}, bf16[4,64,1024]{2,1,0:T(8,128)(2,1)}) %tuple.173), branch_computations={%region_65.65_spmd, %region_66.66_spmd} | conditional | bytes 4194400 | solution.py:792
  475.6 10.9 %collective-permute-done.33 = bf16[4,64,1024]{2,1,0:T(8,128)(2,1)} collective-permute-done((bf16[4,64,1024]{2,1,0:T(8,128)(2,1)}, bf16[4,64,1024]{2,1,0:T(8,128)(2,1)}, u32[]{:S(2)}, u32[]{:S(2)}) %collective-permute-start.33) | collective-permute-done | bytes 524320 | tf_op jit(solution)/shard_map/cond/branch_1_fun/cond/branch_1_fun/ppermute | solution.py:785
  491.9 25.0 %conditional.9 = (bf16[2,4,64,1024]{3,2,1,0:T(8,128)(2,1)}, bf16[2,4,64,1024]{3,2,1,0:T(8,128)(2,1)}) conditional(s32[]{:T(128)} %convert_element_type.133, () %tuple.168, (bf16[2,4,64,1024]{3,2,1,0:T(8,128)(2,1)}, bf16[2,4,64,1024]{3,2,1,0:T(8,128)(2,1)}) %tuple.169), branch_computations={%region_52.52_spmd, %region_53.53_spmd} | conditional | bytes 8388704 | solution.py:792
  493.9 21.8 %collective-permute-done.29 = bf16[2,4,64,1024]{3,2,1,0:T(8,128)(2,1)} collective-permute-done((bf16[2,4,64,1024]{3,2,1,0:T(8,128)(2,1)}, bf16[2,4,64,1024]{3,2,1,0:T(8,128)(2,1)}, u32[]{:S(2)}, u32[]{:S(2)}) %collective-permute-start.29) | collective-permute-done | bytes 1048608 | tf_op jit(solution)/shard_map/cond/branch_1_fun/cond/branch_1_fun/ppermute | solution.py:785
  518.6 11.7 %conditional.10 = (bf16[4,64,1024]{2,1,0:T(8,128)(2,1)}, bf16[4,64,1024]{2,1,0:T(8,128)(2,1)}) conditional(s32[]{:T(128)} %convert_element_type.133, () %tuple.170, (bf16[4,64,1024]{2,1,0:T(8,128)(2,1)S(1)}, bf16[4,64,1024]{2,1,0:T(8,128)(2,1)S(1)}) %second_sums.7), branch_computations={%region_54.54_spmd, %region_55.55_spmd} | conditional | bytes 4194400 | solution.py:792
  519.8 10.1 %collective-permute-done.31 = bf16[4,64,1024]{2,1,0:T(8,128)(2,1)} collective-permute-done((bf16[4,64,1024]{2,1,0:T(8,128)(2,1)S(1)}, bf16[4,64,1024]{2,1,0:T(8,128)(2,1)}, u32[]{:S(2)}, u32[]{:S(2)}) %collective-permute-start.31) | collective-permute-done | bytes 524320 | tf_op jit(solution)/shard_map/cond/branch_1_fun/cond/branch_1_fun/ppermute | solution.py:785
  552.2 6.5 %collective-permute-done.46 = f32[11,1024]{1,0:T(8,128)S(1)} collective-permute-done((f32[11,1024]{1,0:T(8,128)S(1)}, f32[11,1024]{1,0:T(8,128)S(1)}, u32[]{:S(2)}, u32[]{:S(2)}) %collective-permute-start.46) | collective-permute-done | bytes 45088 | tf_op jit(solution)/shard_map/cond/branch_1_fun/ppermute | solution.py:785
  (322 shorter events, 235.4 us)
Async XLA Ops:
  9.6 27.4 %collective-permute-start.35 = (bf16[256,1024]{1,0:T(8,128)(2,1)S(1)}, bf16[256,1024]{1,0:T(8,128)(2,1)}, u32[]{:S(2)}, u32[]{:S(2)}) collective-permute-start(bf16[256,1024]{1,0:T(8,128)(2,1)S(1)} %dynamic-slice_bitcast_fusion), channel_id=1, source_target_pairs={{0,4},{1,5},{2,6},{3,7},{4,0},{5,1},{6,2},{7,3},{8,12},{9,13},{10,... | collective-permute-start | bytes 1572872 | tf_op jit(solution)/shard_map/cond/branch_1_fun/ppermute | solution.py:785
  54.5 24.6 %all-to-all-start.6 = ((bf16[4,3,2,256,128]{4,3,2,1,0:T(8,128)(2,1)}), bf16[4,3,2,256,128]{4,3,2,1,0:T(8,128)(2,1)}, u32[]{:S(2)}, u32[]{:S(2)}) async-start(bf16[4,3,2,256,128]{4,3,2,1,0:T(8,128)(2,1)} %get-tuple-element.1045), calls=%async_computation.11 | async-start | bytes 3145728 | tf_op jit(solution)/shard_map/all_to_all | solution.py:817
  79.1 24.8 %collective-permute-start = (bf16[512,4096]{1,0:T(8,128)(2,1)}, bf16[512,4096]{1,0:T(8,128)(2,1)}, u32[]{:S(2)}, u32[]{:S(2)}) collective-permute-start(bf16[512,4096]{1,0:T(8,128)(2,1)} %get-tuple-element.549), channel_id=1, source_target_pairs={{0,1},{1,0},{2,3},{3,2},{4,5},{5,4},{6,7},{7,6},{8,9},{9,8},{10,11... | collective-permute-start | bytes 12582920 | tf_op jit(solution)/shard_map/cond/branch_1_fun/ppermute | solution.py:785
  79.1 24.8 %all-to-all-start = ((bf16[4,3,2,256,128]{4,3,2,1,0:T(8,128)(2,1)}), bf16[4,3,2,256,128]{4,3,2,1,0:T(8,128)(2,1)}, u32[]{:S(2)}, u32[]{:S(2)}) async-start(bf16[4,3,2,256,128]{4,3,2,1,0:T(8,128)(2,1)} %get-tuple-element.548), calls=%async_computation | async-start | bytes 3145728 | tf_op jit(solution)/shard_map/cond/branch_1_fun/all_to_all | solution.py:817
  83.8 19.8 %collective-permute-start.1 = (bf16[512,1024]{1,0:T(8,128)(2,1)}, bf16[512,1024]{1,0:T(8,128)(2,1)}, u32[]{:S(2)}, u32[]{:S(2)}) collective-permute-start(bf16[512,1024]{1,0:T(8,128)(2,1)} %get-tuple-element.550), channel_id=1, source_target_pairs={{0,1},{1,0},{2,3},{3,2},{4,5},{5,4},{6,7},{7,6},{8,9},{9,8},{10,11... | collective-permute-start | bytes 3145736 | tf_op jit(solution)/shard_map/cond/branch_1_fun/ppermute | solution.py:785
  84.4 19.2 %collective-permute-start.2 = (bf16[512,1024]{1,0:T(8,128)(2,1)}, bf16[512,1024]{1,0:T(8,128)(2,1)}, u32[]{:S(2)}, u32[]{:S(2)}) collective-permute-start(bf16[512,1024]{1,0:T(8,128)(2,1)} %get-tuple-element.551), channel_id=1, source_target_pairs={{0,1},{1,0},{2,3},{3,2},{4,5},{5,4},{6,7},{7,6},{8,9},{9,8},{10,11... | collective-permute-start | bytes 3145736 | tf_op jit(solution)/shard_map/cond/branch_1_fun/ppermute | solution.py:785
  104.0 30.8 %all-to-all-start.5 = ((bf16[4,2,256,128]{3,2,1,0:T(8,128)(2,1)}), bf16[4,2,256,128]{3,2,1,0:T(8,128)(2,1)}, u32[]{:S(2)}, u32[]{:S(2)}) async-start(bf16[4,2,256,128]{3,2,1,0:T(8,128)(2,1)} %get-tuple-element.557), calls=%async_computation.5 | async-start | bytes 1048576 | tf_op jit(solution)/shard_map/cond/branch_1_fun/all_to_all | solution.py:817
  108.2 26.6 %collective-permute-start.36 = (bf16[256,1024]{1,0:T(8,128)(2,1)S(1)}, bf16[256,1024]{1,0:T(8,128)(2,1)}, u32[]{:S(2)}, u32[]{:S(2)}) collective-permute-start(bf16[256,1024]{1,0:T(8,128)(2,1)S(1)} %dynamic-slice_bitcast_fusion.1), channel_id=1, source_target_pairs={{0,4},{1,5},{2,6},{3,7},{4,0},{5,1},{6,2},{7,3},{8,12},{9,13},{10,... | collective-permute-start | bytes 1572872 | tf_op jit(solution)/shard_map/cond/branch_1_fun/ppermute | solution.py:785
  190.1 17.9 %collective-permute-start.3 = (bf16[512,4096]{1,0:T(8,128)(2,1)}, bf16[512,4096]{1,0:T(8,128)(2,1)}, u32[]{:S(2)}, u32[]{:S(2)}) collective-permute-start(bf16[512,4096]{1,0:T(8,128)(2,1)} %get-tuple-element.570), channel_id=1, source_target_pairs={{0,1},{1,0},{2,3},{3,2},{4,5},{5,4},{6,7},{7,6},{8,9},{9,8},{10,11... | collective-permute-start | bytes 12582920 | tf_op jit(solution)/shard_map/cond/branch_1_fun/ppermute | solution.py:785
  190.1 17.9 %collective-permute-start.4 = (bf16[512,1024]{1,0:T(8,128)(2,1)S(1)}, bf16[512,1024]{1,0:T(8,128)(2,1)}, u32[]{:S(2)}, u32[]{:S(2)}) collective-permute-start(bf16[512,1024]{1,0:T(8,128)(2,1)S(1)} %get-tuple-element.571), channel_id=1, source_target_pairs={{0,1},{1,0},{2,3},{3,2},{4,5},{5,4},{6,7},{7,6},{8,9},{9,8},{10,11... | collective-permute-start | bytes 3145736 | tf_op jit(solution)/shard_map/cond/branch_1_fun/ppermute | solution.py:785
  214.8 24.9 %collective-permute-start.53 = (bf16[512,4096]{1,0:T(8,128)(2,1)}, bf16[512,4096]{1,0:T(8,128)(2,1)}, u32[]{:S(2)}, u32[]{:S(2)}) collective-permute-start(bf16[512,4096]{1,0:T(8,128)(2,1)} %get-tuple-element.1069), channel_id=1, source_target_pairs={{0,1},{1,0},{2,3},{3,2},{4,5},{5,4},{6,7},{7,6},{8,9},{9,8},{10,11... | collective-permute-start | bytes 12582920 | tf_op jit(solution)/shard_map/ppermute | solution.py:785
  217.9 21.7 %collective-permute-start.52 = (bf16[512,1024]{1,0:T(8,128)(2,1)}, bf16[512,1024]{1,0:T(8,128)(2,1)}, u32[]{:S(2)}, u32[]{:S(2)}) collective-permute-start(bf16[512,1024]{1,0:T(8,128)(2,1)} %get-tuple-element.1066), channel_id=1, source_target_pairs={{0,1},{1,0},{2,3},{3,2},{4,5},{5,4},{6,7},{7,6},{8,9},{9,8},{10,11... | collective-permute-start | bytes 3145736 | tf_op jit(solution)/shard_map/ppermute | solution.py:785
  239.6 24.9 %collective-permute-start.5 = (bf16[512,1024]{1,0:T(8,128)(2,1)}, bf16[512,1024]{1,0:T(8,128)(2,1)}, u32[]{:S(2)}, u32[]{:S(2)}) collective-permute-start(bf16[512,1024]{1,0:T(8,128)(2,1)} %get-tuple-element.572), channel_id=1, source_target_pairs={{0,1},{1,0},{2,3},{3,2},{4,5},{5,4},{6,7},{7,6},{8,9},{9,8},{10,11... | collective-permute-start | bytes 3145736 | tf_op jit(solution)/shard_map/cond/branch_1_fun/ppermute | solution.py:785
  239.8 24.7 %collective-permute-start.6 = (bf16[512,1024]{1,0:T(8,128)(2,1)}, bf16[512,1024]{1,0:T(8,128)(2,1)}, u32[]{:S(2)}, u32[]{:S(2)}) collective-permute-start(bf16[512,1024]{1,0:T(8,128)(2,1)} %get-tuple-element.573), channel_id=1, source_target_pairs={{0,1},{1,0},{2,3},{3,2},{4,5},{5,4},{6,7},{7,6},{8,9},{9,8},{10,11... | collective-permute-start | bytes 3145736 | tf_op jit(solution)/shard_map/cond/branch_1_fun/ppermute | solution.py:785
  240.2 24.3 %collective-permute-start.7 = (bf16[512,1024]{1,0:T(8,128)(2,1)}, bf16[512,1024]{1,0:T(8,128)(2,1)}, u32[]{:S(2)}, u32[]{:S(2)}) collective-permute-start(bf16[512,1024]{1,0:T(8,128)(2,1)} %get-tuple-element.574), channel_id=1, source_target_pairs={{0,1},{1,0},{2,3},{3,2},{4,5},{5,4},{6,7},{7,6},{8,9},{9,8},{10,11... | collective-permute-start | bytes 3145736 | tf_op jit(solution)/shard_map/cond/branch_1_fun/ppermute | solution.py:785
  240.3 24.2 %collective-permute-start.8 = (bf16[512,1024]{1,0:T(8,128)(2,1)}, bf16[512,1024]{1,0:T(8,128)(2,1)}, u32[]{:S(2)}, u32[]{:S(2)}) collective-permute-start(bf16[512,1024]{1,0:T(8,128)(2,1)} %get-tuple-element.575), channel_id=1, source_target_pairs={{0,1},{1,0},{2,3},{3,2},{4,5},{5,4},{6,7},{7,6},{8,9},{9,8},{10,11... | collective-permute-start | bytes 3145736 | tf_op jit(solution)/shard_map/cond/branch_1_fun/ppermute | solution.py:785
  240.7 23.9 %collective-permute-start.9 = (bf16[512,1024]{1,0:T(8,128)(2,1)}, bf16[512,1024]{1,0:T(8,128)(2,1)}, u32[]{:S(2)}, u32[]{:S(2)}) collective-permute-start(bf16[512,1024]{1,0:T(8,128)(2,1)} %get-tuple-element.576), channel_id=1, source_target_pairs={{0,1},{1,0},{2,3},{3,2},{4,5},{5,4},{6,7},{7,6},{8,9},{9,8},{10,11... | collective-permute-start | bytes 3145736 | tf_op jit(solution)/shard_map/cond/branch_1_fun/ppermute | solution.py:785
  240.9 23.7 %all-to-all-start.1 = ((bf16[4,2,256,128]{3,2,1,0:T(8,128)(2,1)}), bf16[4,2,256,128]{3,2,1,0:T(8,128)(2,1)}, u32[]{:S(2)}, u32[]{:S(2)}) async-start(bf16[4,2,256,128]{3,2,1,0:T(8,128)(2,1)} %get-tuple-element.577), calls=%async_computation.1 | async-start | bytes 1048576 | tf_op jit(solution)/shard_map/cond/branch_1_fun/all_to_all | solution.py:817
  264.6 34.1 %collective-permute-start.13 = (bf16[2,4,64,1024]{3,2,1,0:T(8,128)(2,1)}, bf16[2,4,64,1024]{3,2,1,0:T(8,128)(2,1)}, u32[]{:S(2)}, u32[]{:S(2)}) collective-permute-start(bf16[2,4,64,1024]{3,2,1,0:T(8,128)(2,1)} %get-tuple-element.619), channel_id=1, source_target_pairs={{0,8},{1,9},{2,10},{3,11},{4,12},{5,13},{6,14},{7,15},{8,0},{9,1},... | collective-permute-start | bytes 3145736 | tf_op jit(solution)/shard_map/cond/branch_1_fun/ppermute | solution.py:785
  266.2 32.5 %collective-permute-start.14 = (bf16[2,4,64,1024]{3,2,1,0:T(8,128)(2,1)}, bf16[2,4,64,1024]{3,2,1,0:T(8,128)(2,1)}, u32[]{:S(2)}, u32[]{:S(2)}) collective-permute-start(bf16[2,4,64,1024]{3,2,1,0:T(8,128)(2,1)} %get-tuple-element.620), channel_id=1, source_target_pairs={{0,16},{1,17},{2,18},{3,19},{4,20},{5,21},{6,22},{7,23},{8,24},{9,... | collective-permute-start | bytes 3145736 | tf_op jit(solution)/shard_map/cond/branch_1_fun/ppermute | solution.py:785
  267.7 30.9 %all-to-all-start.2 = ((bf16[4,2,256,128]{3,2,1,0:T(8,128)(2,1)}), bf16[4,2,256,128]{3,2,1,0:T(8,128)(2,1)}, u32[]{:S(2)}, u32[]{:S(2)}) async-start(bf16[4,2,256,128]{3,2,1,0:T(8,128)(2,1)} %get-tuple-element.600), calls=%async_computation.2 | async-start | bytes 1048576 | tf_op jit(solution)/shard_map/cond/branch_1_fun/cond/branch_1_fun/all_to_all | solution.py:817
  271.9 26.8 %collective-permute-start.10 = (bf16[256,1024]{1,0:T(8,128)(2,1)}, bf16[256,1024]{1,0:T(8,128)(2,1)}, u32[]{:S(2)}, u32[]{:S(2)}) collective-permute-start(bf16[256,1024]{1,0:T(8,128)(2,1)} %get-tuple-element.601), channel_id=1, source_target_pairs={{0,4},{1,5},{2,6},{3,7},{4,0},{5,1},{6,2},{7,3},{8,12},{9,13},{10,... | collective-permute-start | bytes 1572872 | tf_op jit(solution)/shard_map/cond/branch_1_fun/cond/branch_1_fun/ppermute | solution.py:785
  273.2 25.5 %collective-permute-start.11 = (bf16[512,1024]{1,0:T(8,128)(2,1)}, bf16[512,1024]{1,0:T(8,128)(2,1)}, u32[]{:S(2)}, u32[]{:S(2)}) collective-permute-start(bf16[512,1024]{1,0:T(8,128)(2,1)} %get-tuple-element.602), channel_id=1, source_target_pairs={{0,1},{1,0},{2,3},{3,2},{4,5},{5,4},{6,7},{7,6},{8,9},{9,8},{10,11... | collective-permute-start | bytes 3145736 | tf_op jit(solution)/shard_map/cond/branch_1_fun/cond/branch_1_fun/ppermute | solution.py:785
  273.3 25.4 %collective-permute-start.12 = (bf16[512,1024]{1,0:T(8,128)(2,1)}, bf16[512,1024]{1,0:T(8,128)(2,1)}, u32[]{:S(2)}, u32[]{:S(2)}) collective-permute-start(bf16[512,1024]{1,0:T(8,128)(2,1)} %get-tuple-element.603), channel_id=1, source_target_pairs={{0,1},{1,0},{2,3},{3,2},{4,5},{5,4},{6,7},{7,6},{8,9},{9,8},{10,11... | collective-permute-start | bytes 3145736 | tf_op jit(solution)/shard_map/cond/branch_1_fun/cond/branch_1_fun/ppermute | solution.py:785
  300.8 36.5 %collective-permute-start.17 = (bf16[2,4,64,1024]{3,2,1,0:T(8,128)(2,1)}, bf16[2,4,64,1024]{3,2,1,0:T(8,128)(2,1)}, u32[]{:S(2)}, u32[]{:S(2)}) collective-permute-start(bf16[2,4,64,1024]{3,2,1,0:T(8,128)(2,1)} %get-tuple-element.638), channel_id=1, source_target_pairs={{0,8},{1,9},{2,10},{3,11},{4,12},{5,13},{6,14},{7,15},{8,0},{9,1},... | collective-permute-start | bytes 3145736 | tf_op jit(solution)/shard_map/cond/branch_1_fun/ppermute | solution.py:785
  301.3 36.0 %collective-permute-start.18 = (bf16[2,4,64,1024]{3,2,1,0:T(8,128)(2,1)}, bf16[2,4,64,1024]{3,2,1,0:T(8,128)(2,1)}, u32[]{:S(2)}, u32[]{:S(2)}) collective-permute-start(bf16[2,4,64,1024]{3,2,1,0:T(8,128)(2,1)} %get-tuple-element.639), channel_id=1, source_target_pairs={{0,16},{1,17},{2,18},{3,19},{4,20},{5,21},{6,22},{7,23},{8,24},{9,... | collective-permute-start | bytes 3145736 | tf_op jit(solution)/shard_map/cond/branch_1_fun/ppermute | solution.py:785
  301.8 35.5 %collective-permute-start.15 = (bf16[4,64,1024]{2,1,0:T(8,128)(2,1)}, bf16[4,64,1024]{2,1,0:T(8,128)(2,1)}, u32[]{:S(2)}, u32[]{:S(2)}) collective-permute-start(bf16[4,64,1024]{2,1,0:T(8,128)(2,1)} %get-tuple-element.636), channel_id=1, source_target_pairs={{0,16},{1,17},{2,18},{3,19},{4,20},{5,21},{6,22},{7,23},{8,24},{9,... | collective-permute-start | bytes 1572872 | tf_op jit(solution)/shard_map/cond/branch_1_fun/ppermute | solution.py:785
  303.3 34.0 %collective-permute-start.16 = (bf16[4,64,1024]{2,1,0:T(8,128)(2,1)}, bf16[4,64,1024]{2,1,0:T(8,128)(2,1)}, u32[]{:S(2)}, u32[]{:S(2)}) collective-permute-start(bf16[4,64,1024]{2,1,0:T(8,128)(2,1)} %get-tuple-element.637), channel_id=1, source_target_pairs={{0,8},{1,9},{2,10},{3,11},{4,12},{5,13},{6,14},{7,15},{8,0},{9,1},... | collective-permute-start | bytes 1572872 | tf_op jit(solution)/shard_map/cond/branch_1_fun/ppermute | solution.py:785
  304.8 29.2 %all-to-all-start.3 = ((bf16[4,3,2,256,128]{4,3,2,1,0:T(8,128)(2,1)}), bf16[4,3,2,256,128]{4,3,2,1,0:T(8,128)(2,1)}, u32[]{:S(2)}, u32[]{:S(2)}) async-start(bf16[4,3,2,256,128]{4,3,2,1,0:T(8,128)(2,1)} %get-tuple-element.626), calls=%async_computation.3 | async-start | bytes 3145728 | tf_op jit(solution)/shard_map/cond/branch_1_fun/cond/branch_1_fun/all_to_all | solution.py:817
  339.7 24.6 %all-to-all-start.4 = ((bf16[4,3,2,256,128]{4,3,2,1,0:T(8,128)(2,1)}), bf16[4,3,2,256,128]{4,3,2,1,0:T(8,128)(2,1)}, u32[]{:S(2)}, u32[]{:S(2)}) async-start(bf16[4,3,2,256,128]{4,3,2,1,0:T(8,128)(2,1)} %get-tuple-element.640), calls=%async_computation.4 | async-start | bytes 3145728 | tf_op jit(solution)/shard_map/cond/branch_1_fun/all_to_all | solution.py:817
  344.2 15.2 %collective-permute-start.19 = (bf16[4,64,1024]{2,1,0:T(8,128)(2,1)}, bf16[4,64,1024]{2,1,0:T(8,128)(2,1)S(1)}, u32[]{:S(2)}, u32[]{:S(2)}) collective-permute-start(bf16[4,64,1024]{2,1,0:T(8,128)(2,1)} %get-tuple-element.668), channel_id=1, source_target_pairs={{0,16},{1,17},{2,18},{3,19},{4,20},{5,21},{6,22},{7,23},{8,24},{9,... | collective-permute-start | bytes 1572872 | tf_op jit(solution)/shard_map/cond/branch_1_fun/ppermute | solution.py:785
  364.4 64.6 %reduce-scatter.6.cloned.1.call-start = ((), (), s32[]{:S(2)}) async-start(), calls=%async_computation.13 | async-start | bytes 2621440 | tf_op jit(solution)/shard_map/cond/branch_1_fun/reduce_scatter | solution.py:1132
  365.9 25.1 %collective-permute-start.22 = (bf16[2,4,64,1024]{3,2,1,0:T(8,128)(2,1)}, bf16[2,4,64,1024]{3,2,1,0:T(8,128)(2,1)}, u32[]{:S(2)}, u32[]{:S(2)}) collective-permute-start(bf16[2,4,64,1024]{3,2,1,0:T(8,128)(2,1)} %get-tuple-element.698), channel_id=1, source_target_pairs={{0,8},{1,9},{2,10},{3,11},{4,12},{5,13},{6,14},{7,15},{8,0},{9,1},... | collective-permute-start | bytes 3145736 | tf_op jit(solution)/shard_map/cond/branch_1_fun/cond/branch_1_fun/ppermute | solution.py:785
  367.6 24.7 %collective-permute-start.23 = (bf16[2,4,64,1024]{3,2,1,0:T(8,128)(2,1)}, bf16[2,4,64,1024]{3,2,1,0:T(8,128)(2,1)}, u32[]{:S(2)}, u32[]{:S(2)}) collective-permute-start(bf16[2,4,64,1024]{3,2,1,0:T(8,128)(2,1)} %get-tuple-element.699), channel_id=1, source_target_pairs={{0,16},{1,17},{2,18},{3,19},{4,20},{5,21},{6,22},{7,23},{8,24},{9,... | collective-permute-start | bytes 3145736 | tf_op jit(solution)/shard_map/cond/branch_1_fun/cond/branch_1_fun/ppermute | solution.py:785
  407.1 21.7 %collective-permute-start.27 = (bf16[2,4,64,768]{3,2,1,0:T(8,128)(2,1)}, bf16[2,4,64,768]{3,2,1,0:T(8,128)(2,1)}, u32[]{:S(2)}, u32[]{:S(2)}) collective-permute-start(bf16[2,4,64,768]{3,2,1,0:T(8,128)(2,1)} %get-tuple-element.750), channel_id=1, source_target_pairs={{0,8},{1,9},{2,10},{3,11},{4,12},{5,13},{6,14},{7,15},{8,0},{9,1},... | collective-permute-start | bytes 2359304 | tf_op jit(solution)/shard_map/cond/branch_1_fun/cond/branch_1_fun/ppermute | solution.py:785
  408.6 20.3 %collective-permute-start.28 = (bf16[2,4,64,768]{3,2,1,0:T(8,128)(2,1)}, bf16[2,4,64,768]{3,2,1,0:T(8,128)(2,1)}, u32[]{:S(2)}, u32[]{:S(2)}) collective-permute-start(bf16[2,4,64,768]{3,2,1,0:T(8,128)(2,1)} %get-tuple-element.751), channel_id=1, source_target_pairs={{0,16},{1,17},{2,18},{3,19},{4,20},{5,21},{6,22},{7,23},{8,24},{9,... | collective-permute-start | bytes 2359304 | tf_op jit(solution)/shard_map/cond/branch_1_fun/cond/branch_1_fun/ppermute | solution.py:785
  432.5 34.6 %collective-permute-start.38 = (bf16[2,4,64,1024]{3,2,1,0:T(8,128)(2,1)}, bf16[2,4,64,1024]{3,2,1,0:T(8,128)(2,1)}, u32[]{:S(2)}, u32[]{:S(2)}) collective-permute-start(bf16[2,4,64,1024]{3,2,1,0:T(8,128)(2,1)} %get-tuple-element.841), channel_id=1, source_target_pairs={{0,8},{1,9},{2,10},{3,11},{4,12},{5,13},{6,14},{7,15},{8,0},{9,1},... | collective-permute-start | bytes 3145736 | tf_op jit(solution)/shard_map/cond/branch_1_fun/ppermute | solution.py:785
  433.9 33.2 %collective-permute-start.39 = (bf16[2,4,64,1024]{3,2,1,0:T(8,128)(2,1)}, bf16[2,4,64,1024]{3,2,1,0:T(8,128)(2,1)}, u32[]{:S(2)}, u32[]{:S(2)}) collective-permute-start(bf16[2,4,64,1024]{3,2,1,0:T(8,128)(2,1)} %get-tuple-element.842), channel_id=1, source_target_pairs={{0,16},{1,17},{2,18},{3,19},{4,20},{5,21},{6,22},{7,23},{8,24},{9,... | collective-permute-start | bytes 3145736 | tf_op jit(solution)/shard_map/cond/branch_1_fun/ppermute | solution.py:785
  434.8 32.3 %collective-permute-start.40 = (bf16[4,64,768]{2,1,0:T(8,128)(2,1)S(1)}, bf16[4,64,768]{2,1,0:T(8,128)(2,1)}, u32[]{:S(2)}, u32[]{:S(2)}) collective-permute-start(bf16[4,64,768]{2,1,0:T(8,128)(2,1)S(1)} %get-tuple-element.843), channel_id=1, source_target_pairs={{0,16},{1,17},{2,18},{3,19},{4,20},{5,21},{6,22},{7,23},{8,24},{9,... | collective-permute-start | bytes 1179656 | tf_op jit(solution)/shard_map/cond/branch_1_fun/ppermute | solution.py:785
  436.0 31.1 %collective-permute-start.41 = (bf16[4,64,768]{2,1,0:T(8,128)(2,1)}, bf16[4,64,768]{2,1,0:T(8,128)(2,1)}, u32[]{:S(2)}, u32[]{:S(2)}) collective-permute-start(bf16[4,64,768]{2,1,0:T(8,128)(2,1)} %get-tuple-element.844), channel_id=1, source_target_pairs={{0,8},{1,9},{2,10},{3,11},{4,12},{5,13},{6,14},{7,15},{8,0},{9,1},... | collective-permute-start | bytes 1179656 | tf_op jit(solution)/shard_map/cond/branch_1_fun/ppermute | solution.py:785
  436.6 30.5 %reduce-scatter.8.cloned.1.call-start = ((), (), s32[]{:S(2)}) async-start(), calls=%async_computation.14 | async-start | bytes 1310720 | tf_op jit(solution)/shard_map/cond/branch_1_fun/cond/branch_1_fun/reduce_scatter | solution.py:1132
  436.6 17.1 %collective-permute-start.37 = (bf16[512,4096]{1,0:T(8,128)(2,1)}, bf16[512,4096]{1,0:T(8,128)(2,1)}, u32[]{:S(2)}, u32[]{:S(2)}) collective-permute-start(bf16[512,4096]{1,0:T(8,128)(2,1)} %get-tuple-element.805.refs_2_.grad_ref), channel_id=1, source_target_pairs={{0,1},{1,0},{2,3},{3,2},{4,5},{5,4},{6,7},{7,6},{8,9},{9,8},{10,11... | collective-permute-start | bytes 12582920 | tf_op jit(solution)/shard_map/cond/branch_1_fun/cond/branch_1_fun/ppermute | solution.py:785
  469.8 99.5 %reduce-scatter.12.cloned.1.call-start = ((), (), s32[]{:S(2)}) async-start(), calls=%async_computation.16 | async-start | bytes 983040 | tf_op jit(solution)/shard_map/cond/branch_1_fun/reduce_scatter | solution.py:1132
  472.5 98.5 %reduce-scatter.14.cloned.1.call-start = ((), (), s32[]{:S(2)}) async-start(), calls=%async_computation.17 | async-start | bytes 1310720 | tf_op jit(solution)/shard_map/cond/branch_1_fun/reduce_scatter | solution.py:1132
  490.5 82.4 %reduce-scatter.10.cloned.1.call-start = ((), (), s32[]{:S(2)}) async-start(), calls=%async_computation.15 | async-start | bytes 1310720 | tf_op jit(solution)/shard_map/cond/branch_1_fun/reduce_scatter | solution.py:1132
  490.6 42.4 %collective-permute-start.42 = (bf16[256,1024]{1,0:T(8,128)(2,1)}, bf16[256,1024]{1,0:T(8,128)(2,1)}, u32[]{:S(2)}, u32[]{:S(2)}) collective-permute-start(bf16[256,1024]{1,0:T(8,128)(2,1)} %get-tuple-element.867), channel_id=1, source_target_pairs={{0,4},{1,5},{2,6},{3,7},{4,0},{5,1},{6,2},{7,3},{8,12},{9,13},{10,... | collective-permute-start | bytes 1572872 | tf_op jit(solution)/shard_map/cond/branch_1_fun/ppermute | solution.py:785
  491.9 23.8 %collective-permute-start.29 = (bf16[2,4,64,1024]{3,2,1,0:T(8,128)(2,1)}, bf16[2,4,64,1024]{3,2,1,0:T(8,128)(2,1)}, u32[]{:S(2)}, u32[]{:S(2)}) collective-permute-start(bf16[2,4,64,1024]{3,2,1,0:T(8,128)(2,1)} %get-tuple-element.845), channel_id=1, source_target_pairs={{0,8},{1,9},{2,10},{3,11},{4,12},{5,13},{6,14},{7,15},{8,0},{9,1},... | collective-permute-start | bytes 3145736 | tf_op jit(solution)/shard_map/cond/branch_1_fun/cond/branch_1_fun/ppermute | solution.py:785
  493.4 23.5 %collective-permute-start.30 = (bf16[2,4,64,1024]{3,2,1,0:T(8,128)(2,1)}, bf16[2,4,64,1024]{3,2,1,0:T(8,128)(2,1)}, u32[]{:S(2)}, u32[]{:S(2)}) collective-permute-start(bf16[2,4,64,1024]{3,2,1,0:T(8,128)(2,1)} %get-tuple-element.846), channel_id=1, source_target_pairs={{0,16},{1,17},{2,18},{3,19},{4,20},{5,21},{6,22},{7,23},{8,24},{9,... | collective-permute-start | bytes 3145736 | tf_op jit(solution)/shard_map/cond/branch_1_fun/cond/branch_1_fun/ppermute | solution.py:785
  (64 other events, 607.7 us)
Sparse Core Ops, SparseCore 0:
  367.5 43.8 reduce-scatter.5
  440.4 26.6 reduce-scatter.7
  473.0 23.4 reduce-scatter.11
  498.8 34.7 reduce-scatter.13
  537.9 28.9 reduce-scatter.9
